TPU v7x, 32 devices: a whole 2x2x4 slice. The times are simulated.
32 devices in a mesh: seq: 8 (over z, x), shard: 4 (over y, core).
Axes of the slice: x: 2, y: 2, z: 4, core: 2. Of those that a mesh axis runs over, the one named last changes fastest.
Arguments:
- tokens: bfloat16 [32768, 640], P(('seq', 'shard')), may hold values from -6 to 6
- query_weight: bfloat16 [640, 1024], P('shard')
- key_weight: bfloat16 [640, 256], P('shard')
- value_weight: bfloat16 [640, 256], P('shard'), may hold values from -0.25 to 0.25
- out_weight: bfloat16 [1024, 640], P('shard'), may hold values from -0.1875 to 0.1875
- gate_weight: bfloat16 [640, 2048], P('shard'), may hold values from -0.25 to 0.25
- up_weight: bfloat16 [640, 2048], P('shard'), may hold values from -0.25 to 0.25
- down_weight: bfloat16 [2048, 640], P('shard'), may hold values from -0.125 to 0.125
- input_gain: bfloat16 [640], P('shard'), may hold values from 0.25 to 1.75
- query_gain: bfloat16 [256], P('shard'), may hold values from 0.5 to 2
- key_gain: bfloat16 [256], P('shard'), may hold values from 0.5 to 2
- attended_gain: bfloat16 [640], P('shard'), may hold values from 0.25 to 1.75
- middle_gain: bfloat16 [640], P('shard'), may hold values from 0.25 to 1.75
- output_gain: bfloat16 [640], P('shard'), may hold values from 0.25 to 1.75
- cotangent: bfloat16 [32768, 640], P(('seq', 'shard')), may hold values from -12 to 12
Outputs:
- block_out: bfloat16 [32768, 640], P(('seq', 'shard'))
- grad_tokens: bfloat16 [32768, 640], P(('seq', 'shard'))
- grad_query_weight: float32 [640, 1024], P('shard')
- grad_key_weight: float32 [640, 256], P('shard')
- grad_value_weight: float32 [640, 256], P('shard')
- grad_out_weight: float32 [1024, 640], P('shard')
- grad_gate_weight: float32 [640, 2048], P('shard')
- grad_up_weight: float32 [640, 2048], P('shard')
- grad_down_weight: float32 [2048, 640], P('shard')
- grad_input_gain: float32 [640], P('shard')
- grad_query_gain: float32 [256], P('shard')
- grad_key_gain: float32 [256], P('shard')
- grad_attended_gain: float32 [640], P('shard')
- grad_middle_gain: float32 [640], P('shard')
- grad_output_gain: float32 [640], P('shard')
All inputs are finite; a program needn't handle non-finite values.
Results may differ from a plain program's by a relative error of at most 0.025.
Values may be sent and summed in bfloat16 or wider, within the bound.
No kernel may reach another device: no remote copies, remote signals or barrier semaphores. Data moves between devices by JAX's collectives and lax.ppermute only.
A program may use at most 256 MiB of HBM per device.

v0:
```python
import jax
import jax.numpy as jnp
from jax import lax
from jax.sharding import PartitionSpec as P

HEADS = 4
HEAD_DIM = 256
WINDOW = 512
SEQ_CAP = 8192


EPS = 1e-06
ROPE_BASE = 10000.0
MASKED = -1e30


def shifted(x, axis, by):
    length = lax.axis_size(axis)
    pairs = [(i, i + by) for i in range(length) if 0 <= i + by < length]
    return lax.ppermute(x, axis, pairs)


def normalize(values_in, weights):
    factor = lax.rsqrt(jnp.mean(values_in * values_in, axis=-1, keepdims=True) + EPS)
    return values_in * factor * weights


def normalize_back(values_in, weights, incoming):
    factor = lax.rsqrt(jnp.mean(values_in * values_in, axis=-1, keepdims=True) + EPS)
    united = values_in * factor
    scaled = incoming * weights
    result = factor * (scaled - united * jnp.mean(scaled * united, axis=-1, keepdims=True))
    return (result, incoming * united)


def column_total(terms):
    return jnp.sum(terms.reshape(-1, terms.shape[-1]), axis=0)


def rotary_tables(positions):
    halfway = HEAD_DIM // 2
    frequencies = ROPE_BASE ** (-(jnp.arange(halfway, dtype=jnp.float32) * 2.0 / HEAD_DIM))
    angles = positions.astype(jnp.float32)[:, None] * frequencies[None, :]
    return (jnp.cos(angles), jnp.sin(angles))


def rotate(values_in, cosine_table, sine_table):
    halfway = values_in.shape[-1] // 2
    first_half = values_in[..., :halfway]
    second_half = values_in[..., halfway:]
    return jnp.concatenate(
        [
            first_half * cosine_table - second_half * sine_table,
            second_half * cosine_table + first_half * sine_table,
        ],
        axis=-1,
    )


def rotate_back(values_in, cosine_table, sine_table):
    halfway = values_in.shape[-1] // 2
    first_half = values_in[..., :halfway]
    second_half = values_in[..., halfway:]
    return jnp.concatenate(
        [
            first_half * cosine_table + second_half * sine_table,
            second_half * cosine_table - first_half * sine_table,
        ],
        axis=-1,
    )


def gelu_pair(gate_proj):
    activated, pullback = jax.vjp(lambda inner: jax.nn.gelu(inner, approximate=True), gate_proj)
    return (activated, pullback(jnp.ones_like(gate_proj))[0])


def window_scores(queries, keys_block, query_pos, key_pos):
    scores = jnp.einsum(
        "qhd,kd->hqk", queries, keys_block, preferred_element_type=jnp.float32
    ) * HEAD_DIM ** (-0.5)
    distance_grid = query_pos[:, None] - key_pos[None, :]
    allowed = (distance_grid >= 0) & (distance_grid < WINDOW) & (key_pos[None, :] >= 0)
    return jnp.where(allowed[None], scores, MASKED)


def send_tail(keys_tail, values_tail, distance):
    return shifted((keys_tail, values_tail), ("seq", "shard"), distance)


def send_back(keys_piece, values_piece, distance):
    return (
        shifted(keys_piece.astype(jnp.bfloat16), ("seq", "shard"), -distance).astype(
            keys_piece.dtype
        ),
        shifted(values_piece.astype(jnp.bfloat16), ("seq", "shard"), -distance).astype(
            values_piece.dtype
        ),
    )


def shards(
    tokens,
    query_weight,
    key_weight,
    value_weight,
    out_weight,
    gate_weight,
    up_weight,
    down_weight,
    input_gain,
    query_gain,
    key_gain,
    attended_gain,
    middle_gain,
    output_gain,
    cotangent,
):
    (
        query_full,
        key_full,
        value_full,
        out_full,
        gate_full,
        up_full,
        down_full,
        input_whole,
        query_whole,
        key_whole,
        attended_whole,
        middle_whole,
        output_whole,
    ) = (
        lax.all_gather(query_weight, "shard", axis=0, tiled=True),
        lax.all_gather(key_weight, "shard", axis=0, tiled=True),
        lax.all_gather(value_weight, "shard", axis=0, tiled=True),
        lax.all_gather(out_weight, "shard", axis=0, tiled=True),
        lax.all_gather(gate_weight, "shard", axis=0, tiled=True),
        lax.all_gather(up_weight, "shard", axis=0, tiled=True),
        lax.all_gather(down_weight, "shard", axis=0, tiled=True),
        lax.all_gather(input_gain, "shard", axis=0, tiled=True),
        lax.all_gather(query_gain, "shard", axis=0, tiled=True),
        lax.all_gather(key_gain, "shard", axis=0, tiled=True),
        lax.all_gather(attended_gain, "shard", axis=0, tiled=True),
        lax.all_gather(middle_gain, "shard", axis=0, tiled=True),
        lax.all_gather(output_gain, "shard", axis=0, tiled=True),
    )
    input_scale = input_whole.astype(jnp.float32)
    query_scale = query_whole.astype(jnp.float32)
    key_scale = key_whole.astype(jnp.float32)
    attended_scale = attended_whole.astype(jnp.float32)
    middle_scale = middle_whole.astype(jnp.float32)
    output_scale = output_whole.astype(jnp.float32)
    count_rows = tokens.shape[0]
    sequence_length = min(SEQ_CAP, count_rows * lax.axis_size("seq") * lax.axis_size("shard"))
    linear_rank = lax.axis_index("seq") * lax.axis_size("shard") + lax.axis_index("shard")
    first_pos = linear_rank * count_rows % sequence_length
    positions = first_pos + jnp.arange(count_rows, dtype=jnp.int32)
    cosine_table, sine_table = rotary_tables(positions)
    inputs = tokens.astype(jnp.float32)
    normed_in = normalize(inputs, input_scale).astype(jnp.bfloat16)
    query_proj = jnp.dot(normed_in, query_full, preferred_element_type=jnp.float32).reshape(
        count_rows, HEADS, HEAD_DIM
    )
    key_raw = jnp.dot(normed_in, key_full, preferred_element_type=jnp.float32)
    value_raw = jnp.dot(normed_in, value_full, preferred_element_type=jnp.float32)
    query_rot = rotate(
        normalize(query_proj, query_scale), cosine_table[:, None], sine_table[:, None]
    ).astype(jnp.bfloat16)
    key_rot = rotate(normalize(key_raw, key_scale), cosine_table, sine_table).astype(jnp.bfloat16)
    value_rnd = value_raw.astype(jnp.bfloat16)
    reach_devices = -(-WINDOW // count_rows)
    tail_rows = min(WINDOW, count_rows)
    halo_rows = reach_devices * tail_rows
    distance = 1
    arrived = send_tail(
        key_rot[count_rows - tail_rows :], value_rnd[count_rows - tail_rows :], distance
    )
    key_parts = [arrived[0]]
    value_parts = [arrived[1]]
    keys_all = jnp.concatenate(key_parts + [key_rot], axis=0)
    values_all = jnp.concatenate(value_parts + [value_rnd], axis=0)
    block_rows = min(count_rows, 512)
    begin_rows = list(range(0, count_rows, block_rows))

    def window(begin_row):
        lowest_row = begin_row + halo_rows - WINDOW
        queries = query_rot[begin_row : begin_row + block_rows]
        keys_block = keys_all[lowest_row : lowest_row + block_rows + WINDOW]
        values_block = values_all[lowest_row : lowest_row + block_rows + WINDOW]
        query_pos = positions[begin_row : begin_row + block_rows]
        key_pos = first_pos + begin_row - WINDOW + jnp.arange(block_rows + WINDOW, dtype=jnp.int32)
        return (
            lowest_row,
            queries,
            keys_block,
            values_block,
            window_scores(queries, keys_block, query_pos, key_pos),
        )

    attended_parts = []
    logsums = []
    for begin_row in begin_rows:
        lowest_row, queries, keys_block, values_block, scores = window(begin_row)
        highest = jnp.max(scores, axis=-1, keepdims=True)
        logsum = highest + jnp.log(jnp.sum(jnp.exp(scores - highest), axis=-1, keepdims=True))
        weighting = jnp.exp(scores - logsum).astype(jnp.bfloat16)
        mixture = jnp.einsum(
            "hqk,kd->qhd", weighting, values_block, preferred_element_type=jnp.float32
        )
        attended_parts.append(mixture.astype(jnp.bfloat16))
        logsums.append(logsum)
    attended = jnp.concatenate(attended_parts, axis=0).reshape(count_rows, HEADS * HEAD_DIM)
    attn_proj = jnp.dot(attended, out_full, preferred_element_type=jnp.float32)
    middle = inputs + normalize(attn_proj, attended_scale)
    normed_mid = normalize(middle, middle_scale).astype(jnp.bfloat16)
    gate_proj = jnp.dot(normed_mid, gate_full, preferred_element_type=jnp.float32)
    up_proj = jnp.dot(normed_mid, up_full, preferred_element_type=jnp.float32)
    activated, gelu_slope = gelu_pair(gate_proj)
    hidden = (activated * up_proj).astype(jnp.bfloat16)
    down_proj = jnp.dot(hidden, down_full, preferred_element_type=jnp.float32)
    block_out = (middle + normalize(down_proj, output_scale)).astype(jnp.bfloat16)
    incoming = cotangent.astype(jnp.float32)
    query_again, key_again, value_again, out_again, gate_again, up_again, down_again = (
        query_full,
        key_full,
        value_full,
        out_full,
        gate_full,
        up_full,
        down_full,
    )
    d_down, output_terms = normalize_back(down_proj, output_scale, incoming)
    d_down_rnd = d_down.astype(jnp.bfloat16)
    grad_down = jnp.dot(hidden.T, d_down_rnd, preferred_element_type=jnp.float32)
    d_hidden = jnp.dot(d_down_rnd, down_again.T, preferred_element_type=jnp.float32)
    d_gate = (d_hidden * up_proj * gelu_slope).astype(jnp.bfloat16)
    d_up = (d_hidden * activated).astype(jnp.bfloat16)
    grad_gate = jnp.dot(normed_mid.T, d_gate, preferred_element_type=jnp.float32)
    grad_up = jnp.dot(normed_mid.T, d_up, preferred_element_type=jnp.float32)
    d_normed_mid = jnp.dot(d_gate, gate_again.T, preferred_element_type=jnp.float32) + jnp.dot(
        d_up, up_again.T, preferred_element_type=jnp.float32
    )
    d_middle_part, middle_terms = normalize_back(middle, middle_scale, d_normed_mid)
    d_middle = incoming + d_middle_part
    d_attn, attended_terms = normalize_back(attn_proj, attended_scale, d_middle)
    d_attn_rnd = d_attn.astype(jnp.bfloat16)
    grad_out = jnp.dot(attended.T, d_attn_rnd, preferred_element_type=jnp.float32)
    d_attended = (
        jnp.dot(d_attn_rnd, out_again.T, preferred_element_type=jnp.float32)
        .astype(jnp.bfloat16)
        .reshape(count_rows, HEADS, HEAD_DIM)
    )
    key_grad = jnp.zeros((halo_rows + count_rows, HEAD_DIM), jnp.float32)
    value_grad = jnp.zeros((halo_rows + count_rows, HEAD_DIM), jnp.float32)
    query_grads = []
    for index_block, begin_row in enumerate(begin_rows):
        lowest_row, queries, keys_block, values_block, scores = window(begin_row)
        weighting = jnp.exp(scores - logsums[index_block])
        weighting_rnd = weighting.astype(jnp.bfloat16)
        d_out_block = d_attended[begin_row : begin_row + block_rows]
        d_weighting = jnp.einsum(
            "qhd,kd->hqk", d_out_block, values_block, preferred_element_type=jnp.float32
        )
        row_dot = jnp.sum(weighting * d_weighting, axis=-1, keepdims=True)
        d_scores = (weighting * (d_weighting - row_dot) * HEAD_DIM ** (-0.5)).astype(jnp.bfloat16)
        query_grads.append(
            jnp.einsum("hqk,kd->qhd", d_scores, keys_block, preferred_element_type=jnp.float32)
        )
        key_grad = key_grad.at[lowest_row : lowest_row + block_rows + WINDOW].add(
            jnp.einsum("hqk,qhd->kd", d_scores, queries, preferred_element_type=jnp.float32)
        )
        value_grad = value_grad.at[lowest_row : lowest_row + block_rows + WINDOW].add(
            jnp.einsum(
                "hqk,qhd->kd", weighting_rnd, d_out_block, preferred_element_type=jnp.float32
            )
        )
    key_local = key_grad[halo_rows:]
    value_local = value_grad[halo_rows:]
    distance = 1
    offset_row = (reach_devices - distance) * tail_rows
    returned = send_back(
        key_grad[offset_row : offset_row + tail_rows],
        value_grad[offset_row : offset_row + tail_rows],
        distance,
    )
    key_local = key_local.at[count_rows - tail_rows :].add(returned[0])
    value_local = value_local.at[count_rows - tail_rows :].add(returned[1])
    d_query_rot = jnp.concatenate(query_grads, axis=0)
    d_query, query_terms = normalize_back(
        query_proj,
        query_scale,
        rotate_back(d_query_rot, cosine_table[:, None], sine_table[:, None]),
    )
    d_key, key_terms = normalize_back(
        key_raw, key_scale, rotate_back(key_local, cosine_table, sine_table)
    )
    d_query_rnd = d_query.reshape(count_rows, HEADS * HEAD_DIM).astype(jnp.bfloat16)
    d_key_rnd = d_key.astype(jnp.bfloat16)
    d_value_rnd = value_local.astype(jnp.bfloat16)
    grad_query = jnp.dot(normed_in.T, d_query_rnd, preferred_element_type=jnp.float32)
    grad_key = jnp.dot(normed_in.T, d_key_rnd, preferred_element_type=jnp.float32)
    grad_value = jnp.dot(normed_in.T, d_value_rnd, preferred_element_type=jnp.float32)
    d_normed_in = (
        jnp.dot(d_query_rnd, query_again.T, preferred_element_type=jnp.float32)
        + jnp.dot(d_key_rnd, key_again.T, preferred_element_type=jnp.float32)
        + jnp.dot(d_value_rnd, value_again.T, preferred_element_type=jnp.float32)
    )
    d_inputs, input_terms = normalize_back(inputs, input_scale, d_normed_in)
    grad_tokens = (d_middle + d_inputs).astype(jnp.bfloat16)
    sum_input = column_total(input_terms)
    sum_query = column_total(query_terms)
    sum_key = column_total(key_terms)
    sum_attended = column_total(attended_terms)
    sum_middle = column_total(middle_terms)
    sum_output = column_total(output_terms)
    (
        total_query,
        total_key,
        total_value,
        total_out,
        total_gate,
        total_up,
        total_down,
        total_input_g,
        total_query_g,
        total_key_g,
        total_attended_g,
        total_middle_g,
        total_output_g,
    ) = (
        lax.psum(grad_query.astype(jnp.bfloat16), "seq").astype(jnp.float32),
        lax.psum(grad_key.astype(jnp.bfloat16), "seq").astype(jnp.float32),
        lax.psum(grad_value.astype(jnp.bfloat16), "seq").astype(jnp.float32),
        lax.psum(grad_out.astype(jnp.bfloat16), "seq").astype(jnp.float32),
        lax.psum(grad_gate.astype(jnp.bfloat16), "seq").astype(jnp.float32),
        lax.psum(grad_up.astype(jnp.bfloat16), "seq").astype(jnp.float32),
        lax.psum(grad_down.astype(jnp.bfloat16), "seq").astype(jnp.float32),
        lax.psum(sum_input.astype(jnp.bfloat16), "seq").astype(jnp.float32),
        lax.psum(sum_query.astype(jnp.bfloat16), "seq").astype(jnp.float32),
        lax.psum(sum_key.astype(jnp.bfloat16), "seq").astype(jnp.float32),
        lax.psum(sum_attended.astype(jnp.bfloat16), "seq").astype(jnp.float32),
        lax.psum(sum_middle.astype(jnp.bfloat16), "seq").astype(jnp.float32),
        lax.psum(sum_output.astype(jnp.bfloat16), "seq").astype(jnp.float32),
    )
    reduced = (
        lax.psum_scatter(
            total_query.astype(jnp.bfloat16), "shard", scatter_dimension=0, tiled=True
        ).astype(jnp.float32),
        lax.psum_scatter(
            total_key.astype(jnp.bfloat16), "shard", scatter_dimension=0, tiled=True
        ).astype(jnp.float32),
        lax.psum_scatter(
            total_value.astype(jnp.bfloat16), "shard", scatter_dimension=0, tiled=True
        ).astype(jnp.float32),
        lax.psum_scatter(
            total_out.astype(jnp.bfloat16), "shard", scatter_dimension=0, tiled=True
        ).astype(jnp.float32),
        lax.psum_scatter(
            total_gate.astype(jnp.bfloat16), "shard", scatter_dimension=0, tiled=True
        ).astype(jnp.float32),
        lax.psum_scatter(
            total_up.astype(jnp.bfloat16), "shard", scatter_dimension=0, tiled=True
        ).astype(jnp.float32),
        lax.psum_scatter(
            total_down.astype(jnp.bfloat16), "shard", scatter_dimension=0, tiled=True
        ).astype(jnp.float32),
        lax.psum_scatter(
            total_input_g.astype(jnp.bfloat16), "shard", scatter_dimension=0, tiled=True
        ).astype(jnp.float32),
        lax.psum_scatter(
            total_query_g.astype(jnp.bfloat16), "shard", scatter_dimension=0, tiled=True
        ).astype(jnp.float32),
        lax.psum_scatter(
            total_key_g.astype(jnp.bfloat16), "shard", scatter_dimension=0, tiled=True
        ).astype(jnp.float32),
        lax.psum_scatter(
            total_attended_g.astype(jnp.bfloat16), "shard", scatter_dimension=0, tiled=True
        ).astype(jnp.float32),
        lax.psum_scatter(
            total_middle_g.astype(jnp.bfloat16), "shard", scatter_dimension=0, tiled=True
        ).astype(jnp.float32),
        lax.psum_scatter(
            total_output_g.astype(jnp.bfloat16), "shard", scatter_dimension=0, tiled=True
        ).astype(jnp.float32),
    )
    return (
        block_out,
        grad_tokens,
        reduced[0],
        reduced[1],
        reduced[2],
        reduced[3],
        reduced[4],
        reduced[5],
        reduced[6],
        reduced[7],
        reduced[8],
        reduced[9],
        reduced[10],
        reduced[11],
        reduced[12],
    )


def solution(mesh):
    in_specs = (
        P(("seq", "shard"), None),
        P("shard", None),
        P("shard", None),
        P("shard", None),
        P("shard", None),
        P("shard", None),
        P("shard", None),
        P("shard", None),
        P("shard"),
        P("shard"),
        P("shard"),
        P("shard"),
        P("shard"),
        P("shard"),
        P(("seq", "shard"), None),
    )
    out_specs = (
        P(("seq", "shard"), None),
        P(("seq", "shard"), None),
        P("shard", None),
        P("shard", None),
        P("shard", None),
        P("shard", None),
        P("shard", None),
        P("shard", None),
        P("shard", None),
        P("shard"),
        P("shard"),
        P("shard"),
        P("shard"),
        P("shard"),
        P("shard"),
    )
    return jax.shard_map(shards, mesh=mesh, in_specs=in_specs, out_specs=out_specs, check_vma=False)
```

profile of v0, /device:TPU:0, one launch (start us, length us, event | category | flops | bytes accessed | tf_op | source)
XLA Modules:
  0.0 621.5 jit_solution(9237992770147965201)
XLA Ops:
  14.9 8.7 %all-reduce.17 = (bf16[640]{0:T(1024)(128)(2,1)S(1)}, bf16[256]{0:T(256)(128)(2,1)S(1)}, bf16[256]{0:T(256)(128)(2,1)S(1)}, bf16[640]{0:T(1024)(128)(2,1)S(1)}, ...) all-reduce(bf16[640]{0:T(1024)(128)(2,1)S(1)} %dynamic-update-slice, ...), channel_id=1, replica_groups=mesh['seq'=8,'shard'=4] {'shard'}, use_global_device_ids=true, to_apply=%add.2 | all-reduce | flops 3072 | bytes 12288
  23.6 7.9 %all_gather.40 = bf16[640,256]{1,0:T(8,128)(2,1)S(1)} all-gather(bf16[160,256]{1,0:T(8,128)(2,1)S(1)} %copy-done.42), channel_id=1, replica_groups=mesh['seq'=8,'shard'=4] {'shard'}, dimensions={0}, use_global_device_ids=true | all-gather | bytes 409600 | tf_op jit(solution)/shard_map/all_gather | solution.py:136
  33.4 3.0 collective-permute-start
  36.4 6.2 all_gather.41
  43.6 3.0 multiply_cosine_fusion
  47.4 2.9 collective-permute-start.1
  58.3 5.3 multiply_reduce_fusion.1
  63.6 5.4 copy.100
  68.9 2.6 multiply_multiply_fusion.3
  80.3 2.7 fusion.18
  86.3 3.6 fusion.51
  90.2 3.7 multiply_reduce_fusion.8
  96.7 8.9 %fusion.138 = f32[1024,2048]{1,0:T(8,128)} fusion(bf16[1024,640]{0,1:T(8,128)(2,1)} %multiply_convert_fusion.3, bf16[640,2048]{1,0:T(8,128)(2,1)} %all-gather.10.cloned.1.call-done), kind=kOutput, calls=%fused_computation.222 | convolution fusion | flops 2684354560 | bytes 12320768 | tf_op jit(solution)/shard_map/dot_general | solution.py:217
  106.8 11.3 %multiply_convert_fusion.1 = (bf16[1024,2048]{1,0:T(8,128)(2,1)}, f32[1024,2048]{1,0:T(8,128)}) fusion(f32[1024,2048]{1,0:T(8,128)} %fusion.138, bf16[1024,640]{0,1:T(8,128)(2,1)} %multiply_convert_fusion.3, bf16[640,2048]{1,0:T(8,128)(2,1)} %all-gather.12.cloned.1.call-done), kind=kOutput, calls=%fused_computation.25 | convolution fusion | flops 2705326080 | bytes 24903680 | tf_op jit(solution)/shard_map/dot_general | solution.py:218
  118.2 15.7 %all-gather.14.cloned.1.call-done = bf16[2048,640]{1,0:T(8,128)(2,1)} async-done(((bf16[512,640]{1,0:T(8,128)(2,1)}), bf16[2048,640]{1,0:T(8,128)(2,1)}) %all-gather.14.cloned.1.call-update) | async-done | bytes 2621456 | tf_op jit(solution)/shard_map/all_gather | solution.py:140
  133.9 5.9 multiply_reduce_fusion.6
  145.1 13.4 %multiply_convert_fusion = (bf16[1024,2048]{1,0:T(8,128)(2,1)}, bf16[1024,2048]{1,0:T(8,128)(2,1)}) fusion(f32[1024,2048]{1,0:T(8,128)S(1)} %copy-done.64, f32[1024,2048]{1,0:T(8,128)} %get-tuple-element.205, bf16[1024,640]{0,1:T(8,128)(2,1)S(1)} %get-tuple-element.178, bf16[2048,640]{1,0:T(8,128)(2,1)S(1)} %copy-done.55), kind=kOutput, calls=%fused_computation.24 | convolution fusion | flops 2732589056 | bytes 29097984 | tf_op jit(solution)/shard_map/dot_general | solution.py:236
  158.5 5.3 fusion.139
  163.8 3.4 multiply_reduce_fusion.2
  177.0 3.1 fusion.56
  180.0 4.5 fusion.77
  184.5 15.0 %convolution_bitcast_fusion = f32[512,4,256]{2,0,1:T(8,128)} fusion(f32[1024,512,4]{1,0,2:T(8,128)} %fusion.77, f32[1024,512,4]{1,0,2:T(8,128)} %copy-done.11, f32[4,512]{1,0:T(4,128)S(1)} %log_add_fusion, pred[512,1024]{0,1:T(8,128)(4,1)S(1)} %copy-done.23, bf16[1024,128]{0,1:T(8,128)(2,1)S(1)} %get-tuple-element.188, bf16[1024,128]{0,1:T(8,128)(2,1)S(1)} %copy-done.38), kind=kOutput, calls=%fused_computation.105 | convolution fusion | flops 1097862144 | bytes 19931136 | tf_op jit(solution)/shard_map/hqk,kd->qhd/dot_general | solution.py:268
  199.6 5.5 fusion.86
  205.0 15.0 %fusion.54 = f32[1024,256]{0,1:T(8,128)} fusion(f32[1024,512,4]{1,0,2:T(8,128)} %fusion.86, f32[1024,512,4]{1,0,2:T(8,128)} %copy-done.10, f32[4,512]{1,0:T(4,128)S(1)} %log_add_fusion.1, pred[512,1024]{0,1:T(8,128)(4,1)S(1)} %copy-done.21, bf16[1024,4,128]{2,0,1:T(8,128)(2,1)} %copy-done.34, bf16[1024,4,128]{2,0,1:T(8,128)(2,1)} %copy-done.36), kind=kOutput, calls=%fused_computation.123 | convolution fusion | flops 1098910720 | bytes 37765120 | tf_op jit(solution)/shard_map/hqk,qhd->kd/dot_general | solution.py:271
  220.1 14.2 %fusion.55 = f32[1024,256]{0,1:T(8,128)S(1)} fusion(f32[1024,512,4]{1,0,2:T(8,128)} %fusion.77, f32[1024,512,4]{1,0,2:T(8,128)} %copy-done.11, f32[4,512]{1,0:T(4,128)S(1)} %log_add_fusion, pred[512,1024]{0,1:T(8,128)(4,1)S(1)} %copy-done.23, f32[1024,256]{0,1:T(8,128)} %fusion.54, bf16[1024,4,128]{2,0,1:T(8,128)(2,1)} %copy-done.36, ...), kind=kOutput, calls=%fused_computation.124 | convolution fusion | flops 1099172864 | bytes 38813696 | tf_op jit(solution)/shard_map/hqk,qhd->kd/dot_general | solution.py:271
  237.9 15.2 %convolution_bitcast_fusion.1 = f32[512,4,256]{2,0,1:T(8,128)} fusion(f32[1024,512,4]{1,0,2:T(8,128)} %fusion.86, f32[1024,512,4]{1,0,2:T(8,128)} %copy-done.10, f32[4,512]{1,0:T(4,128)S(1)} %log_add_fusion.1, pred[512,1024]{0,1:T(8,128)(4,1)S(1)} %copy-done.21, bf16[512,256]{0,1:T(8,128)(2,1)} %collective-permute-done.1, ...), kind=kOutput, calls=%fused_computation.106 | convolution fusion | flops 1098386432 | bytes 20193280 | tf_op jit(solution)/shard_map/hqk,kd->qhd/dot_general | solution.py:268
  258.3 5.1 multiply_add_fusion
  266.8 4.9 multiply_reduce_fusion
  271.8 5.4 copy.119
  277.2 4.3 fusion.22
  282.8 2.6 convolution_convert_fusion.5
  285.5 4.8 convolution_convert_fusion.4
  290.8 7.0 %convolution_convert_fusion.2 = bf16[640,2048]{1,0:T(8,128)(2,1)} fusion(bf16[1024,640]{0,1:T(8,128)(2,1)} %multiply_convert_fusion.3, bf16[1024,2048]{1,0:T(8,128)(2,1)} %get-tuple-element.171), kind=kOutput, calls=%fused_computation.61 | convolution fusion | flops 2685665280 | bytes 8126464 | tf_op jit(solution)/shard_map/dot_general | solution.py:239
  297.9 7.0 %convolution_convert_fusion.1 = bf16[640,2048]{1,0:T(8,128)(2,1)} fusion(bf16[1024,640]{0,1:T(8,128)(2,1)} %multiply_convert_fusion.3, bf16[1024,2048]{1,0:T(8,128)(2,1)} %get-tuple-element.170), kind=kOutput, calls=%fused_computation.60 | convolution fusion | flops 2685665280 | bytes 8126464 | tf_op jit(solution)/shard_map/dot_general | solution.py:240
  305.0 7.7 %convolution_convert_fusion = bf16[2048,640]{1,0:T(8,128)(2,1)} fusion(bf16[1024,2048]{1,0:T(8,128)(2,1)} %get-tuple-element.204, bf16[1024,640]{0,1:T(8,128)(2,1)} %copy-done.29), kind=kOutput, calls=%fused_computation.59 | convolution fusion | flops 2685665280 | bytes 8126464 | tf_op jit(solution)/shard_map/dot_general | solution.py:235
  313.0 21.5 %reduce-scatter.8.cloned.1.call-done = bf16[160,1024]{1,0:T(8,128)(2,1)} async-done(((bf16[640,1024]{1,0:T(8,128)(2,1)}), bf16[160,1024]{1,0:T(8,128)(2,1)}) %reduce-scatter.8.cloned.1.call-update) | async-done | bytes 327696 | tf_op jit(solution)/shard_map/reduce_scatter | solution.py:347
  334.5 29.9 %reduce-scatter.14.cloned.1.call-done = bf16[256,640]{1,0:T(8,128)(2,1)} async-done(((bf16[1024,640]{1,0:T(8,128)(2,1)}), bf16[256,640]{1,0:T(8,128)(2,1)}) %reduce-scatter.14.cloned.1.call-update) | async-done | bytes 327696 | tf_op jit(solution)/shard_map/reduce_scatter | solution.py:356
  364.3 37.1 %reduce-scatter.16.cloned.1.call-done = bf16[160,2048]{1,0:T(8,128)(2,1)} async-done(((bf16[640,2048]{1,0:T(8,128)(2,1)}), bf16[160,2048]{1,0:T(8,128)(2,1)}) %reduce-scatter.16.cloned.1.call-update) | async-done | bytes 655376 | tf_op jit(solution)/shard_map/reduce_scatter | solution.py:359
  401.4 37.4 %reduce-scatter.18.cloned.1.call-done = bf16[160,2048]{1,0:T(8,128)(2,1)} async-done(((bf16[640,2048]{1,0:T(8,128)(2,1)}), bf16[160,2048]{1,0:T(8,128)(2,1)}) %reduce-scatter.18.cloned.1.call-update) | async-done | bytes 655376 | tf_op jit(solution)/shard_map/reduce_scatter | solution.py:362
  438.8 37.1 %reduce-scatter.20.cloned.1.call-done = bf16[512,640]{1,0:T(8,128)(2,1)} async-done(((bf16[2048,640]{1,0:T(8,128)(2,1)}), bf16[512,640]{1,0:T(8,128)(2,1)}) %reduce-scatter.20.cloned.1.call-update) | async-done | bytes 655376 | tf_op jit(solution)/shard_map/reduce_scatter | solution.py:365
  477.3 5.4 copy.131
  483.7 5.5 reshape.462
  490.6 4.3 copy.130
  494.9 2.7 copy.129
  500.2 3.4 fusion.23
  510.7 6.2 %all-reduce.16 = (bf16[640]{0:T(1024)(128)(2,1)S(1)}, bf16[256]{0:T(256)(128)(2,1)S(1)}, bf16[256]{0:T(256)(128)(2,1)S(1)}, bf16[640]{0:T(1024)(128)(2,1)S(1)}, ...) all-reduce(bf16[640]{0:T(1024)(128)(2,1)S(1)} %get-tuple-element.13, ...), channel_id=9, replica_groups=mesh['seq'=8,'shard'=4] {'shard'}, use_global_device_ids=true, to_apply=%region_34.35.clone | all-reduce | flops 3072 | bytes 12288
  517.5 21.5 %all-reduce.14 = (bf16[160]{0:T(256)(128)(2,1)S(1)}, bf16[64]{0:T(256)(128)(2,1)S(1)}, bf16[64]{0:T(256)(128)(2,1)S(1)}, bf16[160]{0:T(256)(128)(2,1)S(1)}, bf16...) all-reduce(bf16[160]{0:T(256)(128)(2,1)S(1)} %dynamic-slice.53, ...), channel_id=1, replica_groups=mesh['seq'=8,'shard'=4] {'seq'}, use_global_device_ids=true, to_apply=%region_33.34 | all-reduce | flops 768 | bytes 3072 | tf_op jit(solution)/shard_map/psum | solution.py:339
  542.2 61.9 %all-reduce.20.cloned.1.call-done = (bf16[160,1024]{1,0:T(8,128)(2,1)}, bf16[160,256]{1,0:T(8,128)(2,1)}, bf16[160,256]{1,0:T(8,128)(2,1)}, bf16[256,640]{1,0:T(...) async-done(((bf16[160,1024]{1,0:T(8,128)(2,1)}, bf16[160,256]{1,0:T(8,128)(2,1)}, bf16[160,256]{1,0:T(8,128)(2,1)}, ...) | async-done | bytes 2785296 | tf_op jit(solution)/shard_map/psum | solution.py:332
  (284 shorter events, 89.4 us)
Async XLA Ops:
  7.2 5.6 copy-start.30
  7.2 6.2 %copy-start.58 = (bf16[64]{0:T(256)(128)(2,1)S(1)}, bf16[64]{0:T(256)(128)(2,1)}, u32[]{:S(2)}) copy-start(bf16[64]{0:T(256)(128)(2,1)} %param.37) | copy-start | bytes 388
  7.2 6.5 %copy-start.59 = (bf16[64]{0:T(256)(128)(2,1)S(1)}, bf16[64]{0:T(256)(128)(2,1)}, u32[]{:S(2)}) copy-start(bf16[64]{0:T(256)(128)(2,1)} %param.36) | copy-start | bytes 388
  7.2 6.7 %copy-start.60 = (bf16[160]{0:T(256)(128)(2,1)S(1)}, bf16[160]{0:T(256)(128)(2,1)}, u32[]{:S(2)}) copy-start(bf16[160]{0:T(256)(128)(2,1)} %param.35) | copy-start | bytes 964
  7.2 7.0 %copy-start.61 = (bf16[160]{0:T(256)(128)(2,1)S(1)}, bf16[160]{0:T(256)(128)(2,1)}, u32[]{:S(2)}) copy-start(bf16[160]{0:T(256)(128)(2,1)} %param.38) | copy-start | bytes 964
  7.2 7.2 %copy-start.62 = (bf16[160]{0:T(256)(128)(2,1)S(1)}, bf16[160]{0:T(256)(128)(2,1)}, u32[]{:S(2)}) copy-start(bf16[160]{0:T(256)(128)(2,1)} %param.39) | copy-start | bytes 964
  7.2 7.4 %copy-start.63 = (bf16[160]{0:T(256)(128)(2,1)S(1)}, bf16[160]{0:T(256)(128)(2,1)}, u32[]{:S(2)}) copy-start(bf16[160]{0:T(256)(128)(2,1)} %param.40) | copy-start | bytes 964
  7.3 16.3 %copy-start.42 = (bf16[160,256]{1,0:T(8,128)(2,1)S(1)}, bf16[160,256]{1,0:T(8,128)(2,1)}, u32[]{:S(2)}) copy-start(bf16[160,256]{1,0:T(8,128)(2,1)} %param.30) | copy-start | bytes 245764
  7.3 51.0 %all-gather.6.cloned.1.call-start = ((), (), s32[]{:S(2)}) async-start(), calls=%async_computation.7 | async-start | bytes 1638400 | tf_op jit(solution)/shard_map/all_gather | solution.py:134
  8.0 82.2 %all-gather.8.cloned.1.call-start = ((), (), s32[]{:S(2)}) async-start(), calls=%async_computation.8 | async-start | bytes 1638400 | tf_op jit(solution)/shard_map/all_gather | solution.py:137
  8.7 88.0 %all-gather.10.cloned.1.call-start = ((), (), s32[]{:S(2)}) async-start(), calls=%async_computation.9 | async-start | bytes 3276800 | tf_op jit(solution)/shard_map/all_gather | solution.py:138
  9.5 97.4 %all-gather.12.cloned.1.call-start = ((), (), s32[]{:S(2)}) async-start(), calls=%async_computation.10 | async-start | bytes 3276800 | tf_op jit(solution)/shard_map/all_gather | solution.py:139
  10.1 123.8 %all-gather.14.cloned.1.call-start = ((), (), s32[]{:S(2)}) async-start(), calls=%async_computation.11 | async-start | bytes 3276800 | tf_op jit(solution)/shard_map/all_gather | solution.py:140
  13.4 44.9 %copy-start = (bf16[1024,640]{0,1:T(8,128)(2,1)}, bf16[1024,640]{0,1:T(8,128)(2,1)S(1)}, u32[]{:S(2)}) copy-start(bf16[1024,640]{0,1:T(8,128)(2,1)S(1)} %copy.99) | copy-start | bytes 3932164
  31.8 4.6 copy-start.43
  33.4 51.7 %collective-permute-start = (bf16[512,256]{1,0:T(8,128)(2,1)}, bf16[512,256]{1,0:T(8,128)(2,1)}, u32[]{:S(2)}, u32[]{:S(2)}) collective-permute-start(bf16[512,256]{1,0:T(8,128)(2,1)} %slice.212), channel_id=1, source_target_pairs={{0,1},{1,2},{2,3},{3,4},{4,5},{5,6},{6,7},{7,8},{8,9},{9,10},{10,1... | collective-permute-start | bytes 786440 | tf_op jit(solution)/shard_map/ppermute | solution.py:20
  36.3 7.2 %copy-start.49 = (f32[256]{0:T(256)}, f32[256]{0:T(256)S(1)}, u32[]{:S(2)}) copy-start(f32[256]{0:T(256)S(1)} %convert_element_type.217) | copy-start | bytes 3076
  36.3 7.2 %copy-start.51 = (f32[128]{0:T(128)}, f32[128]{0:T(128)S(1)}, u32[]{:S(2)}) copy-start(f32[128]{0:T(128)S(1)} %negate_power_fusion) | copy-start | bytes 1540
  36.4 7.2 %copy-start.46 = (f32[1024]{0:T(1024)}, f32[1024]{0:T(1024)S(1)}, u32[]{:S(2)}) copy-start(f32[1024]{0:T(1024)S(1)} %fusion.93) | copy-start | bytes 12292
  46.6 33.7 %copy-start.37 = (bf16[1024,128]{0,1:T(8,128)(2,1)}, bf16[1024,128]{0,1:T(8,128)(2,1)S(1)}, u32[]{:S(2)}) copy-start(bf16[1024,128]{0,1:T(8,128)(2,1)S(1)} %get-tuple-element.189) | copy-start | bytes 786436
  47.4 32.9 %collective-permute-start.1 = (bf16[512,256]{0,1:T(8,128)(2,1)}, bf16[512,256]{0,1:T(8,128)(2,1)}, u32[]{:S(2)}, u32[]{:S(2)}) collective-permute-start(bf16[512,256]{0,1:T(8,128)(2,1)} %fusion.83), channel_id=1, source_target_pairs={{0,1},{1,2},{2,3},{3,4},{4,5},{5,6},{6,7},{7,8},{8,9},{9,10},{10,1... | collective-permute-start | bytes 786440 | tf_op jit(solution)/shard_map/ppermute | solution.py:20
  50.3 262.6 %reduce-scatter.10.cloned.1.call-start = ((), (), s32[]{:S(2)}) async-start(), calls=%async_computation.13 | async-start | bytes 409600 | tf_op jit(solution)/shard_map/reduce_scatter | solution.py:350
  53.6 18.0 %copy-start.13 = (f32[1024,128]{1,0:T(8,128)}, f32[1024,128]{1,0:T(8,128)S(1)}, u32[]{:S(2)}) copy-start(f32[1024,128]{1,0:T(8,128)S(1)} %copy.102) | copy-start | bytes 1572868
  55.1 16.5 %copy-start.14 = (f32[1024,128]{1,0:T(8,128)}, f32[1024,128]{1,0:T(8,128)S(1)}, u32[]{:S(2)}) copy-start(f32[1024,128]{1,0:T(8,128)S(1)} %copy.101) | copy-start | bytes 1572868
  72.2 8.1 %copy-start.34 = (bf16[1024,4,128]{2,0,1:T(8,128)(2,1)}, bf16[1024,4,128]{2,0,1:T(8,128)(2,1)S(1)}, u32[]{:S(2)}) copy-start(bf16[1024,4,128]{2,0,1:T(8,128)(2,1)S(1)} %get-tuple-element.174) | copy-start | bytes 3145732
  72.2 8.1 %copy-start.36 = (bf16[1024,4,128]{2,0,1:T(8,128)(2,1)}, bf16[1024,4,128]{2,0,1:T(8,128)(2,1)S(1)}, u32[]{:S(2)}) copy-start(bf16[1024,4,128]{2,0,1:T(8,128)(2,1)S(1)} %get-tuple-element.175) | copy-start | bytes 3145732
  133.9 5.9 copy-start.7
  142.6 15.9 %copy-start.29 = (bf16[1024,640]{0,1:T(8,128)(2,1)}, bf16[1024,640]{0,1:T(8,128)(2,1)S(1)}, u32[]{:S(2)}) copy-start(bf16[1024,640]{0,1:T(8,128)(2,1)S(1)} %get-tuple-element.178) | copy-start | bytes 3932164
  145.1 13.4 %copy-start.53 = (bf16[640,2048]{1,0:T(8,128)(2,1)S(1)}, bf16[640,2048]{1,0:T(8,128)(2,1)}, u32[]{:S(2)}) copy-start(bf16[640,2048]{1,0:T(8,128)(2,1)} %all-gather.10.cloned.1.call-done) | copy-start | bytes 7864324
  158.5 5.3 copy-start.54
  158.5 5.3 copy-start.65
  205.0 15.0 %copy-start.35 = (bf16[1024,4,128]{2,0,1:T(8,128)(2,1)S(1)}, bf16[1024,4,128]{2,0,1:T(8,128)(2,1)}, u32[]{:S(2)}) copy-start(bf16[1024,4,128]{2,0,1:T(8,128)(2,1)} %copy-done.34) | copy-start | bytes 3145732
  235.3 18.0 %copy-start.47 = (f32[1024]{0:T(1024)S(1)}, f32[1024]{0:T(1024)}, u32[]{:S(2)}) copy-start(f32[1024]{0:T(1024)} %copy-done.46) | copy-start | bytes 12292
  235.3 18.0 %copy-start.52 = (f32[128]{0:T(128)S(1)}, f32[128]{0:T(128)}, u32[]{:S(2)}) copy-start(f32[128]{0:T(128)} %copy-done.51) | copy-start | bytes 1540
  235.3 28.1 %collective-permute-start.3 = (bf16[512,256]{1,0:T(8,128)(2,1)}, bf16[512,256]{1,0:T(8,128)(2,1)}, u32[]{:S(2)}, u32[]{:S(2)}) collective-permute-start(bf16[512,256]{1,0:T(8,128)(2,1)} %slice.287), channel_id=1, source_target_pairs={{1,0},{2,1},{3,2},{4,3},{5,4},{6,5},{7,6},{8,7},{9,8},{10,9},{11,1... | collective-permute-start | bytes 786440 | tf_op jit(solution)/shard_map/ppermute | solution.py:20
  236.6 16.6 %collective-permute-start.2 = (bf16[512,256]{0,1:T(8,128)(2,1)S(1)}, bf16[512,256]{0,1:T(8,128)(2,1)S(1)}, u32[]{:S(2)}, u32[]{:S(2)}) collective-permute-start(bf16[512,256]{0,1:T(8,128)(2,1)S(1)} %slice.288), channel_id=1, source_target_pairs={{1,0},{2,1},{3,2},{4,3},{5,4},{6,5},{7,6},{8,7},{9,8},{10,9},{11,1... | collective-permute-start | bytes 786440 | tf_op jit(solution)/shard_map/ppermute | solution.py:20
  258.3 54.7 %reduce-scatter.12.cloned.1.call-start = ((), (), s32[]{:S(2)}) async-start(), calls=%async_computation.14 | async-start | bytes 409600 | tf_op jit(solution)/shard_map/reduce_scatter | solution.py:353
  258.3 5.1 copy-start.15
  266.8 67.7 %reduce-scatter.8.cloned.1.call-start = ((), (), s32[]{:S(2)}) async-start(), calls=%async_computation.12 | async-start | bytes 1638400 | tf_op jit(solution)/shard_map/reduce_scatter | solution.py:347
  271.8 5.4 copy-start.48
  285.4 78.9 %reduce-scatter.14.cloned.1.call-start = ((), (), s32[]{:S(2)}) async-start(), calls=%async_computation.15 | async-start | bytes 1638400 | tf_op jit(solution)/shard_map/reduce_scatter | solution.py:356
  290.3 111.1 %reduce-scatter.16.cloned.1.call-start = ((), (), s32[]{:S(2)}) async-start(), calls=%async_computation.16 | async-start | bytes 3276800 | tf_op jit(solution)/shard_map/reduce_scatter | solution.py:359
  297.9 141.0 %reduce-scatter.18.cloned.1.call-start = ((), (), s32[]{:S(2)}) async-start(), calls=%async_computation.17 | async-start | bytes 3276800 | tf_op jit(solution)/shard_map/reduce_scatter | solution.py:362
  304.9 171.0 %reduce-scatter.20.cloned.1.call-start = ((), (), s32[]{:S(2)}) async-start(), calls=%async_computation.18 | async-start | bytes 3276800 | tf_op jit(solution)/shard_map/reduce_scatter | solution.py:365
  312.7 291.5 %all-reduce.20.cloned.1.call-start = ((), (), s32[]{:S(2)}) async-start(), calls=%async_computation.19 | async-start | bytes 5570560 | tf_op jit(solution)/shard_map/psum | solution.py:332
  604.2 7.0 %copy-start.41 = (bf16[160,2048]{1,0:T(8,128)(2,1)S(1)}, bf16[160,2048]{1,0:T(8,128)(2,1)}, u32[]{:S(2)}) copy-start(bf16[160,2048]{1,0:T(8,128)(2,1)} %get-tuple-element.152) | copy-start | bytes 1966084
  604.2 8.2 %copy-start.40 = (bf16[160,2048]{1,0:T(8,128)(2,1)S(1)}, bf16[160,2048]{1,0:T(8,128)(2,1)}, u32[]{:S(2)}) copy-start(bf16[160,2048]{1,0:T(8,128)(2,1)} %get-tuple-element.153) | copy-start | bytes 1966084
  607.7 5.9 copy-start.39
  (39 other events, 100.0 us)
Sparse Core Ops, SparseCore 0:
  9.7 22.7 all-gather.5
  34.0 18.1 all-gather.7
  53.8 25.9 all-gather.9
  81.3 25.5 all-gather.11
  108.3 25.5 all-gather.13
  258.4 23.2 reduce-scatter.9
  284.3 20.4 reduce-scatter.11
  307.9 26.5 reduce-scatter.7
  337.8 26.5 reduce-scatter.13
  366.7 34.6 reduce-scatter.15
  404.1 34.6 reduce-scatter.17
  441.2 34.6 reduce-scatter.19
  481.2 122.9 all-reduce.19
where the time goes:
time: 627 us; the launch traced here: 621 us
  waiting for transfers between devices  245 us (39%)
  matrix products  181 us (29%)
  local copies, waits for them, and re-layouts  60.6 us (10%)
  other arithmetic  57.1 us (9%)
  blocking collectives  50.5 us (8%)
  between operations  17.8 us (3%)
  starting transfers between devices  10.1 us (2%)
    psum x1, waiting for transfers between devices, shards(): lax.psum(grad_query.astype(jnp.bfloat16), 'seq').astype(jnp.float32)  61.9 us
    reduce_scatter x1, waiting for transfers between devices, shards(): lax.psum_scatter(total_up.astype(jnp.bfloat16), 'shard', scatter_dimensio...  37.4 us
    reduce_scatter x1, waiting for transfers between devices, shards(): lax.psum_scatter(total_down.astype(jnp.bfloat16), 'shard', scatter_dimens...  37.1 us
    reduce_scatter x1, waiting for transfers between devices, shards(): lax.psum_scatter(total_gate.astype(jnp.bfloat16), 'shard', scatter_dimens...  37.1 us
    dot_general x2, matrix products, shards(): jnp.einsum('hqk,kd->qhd', d_scores, keys_block, preferred_element_type=jn...  30.3 us
    reduce_scatter x1, waiting for transfers between devices, shards(): lax.psum_scatter(total_out.astype(jnp.bfloat16), 'shard', scatter_dimensi...  29.9 us
    dot_general x2, matrix products, shards(): jnp.einsum('hqk,qhd->kd', d_scores, queries, preferred_element_type=jnp.f...  29.2 us
    unnamed x165, local copies, waits for them, and re-layouts  25.3 us
  transfers between devices with their start and end apart: 17, of which 8 were waited for; matrix products, arithmetic and copies ran while one was open for 29% of the time, Pallas kernels for 0%

commit v1 on v0

v1 whole, which is shorter than its diff:
```python
import jax
import jax.numpy as jnp
from jax import lax
from jax.experimental import pallas as pl
from jax.experimental.pallas import tpu as pltpu
from jax.sharding import PartitionSpec as P

D = 640
HEADS = 4
HEAD_DIM = 256
FF = 2048
WINDOW = 512
SEQ_CAP = 8192
HALF = 512
QB = 256
ROWS = HEADS * QB
CHUNK = 512

EPS = 1e-06
ROPE_BASE = 10000.0
LOG2E = 1.4426950408889634
LN2 = 0.6931471805599453
SCALE = HEAD_DIM**-0.5

F32 = jnp.float32
BF16 = jnp.bfloat16
VM = pl.BlockSpec(memory_space=pltpu.VMEM)
SM = pl.BlockSpec(memory_space=pltpu.SMEM)
HB = pl.BlockSpec(memory_space=pl.ANY)
NN = (((1,), (0,)), ((), ()))
NT = (((1,), (1,)), ((), ()))
TN = (((0,), (0,)), ((), ()))


def dot(a, b, dims=NN):
    return lax.dot_general(a, b, dims, preferred_element_type=F32)


def params():
    return pltpu.CompilerParams(vmem_limit_bytes=60 * 2**20)


def sds(shape, dtype=BF16):
    return jax.ShapeDtypeStruct(shape, dtype)


def cost(flops, nbytes):
    return pl.CostEstimate(flops=int(flops), bytes_accessed=int(nbytes), transcendentals=0)


def rms_factor(v):
    return lax.rsqrt(jnp.mean(v * v, axis=-1, keepdims=True) + EPS)


def norm_back(v, factor, gain, incoming):
    united = v * factor
    scaled = incoming * gain
    back = factor * (scaled - united * jnp.mean(scaled * united, axis=-1, keepdims=True))
    return back, jnp.sum(incoming * united, axis=0, keepdims=True)


def offsets(me, rows):
    return (
        me * rows,
        (me + 1 - 2 * (me % 2)) * rows,
        ((me + 2) % 4) * rows,
        (3 - me) * rows,
    )


def place_copies(me, pieces, src_of, buf, rows, sems, first):
    copies = []
    for k, off in enumerate(offsets(me, rows)):
        copies.append(
            pltpu.make_async_copy(
                src_of(pieces[k]),
                buf.at[pl.ds(pl.multiple_of(off, 32), rows)],
                sems.at[first + k],
            )
        )
    return copies


def pre_kernel(me_ref, tok, gains, cos_ref, sin_ref, w0, w1, w2, w3, nin_o, qraw_o, qs_o, kraw_o, kv_o, wbuf, sems):
    rows = D // 4
    copies = place_copies(
        me_ref[0], (w0, w1, w2, w3), lambda w: w.at[pl.ds(0, rows)], wbuf, rows, sems, 0
    )
    for c in copies:
        c.start()
    x = tok[...].astype(F32)
    nin = (x * rms_factor(x) * gains[0:1, :]).astype(BF16)
    nin_o[...] = nin
    cos = cos_ref[...]
    sin = sin_ref[...]
    hd = HEAD_DIM // 2
    for c in copies:
        c.wait()
    for h in range(HEADS):
        q = dot(nin, wbuf[:, HEAD_DIM * h : HEAD_DIM * (h + 1)])
        qraw_o[h] = q.astype(BF16)
        u = q * (rms_factor(q) * (SCALE * LOG2E)) * gains[4:5, :HEAD_DIM]
        u1 = u[:, :hd]
        u2 = u[:, hd:]
        qs_o[h, :, :hd] = (u1 * cos - u2 * sin).astype(BF16)
        qs_o[h, :, hd:] = (u2 * cos + u1 * sin).astype(BF16)
    base = HEADS * HEAD_DIM
    k = dot(nin, wbuf[:, base : base + HEAD_DIM])
    kraw_o[...] = k.astype(BF16)
    u = k * rms_factor(k) * gains[5:6, :HEAD_DIM]
    u1 = u[:, :hd]
    u2 = u[:, hd:]
    kv_o[:, :hd] = (u1 * cos - u2 * sin).astype(BF16)
    kv_o[:, hd:HEAD_DIM] = (u2 * cos + u1 * sin).astype(BF16)
    kv_o[:, HEAD_DIM:] = dot(nin, wbuf[:, base + HEAD_DIM :]).astype(BF16)


def pre(me, tok, gains, cos, sin, pieces, half):
    part = pl.BlockSpec((HALF, D), lambda i: (half, 0))
    tab = pl.BlockSpec((HALF, HEAD_DIM // 2), lambda i: (half, 0))
    return pl.pallas_call(
        pre_kernel,
        grid=(1,),
        out_shape=(
            sds((HALF, D)),
            sds((HEADS, HALF, HEAD_DIM)),
            sds((HEADS, HALF, HEAD_DIM)),
            sds((HALF, HEAD_DIM)),
            sds((HALF, 2 * HEAD_DIM)),
        ),
        in_specs=[SM, part, VM, tab, tab, HB, HB, HB, HB],
        out_specs=(VM,) * 5,
        scratch_shapes=[pltpu.VMEM((D, 6 * HEAD_DIM), BF16), pltpu.SemaphoreType.DMA((4,))],
        compiler_params=params(),
        cost_estimate=cost(2 * HALF * D * 1536, 5e6),
        name="pre",
    )(me, tok, gains, cos, sin, *pieces)


def key_blocks(j, kvp, kvs, lo, hi):
    blocks = (kvp[0:QB, lo:hi], kvp[QB : 2 * QB, lo:hi], kvs[0:QB, lo:hi], kvs[QB : 2 * QB, lo:hi])
    return blocks[j : j + 3]


def upper_mask():
    row = lax.broadcasted_iota(jnp.int32, (HEADS, QB, QB), 1).reshape(ROWS, QB)
    col = lax.broadcasted_iota(jnp.int32, (ROWS, QB), 1)
    return col > row


def att_kernel(masked, flag_ref, qs, kvp, kvs, o_o, pm_o, p1_o):
    upper = upper_mask()
    for j in range(2):
        sl = slice(QB * j, QB * (j + 1))
        q = qs[:, sl, :].reshape(ROWS, HEAD_DIM)
        k0, k1, k2 = key_blocks(j, kvp, kvs, 0, HEAD_DIM)
        v0, v1, v2 = key_blocks(j, kvp, kvs, HEAD_DIM, 2 * HEAD_DIM)
        em = jnp.exp2(jnp.where(upper, dot(q, k0, NT), dot(q, k2, NT)))
        e1 = jnp.exp2(dot(q, k1, NT))
        if masked:
            keep = flag_ref[0].astype(F32)
            em = em * jnp.where(upper, keep, 1.0)
            if j == 0:
                e1 = e1 * keep
        inv = 1.0 / jnp.sum(em + e1, axis=-1, keepdims=True)
        pm = (em * inv).astype(BF16)
        p1 = (e1 * inv).astype(BF16)
        zero = jnp.zeros_like(pm)
        out = dot(p1, v1) + dot(jnp.where(upper, pm, zero), v0) + dot(jnp.where(upper, zero, pm), v2)
        pm_o[:, sl, :] = pm.reshape(HEADS, QB, QB)
        p1_o[:, sl, :] = p1.reshape(HEADS, QB, QB)
        o_o[:, sl, :] = out.astype(BF16).reshape(HEADS, QB, HEAD_DIM)


def att(flag, qs, kvp, kvs, masked):
    shp = sds((HEADS, HALF, HEAD_DIM))

    def body(*refs):
        att_kernel(masked, *refs)

    return pl.pallas_call(
        body,
        out_shape=(shp, shp, shp),
        in_specs=[SM, VM, VM, VM],
        out_specs=(VM,) * 3,
        compiler_params=params(),
        cost_estimate=cost(12e9 / 4, 5e6),
        name="att",
    )(flag, qs, kvp, kvs)


def att_back_kernel(qs, qraw, kvp, kvs, pm_i, p1_i, do_i, gains, cos_ref, sin_ref, dq_o, dkvp_o, dkvs_o, gain_o, acc):
    upper = upper_mask()
    hd = HEAD_DIM // 2
    acc[...] = jnp.zeros_like(acc)
    gsum = jnp.zeros((1, HEAD_DIM), F32)
    for j in range(2):
        sl = slice(QB * j, QB * (j + 1))
        q = qs[:, sl, :].reshape(ROWS, HEAD_DIM)
        do = do_i[:, sl, :].reshape(ROWS, HEAD_DIM)
        k0, k1, k2 = key_blocks(j, kvp, kvs, 0, HEAD_DIM)
        v0, v1, v2 = key_blocks(j, kvp, kvs, HEAD_DIM, 2 * HEAD_DIM)
        pmb = pm_i[:, sl, :].reshape(ROWS, QB)
        p1b = p1_i[:, sl, :].reshape(ROWS, QB)
        dpm = jnp.where(upper, dot(do, v0, NT), dot(do, v2, NT))
        dp1 = dot(do, v1, NT)
        pm = pmb.astype(F32)
        p1 = p1b.astype(F32)
        total = jnp.sum(pm * dpm + p1 * dp1, axis=-1, keepdims=True)
        dsm = (pm * (dpm - total)).astype(BF16)
        ds1 = (p1 * (dp1 - total)).astype(BF16)
        zero = jnp.zeros_like(dsm)
        ds0 = jnp.where(upper, dsm, zero)
        ds2 = jnp.where(upper, zero, dsm)
        p0 = jnp.where(upper, pmb, zero)
        p2 = jnp.where(upper, zero, pmb)
        for t, (ds, p) in enumerate(((ds0, p0), (ds1, p1b), (ds2, p2))):
            at = slice(QB * (j + t), QB * (j + t + 1))
            acc[at, :HEAD_DIM] += dot(ds, q, TN) * LN2
            acc[at, HEAD_DIM:] += dot(p, do, TN)
        dq = (dot(ds0, k0) + dot(ds1, k1) + dot(ds2, k2)) * SCALE
        cos = cos_ref[sl, :]
        sin = sin_ref[sl, :]
        gain = gains[4:5, :HEAD_DIM]
        for h in range(HEADS):
            d1 = dq[QB * h : QB * (h + 1), :hd]
            d2 = dq[QB * h : QB * (h + 1), hd:]
            inc = jnp.concatenate([d1 * cos + d2 * sin, d2 * cos - d1 * sin], axis=-1)
            raw = qraw[h, sl, :].astype(F32)
            back, terms = norm_back(raw, rms_factor(raw), gain, inc)
            gsum = gsum + terms
            dq_o[sl, HEAD_DIM * h : HEAD_DIM * (h + 1)] = back.astype(BF16)
    dkvp_o[...] = acc[:HALF, :].astype(BF16)
    dkvs_o[...] = acc[HALF:, :]
    gain_o[...] = jnp.broadcast_to(gsum, (8, HEAD_DIM))


def att_back(qs, qraw, kvp, kvs, pm, p1, do, gains, cos, sin, half):
    dospec = pl.BlockSpec((HEADS, HALF, HEAD_DIM), lambda i: (0, half, 0))
    tab = pl.BlockSpec((HALF, HEAD_DIM // 2), lambda i: (half, 0))
    return pl.pallas_call(
        att_back_kernel,
        grid=(1,),
        out_shape=(
            sds((HALF, HEADS * HEAD_DIM)),
            sds((HALF, 2 * HEAD_DIM)),
            sds((HALF, 2 * HEAD_DIM), F32),
            sds((8, HEAD_DIM), F32),
        ),
        in_specs=[VM, VM, VM, VM, VM, VM, dospec, VM, tab, tab],
        out_specs=(VM,) * 4,
        scratch_shapes=[pltpu.VMEM((2 * HALF, 2 * HEAD_DIM), F32)],
        compiler_params=params(),
        cost_estimate=cost(24e9 / 4, 9e6),
        name="att_back",
    )(qs, qraw, kvp, kvs, pm, p1, do, gains, cos, sin)


def ffn_kernel(
    me_ref, o_lo, o_hi, tok, cot, gains,
    od0, od1, od2, od3, gu0, gu1, gu2, gu3,
    out_o, ap_o, nm_o, dd_o, a_o, b_o, gd_o, gain_o,
    wo, wg, wu, wd, hid, down, sems,
):
    me = me_ref[0]
    ods = (od0, od1, od2, od3)
    gus = (gu0, gu1, gu2, gu3)
    ro = HEADS * HEAD_DIM // 4
    rf = FF // 4
    rd = D // 4
    c_o = place_copies(me, ods, lambda w: w.at[pl.ds(0, ro)], wo, ro, sems, 0)
    c_g = place_copies(me, gus, lambda w: w.at[:, pl.ds(0, FF)], wg, rd, sems, 4)
    c_u = place_copies(me, gus, lambda w: w.at[:, pl.ds(FF, FF)], wu, rd, sems, 8)
    c_d = place_copies(me, ods, lambda w: w.at[pl.ds(ro, rf)], wd, rf, sems, 12)
    for c in c_o + c_g + c_u + c_d:
        c.start()
    for c in c_o:
        c.wait()
    for half, o in enumerate((o_lo, o_hi)):
        sl = slice(HALF * half, HALF * (half + 1))
        proj = dot(o[0], wo[0:HEAD_DIM, :])
        for h in range(1, HEADS):
            proj = proj + dot(o[h], wo[HEAD_DIM * h : HEAD_DIM * (h + 1), :])
        ap_o[sl, :] = proj.astype(BF16)
        mid = tok[sl, :].astype(F32) + proj * rms_factor(proj) * gains[1:2, :]
        nm_o[sl, :] = (mid * rms_factor(mid) * gains[2:3, :]).astype(BF16)
    for c in c_g + c_u:
        c.wait()
    down[...] = jnp.zeros_like(down)
    for c in c_d:
        c.wait()

    def chunk(i, _):
        cs = pl.ds(pl.multiple_of(i * CHUNK, CHUNK), CHUNK)
        g = dot(nm_o[...], wg[:, cs])
        u = dot(nm_o[...], wu[:, cs])
        c0 = 0.7978845608028654
        c1 = 0.044715 * c0
        g2 = g * g
        t = jnp.tanh(g * (c0 + c1 * g2))
        h = 0.5 + 0.5 * t
        a = g * h
        slope = h + a * (1.0 - h) * (2.0 * c0 + (6.0 * c1) * g2)
        hc = (a * u).astype(BF16)
        hid[:, cs] = hc
        a_o[:, cs] = a.astype(BF16)
        b_o[:, cs] = (u * slope).astype(BF16)
        down[...] += dot(hc, wd[cs, :])
        return 0

    lax.fori_loop(0, FF // CHUNK, chunk, 0)
    gsum = jnp.zeros((1, D), F32)
    for half in range(2):
        sl = slice(HALF * half, HALF * (half + 1))
        dn = down[sl, :]
        proj = ap_o[sl, :].astype(F32)
        mid = tok[sl, :].astype(F32) + proj * rms_factor(proj) * gains[1:2, :]
        fac = rms_factor(dn)
        out_o[sl, :] = (mid + dn * fac * gains[3:4, :]).astype(BF16)
        back, terms = norm_back(dn, fac, gains[3:4, :], cot[sl, :].astype(F32))
        dd_o[sl, :] = back.astype(BF16)
        gsum = gsum + terms
    gain_o[...] = jnp.broadcast_to(gsum, (8, D))

    def grad(i, _):
        cs = pl.ds(pl.multiple_of(i * CHUNK, CHUNK), CHUNK)
        gd_o[cs, :] = dot(hid[:, cs], dd_o[...], TN).astype(BF16)
        return 0

    lax.fori_loop(0, FF // CHUNK, grad, 0)


def ffn(me, o_lo, o_hi, tok, cot, gains, ods, gus):
    t = tok.shape[0]
    return pl.pallas_call(
        ffn_kernel,
        out_shape=(
            sds((t, D)),
            sds((t, D)),
            sds((t, D)),
            sds((t, D)),
            sds((t, FF)),
            sds((t, FF)),
            sds((FF, D)),
            sds((8, D), F32),
        ),
        in_specs=[SM] + [VM] * 5 + [HB] * 8,
        out_specs=(VM,) * 8,
        scratch_shapes=[
            pltpu.VMEM((HEADS * HEAD_DIM, D), BF16),
            pltpu.VMEM((D, FF), BF16),
            pltpu.VMEM((D, FF), BF16),
            pltpu.VMEM((FF, D), BF16),
            pltpu.VMEM((t, FF), BF16),
            pltpu.VMEM((t, D), F32),
            pltpu.SemaphoreType.DMA((16,)),
        ],
        compiler_params=params(),
        cost_estimate=cost(12e9, 30e6),
        name="ffn",
    )(me, o_lo, o_hi, tok, cot, gains, *ods, *gus)


def ffn_back_kernel(
    me_ref, o_lo, o_hi, tok, cot, gains, ap, nm, dd, a_i, b_i,
    od0, od1, od2, od3, gu0, gu1, gu2, gu3,
    ggu_o, go_o, do_o, dmid_o, gain_o,
    wo, wg, wu, wd, dnm, datt, sems,
):
    me = me_ref[0]
    ods = (od0, od1, od2, od3)
    gus = (gu0, gu1, gu2, gu3)
    ro = HEADS * HEAD_DIM // 4
    rf = FF // 4
    rd = D // 4
    c_d = place_copies(me, ods, lambda w: w.at[pl.ds(ro, rf)], wd, rf, sems, 12)
    c_g = place_copies(me, gus, lambda w: w.at[:, pl.ds(0, FF)], wg, rd, sems, 4)
    c_u = place_copies(me, gus, lambda w: w.at[:, pl.ds(FF, FF)], wu, rd, sems, 8)
    c_o = place_copies(me, ods, lambda w: w.at[pl.ds(0, ro)], wo, ro, sems, 0)
    for c in c_d + c_g + c_u + c_o:
        c.start()
    dnm[...] = jnp.zeros_like(dnm)
    for c in c_d + c_g + c_u:
        c.wait()

    def chunk(i, _):
        at = pl.multiple_of(i * CHUNK, CHUNK)
        cs = pl.ds(at, CHUNK)
        dh = dot(dd[...], wd[cs, :], NT)
        dg = (dh * b_i[:, cs].astype(F32)).astype(BF16)
        du = (dh * a_i[:, cs].astype(F32)).astype(BF16)
        dnm[...] += dot(dg, wg[:, cs], NT) + dot(du, wu[:, cs], NT)
        ggu_o[:, cs] = dot(nm[...], dg, TN).astype(BF16)
        ggu_o[:, pl.ds(FF + at, CHUNK)] = dot(nm[...], du, TN).astype(BF16)
        return 0

    lax.fori_loop(0, FF // CHUNK, chunk, 0)
    for c in c_o:
        c.wait()
    gm = jnp.zeros((1, D), F32)
    ga = jnp.zeros((1, D), F32)
    for half in range(2):
        sl = slice(HALF * half, HALF * (half + 1))
        proj = ap[sl, :].astype(F32)
        pfac = rms_factor(proj)
        mid = tok[sl, :].astype(F32) + proj * pfac * gains[1:2, :]
        back, terms = norm_back(mid, rms_factor(mid), gains[2:3, :], dnm[sl, :])
        dmid = cot[sl, :].astype(F32) + back
        gm = gm + terms
        dmid_o[sl, :] = dmid.astype(BF16)
        back, terms = norm_back(proj, pfac, gains[1:2, :], dmid)
        ga = ga + terms
        datt[sl, :] = back.astype(BF16)
    gain_o[0:8, :] = jnp.broadcast_to(gm, (8, D))
    gain_o[8:16, :] = jnp.broadcast_to(ga, (8, D))
    for h in range(HEADS):
        at = slice(HEAD_DIM * h, HEAD_DIM * (h + 1))
        do_o[h] = dot(datt[...], wo[at, :], NT).astype(BF16)
        go_o[at, :] = (dot(o_lo[h], datt[:HALF, :], TN) + dot(o_hi[h], datt[HALF:, :], TN)).astype(BF16)


def ffn_back(me, o_lo, o_hi, tok, cot, gains, ap, nm, dd, a, b, ods, gus):
    t = tok.shape[0]
    return pl.pallas_call(
        ffn_back_kernel,
        out_shape=(
            sds((D, 2 * FF)),
            sds((HEADS * HEAD_DIM, D)),
            sds((HEADS, t, HEAD_DIM)),
            sds((t, D)),
            sds((16, D), F32),
        ),
        in_specs=[SM] + [VM] * 10 + [HB] * 8,
        out_specs=(VM,) * 5,
        scratch_shapes=[
            pltpu.VMEM((HEADS * HEAD_DIM, D), BF16),
            pltpu.VMEM((D, FF), BF16),
            pltpu.VMEM((D, FF), BF16),
            pltpu.VMEM((FF, D), BF16),
            pltpu.VMEM((t, D), F32),
            pltpu.VMEM((t, D), BF16),
            pltpu.SemaphoreType.DMA((16,)),
        ],
        compiler_params=params(),
        cost_estimate=cost(16e9, 30e6),
        name="ffn_back",
    )(me, o_lo, o_hi, tok, cot, gains, ap, nm, dd, a, b, *ods, *gus)


def post_kernel(
    me_ref, tok, dmid, nin_lo, nin_hi, dq_lo, dq_hi, kv_a, kv_b, kv_c, kv_d, kraw_lo, kraw_hi,
    gains, cos_ref, sin_ref, w0, w1, w2, w3,
    gt_o, gw_o, gin_o, gk_o,
    wbuf, dkv, sems,
):
    rows = D // 4
    copies = place_copies(
        me_ref[0], (w0, w1, w2, w3), lambda w: w.at[pl.ds(0, rows)], wbuf, rows, sems, 0
    )
    for c in copies:
        c.start()
    hd = HEAD_DIM // 2
    base = HEADS * HEAD_DIM
    gk = jnp.zeros((1, HEAD_DIM), F32)
    for half, (first, second, kraw) in enumerate(((kv_a, kv_b, kraw_lo), (kv_c, kv_d, kraw_hi))):
        sl = slice(HALF * half, HALF * (half + 1))
        both = first[...].astype(F32) + second[...].astype(F32)
        cos = cos_ref[sl, :]
        sin = sin_ref[sl, :]
        d1 = both[:, :hd]
        d2 = both[:, hd:HEAD_DIM]
        inc = jnp.concatenate([d1 * cos + d2 * sin, d2 * cos - d1 * sin], axis=-1)
        raw = kraw[...].astype(F32)
        back, terms = norm_back(raw, rms_factor(raw), gains[5:6, :HEAD_DIM], inc)
        gk = gk + terms
        dkv[sl, :HEAD_DIM] = back.astype(BF16)
        dkv[sl, HEAD_DIM:] = both[:, HEAD_DIM:].astype(BF16)
    gk_o[...] = jnp.broadcast_to(gk, (8, HEAD_DIM))
    gw_o[:, :base] = (dot(nin_lo[...], dq_lo[...], TN) + dot(nin_hi[...], dq_hi[...], TN)).astype(BF16)
    gw_o[:, base:] = (
        dot(nin_lo[...], dkv[:HALF, :], TN) + dot(nin_hi[...], dkv[HALF:, :], TN)
    ).astype(BF16)
    for c in copies:
        c.wait()
    gi = jnp.zeros((1, D), F32)
    for half, dq in enumerate((dq_lo, dq_hi)):
        sl = slice(HALF * half, HALF * (half + 1))
        dnin = dot(dq[...], wbuf[:, :base], NT) + dot(dkv[sl, :], wbuf[:, base:], NT)
        x = tok[sl, :].astype(F32)
        back, terms = norm_back(x, rms_factor(x), gains[0:1, :], dnin)
        gi = gi + terms
        gt_o[sl, :] = (dmid[sl, :].astype(F32) + back).astype(BF16)
    gin_o[...] = jnp.broadcast_to(gi, (8, D))


def post(me, tok, dmid, nins, dqs, kvs, kraws, gains, cos, sin, pieces):
    t = tok.shape[0]
    return pl.pallas_call(
        post_kernel,
        out_shape=(
            sds((t, D)),
            sds((D, 6 * HEAD_DIM)),
            sds((8, D), F32),
            sds((8, HEAD_DIM), F32),
        ),
        in_specs=[SM] + [VM] * 15 + [HB] * 4,
        out_specs=(VM,) * 4,
        scratch_shapes=[
            pltpu.VMEM((D, 6 * HEAD_DIM), BF16),
            pltpu.VMEM((t, 2 * HEAD_DIM), BF16),
            pltpu.SemaphoreType.DMA((4,)),
        ],
        compiler_params=params(),
        cost_estimate=cost(4e9, 15e6),
        name="post",
    )(me, tok, dmid, *nins, *dqs, *kvs, *kraws, gains, cos, sin, *pieces)


def flip(x, axis, bit):
    n = lax.axis_size(axis)
    return lax.ppermute(x, axis, [(i, i ^ bit) for i in range(n)])


def gather_pieces(x):
    near = flip(x, "shard", 1)
    far = flip(x, "shard", 2)
    return (x, near, far, flip(far, "shard", 1))


def pick(x, index, axis):
    return lax.dynamic_index_in_dim(x, index, axis, keepdims=False)


def joined(a, b):
    return (a.astype(F32) + b.astype(F32)).astype(BF16)


def reduce_grad(x):
    rows, cols = x.shape[1:]
    shard = lax.axis_index("shard")
    core = shard % 2
    y = shard // 2
    x = x.reshape(2, 2, rows, cols)
    acc = joined(pick(x, core, 1), flip(pick(x, 1 - core, 1), "shard", 1))
    acc = joined(pick(acc, y, 0), flip(pick(acc, 1 - y, 0), "shard", 2))
    seq = lax.axis_index("seq")
    bits = []
    bit = 1
    while bit < lax.axis_size("seq"):
        bits.append(bit)
        bit *= 2
    for bit in bits[:-1]:
        here = (seq // bit) % 2
        acc = acc.reshape(2, acc.shape[0] // 2, cols)
        acc = joined(pick(acc, here, 0), flip(pick(acc, 1 - here, 0), "seq", bit))
    acc = joined(acc, flip(acc, "seq", bits[-1]))
    for bit in reversed(bits[:-1]):
        here = (seq // bit) % 2
        other = flip(acc, "seq", bit)
        acc = jnp.concatenate(
            [jnp.where(here == 0, acc, other), jnp.where(here == 0, other, acc)], axis=0
        )
    return acc.astype(F32)


def shards(
    tokens,
    query_weight,
    key_weight,
    value_weight,
    out_weight,
    gate_weight,
    up_weight,
    down_weight,
    input_gain,
    query_gain,
    key_gain,
    attended_gain,
    middle_gain,
    output_gain,
    cotangent,
):
    n_seq = lax.axis_size("seq")
    n_shard = lax.axis_size("shard")
    shard = lax.axis_index("shard")
    me = shard.reshape(1).astype(jnp.int32)
    count = tokens.shape[0]
    total = count * n_seq * n_shard
    length = min(SEQ_CAP, total)
    rank = lax.axis_index("seq") * n_shard + shard
    first_pos = rank * count % length
    flag = (first_pos > 0).reshape(1).astype(jnp.int32)

    gain_row = jnp.concatenate(
        [input_gain, attended_gain, middle_gain, output_gain, query_gain, key_gain]
    )
    wide = 6 * HEAD_DIM
    qkv_own = jnp.concatenate(
        [
            jnp.concatenate([query_weight, key_weight, value_weight], axis=1),
            jnp.pad(gain_row[None], ((0, 15), (0, wide - gain_row.shape[0]))),
        ],
        axis=0,
    )
    qkv = gather_pieces(qkv_own)
    gd = D // 4
    gh = HEAD_DIM // 4
    rows = jnp.stack([p[gd, : gain_row.shape[0]] for p in qkv])
    order = jnp.stack([shard, shard ^ 1, shard ^ 2, shard ^ 3])
    rows = jnp.zeros_like(rows).at[order].set(rows).astype(F32)
    gain_list = [rows[:, gd * i : gd * (i + 1)].reshape(1, D) for i in range(4)]
    gain_list += [
        jnp.pad(
            rows[:, 4 * gd + gh * i : 4 * gd + gh * (i + 1)].reshape(1, HEAD_DIM),
            ((0, 0), (0, D - HEAD_DIM)),
        )
        for i in range(2)
    ]
    gains = jnp.concatenate(gain_list + [jnp.zeros((2, D), F32)], axis=0)

    positions = first_pos + jnp.arange(count, dtype=jnp.int32)
    hd = HEAD_DIM // 2
    freq = ROPE_BASE ** (-(jnp.arange(hd, dtype=F32) * 2.0 / HEAD_DIM))
    angles = positions.astype(F32)[:, None] * freq[None, :]
    cos = jnp.cos(angles)
    sin = jnp.sin(angles)

    gus = gather_pieces(jnp.concatenate([gate_weight, up_weight], axis=1))
    ods = gather_pieces(jnp.concatenate([out_weight, down_weight], axis=0))

    nin_hi, qraw_hi, qs_hi, kraw_hi, kv_hi = pre(me, tokens, gains, cos, sin, qkv, 1)
    ranks = n_seq * n_shard
    per_seq = length // count
    pairs = [(i, i + 1) for i in range(ranks - 1) if (i + 1) % per_seq]
    halo = lax.ppermute(kv_hi, ("seq", "shard"), pairs)
    nin_lo, qraw_lo, qs_lo, kraw_lo, kv_lo = pre(me, tokens, gains, cos, sin, qkv, 0)
    o_hi, pm_hi, p1_hi = att(flag, qs_hi, kv_lo, kv_hi, False)
    o_lo, pm_lo, p1_lo = att(flag, qs_lo, halo, kv_lo, True)

    block_out, ap, nm, dd, a, b, g_down, gain_out = ffn(
        me, o_lo, o_hi, tokens, cotangent, gains, ods, gus
    )
    r_down = reduce_grad(g_down.reshape(4, FF // 4, D))
    g_gu, g_out, d_o, d_mid, gain_mid = ffn_back(
        me, o_lo, o_hi, tokens, cotangent, gains, ap, nm, dd, a, b, ods, gus
    )
    r_gu = reduce_grad(g_gu.reshape(4, D // 4, 2 * FF))
    r_out = reduce_grad(g_out.reshape(4, HEADS * HEAD_DIM // 4, D))

    dq_lo, kv_back, kv_a, gq_lo = att_back(
        qs_lo, qraw_lo, halo, kv_lo, pm_lo, p1_lo, d_o, gains, cos, sin, 0
    )
    returned = lax.ppermute(kv_back, ("seq", "shard"), [(j, i) for i, j in pairs])
    dq_hi, kv_b, kv_c, gq_hi = att_back(
        qs_hi, qraw_hi, kv_lo, kv_hi, pm_hi, p1_hi, d_o, gains, cos, sin, 1
    )
    grad_tokens, g_qkv, gain_in, gain_k = post(
        me,
        tokens,
        d_mid,
        (nin_lo, nin_hi),
        (dq_lo, dq_hi),
        (kv_a, kv_b, kv_c, returned),
        (kraw_lo, kraw_hi),
        gains,
        cos,
        sin,
        qkv,
    )
    gain_q = gq_lo[0] + gq_hi[0]
    parts = [gain_in[0], gain_mid[8], gain_mid[0], gain_out[0], gain_q, gain_k[0]]
    packed = jnp.concatenate([p.reshape(4, -1) for p in parts], axis=1).astype(BF16)
    packed = jnp.pad(packed[:, None], ((0, 0), (0, 15), (0, wide - packed.shape[1])))
    last = reduce_grad(jnp.concatenate([g_qkv.reshape(4, D // 4, wide), packed], axis=1))
    tail = last[gd]
    qd = HEADS * HEAD_DIM
    return (
        block_out,
        grad_tokens,
        last[:gd, :qd],
        last[:gd, qd : qd + HEAD_DIM],
        last[:gd, qd + HEAD_DIM :],
        r_out,
        r_gu[:, :FF],
        r_gu[:, FF:],
        r_down,
        tail[:gd],
        tail[4 * gd : 4 * gd + gh],
        tail[4 * gd + gh : 4 * gd + 2 * gh],
        tail[gd : 2 * gd],
        tail[2 * gd : 3 * gd],
        tail[3 * gd : 4 * gd],
    )


def solution(mesh):
    token = P(("seq", "shard"), None)
    matrix = P("shard", None)
    vector = P("shard")
    in_specs = (token,) + (matrix,) * 7 + (vector,) * 6 + (token,)
    out_specs = (token, token) + (matrix,) * 7 + (vector,) * 6
    return jax.shard_map(shards, mesh=mesh, in_specs=in_specs, out_specs=out_specs, check_vma=False)
```

time: 627 us -> 348 us (0.56)
  matrix products: 181 us -> 0 us
  Pallas kernels: 0 us -> 117 us
  waiting for transfers between devices: 245 us -> 149 us
  blocking collectives: 50.5 us -> 0 us
  other arithmetic: 57.1 us -> 15.9 us
  local copies, waits for them, and re-layouts: 60.6 us -> 20.3 us
  starting transfers between devices: 10.1 us -> 40.4 us
  between operations: 17.8 us -> 1.77 us
    dot_general x33 -> x0, matrix products: 181 us -> none  [the longest x2 30.3 us: shards(): jnp.einsum('hqk,kd->qhd', d_scores, keys_block, preferred_element_type=jn...]
    reduce_scatter x7 -> x0, waiting for transfers between devices: 163 us -> none  [the longest x1 37.4 us: shards(): lax.psum_scatter(total_up.astype(jnp.bfloat16), 'shard', scatter_dimensio...]
    ppermute x4 -> x39, waiting for transfers between devices: 0.01 us -> 149 us  [the longest x37 149 us: flip(): return lax.ppermute(x, axis, [(i, i ^ bit) for i in range(n)])]
    pallas_call x0 -> x9, Pallas kernels: none -> 117 us  [the longest x1 33.9 us: ffn_back(): pl.pallas_call(ffn_back_kernel, out_shape=(sds((D, 2 * FF)), sds((HEADS *...]
    psum x1 -> x0, waiting for transfers between devices: 61.9 us -> none  [shards(): lax.psum(grad_query.astype(jnp.bfloat16), 'seq').astype(jnp.float32)]
    ppermute x4 -> x39, starting transfers between devices: 8.49 us -> 40.4 us  [the longest x37 36.6 us: flip(): return lax.ppermute(x, axis, [(i, i ^ bit) for i in range(n)])]
    psum x1 -> x0, blocking collectives: 21.5 us -> none  [shards(): lax.psum(sum_input.astype(jnp.bfloat16), 'seq').astype(jnp.float32)]
    unnamed x165 -> x53, local copies, waits for them, and re-layouts: 25.3 us -> 4.37 us
  transfers between devices with their start and end apart: 17 -> 39, of which waited for: 8 -> 18; matrix products, arithmetic and copies ran while one was open for 29% -> 9% of each run, Pallas kernels for 0% -> 13%
where the time goes in v1:
time: 348 us; the launch traced here: 344 us
  waiting for transfers between devices  149 us (43%)
  Pallas kernels  117 us (34%)
  starting transfers between devices  40.4 us (12%)
  local copies, waits for them, and re-layouts  20.3 us (6%)
  other arithmetic  15.9 us (5%)
    ppermute x37, waiting for transfers between devices, flip(): return lax.ppermute(x, axis, [(i, i ^ bit) for i in range(n)])  149 us
    ppermute x37, starting transfers between devices, flip(): return lax.ppermute(x, axis, [(i, i ^ bit) for i in range(n)])  36.6 us
    pallas_call x1, Pallas kernels, ffn_back(): pl.pallas_call(ffn_back_kernel, out_shape=(sds((D, 2 * FF)), sds((HEADS *...  33.9 us
    pallas_call x1, Pallas kernels, ffn(): pl.pallas_call(ffn_kernel, out_shape=(sds((t, D)), sds((t, D)), sds((t, D...  29.9 us
    pallas_call x2, Pallas kernels, att_back(): pl.pallas_call(att_back_kernel, grid=(1,), out_shape=(sds((HALF, HEADS *...  18.7 us
    pallas_call x1, Pallas kernels, post(): pl.pallas_call(post_kernel, out_shape=(sds((t, D)), sds((D, 6 * HEAD_DIM)...  12.2 us
    pallas_call x2, Pallas kernels, pre(): pl.pallas_call(pre_kernel, grid=(1,), out_shape=(sds((HALF, D)), sds((HEA...  11.4 us
    pallas_call x2, Pallas kernels, att(): pl.pallas_call(body, out_shape=(shp, shp, shp), in_specs=[SM, VM, VM, VM]...  10.4 us
  transfers between devices with their start and end apart: 39, of which 18 were waited for; matrix products, arithmetic and copies ran while one was open for 9% of the time, Pallas kernels for 13%

profile of v1, /device:TPU:0, one launch (start us, length us, event | category | flops | bytes accessed | tf_op | source)
XLA Modules:
  0.0 343.5 jit_solution(782997070842786300)
XLA Ops:
  0.7 2.1 constant_dynamic-update-slice_fusion.3
  3.7 3.0 collective-permute-start.8
  8.7 1.9 collective-permute-start.5
  11.2 36.9 %collective-permute-done.1.w2 = bf16[176,1536]{1,0:T(8,128)(2,1)S(1)} collective-permute-done((bf16[176,1536]{1,0:T(8,128)(2,1)S(1)}, bf16[176,1536]{1,0:T(8,128)(2,1)S(1)}, u32[]{:S(2)}, u32[]{:S(2)}) %collective-permute-start.1) | collective-permute-done | bytes 540704 | tf_op jit(solution)/shard_map/ppermute | solution.py:521
  48.2 3.1 multiply_sine_fusion
  51.9 16.5 %collective-permute-done.5.od2 = bf16[768,640]{1,0:T(8,128)(2,1)} collective-permute-done((bf16[768,640]{1,0:T(8,128)(2,1)}, bf16[768,640]{1,0:T(8,128)(2,1)}, u32[]{:S(2)}, u32[]{:S(2)}) %collective-permute-start.5) | collective-permute-done | bytes 983072 | tf_op jit(solution)/shard_map/ppermute | solution.py:521
  71.0 5.7 %pre.3 = (bf16[512,640]{1,0:T(8,128)(2,1)}, bf16[4,512,256]{2,1,0:T(8,128)(2,1)}, bf16[4,512,256]{2,1,0:T(8,128)(2,1)}, bf16[512,256]{1,0:T(8,128)(2,1)}, bf16[512,512]{1,0:T(8,128)(2,1)}) custom-call(s32[1]{0:T(128)} %bitcast.me_ref, bf16[1024,640]{1,0:T(8,128)(2,1)} %tok.9, f32[8,640]{1,0:T(8,128)} %concatenate.95.gains, ...), custom_call_target="tpu_custom_call" | custom-call | flops 1006632960 | bytes 5000000 | tf_op jit(solution)/shard_map/pre/pallas_call | solution.py:121
  76.7 2.2 collective-permute-start.3
  79.1 5.7 %pre.2 = (bf16[512,640]{1,0:T(8,128)(2,1)}, bf16[4,512,256]{2,1,0:T(8,128)(2,1)}, bf16[4,512,256]{2,1,0:T(8,128)(2,1)}, bf16[512,256]{1,0:T(8,128)(2,1)}, bf16[512,512]{1,0:T(8,128)(2,1)}) custom-call(s32[1]{0:T(128)} %bitcast.me_ref, bf16[1024,640]{1,0:T(8,128)(2,1)} %tok.9, f32[8,640]{1,0:T(8,128)} %concatenate.95.gains, ...), custom_call_target="tpu_custom_call" | custom-call | flops 1006632960 | bytes 5000000 | tf_op jit(solution)/shard_map/pre/pallas_call | solution.py:121
  84.8 5.2 %att.3 = (bf16[4,512,256]{2,1,0:T(8,128)(2,1)}, bf16[4,512,256]{2,1,0:T(8,128)(2,1)}, bf16[4,512,256]{2,1,0:T(8,128)(2,1)}) custom-call(s32[1]{0:T(128)} %bitcast.1.refs_0_, bf16[4,512,256]{2,1,0:T(8,128)(2,1)} %get-tuple-element.60.refs_1_.qs, bf16[512,512]{1,0:T(8,128)(2,1)} %get-tuple-element.58.refs_3_.refs_2_.kvs.kvp, ...), custom_call_target="tpu_custom_call" | custom-call | flops 3000000000 | bytes 5000000 | tf_op jit(solution)/shard_map/att/pallas_call | solution.py:181
  90.7 5.2 %att.2 = (bf16[4,512,256]{2,1,0:T(8,128)(2,1)}, bf16[4,512,256]{2,1,0:T(8,128)(2,1)}, bf16[4,512,256]{2,1,0:T(8,128)(2,1)}) custom-call(s32[1]{0:T(128)} %bitcast.1.refs_0_, bf16[4,512,256]{2,1,0:T(8,128)(2,1)} %get-tuple-element.56.refs_1_.qs, bf16[512,512]{1,0:T(8,128)(2,1)} %copy-done.22, bf16[512,512]{1,0:T(8,128)(2,1)} %get-tuple-element.58.refs_3_.refs_2_.kvs.kvp), custom_call_target="tpu_custom_call" | custom-call | flops 3000000000 | bytes 5000000 | tf_op jit(solution)/shard_map/att/pallas_call | solution.py:181
  96.0 29.9 %ffn.1 = (bf16[1024,640]{1,0:T(8,128)(2,1)}, bf16[1024,640]{1,0:T(8,128)(2,1)}, bf16[1024,640]{1,0:T(8,128)(2,1)}, bf16[1024,640]{1,0:T(8,128)(2,1)}, bf16[1024,...) custom-call(s32[1]{0:T(128)} %bitcast.me_ref, ...), custom_call_target="tpu_custom_call" | custom-call | flops 12000000000 | bytes 30000000 | tf_op jit(solution)/shard_map/ffn/pallas_call | solution.py:335
  125.9 33.9 %ffn_back.1 = (bf16[640,4096]{1,0:T(8,128)(2,1)}, bf16[1024,640]{1,0:T(8,128)(2,1)}, bf16[4,1024,256]{2,1,0:T(8,128)(2,1)}, bf16[1024,640]{1,0:T(8,128)(2,1)}, f32[16,640]{1,0:T(8,128)}) custom-call(s32[1]{0:T(128)} %bitcast.me_ref, bf16[4,512,256]{2,1,0:T(8,128)(2,1)} %get-tuple-element.59.o_lo, bf16[4,512,256]{2,1,0:T(8,128)(2,1)} %get-tuple-element.61.o_hi, ...), custom_call_target="tpu_custom_call" | custom-call | flops 16000000000 | bytes 30000000 | tf_op jit(solution)/shard_map/ffn_back/pallas_call | solution.py:424
  159.9 9.3 %att_back.2 = (bf16[512,1024]{1,0:T(8,128)(2,1)}, bf16[512,512]{1,0:T(8,128)(2,1)}, f32[512,512]{1,0:T(8,128)}, f32[8,256]{1,0:T(8,128)}) custom-call(bf16[4,512,256]{2,1,0:T(8,128)(2,1)} %get-tuple-element.56.refs_1_.qs, bf16[4,512,256]{2,1,0:T(8,128)(2,1)} %get-tuple-element.71.qraw, bf16[512,512]{1,0:T(8,128)(2,1)} %copy-done.22, ...), custom_call_target="tpu_custom_call" | custom-call | flops 6000000000 | bytes 9000000 | tf_op jit(solution)/shard_map/att_back/pallas_call | solution.py:241
  169.1 1.5 collective-permute-start.10
  172.3 2.4 collective-permute-start.18
  174.8 9.4 %att_back.3 = (bf16[512,1024]{1,0:T(8,128)(2,1)}, bf16[512,512]{1,0:T(8,128)(2,1)}, f32[512,512]{1,0:T(8,128)}, f32[8,256]{1,0:T(8,128)}) custom-call(bf16[4,512,256]{2,1,0:T(8,128)(2,1)} %get-tuple-element.60.refs_1_.qs, bf16[4,512,256]{2,1,0:T(8,128)(2,1)} %get-tuple-element.76.qraw, bf16[512,512]{1,0:T(8,128)(2,1)} %get-tuple-element.58.refs_3_.refs_2_.kvs.kvp, ...), custom_call_target="tpu_custom_call" | custom-call | flops 6000000000 | bytes 9000000 | tf_op jit(solution)/shard_map/att_back/pallas_call | solution.py:241
  187.3 1.7 collective-permute-start.19
  189.0 12.2 %post.1 = (bf16[1024,640]{1,0:T(8,128)(2,1)}, bf16[640,1536]{1,0:T(8,128)(2,1)}, f32[8,640]{1,0:T(8,128)}, f32[8,256]{1,0:T(8,128)}) custom-call(s32[1]{0:T(128)} %bitcast.me_ref, bf16[1024,640]{1,0:T(8,128)(2,1)} %tok.9, bf16[1024,640]{1,0:T(8,128)(2,1)} %get-tuple-element.68.dmid, bf16[512,640]{1,0:T(8,128)(2,1)} %get-tuple-element.69.nin_lo, ...), custom_call_target="tpu_custom_call" | custom-call | flops 4000000000 | bytes 15000000 | tf_op jit(solution)/shard_map/post/pallas_call | solution.py:498
  201.4 1.6 collective-permute-start.20
  204.7 3.1 collective-permute-done.20
  207.8 1.9 collective-permute-start.21
  209.9 2.7 collective-permute-done.21
  212.6 2.7 collective-permute-start.22
  215.3 2.2 dynamic-slice_bitcast_fusion
  218.0 1.6 collective-permute-start.23
  219.7 1.6 fusion.1
  221.4 1.2 collective-permute-start.33
  222.7 1.8 collective-permute-start.24
  226.0 2.3 collective-permute-done.24
  229.3 9.9 %collective-permute-done.33 = bf16[512,640]{1,0:T(8,128)(2,1)S(1)} collective-permute-done((bf16[512,640]{1,0:T(8,128)(2,1)S(1)}, bf16[512,640]{1,0:T(8,128)(2,1)S(1)}, u32[]{:S(2)}, u32[]{:S(2)}) %collective-permute-start.33) | collective-permute-done | bytes 655392 | tf_op jit(solution)/shard_map/ppermute | solution.py:521
  239.3 1.6 collective-permute-start.34
  240.9 8.6 %collective-permute-done.12 = bf16[176,1536]{1,0:T(8,128)(2,1)S(1)} collective-permute-done((bf16[176,1536]{1,0:T(8,128)(2,1)S(1)}, bf16[176,1536]{1,0:T(8,128)(2,1)S(1)}, u32[]{:S(2)}, u32[]{:S(2)}) %collective-permute-start.12) | collective-permute-done | bytes 540704 | tf_op jit(solution)/shard_map/ppermute | solution.py:521
  249.6 1.6 collective-permute-start.13
  254.6 1.4 collective-permute-start.26
  259.9 3.1 collective-permute-done.14
  263.1 8.6 %collective-permute-done.36 = bf16[128,640]{1,0:T(8,128)(2,1)S(1)} collective-permute-done((bf16[128,640]{1,0:T(8,128)(2,1)S(1)}, bf16[128,640]{1,0:T(8,128)(2,1)S(1)}, u32[]{:S(2)}, u32[]{:S(2)}) %collective-permute-start.36) | collective-permute-done | bytes 163872 | tf_op jit(solution)/shard_map/ppermute | solution.py:521
  271.9 11.9 %collective-permute-done.26 = bf16[160,4096]{1,0:T(8,128)(2,1)} collective-permute-done((bf16[160,4096]{1,0:T(8,128)(2,1)}, bf16[160,4096]{1,0:T(8,128)(2,1)}, u32[]{:S(2)}, u32[]{:S(2)}) %collective-permute-start.26) | collective-permute-done | bytes 1310752 | tf_op jit(solution)/shard_map/ppermute | solution.py:521
  283.8 1.7 fusion.2
  286.3 1.6 collective-permute-start.16
  288.0 1.6 collective-permute-start.38
  289.5 13.8 %collective-permute-done.27 = bf16[80,4096]{1,0:T(8,128)(2,1)S(1)} collective-permute-done((bf16[80,4096]{1,0:T(8,128)(2,1)S(1)}, bf16[80,4096]{1,0:T(8,128)(2,1)S(1)}, u32[]{:S(2)}, u32[]{:S(2)}) %collective-permute-start.27) | collective-permute-done | bytes 655392 | tf_op jit(solution)/shard_map/ppermute | solution.py:521
  303.5 1.7 collective-permute-start.28
  305.9 5.6 %collective-permute-done.28 = bf16[40,4096]{1,0:T(8,128)(2,1)S(1)} collective-permute-done((bf16[40,4096]{1,0:T(8,128)(2,1)S(1)}, bf16[40,4096]{1,0:T(8,128)(2,1)S(1)}, u32[]{:S(2)}, u32[]{:S(2)}) %collective-permute-start.28) | collective-permute-done | bytes 327712 | tf_op jit(solution)/shard_map/ppermute | solution.py:521
  312.6 10.5 %collective-permute-done.29 = bf16[40,4096]{1,0:T(8,128)(2,1)S(1)} collective-permute-done((bf16[40,4096]{1,0:T(8,128)(2,1)S(1)}, bf16[40,4096]{1,0:T(8,128)(2,1)S(1)}, u32[]{:S(2)}, u32[]{:S(2)}) %collective-permute-start.29) | collective-permute-done | bytes 327712 | tf_op jit(solution)/shard_map/ppermute | solution.py:521
  324.0 6.3 %collective-permute-done.30 = bf16[40,4096]{1,0:T(8,128)(2,1)S(1)} collective-permute-done((bf16[40,4096]{1,0:T(8,128)(2,1)S(1)}, bf16[40,4096]{1,0:T(8,128)(2,1)S(1)}, u32[]{:S(2)}, u32[]{:S(2)}) %collective-permute-start.30) | collective-permute-done | bytes 327712 | tf_op jit(solution)/shard_map/ppermute | solution.py:521
  334.5 6.5 %collective-permute-done.31 = bf16[80,4096]{1,0:T(8,128)(2,1)S(1)} collective-permute-done((bf16[80,4096]{1,0:T(8,128)(2,1)S(1)}, bf16[80,4096]{1,0:T(8,128)(2,1)S(1)}, u32[]{:S(2)}, u32[]{:S(2)}) %collective-permute-start.31) | collective-permute-done | bytes 655392 | tf_op jit(solution)/shard_map/ppermute | solution.py:521
  341.6 1.7 fusion.35
  (190 shorter events, 33.7 us)
Async XLA Ops:
  3.7 65.4 %collective-permute-start.8 = (bf16[160,4096]{1,0:T(8,128)(2,1)}, bf16[160,4096]{1,0:T(8,128)(2,1)}, u32[]{:S(2)}, u32[]{:S(2)}) collective-permute-start(bf16[160,4096]{1,0:T(8,128)(2,1)} %constant_dynamic-update-slice_fusion.2.gu0), channel_id=1, source_target_pairs={{0,2},{1,3},{2,0},{3,1},{4,6},{5,7},{6,4},{7,5},{8,10},{9,11},{10,... | collective-permute-start | bytes 3932168 | tf_op jit(solution)/shard_map/ppermute | solution.py:521
  6.9 44.4 %copy-start.1 = (bf16[176,1536]{1,0:T(8,128)(2,1)}, bf16[176,1536]{1,0:T(8,128)(2,1)S(1)}, u32[]{:S(2)}) copy-start(bf16[176,1536]{1,0:T(8,128)(2,1)S(1)} %fusion.16.w0) | copy-start | bytes 1622020
  6.9 41.2 %collective-permute-start.1 = (bf16[176,1536]{1,0:T(8,128)(2,1)S(1)}, bf16[176,1536]{1,0:T(8,128)(2,1)S(1)}, u32[]{:S(2)}, u32[]{:S(2)}) collective-permute-start(bf16[176,1536]{1,0:T(8,128)(2,1)S(1)} %fusion.16.w0), channel_id=1, source_target_pairs={{0,2},{1,3},{2,0},{3,1},{4,6},{5,7},{6,4},{7,5},{8,10},{9,11},{10,... | collective-permute-start | bytes 1622024 | tf_op jit(solution)/shard_map/ppermute | solution.py:521
  8.7 59.7 %collective-permute-start.5 = (bf16[768,640]{1,0:T(8,128)(2,1)}, bf16[768,640]{1,0:T(8,128)(2,1)}, u32[]{:S(2)}, u32[]{:S(2)}) collective-permute-start(bf16[768,640]{1,0:T(8,128)(2,1)} %constant_dynamic-update-slice_fusion.od0), channel_id=1, source_target_pairs={{0,2},{1,3},{2,0},{3,1},{4,6},{5,7},{6,4},{7,5},{8,10},{9,11},{10,... | collective-permute-start | bytes 2949128 | tf_op jit(solution)/shard_map/ppermute | solution.py:521
  10.7 40.6 %collective-permute-start = (bf16[176,1536]{1,0:T(8,128)(2,1)S(1)}, bf16[176,1536]{1,0:T(8,128)(2,1)S(1)}, u32[]{:S(2)}, u32[]{:S(2)}) collective-permute-start(bf16[176,1536]{1,0:T(8,128)(2,1)S(1)} %fusion.16.w0), channel_id=1, source_target_pairs={{0,1},{1,0},{2,3},{3,2},{4,5},{5,4},{6,7},{7,6},{8,9},{9,8},{10,11... | collective-permute-start | bytes 1622024 | tf_op jit(solution)/shard_map/ppermute | solution.py:521
  10.7 85.3 %collective-permute-start.7 = (bf16[160,4096]{1,0:T(8,128)(2,1)}, bf16[160,4096]{1,0:T(8,128)(2,1)}, u32[]{:S(2)}, u32[]{:S(2)}) collective-permute-start(bf16[160,4096]{1,0:T(8,128)(2,1)} %constant_dynamic-update-slice_fusion.2.gu0), channel_id=1, source_target_pairs={{0,1},{1,0},{2,3},{3,2},{4,5},{5,4},{6,7},{7,6},{8,9},{9,8},{10,11... | collective-permute-start | bytes 3932168 | tf_op jit(solution)/shard_map/ppermute | solution.py:521
  48.1 22.9 %copy-start.4 = (bf16[176,1536]{1,0:T(8,128)(2,1)}, bf16[176,1536]{1,0:T(8,128)(2,1)S(1)}, u32[]{:S(2)}) copy-start(bf16[176,1536]{1,0:T(8,128)(2,1)S(1)} %collective-permute-done.1.w2) | copy-start | bytes 1622020
  48.1 20.3 %collective-permute-start.2 = (bf16[176,1536]{1,0:T(8,128)(2,1)S(1)}, bf16[176,1536]{1,0:T(8,128)(2,1)S(1)}, u32[]{:S(2)}, u32[]{:S(2)}) collective-permute-start(bf16[176,1536]{1,0:T(8,128)(2,1)S(1)} %collective-permute-done.1.w2), channel_id=1, source_target_pairs={{0,1},{1,0},{2,3},{3,2},{4,5},{5,4},{6,7},{7,6},{8,9},{9,8},{10,11... | collective-permute-start | bytes 1622024 | tf_op jit(solution)/shard_map/ppermute | solution.py:521
  51.3 19.7 %copy-start.5 = (bf16[176,1536]{1,0:T(8,128)(2,1)}, bf16[176,1536]{1,0:T(8,128)(2,1)S(1)}, u32[]{:S(2)}) copy-start(bf16[176,1536]{1,0:T(8,128)(2,1)S(1)} %collective-permute-done.w1) | copy-start | bytes 1622020
  51.3 44.6 %collective-permute-start.4 = (bf16[768,640]{1,0:T(8,128)(2,1)}, bf16[768,640]{1,0:T(8,128)(2,1)}, u32[]{:S(2)}, u32[]{:S(2)}) collective-permute-start(bf16[768,640]{1,0:T(8,128)(2,1)} %constant_dynamic-update-slice_fusion.od0), channel_id=1, source_target_pairs={{0,1},{1,0},{2,3},{3,2},{4,5},{5,4},{6,7},{7,6},{8,9},{9,8},{10,11... | collective-permute-start | bytes 2949128 | tf_op jit(solution)/shard_map/ppermute | solution.py:521
  68.4 27.5 %collective-permute-start.6 = (bf16[768,640]{1,0:T(8,128)(2,1)}, bf16[768,640]{1,0:T(8,128)(2,1)}, u32[]{:S(2)}, u32[]{:S(2)}) collective-permute-start(bf16[768,640]{1,0:T(8,128)(2,1)} %collective-permute-done.5.od2), channel_id=1, source_target_pairs={{0,1},{1,0},{2,3},{3,2},{4,5},{5,4},{6,7},{7,6},{8,9},{9,8},{10,11... | collective-permute-start | bytes 2949128 | tf_op jit(solution)/shard_map/ppermute | solution.py:521
  69.1 26.9 %collective-permute-start.9 = (bf16[160,4096]{1,0:T(8,128)(2,1)}, bf16[160,4096]{1,0:T(8,128)(2,1)}, u32[]{:S(2)}, u32[]{:S(2)}) collective-permute-start(bf16[160,4096]{1,0:T(8,128)(2,1)} %collective-permute-done.8.gu2), channel_id=1, source_target_pairs={{0,1},{1,0},{2,3},{3,2},{4,5},{5,4},{6,7},{7,6},{8,9},{9,8},{10,11... | collective-permute-start | bytes 3932168 | tf_op jit(solution)/shard_map/ppermute | solution.py:521
  76.7 13.2 %collective-permute-start.3 = (bf16[512,512]{1,0:T(8,128)(2,1)}, bf16[512,512]{1,0:T(8,128)(2,1)S(1)}, u32[]{:S(2)}, u32[]{:S(2)}) collective-permute-start(bf16[512,512]{1,0:T(8,128)(2,1)} %get-tuple-element.57.refs_3_.kvs), channel_id=1, source_target_pairs={{0,1},{1,2},{2,3},{3,4},{4,5},{5,6},{6,7},{8,9},{9,10},{10,11},{11... | collective-permute-start | bytes 1572872 | tf_op jit(solution)/shard_map/ppermute | solution.py:635
  159.8 10.8 %copy-start.15 = (f32[16,640]{1,0:T(8,128)S(1)}, f32[16,640]{1,0:T(8,128)}, u32[]{:S(2)}) copy-start(f32[16,640]{1,0:T(8,128)} %get-tuple-element.89) | copy-start | bytes 122884
  159.9 11.6 %copy-start.7 = (bf16[1024,640]{1,0:T(8,128)(2,1)S(1)}, bf16[1024,640]{1,0:T(8,128)(2,1)}, u32[]{:S(2)}) copy-start(bf16[1024,640]{1,0:T(8,128)(2,1)} %get-tuple-element.94) | copy-start | bytes 3932164
  169.1 19.9 %collective-permute-start.10 = (bf16[512,512]{1,0:T(8,128)(2,1)}, bf16[512,512]{1,0:T(8,128)(2,1)}, u32[]{:S(2)}, u32[]{:S(2)}) collective-permute-start(bf16[512,512]{1,0:T(8,128)(2,1)} %get-tuple-element.83), channel_id=1, source_target_pairs={{1,0},{2,1},{3,2},{4,3},{5,4},{6,5},{7,6},{9,8},{10,9},{11,10},{12... | collective-permute-start | bytes 1572872 | tf_op jit(solution)/shard_map/ppermute | solution.py:653
  172.3 14.2 %collective-permute-start.18 = (bf16[2,256,640]{2,1,0:T(8,128)(2,1)}, bf16[2,256,640]{2,1,0:T(8,128)(2,1)S(1)}, u32[]{:S(2)}, u32[]{:S(2)}) collective-permute-start(bf16[2,256,640]{2,1,0:T(8,128)(2,1)} %dynamic-slice_bitcast_fusion.5), channel_id=1, source_target_pairs={{0,1},{1,0},{2,3},{3,2},{4,5},{5,4},{6,7},{7,6},{8,9},{9,8},{10,11... | collective-permute-start | bytes 1966088 | tf_op jit(solution)/shard_map/ppermute | solution.py:521
  174.8 10.5 %copy-start.2 = (bf16[2048,640]{1,0:T(8,128)(2,1)S(1)}, bf16[2048,640]{1,0:T(8,128)(2,1)}, u32[]{:S(2)}) copy-start(bf16[2048,640]{1,0:T(8,128)(2,1)} %get-tuple-element.96) | copy-start | bytes 7864324
  186.5 33.2 %collective-permute-start.32 = (bf16[2,512,640]{2,1,0:T(8,128)(2,1)}, bf16[2,512,640]{2,1,0:T(8,128)(2,1)}, u32[]{:S(2)}, u32[]{:S(2)}) collective-permute-start(bf16[2,512,640]{2,1,0:T(8,128)(2,1)} %dynamic-slice_bitcast_fusion.1), channel_id=1, source_target_pairs={{0,1},{1,0},{2,3},{3,2},{4,5},{5,4},{6,7},{7,6},{8,9},{9,8},{10,11... | collective-permute-start | bytes 3932168 | tf_op jit(solution)/shard_map/ppermute | solution.py:521
  187.3 13.9 %collective-permute-start.19 = (bf16[256,640]{1,0:T(8,128)(2,1)S(1)}, bf16[256,640]{1,0:T(8,128)(2,1)S(1)}, u32[]{:S(2)}, u32[]{:S(2)}) collective-permute-start(bf16[256,640]{1,0:T(8,128)(2,1)S(1)} %dynamic-slice_bitcast_fusion.9), channel_id=1, source_target_pairs={{0,2},{1,3},{2,0},{3,1},{4,6},{5,7},{6,4},{7,5},{8,10},{9,11},{10,... | collective-permute-start | bytes 983048 | tf_op jit(solution)/shard_map/ppermute | solution.py:521
  201.2 8.5 %copy-start = (bf16[640,1536]{1,0:T(8,128)(2,1)S(1)}, bf16[640,1536]{1,0:T(8,128)(2,1)}, u32[]{:S(2)}) copy-start(bf16[640,1536]{1,0:T(8,128)(2,1)} %get-tuple-element.87) | copy-start | bytes 5898244
  201.4 6.4 %collective-permute-start.20 = (bf16[128,640]{1,0:T(8,128)(2,1)S(1)}, bf16[128,640]{1,0:T(8,128)(2,1)S(1)}, u32[]{:S(2)}, u32[]{:S(2)}) collective-permute-start(bf16[128,640]{1,0:T(8,128)(2,1)S(1)} %dynamic-slice_bitcast_fusion.12), channel_id=1, source_target_pairs={{0,4},{4,0},{8,12},{12,8},{16,20},{20,16},{24,28},{28,24},{1,5},{5... | collective-permute-start | bytes 491528 | tf_op jit(solution)/shard_map/ppermute | solution.py:521
  207.8 4.8 %collective-permute-start.21 = (bf16[64,640]{1,0:T(8,128)(2,1)S(1)}, bf16[64,640]{1,0:T(8,128)(2,1)S(1)}, u32[]{:S(2)}, u32[]{:S(2)}) collective-permute-start(bf16[64,640]{1,0:T(8,128)(2,1)S(1)} %dynamic-slice_bitcast_fusion.14), channel_id=1, source_target_pairs={{0,8},{4,12},{8,0},{12,4},{16,24},{20,28},{24,16},{28,20},{1,9},{5... | collective-permute-start | bytes 245768 | tf_op jit(solution)/shard_map/ppermute | solution.py:521
  209.8 14.7 %collective-permute-start.11 = (bf16[2,176,1536]{2,1,0:T(8,128)(2,1)S(1)}, bf16[2,176,1536]{2,1,0:T(8,128)(2,1)S(1)}, u32[]{:S(2)}, u32[]{:S(2)}) collective-permute-start(bf16[2,176,1536]{2,1,0:T(8,128)(2,1)S(1)} %fusion.8), channel_id=1, source_target_pairs={{0,1},{1,0},{2,3},{3,2},{4,5},{5,4},{6,7},{7,6},{8,9},{9,8},{10,11... | collective-permute-start | bytes 3244040 | tf_op jit(solution)/shard_map/ppermute | solution.py:521
  212.6 5.4 %collective-permute-start.22 = (bf16[64,640]{1,0:T(8,128)(2,1)S(1)}, bf16[64,640]{1,0:T(8,128)(2,1)S(1)}, u32[]{:S(2)}, u32[]{:S(2)}) collective-permute-start(bf16[64,640]{1,0:T(8,128)(2,1)S(1)} %fusion.21), channel_id=1, source_target_pairs={{0,16},{4,20},{8,24},{12,28},{16,0},{20,4},{24,8},{28,12},{1,17},{... | collective-permute-start | bytes 245768 | tf_op jit(solution)/shard_map/ppermute | solution.py:521
  217.4 35.0 %collective-permute-start.25 = (bf16[2,160,4096]{2,1,0:T(8,128)(2,1)S(1)}, bf16[2,160,4096]{2,1,0:T(8,128)(2,1)S(1)}, u32[]{:S(2)}, u32[]{:S(2)}) collective-permute-start(bf16[2,160,4096]{2,1,0:T(8,128)(2,1)S(1)} %dynamic-slice_bitcast_fusion), channel_id=1, source_target_pairs={{0,1},{1,0},{2,3},{3,2},{4,5},{5,4},{6,7},{7,6},{8,9},{9,8},{10,11... | collective-permute-start | bytes 7864328 | tf_op jit(solution)/shard_map/ppermute | solution.py:521
  218.0 4.6 %collective-permute-start.23 = (bf16[64,640]{1,0:T(8,128)(2,1)S(1)}, bf16[64,640]{1,0:T(8,128)(2,1)S(1)}, u32[]{:S(2)}, u32[]{:S(2)}) collective-permute-start(bf16[64,640]{1,0:T(8,128)(2,1)S(1)} %add_convert_fusion.3), channel_id=1, source_target_pairs={{0,8},{4,12},{8,0},{12,4},{16,24},{20,28},{24,16},{28,20},{1,9},{5... | collective-permute-start | bytes 245768 | tf_op jit(solution)/shard_map/ppermute | solution.py:521
  221.3 31.1 %slice-start = ((s8[5242880]{0:T(1024)(128)(4,1)}), s8[4194304]{0:T(1024)(128)(4,1)S(1)}, s32[]{:S(2)}) async-start(s8[5242880]{0:T(1024)(128)(4,1)} %bitcast.113), calls=%async_computation | async-start | bytes 8388608
  221.4 17.7 %collective-permute-start.33 = (bf16[512,640]{1,0:T(8,128)(2,1)S(1)}, bf16[512,640]{1,0:T(8,128)(2,1)S(1)}, u32[]{:S(2)}, u32[]{:S(2)}) collective-permute-start(bf16[512,640]{1,0:T(8,128)(2,1)S(1)} %dynamic-slice_bitcast_fusion.3), channel_id=1, source_target_pairs={{0,2},{1,3},{2,0},{3,1},{4,6},{5,7},{6,4},{7,5},{8,10},{9,11},{10,... | collective-permute-start | bytes 1966088 | tf_op jit(solution)/shard_map/ppermute | solution.py:521
  222.7 5.6 %collective-permute-start.24 = (bf16[128,640]{1,0:T(8,128)(2,1)S(1)}, bf16[128,640]{1,0:T(8,128)(2,1)S(1)}, u32[]{:S(2)}, u32[]{:S(2)}) collective-permute-start(bf16[128,640]{1,0:T(8,128)(2,1)S(1)} %pad_maximum_fusion.3), channel_id=1, source_target_pairs={{0,4},{4,0},{8,12},{12,8},{16,20},{20,16},{24,28},{28,24},{1,5},{5... | collective-permute-start | bytes 491528 | tf_op jit(solution)/shard_map/ppermute | solution.py:521
  224.9 27.6 %slice-start.1 = ((s8[5242880]{0:T(1024)(128)(4,1)}), s8[1048576]{0:T(1024)(128)(4,1)S(1)}, s32[]{:S(2)}) async-start(s8[5242880]{0:T(1024)(128)(4,1)} %bitcast.113), calls=%async_computation.1 | async-start | bytes 2097152
  224.9 24.6 %collective-permute-start.12 = (bf16[176,1536]{1,0:T(8,128)(2,1)S(1)}, bf16[176,1536]{1,0:T(8,128)(2,1)S(1)}, u32[]{:S(2)}, u32[]{:S(2)}) collective-permute-start(bf16[176,1536]{1,0:T(8,128)(2,1)S(1)} %dynamic-slice_bitcast_fusion.6), channel_id=1, source_target_pairs={{0,2},{1,3},{2,0},{3,1},{4,6},{5,7},{6,4},{7,5},{8,10},{9,11},{10,... | collective-permute-start | bytes 1622024 | tf_op jit(solution)/shard_map/ppermute | solution.py:521
  239.3 11.8 %collective-permute-start.34 = (bf16[256,640]{1,0:T(8,128)(2,1)S(1)}, bf16[256,640]{1,0:T(8,128)(2,1)S(1)}, u32[]{:S(2)}, u32[]{:S(2)}) collective-permute-start(bf16[256,640]{1,0:T(8,128)(2,1)S(1)} %dynamic-slice_bitcast_fusion.7), channel_id=1, source_target_pairs={{0,4},{4,0},{8,12},{12,8},{16,20},{20,16},{24,28},{28,24},{1,5},{5... | collective-permute-start | bytes 983048 | tf_op jit(solution)/shard_map/ppermute | solution.py:521
  249.6 7.3 %collective-permute-start.13 = (bf16[88,1536]{1,0:T(8,128)(2,1)S(1)}, bf16[88,1536]{1,0:T(8,128)(2,1)S(1)}, u32[]{:S(2)}, u32[]{:S(2)}) collective-permute-start(bf16[88,1536]{1,0:T(8,128)(2,1)S(1)} %dynamic-slice_bitcast_fusion.10), channel_id=1, source_target_pairs={{0,4},{4,0},{8,12},{12,8},{16,20},{20,16},{24,28},{28,24},{1,5},{5... | collective-permute-start | bytes 811016 | tf_op jit(solution)/shard_map/ppermute | solution.py:521
  252.0 5.8 %collective-permute-start.35 = (bf16[128,640]{1,0:T(8,128)(2,1)}, bf16[128,640]{1,0:T(8,128)(2,1)}, u32[]{:S(2)}, u32[]{:S(2)}) collective-permute-start(bf16[128,640]{1,0:T(8,128)(2,1)} %dynamic-slice_bitcast_fusion.11), channel_id=1, source_target_pairs={{0,8},{4,12},{8,0},{12,4},{16,24},{20,28},{24,16},{28,20},{1,9},{5... | collective-permute-start | bytes 491528 | tf_op jit(solution)/shard_map/ppermute | solution.py:521
  254.6 29.3 %collective-permute-start.26 = (bf16[160,4096]{1,0:T(8,128)(2,1)}, bf16[160,4096]{1,0:T(8,128)(2,1)}, u32[]{:S(2)}, u32[]{:S(2)}) collective-permute-start(bf16[160,4096]{1,0:T(8,128)(2,1)} %dynamic-slice_bitcast_fusion.2), channel_id=1, source_target_pairs={{0,2},{1,3},{2,0},{3,1},{4,6},{5,7},{6,4},{7,5},{8,10},{9,11},{10,... | collective-permute-start | bytes 3932168 | tf_op jit(solution)/shard_map/ppermute | solution.py:521
  257.1 5.9 %collective-permute-start.14 = (bf16[44,1536]{1,0:T(8,128)(2,1)S(1)}, bf16[44,1536]{1,0:T(8,128)(2,1)S(1)}, u32[]{:S(2)}, u32[]{:S(2)}) collective-permute-start(bf16[44,1536]{1,0:T(8,128)(2,1)S(1)} %dynamic-slice_bitcast_fusion.13), channel_id=1, source_target_pairs={{0,8},{4,12},{8,0},{12,4},{16,24},{20,28},{24,16},{28,20},{1,9},{5... | collective-permute-start | bytes 405512 | tf_op jit(solution)/shard_map/ppermute | solution.py:521
  258.7 13.0 %collective-permute-start.36 = (bf16[128,640]{1,0:T(8,128)(2,1)S(1)}, bf16[128,640]{1,0:T(8,128)(2,1)S(1)}, u32[]{:S(2)}, u32[]{:S(2)}) collective-permute-start(bf16[128,640]{1,0:T(8,128)(2,1)S(1)} %fusion.18), channel_id=1, source_target_pairs={{0,16},{4,20},{8,24},{12,28},{16,0},{20,4},{24,8},{28,12},{1,17},{... | collective-permute-start | bytes 491528 | tf_op jit(solution)/shard_map/ppermute | solution.py:521
  263.0 23.2 %collective-permute-start.15 = (bf16[44,1536]{1,0:T(8,128)(2,1)S(1)}, bf16[44,1536]{1,0:T(8,128)(2,1)S(1)}, u32[]{:S(2)}, u32[]{:S(2)}) collective-permute-start(bf16[44,1536]{1,0:T(8,128)(2,1)S(1)} %fusion.20), channel_id=1, source_target_pairs={{0,16},{4,20},{8,24},{12,28},{16,0},{20,4},{24,8},{28,12},{1,17},{... | collective-permute-start | bytes 405512 | tf_op jit(solution)/shard_map/ppermute | solution.py:521
  271.8 16.1 %collective-permute-start.37 = (bf16[128,640]{1,0:T(8,128)(2,1)S(1)}, bf16[128,640]{1,0:T(8,128)(2,1)S(1)}, u32[]{:S(2)}, u32[]{:S(2)}) collective-permute-start(bf16[128,640]{1,0:T(8,128)(2,1)S(1)} %add_convert_fusion.1), channel_id=1, source_target_pairs={{0,8},{4,12},{8,0},{12,4},{16,24},{20,28},{24,16},{28,20},{1,9},{5... | collective-permute-start | bytes 491528 | tf_op jit(solution)/shard_map/ppermute | solution.py:521
  285.6 17.7 %collective-permute-start.27 = (bf16[80,4096]{1,0:T(8,128)(2,1)S(1)}, bf16[80,4096]{1,0:T(8,128)(2,1)S(1)}, u32[]{:S(2)}, u32[]{:S(2)}) collective-permute-start(bf16[80,4096]{1,0:T(8,128)(2,1)S(1)} %dynamic-slice_bitcast_fusion.4), channel_id=1, source_target_pairs={{0,4},{4,0},{8,12},{12,8},{16,20},{20,16},{24,28},{28,24},{1,5},{5... | collective-permute-start | bytes 1966088 | tf_op jit(solution)/shard_map/ppermute | solution.py:521
  286.3 18.9 %collective-permute-start.16 = (bf16[44,1536]{1,0:T(8,128)(2,1)S(1)}, bf16[44,1536]{1,0:T(8,128)(2,1)S(1)}, u32[]{:S(2)}, u32[]{:S(2)}) collective-permute-start(bf16[44,1536]{1,0:T(8,128)(2,1)S(1)} %add_convert_fusion.2), channel_id=1, source_target_pairs={{0,8},{4,12},{8,0},{12,4},{16,24},{20,28},{24,16},{28,20},{1,9},{5... | collective-permute-start | bytes 405512 | tf_op jit(solution)/shard_map/ppermute | solution.py:521
  288.0 45.3 %collective-permute-start.38 = (bf16[256,640]{1,0:T(8,128)(2,1)S(1)}, bf16[256,640]{1,0:T(8,128)(2,1)S(1)}, u32[]{:S(2)}, u32[]{:S(2)}) collective-permute-start(bf16[256,640]{1,0:T(8,128)(2,1)S(1)} %pad_maximum_fusion.1), channel_id=1, source_target_pairs={{0,4},{4,0},{8,12},{12,8},{16,20},{20,16},{24,28},{28,24},{1,5},{5... | collective-permute-start | bytes 983048 | tf_op jit(solution)/shard_map/ppermute | solution.py:521
  303.5 7.9 %collective-permute-start.28 = (bf16[40,4096]{1,0:T(8,128)(2,1)S(1)}, bf16[40,4096]{1,0:T(8,128)(2,1)S(1)}, u32[]{:S(2)}, u32[]{:S(2)}) collective-permute-start(bf16[40,4096]{1,0:T(8,128)(2,1)S(1)} %dynamic-slice_bitcast_fusion.8), channel_id=1, source_target_pairs={{0,8},{4,12},{8,0},{12,4},{16,24},{20,28},{24,16},{28,20},{1,9},{5... | collective-permute-start | bytes 983048 | tf_op jit(solution)/shard_map/ppermute | solution.py:521
  305.3 7.2 %collective-permute-start.17 = (bf16[88,1536]{1,0:T(8,128)(2,1)S(1)}, bf16[88,1536]{1,0:T(8,128)(2,1)S(1)}, u32[]{:S(2)}, u32[]{:S(2)}) collective-permute-start(bf16[88,1536]{1,0:T(8,128)(2,1)S(1)} %pad_maximum_fusion.2), channel_id=1, source_target_pairs={{0,4},{4,0},{8,12},{12,8},{16,20},{20,16},{24,28},{28,24},{1,5},{5... | collective-permute-start | bytes 811016 | tf_op jit(solution)/shard_map/ppermute | solution.py:521
  311.5 11.6 %collective-permute-start.29 = (bf16[40,4096]{1,0:T(8,128)(2,1)S(1)}, bf16[40,4096]{1,0:T(8,128)(2,1)S(1)}, u32[]{:S(2)}, u32[]{:S(2)}) collective-permute-start(bf16[40,4096]{1,0:T(8,128)(2,1)S(1)} %fusion.14), channel_id=1, source_target_pairs={{0,16},{4,20},{8,24},{12,28},{16,0},{20,4},{24,8},{28,12},{1,17},{... | collective-permute-start | bytes 983048 | tf_op jit(solution)/shard_map/ppermute | solution.py:521
  323.1 7.1 %collective-permute-start.30 = (bf16[40,4096]{1,0:T(8,128)(2,1)S(1)}, bf16[40,4096]{1,0:T(8,128)(2,1)S(1)}, u32[]{:S(2)}, u32[]{:S(2)}) collective-permute-start(bf16[40,4096]{1,0:T(8,128)(2,1)S(1)} %add_convert_fusion), channel_id=1, source_target_pairs={{0,8},{4,12},{8,0},{12,4},{16,24},{20,28},{24,16},{28,20},{1,9},{5... | collective-permute-start | bytes 983048 | tf_op jit(solution)/shard_map/ppermute | solution.py:521
  330.4 10.7 %collective-permute-start.31 = (bf16[80,4096]{1,0:T(8,128)(2,1)S(1)}, bf16[80,4096]{1,0:T(8,128)(2,1)S(1)}, u32[]{:S(2)}, u32[]{:S(2)}) collective-permute-start(bf16[80,4096]{1,0:T(8,128)(2,1)S(1)} %pad_maximum_fusion), channel_id=1, source_target_pairs={{0,4},{4,0},{8,12},{12,8},{16,20},{20,16},{24,28},{28,24},{1,5},{5... | collective-permute-start | bytes 1966088 | tf_op jit(solution)/shard_map/ppermute | solution.py:521
  (16 other events, 75.2 us)

commit v2 on v1

v2 whole, which is shorter than its diff:
```python
import jax
import jax.numpy as jnp
from jax import lax
from jax.experimental import pallas as pl
from jax.experimental.pallas import tpu as pltpu
from jax.sharding import PartitionSpec as P

D = 640
HEADS = 4
HEAD_DIM = 256
FF = 2048
WINDOW = 512
SEQ_CAP = 8192
HALF = 512
QB = 256
ROWS = HEADS * QB
CHUNK = 512

EPS = 1e-06
ROPE_BASE = 10000.0
LOG2E = 1.4426950408889634
LN2 = 0.6931471805599453
SCALE = HEAD_DIM**-0.5

F32 = jnp.float32
BF16 = jnp.bfloat16
VM = pl.BlockSpec(memory_space=pltpu.VMEM)
SM = pl.BlockSpec(memory_space=pltpu.SMEM)
HB = pl.BlockSpec(memory_space=pl.ANY)
NN = (((1,), (0,)), ((), ()))
NT = (((1,), (1,)), ((), ()))
TN = (((0,), (0,)), ((), ()))


def dot(a, b, dims=NN):
    return lax.dot_general(a, b, dims, preferred_element_type=F32)


def params():
    return pltpu.CompilerParams(vmem_limit_bytes=16 * 2**20)


def sds(shape, dtype=BF16):
    return jax.ShapeDtypeStruct(shape, dtype)


def cost(flops, nbytes):
    return pl.CostEstimate(flops=int(flops), bytes_accessed=int(nbytes), transcendentals=0)


def rms_factor(v):
    return lax.rsqrt(jnp.mean(v * v, axis=-1, keepdims=True) + EPS)


def norm_back(v, factor, gain, incoming):
    united = v * factor
    scaled = incoming * gain
    back = factor * (scaled - united * jnp.mean(scaled * united, axis=-1, keepdims=True))
    return back, jnp.sum(incoming * united, axis=0, keepdims=True)


def offsets(me, rows):
    return (
        me * rows,
        (me + 1 - 2 * (me % 2)) * rows,
        ((me + 2) % 4) * rows,
        (3 - me) * rows,
    )


def hbm(shape, dtype=BF16):
    return pltpu.HBM(shape, dtype)


ME, XBIT, FLAG, EVEN, YBIT, SECOND, HERE = range(7)


def whole(piece):
    return piece


def place_copies(me_ref, pieces, src_of, buf, rows, sems, first):
    me, b = me_ref[ME], me_ref[XBIT]
    spots = [(p, o, rows) for p, o in zip(pieces, offsets(me, rows))]
    if len(pieces) == 6:
        part = rows // 2
        far, last = spots[2][1], spots[3][1]
        spots = spots[:2]
        for base, p in ((far, pieces[2:4]), (last, pieces[4:6])):
            spots.append((p[0], base + b * part, part))
            spots.append((p[1], base + (1 - b) * part, part))
    copies = []
    for k, (piece, off, n) in enumerate(spots):
        copies.append(
            pltpu.make_async_copy(
                src_of(piece), buf.at[pl.ds(pl.multiple_of(off, 16), n)], sems.at[first + k]
            )
        )
    return copies


def pack_kernel(info, k, v, g0, g1, g2, g3, g4, g5, out):
    rows = D // 4
    out[:rows, :HEAD_DIM] = k[...]
    out[:rows, HEAD_DIM:] = v[...]
    out[rows:, :] = jnp.zeros((16, 2 * HEAD_DIM), BF16)
    for i, g in enumerate((g0, g1, g2, g3, g4, g5)):
        out[rows + i : rows + i + 1, : g.shape[0]] = g[...].reshape(1, -1)


def pack(info, k, v, *gains):
    return pl.pallas_call(
        pack_kernel,
        out_shape=sds((D // 4 + 16, 2 * HEAD_DIM)),
        in_specs=[SM] + [VM] * 8,
        out_specs=VM,
        compiler_params=params(),
        cost_estimate=cost(1e6, 4e5),
        name="pack",
    )(info, k, v, *gains)


def gains_kernel(me_ref, g0, g1, g2, g3, out):
    gd = D // 4
    gh = HEAD_DIM // 4
    wide = jnp.zeros((16, D), F32)
    small = jnp.zeros((16, HEAD_DIM), F32)
    spots = offsets(me_ref[ME], 1)
    for spot, g in zip(spots, (g0, g1, g2, g3)):
        piece = g[...]
        row = lax.broadcasted_iota(jnp.int32, (HEAD_DIM, D), 0)
        col = lax.broadcasted_iota(jnp.int32, (HEAD_DIM, D), 1)
        place = ((col == row + spot * gd) & (row < gd)).astype(BF16)
        wide = wide + dot(piece, place)
        row = lax.broadcasted_iota(jnp.int32, (HEAD_DIM, HEAD_DIM), 0)
        col = lax.broadcasted_iota(jnp.int32, (HEAD_DIM, HEAD_DIM), 1)
        place = ((col == row + spot * gh) & (row < gh)).astype(BF16)
        small = small + dot(piece, place)
    out[0:4, :] = wide[0:4, :]
    out[4:8, :] = jnp.zeros((4, D), F32)
    out[4:8, :HEAD_DIM] = small[4:8, :]


def gains_of(me, pieces):
    part = pl.BlockSpec((16, HEAD_DIM), lambda i: (D // 4 // 16, 0))
    return pl.pallas_call(
        gains_kernel,
        grid=(1,),
        out_shape=sds((8, D), F32),
        in_specs=[SM] + [part] * 4,
        out_specs=VM,
        compiler_params=params(),
        cost_estimate=cost(1e8, 1e5),
        name="gains",
    )(me, *pieces)


def rotated(u, cos, sin):
    hd = HEAD_DIM // 2
    u1 = u[:, :hd]
    u2 = u[:, hd:]
    return (u1 * cos - u2 * sin).astype(BF16), (u2 * cos + u1 * sin).astype(BF16)


def pre_kv_kernel(me_ref, tok, gains, cos_ref, sin_ref, w0, w1, w2, w3, nin_o, kraw_o, lo_o, hi_o, wbuf, sems):
    rows = D // 4
    copies = place_copies(
        me_ref, (w0, w1, w2, w3), lambda w: w.at[pl.ds(0, rows)], wbuf, rows, sems, 0
    )
    for c in copies:
        c.start()
    hd = HEAD_DIM // 2
    x = tok[...].astype(F32)
    nin = (x * rms_factor(x) * gains[0:1, :]).astype(BF16)
    nin_o[...] = nin
    for c in copies:
        c.wait()
    k = dot(nin, wbuf[:, :HEAD_DIM])
    kraw_o[...] = k.astype(BF16)
    r1, r2 = rotated(k * rms_factor(k) * gains[5:6, :HEAD_DIM], cos_ref[...], sin_ref[...])
    v = dot(nin, wbuf[:, HEAD_DIM:]).astype(BF16)
    for half, o in enumerate((lo_o, hi_o)):
        sl = slice(HALF * half, HALF * (half + 1))
        o[:, :hd] = r1[sl]
        o[:, hd:HEAD_DIM] = r2[sl]
        o[:, HEAD_DIM:] = v[sl]


def pre_kv(me, tok, gains, cos, sin, pieces):
    t = tok.shape[0]
    return pl.pallas_call(
        pre_kv_kernel,
        out_shape=(
            sds((t, D)),
            sds((t, HEAD_DIM)),
            sds((HALF, 2 * HEAD_DIM)),
            sds((HALF, 2 * HEAD_DIM)),
        ),
        in_specs=[SM, VM, VM, VM, VM, HB, HB, HB, HB],
        out_specs=(VM,) * 4,
        scratch_shapes=[pltpu.VMEM((D, 2 * HEAD_DIM), BF16), pltpu.SemaphoreType.DMA((4,))],
        compiler_params=params(),
        cost_estimate=cost(2 * t * D * 512, 5e6),
        name="pre_kv",
    )(me, tok, gains, cos, sin, *pieces)


def pre_q_kernel(me_ref, nin_i, gains, cos_ref, sin_ref, w0, w1, w2, w3, qraw_o, qs_o, wbuf, sems):
    rows = D // 4
    hd = HEAD_DIM // 2

    @pl.when(pl.program_id(0) == 0)
    def _():
        copies = place_copies(
            me_ref, (w0, w1, w2, w3), lambda w: w.at[pl.ds(0, rows)], wbuf, rows, sems, 0
        )
        for c in copies:
            c.start()
        for c in copies:
            c.wait()

    q = dot(nin_i[...], wbuf[:, pl.ds(pl.multiple_of(pl.program_id(0) * HEAD_DIM, HEAD_DIM), HEAD_DIM)])
    qraw_o[0] = q.astype(BF16)
    u = q * (rms_factor(q) * (SCALE * LOG2E)) * gains[4:5, :HEAD_DIM]
    r1, r2 = rotated(u, cos_ref[...], sin_ref[...])
    qs_o[0, :, :hd] = r1
    qs_o[0, :, hd:] = r2


def pre_q(me, nin, gains, cos, sin, pieces):
    t = nin.shape[0]
    head = pl.BlockSpec((1, t, HEAD_DIM), lambda h: (h, 0, 0))
    return pl.pallas_call(
        pre_q_kernel,
        grid=(HEADS,),
        out_shape=(hbm((HEADS, t, HEAD_DIM)), sds((HEADS, t, HEAD_DIM))),
        in_specs=[SM, VM, VM, VM, VM, HB, HB, HB, HB],
        out_specs=(head, head),
        scratch_shapes=[pltpu.VMEM((D, HEADS * HEAD_DIM), BF16), pltpu.SemaphoreType.DMA((4,))],
        compiler_params=params(),
        cost_estimate=cost(2 * t * D * 1024, 5e6),
        name="pre_q",
    )(me, nin, gains, cos, sin, *pieces)


def key_blocks(j, kvp, kvs, lo, hi):
    blocks = (kvp[0:QB, lo:hi], kvp[QB : 2 * QB, lo:hi], kvs[0:QB, lo:hi], kvs[QB : 2 * QB, lo:hi])
    return blocks[j : j + 3]


def upper_mask():
    row = lax.broadcasted_iota(jnp.int32, (HEADS, QB, QB), 1).reshape(ROWS, QB)
    col = lax.broadcasted_iota(jnp.int32, (ROWS, QB), 1)
    return col > row


def att_kernel(masked, flag_ref, qs, kvp, kvs, o_o, pm_o, p1_o):
    upper = upper_mask()
    for j in range(2):
        sl = slice(QB * j, QB * (j + 1))
        q = qs[:, sl, :].reshape(ROWS, HEAD_DIM)
        k0, k1, k2 = key_blocks(j, kvp, kvs, 0, HEAD_DIM)
        v0, v1, v2 = key_blocks(j, kvp, kvs, HEAD_DIM, 2 * HEAD_DIM)
        em = jnp.exp2(jnp.where(upper, dot(q, k0, NT), dot(q, k2, NT)))
        e1 = jnp.exp2(dot(q, k1, NT))
        if masked:
            keep = flag_ref[FLAG].astype(F32)
            em = em * jnp.where(upper, keep, 1.0)
            if j == 0:
                e1 = e1 * keep
        inv = 1.0 / jnp.sum(em + e1, axis=-1, keepdims=True)
        pm = (em * inv).astype(BF16)
        p1 = (e1 * inv).astype(BF16)
        zero = jnp.zeros_like(pm)
        out = dot(p1, v1) + dot(jnp.where(upper, pm, zero), v0) + dot(jnp.where(upper, zero, pm), v2)
        pm_o[:, sl, :] = pm.reshape(HEADS, QB, QB)
        p1_o[:, sl, :] = p1.reshape(HEADS, QB, QB)
        o_o[:, sl, :] = out.astype(BF16).reshape(HEADS, QB, HEAD_DIM)


def half_spec(half):
    return pl.BlockSpec((HEADS, HALF, HEAD_DIM), lambda i: (0, half, 0))


def att(flag, qs, kvp, kvs, masked, half):
    shp = sds((HEADS, HALF, HEAD_DIM))

    def body(*refs):
        att_kernel(masked, *refs)

    return pl.pallas_call(
        body,
        grid=(1,),
        out_shape=(shp, shp, shp),
        in_specs=[SM, half_spec(half), VM, VM],
        out_specs=(VM,) * 3,
        compiler_params=params(),
        cost_estimate=cost(12e9 / 4, 5e6),
        name="att",
    )(flag, qs, kvp, kvs)


def att_back_kernel(qs, qraw, kvp, kvs, pm_i, p1_i, do_i, gains, cos_ref, sin_ref, dq_o, dkvp_o, dkvs_o, gain_o, acc):
    upper = upper_mask()
    hd = HEAD_DIM // 2
    acc[...] = jnp.zeros_like(acc)
    gsum = jnp.zeros((1, HEAD_DIM), F32)
    for j in range(2):
        sl = slice(QB * j, QB * (j + 1))
        q = qs[:, sl, :].reshape(ROWS, HEAD_DIM)
        do = do_i[:, sl, :].reshape(ROWS, HEAD_DIM)
        k0, k1, k2 = key_blocks(j, kvp, kvs, 0, HEAD_DIM)
        v0, v1, v2 = key_blocks(j, kvp, kvs, HEAD_DIM, 2 * HEAD_DIM)
        pmb = pm_i[:, sl, :].reshape(ROWS, QB)
        p1b = p1_i[:, sl, :].reshape(ROWS, QB)
        dpm = jnp.where(upper, dot(do, v0, NT), dot(do, v2, NT))
        dp1 = dot(do, v1, NT)
        pm = pmb.astype(F32)
        p1 = p1b.astype(F32)
        total = jnp.sum(pm * dpm + p1 * dp1, axis=-1, keepdims=True)
        dsm = (pm * (dpm - total)).astype(BF16)
        ds1 = (p1 * (dp1 - total)).astype(BF16)
        zero = jnp.zeros_like(dsm)
        ds0 = jnp.where(upper, dsm, zero)
        ds2 = jnp.where(upper, zero, dsm)
        p0 = jnp.where(upper, pmb, zero)
        p2 = jnp.where(upper, zero, pmb)
        for t, (ds, p) in enumerate(((ds0, p0), (ds1, p1b), (ds2, p2))):
            at = slice(QB * (j + t), QB * (j + t + 1))
            acc[at, :HEAD_DIM] += dot(ds, q, TN) * LN2
            acc[at, HEAD_DIM:] += dot(p, do, TN)
        dq = (dot(ds0, k0) + dot(ds1, k1) + dot(ds2, k2)) * SCALE
        cos = cos_ref[sl, :]
        sin = sin_ref[sl, :]
        gain = gains[4:5, :HEAD_DIM]
        for h in range(HEADS):
            d1 = dq[QB * h : QB * (h + 1), :hd]
            d2 = dq[QB * h : QB * (h + 1), hd:]
            inc = jnp.concatenate([d1 * cos + d2 * sin, d2 * cos - d1 * sin], axis=-1)
            raw = qraw[h, sl, :].astype(F32)
            back, terms = norm_back(raw, rms_factor(raw), gain, inc)
            gsum = gsum + terms
            dq_o[sl, HEAD_DIM * h : HEAD_DIM * (h + 1)] = back.astype(BF16)
    dkvp_o[...] = acc[:HALF, :].astype(BF16)
    dkvs_o[...] = acc[HALF:, :]
    gain_o[...] = jnp.broadcast_to(gsum, (8, HEAD_DIM))


def att_back(qs, qraw, kvp, kvs, pm, p1, do, gains, cos, sin, half):
    dospec = half_spec(half)
    tab = pl.BlockSpec((HALF, HEAD_DIM // 2), lambda i: (half, 0))
    return pl.pallas_call(
        att_back_kernel,
        grid=(1,),
        out_shape=(
            sds((HALF, HEADS * HEAD_DIM)),
            sds((HALF, 2 * HEAD_DIM)),
            sds((HALF, 2 * HEAD_DIM), F32),
            sds((8, HEAD_DIM), F32),
        ),
        in_specs=[dospec, dospec, VM, VM, VM, VM, dospec, VM, tab, tab],
        out_specs=(VM,) * 4,
        scratch_shapes=[pltpu.VMEM((2 * HALF, 2 * HEAD_DIM), F32)],
        compiler_params=params(),
        cost_estimate=cost(24e9 / 4, 9e6),
        name="att_back",
    )(qs, qraw, kvp, kvs, pm, p1, do, gains, cos, sin)


def mid_kernel(me_ref, o_lo, o_hi, tok, gains, w0, w1, w2, w3, ap_o, nm_o, wo, sems):
    ro = HEADS * HEAD_DIM // 4
    copies = place_copies(me_ref, (w0, w1, w2, w3), lambda w: w, wo, ro, sems, 0)
    for c in copies:
        c.start()
    for c in copies:
        c.wait()
    for half, o in enumerate((o_lo, o_hi)):
        sl = slice(HALF * half, HALF * (half + 1))
        proj = dot(o[0], wo[0:HEAD_DIM, :])
        for h in range(1, HEADS):
            proj = proj + dot(o[h], wo[HEAD_DIM * h : HEAD_DIM * (h + 1), :])
        ap_o[sl, :] = proj.astype(BF16)
        mid = tok[sl, :].astype(F32) + proj * rms_factor(proj) * gains[1:2, :]
        nm_o[sl, :] = (mid * rms_factor(mid) * gains[2:3, :]).astype(BF16)


def mid_part(me, o_lo, o_hi, tok, gains, outs):
    t = tok.shape[0]
    return pl.pallas_call(
        mid_kernel,
        out_shape=(sds((t, D)), sds((t, D))),
        in_specs=[SM] + [VM] * 4 + [HB] * 4,
        out_specs=(VM, VM),
        scratch_shapes=[
            pltpu.VMEM((HEADS * HEAD_DIM, D), BF16),
            pltpu.SemaphoreType.DMA((4,)),
        ],
        compiler_params=params(),
        cost_estimate=cost(2 * t * D * 1024, 8e6),
        name="mid",
    )(me, o_lo, o_hi, tok, gains, *outs)


FH = FF // 2
STEP = 256


def gate_kernel(me_ref, nm, *rest):
    pieces, (a_o, s_o, wg, sems) = rest[:6], rest[6:]

    @pl.when(pl.program_id(0) == 0)
    def _():
        copies = place_copies(me_ref, pieces, whole, wg, D // 4, sems, 0)
        for c in copies:
            c.start()
        for c in copies:
            c.wait()

    cs = pl.ds(pl.multiple_of(pl.program_id(0) * STEP, STEP), STEP)
    g = dot(nm[...], wg[:, cs])
    c0 = 0.7978845608028654
    c1 = 0.044715 * c0
    g2 = g * g
    t = jnp.tanh(g * (c0 + c1 * g2))
    h = 0.5 + 0.5 * t
    a = g * h
    slope = h + a * (1.0 - h) * (2.0 * c0 + (6.0 * c1) * g2)
    a_o[...] = a.astype(BF16)
    s_o[...] = slope.astype(BF16)


def up_kernel(me_ref, nm, a_i, s_i, *rest):
    pieces, (hid_o, b_o, wu, sems) = rest[:6], rest[6:]

    @pl.when(pl.program_id(0) == 0)
    def _():
        copies = place_copies(me_ref, pieces, whole, wu, D // 4, sems, 0)
        for c in copies:
            c.start()
        for c in copies:
            c.wait()

    cs = pl.ds(pl.multiple_of(pl.program_id(0) * STEP, STEP), STEP)
    u = dot(nm[...], wu[:, cs])
    hid_o[...] = (a_i[...].astype(F32) * u).astype(BF16)
    b_o[...] = (u * s_i[...].astype(F32)).astype(BF16)


def ff(me, nm, pieces, before=()):
    t = nm.shape[0]
    col = pl.BlockSpec((t, STEP), lambda i: (0, i))
    return pl.pallas_call(
        up_kernel if before else gate_kernel,
        grid=(FF // STEP,),
        out_shape=(sds((t, FF)),) * 2,
        in_specs=[SM, VM] + [col] * len(before) + [HB] * 6,
        out_specs=(col,) * 2,
        scratch_shapes=[pltpu.VMEM((D, FF), BF16), pltpu.SemaphoreType.DMA((6,))],
        compiler_params=params(),
        cost_estimate=cost(2 * t * D * FF, 12e6),
        name="up" if before else "gate",
    )(me, nm, *before, *pieces)


def down_kernel(me_ref, hid, tok, cot, ap, gains, *rest):
    pieces, (out_o, dd_o, wd_o, keep_o, send_o, gain_o, sems) = rest[:6], rest[6:]
    rf = FF // 4
    core = me_ref[ME] % 2
    copies = place_copies(me_ref, pieces, whole, wd_o, rf, sems, 0)
    for c in copies:
        c.start()
    for c in copies:
        c.wait()
    gsum = jnp.zeros((1, D), F32)
    for half in range(2):
        sl = slice(HALF * half, HALF * (half + 1))
        dn = dot(hid[sl, :], wd_o[...])
        proj = ap[sl, :].astype(F32)
        mid = tok[sl, :].astype(F32) + proj * rms_factor(proj) * gains[1:2, :]
        fac = rms_factor(dn)
        out_o[sl, :] = (mid + dn * fac * gains[3:4, :]).astype(BF16)
        back, terms = norm_back(dn, fac, gains[3:4, :], cot[sl, :].astype(F32))
        dd_o[sl, :] = back.astype(BF16)
        gsum = gsum + terms
    gain_o[...] = jnp.broadcast_to(gsum, (8, D))
    for y in range(2):
        for part, o in ((core, keep_o), (1 - core, send_o)):
            at = pl.ds(pl.multiple_of((2 * y + part) * rf, rf), rf)
            g = dot(hid[:, at], dd_o[...], TN).astype(BF16)
            for j in range(D // 128):
                o[y, j] = g[:, 128 * j : 128 * (j + 1)]


def down_part(me, hid, tok, cot, ap, gains, pieces):
    t = tok.shape[0]
    return pl.pallas_call(
        down_kernel,
        out_shape=(
            sds((t, D)),
            sds((t, D)),
            sds((FF, D)),
            sds((2, D // 128, FF // 4, 128)),
            sds((2, D // 128, FF // 4, 128)),
            sds((8, D), F32),
        ),
        in_specs=[SM] + [VM] * 5 + [HB] * 6,
        out_specs=(VM,) * 6,
        scratch_shapes=[pltpu.SemaphoreType.DMA((6,))],
        compiler_params=params(),
        cost_estimate=cost(4 * t * D * FF, 20e6),
        name="down",
    )(me, hid, tok, cot, ap, gains, *pieces)


def fb_kernel(half, me_ref, nm, dd, a_i, b_i, wd, *rest):
    gates, ups, rest = rest[:6], rest[6:12], rest[12:]
    first = half == 0
    if first:
        keep_o, send_o, dnm_o, wg, wu, gs, sems = rest
    else:
        dnm_i, keep_o, send_o, dnm_o, wg, wu, gs, sems = rest
    core = me_ref[ME] % 2

    @pl.when(pl.program_id(0) == 0)
    def _():
        copies = []
        for k, (pieces, buf) in enumerate(((gates, wg), (ups, wu))):
            copies += place_copies(
                me_ref, pieces, lambda w: w.at[:, pl.ds(FH * half, FH)], buf, D // 4, sems, 6 * k
            )
        for c in copies:
            c.start()
        for c in copies:
            c.wait()
        if first:
            dnm_o[...] = jnp.zeros_like(dnm_o)
        else:
            dnm_o[...] = dnm_i[...]

    cs = pl.ds(pl.multiple_of(pl.program_id(0) * STEP, STEP), STEP)
    dh = dot(dd[...], wd[...], NT)
    dg = (dh * b_i[...].astype(F32)).astype(BF16)
    du = (dh * a_i[...].astype(F32)).astype(BF16)
    dnm_o[...] += dot(dg, wg[:, cs], NT) + dot(du, wu[:, cs], NT)
    gr = D // 4
    for k, d in enumerate((dg, du)):
        gs[k] = dot(nm[...], d, TN).astype(BF16)
        for y in range(2):
            for part, o in ((core, keep_o), (1 - core, send_o)):
                at = pl.ds(pl.multiple_of((2 * y + part) * gr, gr), gr)
                for j in range(STEP // 128):
                    o[y, k, j] = gs[k, at, 128 * j : 128 * (j + 1)]


def fb(me, nm, dd, a, b, wd, gates, ups, part, dnm):
    t = nm.shape[0]
    steps = FH // STEP
    col = pl.BlockSpec((t, STEP), lambda i: (0, i + steps * part))
    extra = () if dnm is None else (dnm,)

    def body(*refs):
        fb_kernel(part, *refs)

    return pl.pallas_call(
        body,
        grid=(steps,),
        out_shape=(sds((2, 2, FH // 128, D // 4, 128)),) * 2 + (sds((t, D), F32),),
        in_specs=[SM, VM, VM, col, col, pl.BlockSpec((STEP, D), lambda i: (i + steps * part, 0))]
        + [HB] * 12
        + [VM] * len(extra),
        out_specs=(pl.BlockSpec((2, 2, STEP // 128, D // 4, 128), lambda i: (0, 0, i, 0, 0)),) * 2
        + (VM,),
        scratch_shapes=[
            pltpu.VMEM((D, FH), BF16),
            pltpu.VMEM((D, FH), BF16),
            pltpu.VMEM((2, D, STEP), BF16),
            pltpu.SemaphoreType.DMA((12,)),
        ],
        compiler_params=params(),
        cost_estimate=cost(10 * t * D * FH, 16e6),
        name="fb",
    )(me, nm, dd, a, b, wd, *gates, *ups, *extra)


def fe_kernel(me_ref, o_lo, o_hi, tok, cot, gains, ap, dnm, w0, w1, w2, w3, keep_o, send_o, do_o, dmid_o, gain_o, wo, datt, sems):
    ro = HEADS * HEAD_DIM // 4
    copies = place_copies(me_ref, (w0, w1, w2, w3), lambda w: w, wo, ro, sems, 0)
    for c in copies:
        c.start()
    gm = jnp.zeros((1, D), F32)
    ga = jnp.zeros((1, D), F32)
    for half in range(2):
        sl = slice(HALF * half, HALF * (half + 1))
        proj = ap[sl, :].astype(F32)
        pfac = rms_factor(proj)
        mid = tok[sl, :].astype(F32) + proj * pfac * gains[1:2, :]
        back, terms = norm_back(mid, rms_factor(mid), gains[2:3, :], dnm[sl, :])
        dmid = cot[sl, :].astype(F32) + back
        gm = gm + terms
        dmid_o[sl, :] = dmid.astype(BF16)
        back, terms = norm_back(proj, pfac, gains[1:2, :], dmid)
        ga = ga + terms
        datt[sl, :] = back.astype(BF16)
    gain_o[0:8, :] = jnp.broadcast_to(gm, (8, D))
    gain_o[8:16, :] = jnp.broadcast_to(ga, (8, D))
    for c in copies:
        c.wait()
    for h in range(HEADS):
        at = slice(HEAD_DIM * h, HEAD_DIM * (h + 1))
        do_o[h] = dot(datt[...], wo[at, :], NT).astype(BF16)
    core = me_ref[ME] % 2
    for y in range(2):
        for part, o in ((core, keep_o), (1 - core, send_o)):
            h = 2 * y + part
            g = (dot(o_lo[h], datt[:HALF, :], TN) + dot(o_hi[h], datt[HALF:, :], TN)).astype(BF16)
            for j in range(D // 128):
                o[y, j] = g[:, 128 * j : 128 * (j + 1)]


def fe(me, o_lo, o_hi, tok, cot, gains, ap, dnm, outs):
    t = tok.shape[0]
    return pl.pallas_call(
        fe_kernel,
        out_shape=(
            sds((2, D // 128, HEAD_DIM, 128)),
            sds((2, D // 128, HEAD_DIM, 128)),
            sds((HEADS, t, HEAD_DIM)),
            sds((t, D)),
            sds((16, D), F32),
        ),
        in_specs=[SM] + [VM] * 7 + [HB] * 4,
        out_specs=(VM,) * 5,
        scratch_shapes=[
            pltpu.VMEM((HEADS * HEAD_DIM, D), BF16),
            pltpu.VMEM((t, D), BF16),
            pltpu.SemaphoreType.DMA((4,)),
        ],
        compiler_params=params(),
        cost_estimate=cost(4 * t * D * 1024, 14e6),
        name="fe",
    )(me, o_lo, o_hi, tok, cot, gains, ap, dnm, *outs)


LAST = 2048


def post_kernel(
    me_ref, tok, dmid, nin, dq_lo, dq_hi, kv_a, kv_b, kv_c, kv_d, kraw,
    gains, cos_ref, sin_ref, gq_lo, gq_hi, gmid, gdown,
    q0, q1, q2, q3, k0, k1, k2, k3,
    gt_o, keep_o, send_o,
    wq, wkv, dkv, gs, sums, small, sems,
):
    rows = D // 4
    copies = place_copies(me_ref, (q0, q1, q2, q3), lambda w: w, wq, rows, sems, 0)
    copies += place_copies(
        me_ref, (k0, k1, k2, k3), lambda w: w.at[pl.ds(0, rows)], wkv, rows, sems, 4
    )
    for c in copies:
        c.start()
    hd = HEAD_DIM // 2
    gk = jnp.zeros((1, HEAD_DIM), F32)
    for half, (first, second) in enumerate(((kv_a, kv_b), (kv_c, kv_d))):
        sl = slice(HALF * half, HALF * (half + 1))
        both = first[...].astype(F32) + second[...].astype(F32)
        cos = cos_ref[sl, :]
        sin = sin_ref[sl, :]
        d1 = both[:, :hd]
        d2 = both[:, hd:HEAD_DIM]
        inc = jnp.concatenate([d1 * cos + d2 * sin, d2 * cos - d1 * sin], axis=-1)
        raw = kraw[sl, :].astype(F32)
        back, terms = norm_back(raw, rms_factor(raw), gains[5:6, :HEAD_DIM], inc)
        gk = gk + terms
        dkv[sl, :HEAD_DIM] = back.astype(BF16)
        dkv[sl, HEAD_DIM:] = both[:, HEAD_DIM:].astype(BF16)

    core = me_ref[ME] % 2

    def put(slot, g):
        gs[slot] = g.astype(BF16)
        for y in range(2):
            for part, o in ((core, keep_o), (1 - core, send_o)):
                at = pl.ds(pl.multiple_of((2 * y + part) * rows, rows), rows)
                for j in range(2):
                    to = (2 * slot + j) * rows
                    o[y, to : to + rows, :] = gs[slot, at, 128 * j : 128 * (j + 1)]

    for h in range(HEADS):
        cs = slice(HEAD_DIM * h, HEAD_DIM * (h + 1))
        put(h, dot(nin[:HALF, :], dq_lo[:, cs], TN) + dot(nin[HALF:, :], dq_hi[:, cs], TN))
    put(HEADS, dot(nin[...], dkv[:, :HEAD_DIM], TN))
    put(HEADS + 1, dot(nin[...], dkv[:, HEAD_DIM:], TN))
    for c in copies:
        c.wait()
    gi = jnp.zeros((1, D), F32)
    for half, dq in enumerate((dq_lo, dq_hi)):
        sl = slice(HALF * half, HALF * (half + 1))
        dnin = dot(dq[...], wq[...], NT) + dot(dkv[sl, :], wkv[...], NT)
        x = tok[sl, :].astype(F32)
        back, terms = norm_back(x, rms_factor(x), gains[0:1, :], dnin)
        gi = gi + terms
        gt_o[sl, :] = (dmid[sl, :].astype(F32) + back).astype(BF16)
    sums[...] = jnp.zeros_like(sums)
    small[...] = jnp.zeros_like(small)
    sums[0:1, :] = gi
    sums[1:2, :] = gmid[8:9, :]
    sums[2:3, :] = gmid[0:1, :]
    sums[3:4, :] = gdown[0:1, :]
    small[4:5, :] = gq_lo[0:1, :] + gq_hi[0:1, :]
    small[5:6, :] = gk
    gd = D // 4
    gh = HEAD_DIM // 4
    base = 12 * rows
    for y in range(2):
        for part, o in ((core, keep_o), (1 - core, send_o)):
            s = 2 * y + part
            row = lax.broadcasted_iota(jnp.int32, (D, HEAD_DIM), 0)
            col = lax.broadcasted_iota(jnp.int32, (D, HEAD_DIM), 1)
            place = ((row == col + s * gd) & (col < gd)).astype(BF16)
            g = dot(sums[...].astype(BF16), place)
            row = lax.broadcasted_iota(jnp.int32, (HEAD_DIM, HEAD_DIM), 0)
            col = lax.broadcasted_iota(jnp.int32, (HEAD_DIM, HEAD_DIM), 1)
            place = ((row == col + s * gh) & (col < gh)).astype(BF16)
            g = (g + dot(small[...].astype(BF16), place)).astype(BF16)
            o[y, base : base + 16, :] = g[:, :128]
            o[y, base + 16 : base + 32, :] = g[:, 128:]
            o[y, base + 32 :, :] = jnp.zeros((LAST - base - 32, 128), BF16)


def post(me, tok, dmid, nin, dqs, kvs, kraw, gains, cos, sin, sums, qs, kvgs):
    t = tok.shape[0]
    return pl.pallas_call(
        post_kernel,
        out_shape=(
            sds((t, D)),
            sds((2, LAST, 128)),
            sds((2, LAST, 128)),
        ),
        in_specs=[SM] + [VM] * 17 + [HB] * 8,
        out_specs=(VM,) * 3,
        scratch_shapes=[
            pltpu.VMEM((D, HEADS * HEAD_DIM), BF16),
            pltpu.VMEM((D, 2 * HEAD_DIM), BF16),
            pltpu.VMEM((t, 2 * HEAD_DIM), BF16),
            pltpu.VMEM((HEADS + 2, D, HEAD_DIM), BF16),
            pltpu.VMEM((16, D), F32),
            pltpu.VMEM((16, HEAD_DIM), F32),
            pltpu.SemaphoreType.DMA((8,)),
        ],
        compiler_params=params(),
        cost_estimate=cost(4e9, 15e6),
        name="post",
    )(me, tok, dmid, nin, *dqs, *kvs, kraw, gains, cos, sin, *sums, *qs, *kvgs)


def flip(x, axis, bit):
    n = lax.axis_size(axis)
    return lax.ppermute(x, axis, [(i, i ^ bit) for i in range(n)])


def pick(x, index, axis=0):
    return lax.dynamic_index_in_dim(x, index, axis, keepdims=False)


def after(x, *first):
    return lax.optimization_barrier((x,) + first)[0]


def joined(a, b):
    return (a.astype(F32) + b.astype(F32)).astype(BF16)


def small_call(body, name, out_rows, scalars, *arrays, scratch=()):
    size = sum(a.size for a in arrays)
    return pl.pallas_call(
        body,
        out_shape=tuple(sds(r + (128,)) for r in out_rows),
        in_specs=[SM] + [VM] * len(arrays),
        out_specs=(VM,) * len(out_rows),
        scratch_shapes=scratch,
        compiler_params=params(),
        cost_estimate=cost(size, 4 * size),
        name=name,
    )(scalars, *arrays)


def mix_first(scalars, keeps, gots):
    n = len(keeps)
    sizes = [k.shape[1] for k in keeps]
    rows = sum(sizes)

    def body(s, *refs):
        ks, gs = refs[:n], refs[n : 2 * n]
        send, keep, total = refs[2 * n :]
        at = 0
        for k, g, size in zip(ks, gs, sizes):
            for y in range(2):
                total[y, at : at + size, :] = joined(k[y], g[y])
            at += size
        even, y, x = s[EVEN], s[YBIT], s[XBIT]
        for t in range(2):
            for o, flip_it in ((send, 1), (keep, 0)):
                own_y = flip_it + y - 2 * flip_it * y
                own_x = flip_it + x - 2 * flip_it * x
                row = even * own_y + (1 - even) * t
                half = even * t + (1 - even) * own_x
                o[t] = total[row, pl.ds(pl.multiple_of(half * (rows // 2), 16), rows // 2), :]

    shape = (2, rows // 2)
    return small_call(
        body, "mix_first", (shape, shape), scalars, *keeps, *gots,
        scratch=[pltpu.VMEM((2, rows, 128), BF16)],
    )


def mix_half(info, index, keep, got):
    keep = keep.reshape(2, -1, 128)
    got = got.reshape(2, -1, 128)

    def body(i, k, g, send, kept):
        own = i[index]
        send[...] = joined(k[1 - own], g[1 - own])
        kept[...] = joined(k[own], g[own])

    shape = (keep.shape[1],)
    return small_call(body, "mix_half", (shape, shape), info, keep, got)


def mix_sum(info, keep, got):
    def body(i, k, g, o):
        o[...] = joined(k[...], g[...])

    return small_call(body, "mix_sum", (keep.shape[:1],), info, keep, got)[0]


def mix_both(info, index, own, other):
    rows = own.shape[0]

    def body(i, a, b, o):
        o[i[index]] = a[...]
        o[1 - i[index]] = b[...]

    return small_call(body, "mix_both", ((2, rows),), info, own, other)[0].reshape(2 * rows, 128)


class Place:
    def __init__(self, first_pos):
        shard = lax.axis_index("shard")
        seq = lax.axis_index("seq")
        self.n_shard = lax.axis_size("shard")
        self.n = lax.axis_size("seq") * self.n_shard
        core = shard & 1
        y = shard >> 1
        x = seq & 1
        bits = []
        bit = 1
        while bit < lax.axis_size("seq"):
            bits.append(bit)
            bit *= 2
        self.far = [self.n_shard * b for b in bits]
        here = [(seq >> i) & 1 for i in range(len(bits))]
        flag = (first_pos > 0).astype(jnp.int32)
        second = jnp.where(core == 0, x, y)
        self.token = None
        self.info = jnp.stack([shard, x, flag, 1 - core, y, second] + here).astype(jnp.int32)

    def send(self, x, even, odd):
        pairs = [(i, i ^ (even if i % 2 == 0 else odd)) for i in range(self.n)]
        return lax.ppermute(x, ("seq", "shard"), pairs)


ORDER = ("d", "da", "da", "dab", "da", "dabcabcbcbcbc")


class Chain:
    def __init__(self, place):
        self.place = place
        self.keeps = []
        self.gots = []
        self.keep = None
        n = len(place.far)
        self.steps = [self.start, self.second]
        self.steps += [lambda i=i: self.halve(i) for i in range(1, n - 1)]
        self.steps += [self.exchange]
        self.steps += [lambda i=i: self.double(i) for i in range(n - 2, -1, -1)]
        self.count = len(self.steps)

    def add(self, keep, send):
        self.keeps.append(keep.reshape(2, -1, 128))
        self.gots.append(self.place.send(send.reshape(2, -1, 128), 1, 1))

    def wait(self, *first):
        if not first:
            return
        if len(self.steps) == self.count:
            self.gots = [after(g, *first) for g in self.gots]
        else:
            self.got = after(self.got, *first)

    def step(self):
        if self.keep is None:
            self.keeps[0] = self.turn(self.keeps[0])
        else:
            self.keep = self.turn(self.keep)
        return self.steps.pop(0)()

    def go(self, out, even, odd):
        self.got = self.place.send(out, even, odd)
        self.place.token = out

    def turn(self, x):
        return x if self.place.token is None else after(x, self.place.token)

    def start(self):
        out, self.keep = mix_first(self.place.info, self.keeps, self.gots)
        self.go(out, 2, self.place.far[0])
        return out

    def second(self):
        out, self.keep = mix_half(self.place.info, SECOND, self.keep, self.got)
        self.go(out, self.place.far[0], 2)
        return out

    def halve(self, i):
        keep, got = self.keep, self.got
        out, self.keep = mix_half(self.place.info, HERE + i, keep, got)
        self.go(out, self.place.far[i], self.place.far[i])
        return out

    def exchange(self):
        self.keep = mix_sum(self.place.info, self.keep, self.got)
        self.go(self.keep, self.place.far[-1], self.place.far[-1])
        return self.keep

    def double(self, i):
        if i == len(self.place.far) - 2:
            self.keep = mix_sum(self.place.info, self.keep, self.got)
        else:
            self.keep = mix_both(self.place.info, HERE + i + 1, self.keep, self.got)
        self.go(self.keep, self.place.far[i], self.place.far[i])
        return self.keep


def gather_halves(info, own, other, total):
    total[info[HERE]] = own[...]
    total[1 - info[HERE]] = other[...]


def spread(o, total, at, rows, blocks):
    half = total.shape[1]
    for j in range(blocks):
        done = 0
        while done < rows:
            part, row = divmod(at + j * rows + done, half)
            n = min(rows - done, half - row)
            o[done : done + n, 128 * j : 128 * (j + 1)] = total[part, row : row + n, :].astype(o.dtype)
            done += n


def finish_one(info, own, other):
    def body(i, a, b, down, total):
        gather_halves(i, a, b, total)
        spread(down, total, 0, FF // 4, D // 128)

    return pl.pallas_call(
        body,
        out_shape=hbm((FF // 4, D), F32),
        in_specs=[SM, VM, VM],
        out_specs=VM,
        scratch_shapes=[pltpu.VMEM((2,) + own.shape, BF16)],
        compiler_params=params(),
        cost_estimate=cost(1e7, 1e7),
        name="finish_one",
    )(info, own, other)


def finish_two(info, own_a, other_a, own_b, other_b):
    gr = D // 4
    blocks = FH // 128

    def body(i, a, oa, b, ob, gate, up, out, total_a, total_b):
        gather_halves(i, a, oa, total_a)
        gather_halves(i, b, ob, total_b)
        for k, total in enumerate((total_a, total_b)):
            spread(gate.at[:, pl.ds(FH * k, FH)], total, 0, gr, blocks)
            spread(up.at[:, pl.ds(FH * k, FH)], total, gr * blocks, gr, blocks)
        spread(out, total_b, 2 * gr * blocks, HEAD_DIM, D // 128)

    return pl.pallas_call(
        body,
        out_shape=(hbm((gr, FF), F32), hbm((gr, FF), F32), hbm((HEAD_DIM, D), F32)),
        in_specs=[SM] + [VM] * 4,
        out_specs=(VM,) * 3,
        scratch_shapes=[
            pltpu.VMEM((2,) + own_a.shape, BF16),
            pltpu.VMEM((2,) + own_b.shape, BF16),
        ],
        compiler_params=params(),
        cost_estimate=cost(1e7, 1e7),
        name="finish_two",
    )(info, own_a, other_a, own_b, other_b)


def finish_three(info, own, other):
    gr = D // 4

    def body(i, a, b, query, key, value, gains, total):
        gather_halves(i, a, b, total)
        spread(query, total, 0, gr, 8)
        spread(key, total, 8 * gr, gr, 2)
        spread(value, total, 10 * gr, gr, 2)
        spread(gains, total, 12 * gr, 16, 2)

    return pl.pallas_call(
        body,
        out_shape=(
            hbm((gr, HEADS * HEAD_DIM), F32),
            hbm((gr, HEAD_DIM), F32),
            hbm((gr, HEAD_DIM), F32),
            sds((16, HEAD_DIM), F32),
        ),
        in_specs=[SM, VM, VM],
        out_specs=(VM,) * 4,
        scratch_shapes=[pltpu.VMEM((2,) + own.shape, BF16)],
        compiler_params=params(),
        cost_estimate=cost(1e7, 1e7),
        name="finish_three",
    )(info, own, other)


def shards(
    tokens,
    query_weight,
    key_weight,
    value_weight,
    out_weight,
    gate_weight,
    up_weight,
    down_weight,
    input_gain,
    query_gain,
    key_gain,
    attended_gain,
    middle_gain,
    output_gain,
    cotangent,
):
    n_seq = lax.axis_size("seq")
    n_shard = lax.axis_size("shard")
    shard = lax.axis_index("shard")
    x_bit = lax.axis_index("seq") & 1
    count = tokens.shape[0]
    total = count * n_seq * n_shard
    length = min(SEQ_CAP, total)
    rank = lax.axis_index("seq") * n_shard + shard
    first_pos = rank * count % length
    place = Place(first_pos)
    me = flag = place.info
    gd = D // 4
    gh = HEAD_DIM // 4

    kvg = pack(
        me,
        key_weight,
        value_weight,
        input_gain,
        attended_gain,
        middle_gain,
        output_gain,
        query_gain,
        key_gain,
    )
    def near(x):
        return flip(x, "shard", 1)

    def far(x):
        return flip(x, "shard", 2)

    q_far = far(query_weight)
    kvg_far = far(kvg)
    kvgs = (kvg, near(kvg), kvg_far, near(kvg_far))
    q_near = near(query_weight)
    out_near, gate_near, up_near, down_near = (
        near(out_weight), near(gate_weight), near(up_weight), near(down_weight)
    )

    def half(w):
        return pick(w.reshape(2, w.shape[0] // 2, w.shape[1]), x_bit)

    def relay(x):
        return flip(x, "seq", 1)

    gate_half, up_half, down_half = half(gate_weight), half(up_weight), half(down_weight)

    positions = first_pos + jnp.arange(count, dtype=jnp.int32)
    hd = HEAD_DIM // 2
    freq = ROPE_BASE ** (-(jnp.arange(hd, dtype=F32) * 2.0 / HEAD_DIM))
    angles = positions.astype(F32)[:, None] * freq[None, :]
    cos = jnp.cos(angles)
    sin = jnp.sin(angles)

    gains = gains_of(me, kvgs)
    nin, kraw, kv_lo, kv_hi = pre_kv(me, tokens, gains, cos, sin, kvgs)
    ranks = n_seq * n_shard
    per_seq = length // count
    pairs = [(i, i + 1) for i in range(ranks - 1) if (i + 1) % per_seq]
    halo = lax.ppermute(kv_hi, ("seq", "shard"), pairs)
    out_far = far(out_weight)
    q_far = after(q_far, nin)
    qs_w = (query_weight, q_near, q_far, near(q_far))
    gate_a = far(gate_half)
    qraw, qs = pre_q(me, nin, gains, cos, sin, qs_w)
    o_hi, pm_hi, p1_hi = att(flag, qs, kv_lo, kv_hi, False, 1)
    o_lo, pm_lo, p1_lo = att(flag, after(qs, o_hi), halo, kv_lo, True, 0)
    out_far = after(out_far, o_lo)
    gate_a = after(gate_a, o_lo)
    up_a = far(after(up_half, gate_a))
    gate_b = relay(gate_a)
    outs = (out_weight, out_near, out_far, near(out_far))
    ap, nm = mid_part(me, o_lo, o_hi, tokens, gains, outs)
    gate_b = after(gate_b, nm)
    up_a = after(up_a, nm)
    down_a = far(after(down_half, up_a))
    up_b = relay(up_a)
    gates = (gate_weight, gate_near, gate_a, gate_b, near(gate_a), near(gate_b))
    act, slope = ff(me, nm, gates)
    up_b = after(up_b, act)
    down_a = after(down_a, act)
    down_b = relay(down_a)
    ups = (up_weight, up_near, up_a, up_b, near(up_a), near(up_b))
    hid, bact = ff(me, nm, ups, (act, slope))
    down_b = after(down_b, hid)
    downs = (down_weight, down_near, down_a, down_b, near(down_a), near(down_b))
    block_out, dd, wd, keep, send, gain_down = down_part(
        me, hid, tokens, cotangent, ap, gains, downs
    )
    chains = {name: Chain(place) for name in "abcd"}

    def advance(order, *first):
        for name in order:
            chain = chains[name]
            if chain.steps:
                chain.wait(*first)
                chain.step()

    chains["d"].add(keep, send)
    keep, send, dnm = fb(me, nm, dd, act, bact, wd, gates, ups, 0, None)
    chains["a"].add(keep, send)
    advance(ORDER[0], dnm)
    dnm = after(dnm, place.token)
    keep, send, dnm = fb(me, nm, dd, act, bact, wd, gates, ups, 1, dnm)
    chains["b"].add(keep, send)
    advance(ORDER[1], dnm)
    keep, send, d_o, d_mid, gain_mid = fe(
        me, o_lo, o_hi, tokens, cotangent, gains, ap, after(dnm, place.token), outs
    )
    chains["b"].add(keep, send)
    advance(ORDER[2], d_o)
    dq_lo, kv_back, kv_a, gq_lo = att_back(
        qs, qraw, halo, kv_lo, pm_lo, p1_lo, after(d_o, place.token), gains, cos, sin, 0
    )
    returned = lax.ppermute(kv_back, ("seq", "shard"), [(j, i) for i, j in pairs])
    advance(ORDER[3], dq_lo)
    dq_hi, kv_b, kv_c, gq_hi = att_back(
        qs, qraw, kv_lo, kv_hi, pm_hi, p1_hi, after(d_o, dq_lo, place.token), gains, cos, sin, 1
    )
    advance(ORDER[4], dq_hi)
    grad_tokens, keep, send = post(
        me,
        tokens,
        d_mid,
        nin,
        (dq_lo, after(dq_hi, place.token)),
        (kv_a, kv_b, kv_c, returned),
        kraw,
        gains,
        cos,
        sin,
        (gq_lo, gq_hi, gain_mid, gain_down),
        qs_w,
        kvgs,
    )
    chains["c"].add(keep, send)
    advance(ORDER[5], keep)
    for name in "dacb":
        advance(name * len(chains[name].steps))
    r_down = finish_one(me, chains["d"].keep, chains["d"].got)
    r_query, r_key, r_value, tail = finish_three(me, chains["c"].keep, chains["c"].got)
    r_gate, r_up, r_out = finish_two(
        me, chains["a"].keep, chains["a"].got, chains["b"].keep, chains["b"].got
    )
    return (
        block_out,
        grad_tokens,
        r_query,
        r_key,
        r_value,
        r_out,
        r_gate,
        r_up,
        r_down,
        tail[0, :gd],
        tail[4, :gh],
        tail[5, :gh],
        tail[1, :gd],
        tail[2, :gd],
        tail[3, :gd],
    )


def solution(mesh):
    token = P(("seq", "shard"), None)
    matrix = P("shard", None)
    vector = P("shard")
    in_specs = (token,) + (matrix,) * 7 + (vector,) * 6 + (token,)
    out_specs = (token, token) + (matrix,) * 7 + (vector,) * 6
    return jax.shard_map(shards, mesh=mesh, in_specs=in_specs, out_specs=out_specs, check_vma=False)
```

time: 348 us -> 269 us (0.77)
  waiting for transfers between devices: 149 us -> 67.3 us
  other arithmetic: 15.9 us -> 1.89 us
  Pallas kernels: 117 us -> 130 us
  starting transfers between devices: 40.4 us -> 49.2 us
  local copies, waits for them, and re-layouts: 20.3 us -> 14.4 us
    ppermute x37 -> x24, waiting for transfers between devices: 149 us -> 9.75 us  [flip(): return lax.ppermute(x, axis, [(i, i ^ bit) for i in range(n)])]
    ppermute x0 -> x29, waiting for transfers between devices: none -> 57.5 us  [send(): return lax.ppermute(x, ('seq', 'shard'), pairs)]
    ppermute x0 -> x29, starting transfers between devices: none -> 27.3 us  [send(): return lax.ppermute(x, ('seq', 'shard'), pairs)]
    pallas_call x7 -> x41, Pallas kernels: 97.8 us -> 119 us  [the longest x2 28.6 us: fb(): pl.pallas_call(body, grid=(steps,), out_shape=(sds((2, 2, FH // 128, D //...]
    ppermute x37 -> x24, starting transfers between devices: 36.6 us -> 17.9 us  [flip(): return lax.ppermute(x, axis, [(i, i ^ bit) for i in range(n)])]
    convert_element_type x24 -> x0, other arithmetic: 9.21 us -> none  [the longest x20 6.81 us: joined(): return (a.astype(F32) + b.astype(F32)).astype(BF16)]
    unnamed x53 -> x86, local copies, waits for them, and re-layouts: 4.37 us -> 12.1 us
    pallas_call x2, Pallas kernels: 18.7 us -> 11.3 us  [att_back(): pl.pallas_call(att_back_kernel, grid=(1,), out_shape=(sds((HALF, HEADS *...]
  transfers between devices with their start and end apart: 39 -> 55, of which waited for: 18 -> 16; matrix products, arithmetic and copies ran while one was open for 9% -> 2% of each run, Pallas kernels for 13% -> 44%
where the time goes in v2:
time: 269 us; the launch traced here: 265 us
  Pallas kernels  130 us (48%)
  waiting for transfers between devices  67.3 us (25%)
  starting transfers between devices  49.2 us (18%)
  local copies, waits for them, and re-layouts  14.4 us (5%)
    ppermute x29, waiting for transfers between devices, send(): return lax.ppermute(x, ('seq', 'shard'), pairs)  57.5 us
    pallas_call x2, Pallas kernels, fb(): pl.pallas_call(body, grid=(steps,), out_shape=(sds((2, 2, FH // 128, D //...  28.6 us
    ppermute x29, starting transfers between devices, send(): return lax.ppermute(x, ('seq', 'shard'), pairs)  27.3 us
    pallas_call x2, Pallas kernels, ff(): pl.pallas_call(up_kernel if before else gate_kernel, grid=(FF // STEP,),...  18.2 us
    ppermute x24, starting transfers between devices, flip(): return lax.ppermute(x, axis, [(i, i ^ bit) for i in range(n)])  17.9 us
    pallas_call x24, Pallas kernels, small_call(): pl.pallas_call(body, out_shape=tuple((sds(r + (128,)) for r in out_rows))...  17.6 us
    unnamed x86, local copies, waits for them, and re-layouts  12.1 us
    pallas_call x2, Pallas kernels, att_back(): pl.pallas_call(att_back_kernel, grid=(1,), out_shape=(sds((HALF, HEADS *...  11.3 us
  transfers between devices with their start and end apart: 55, of which 16 were waited for; matrix products, arithmetic and copies ran while one was open for 2% of the time, Pallas kernels for 44%

profile of v2, /device:TPU:0, one launch (start us, length us, event | category | flops | bytes accessed | tf_op | source)
XLA Modules:
  0.0 264.7 jit_solution(902988974938193489)
XLA Ops:
  7.1 3.0 %collective-permute-start.1 = (bf16[176,512]{1,0:T(8,128)(2,1)S(1)}, bf16[176,512]{1,0:T(8,128)(2,1)S(1)}, u32[]{:S(2)}, u32[]{:S(2)}) collective-permute-start(bf16[176,512]{1,0:T(8,128)(2,1)S(1)} %pack.1.g0.w0.k0), channel_id=1, source_target_pairs={{0,2},{1,3},{2,0},{3,1},{4,6},{5,7},{6,4},{7,5},{8,10},{9,11},{10,... | collective-permute-start | bytes 540680 | tf_op jit(solution)/shard_map/ppermute | solution.py:758
  10.7 4.8 %collective-permute-done.1.g2.w2.k2 = bf16[176,512]{1,0:T(8,128)(2,1)S(1)} collective-permute-done((bf16[176,512]{1,0:T(8,128)(2,1)S(1)}, bf16[176,512]{1,0:T(8,128)(2,1)S(1)}, u32[]{:S(2)}, u32[]{:S(2)}) %collective-permute-start.1) | collective-permute-done | bytes 180256 | tf_op jit(solution)/shard_map/ppermute | solution.py:758
  15.5 1.9 multiply_sine_fusion
  18.3 3.2 %pre_kv.1 = (bf16[1024,640]{1,0:T(8,128)(2,1)S(1)}, bf16[1024,256]{1,0:T(8,128)(2,1)S(1)}, bf16[512,512]{1,0:T(8,128)(2,1)S(1)}, bf16[512,512]{1,0:T(8,128)(2,1)S(1)}) custom-call(s32[9]{0:T(128)S(1)} %stack.43.info.me_ref.refs_0_.s.i, bf16[1024,640]{1,0:T(8,128)(2,1)S(1)} %copy-done, f32[8,640]{1,0:T(8,128)S(1)} %gains.1, ...), custom_call_target="tpu_custom_call" | custom-call | flops 671088640 | bytes 5000000 | tf_op jit(solution)/shard_map/pre_kv/pallas_call | solution.py:191
  24.9 2.1 collective-permute-start.8
  27.2 2.4 collective-permute-start.6
  33.0 5.7 %pre_q.1 = (bf16[4,1024,256]{2,1,0:T(8,128)(2,1)}, bf16[4,1024,256]{2,1,0:T(8,128)(2,1)S(1)}) custom-call(s32[9]{0:T(128)S(1)} %stack.43.info.me_ref.refs_0_.s.i, bf16[1024,640]{1,0:T(8,128)(2,1)S(1)} %copy-done.15, f32[8,640]{1,0:T(8,128)S(1)} %gains.1, f32[1024,128]{1,0:T(8,128)S(1)} %get-tuple-element.302.cos_ref, ...), custom_call_target="tpu_custom_call" | custom-call | flops 1342177280 | bytes 5000000 | tf_op jit(solution)/shard_map/pre_q/pallas_call | solution.py:233
  38.8 3.2 %att.2 = (bf16[4,512,256]{2,1,0:T(8,128)(2,1)S(1)}, bf16[4,512,256]{2,1,0:T(8,128)(2,1)S(1)}, bf16[4,512,256]{2,1,0:T(8,128)(2,1)S(1)}) custom-call(s32[9]{0:T(128)S(1)} %stack.43.info.me_ref.refs_0_.s.i, bf16[4,1024,256]{2,1,0:T(8,128)(2,1)S(1)} %get-tuple-element.161.refs_1_.qs, bf16[512,512]{1,0:T(8,128)(2,1)S(1)} %copy-done.20, ...), custom_call_target="tpu_custom_call" | custom-call | flops 3000000000 | bytes 5000000 | tf_op jit(solution)/shard_map/att/pallas_call | solution.py:291
  42.1 3.3 %att.3 = (bf16[4,512,256]{2,1,0:T(8,128)(2,1)S(1)}, bf16[4,512,256]{2,1,0:T(8,128)(2,1)S(1)}, bf16[4,512,256]{2,1,0:T(8,128)(2,1)S(1)}) custom-call(s32[9]{0:T(128)S(1)} %stack.43.info.me_ref.refs_0_.s.i, bf16[4,1024,256]{2,1,0:T(8,128)(2,1)S(1)} %get-tuple-element.161.refs_1_.qs, bf16[512,512]{1,0:T(8,128)(2,1)S(1)} %collective-permute-done.6.refs_2_.kvp, ...), custom_call_target="tpu_custom_call" | custom-call | flops 3000000000 | bytes 5000000 | tf_op jit(solution)/shard_map/att/pallas_call | solution.py:291
  46.4 2.5 collective-permute-start.9
  50.1 2.6 collective-permute-start.16
  52.7 4.5 %mid.1 = (bf16[1024,640]{1,0:T(8,128)(2,1)S(1)}, bf16[1024,640]{1,0:T(8,128)(2,1)S(1)}) custom-call(s32[9]{0:T(128)S(1)} %stack.43.info.me_ref.refs_0_.s.i, bf16[4,512,256]{2,1,0:T(8,128)(2,1)S(1)} %get-tuple-element.162.o_lo, bf16[4,512,256]{2,1,0:T(8,128)(2,1)S(1)} %get-tuple-element.160.o_hi, bf16[1024,640]{1,0:T(8,128)(2,1)S(1)} %copy-done, ...), custom_call_target="tpu_custom_call" | custom-call | flops 1342177280 | bytes 8000000 | tf_op jit(solution)/shard_map/mid/pallas_call | solution.py:389
  57.2 1.8 collective-permute-done.12.rest_3_.refs_9_
  59.5 1.5 collective-permute-done.16.rest_2_.refs_14_
  61.7 1.8 collective-permute-start.21
  63.5 9.6 %gate.1 = (bf16[1024,2048]{1,0:T(8,128)(2,1)S(1)}, bf16[1024,2048]{1,0:T(8,128)(2,1)S(1)}) custom-call(s32[9]{0:T(128)S(1)} %stack.43.info.me_ref.refs_0_.s.i, bf16[1024,640]{1,0:T(8,128)(2,1)S(1)} %get-tuple-element.164.nm.refs_1_, bf16[160,2048]{1,0:T(8,128)(2,1)S(1)} %copy-done.5, bf16[160,2048]{1,0:T(8,128)(2,1)S(1)} %collective-permute-done.10.rest_1_.refs_7_, ...), custom_call_target="tpu_custom_call" | custom-call | flops 2684354560 | bytes 12000000 | tf_op jit(solution)/shard_map/gate/pallas_call | solution.py:452
  73.4 1.5 collective-permute-start.22
  75.4 8.6 %up.1 = (bf16[1024,2048]{1,0:T(8,128)(2,1)S(1)}, bf16[1024,2048]{1,0:T(8,128)(2,1)S(1)}) custom-call(s32[9]{0:T(128)S(1)} %stack.43.info.me_ref.refs_0_.s.i, bf16[1024,640]{1,0:T(8,128)(2,1)S(1)} %get-tuple-element.164.nm.refs_1_, bf16[1024,2048]{1,0:T(8,128)(2,1)S(1)} %get-tuple-element.167.a_i.refs_3_, bf16[1024,2048]{1,0:T(8,128)(2,1)S(1)} %get-tuple-element.168.s_i, ...), custom_call_target="tpu_custom_call" | custom-call | flops 2684354560 | bytes 12000000 | tf_op jit(solution)/shard_map/up/pallas_call | solution.py:452
  84.2 1.6 collective-permute-done.24.rest_5_
  85.7 9.8 %down.1 = (bf16[1024,640]{1,0:T(8,128)(2,1)}, bf16[1024,640]{1,0:T(8,128)(2,1)S(1)}, bf16[2048,640]{1,0:T(8,128)(2,1)S(1)}, bf16[2,5,512,128]{3,2,1,0:T(8,128)(2...) custom-call(s32[9]{0:T(128)S(1)} %stack.43.info.me_ref.refs_0_.s.i, ...), custom_call_target="tpu_custom_call" | custom-call | flops 5368709120 | bytes 20000000 | tf_op jit(solution)/shard_map/down/pallas_call | solution.py:496
  95.8 14.3 %fb.2 = (bf16[2,2,8,160,128]{4,3,2,1,0:T(8,128)(2,1)S(1)}, bf16[2,2,8,160,128]{4,3,2,1,0:T(8,128)(2,1)S(1)}, f32[1024,640]{1,0:T(8,128)S(1)}) custom-call(s32[9]{0:T(128)S(1)} %stack.43.info.me_ref.refs_0_.s.i, bf16[1024,640]{1,0:T(8,128)(2,1)S(1)} %get-tuple-element.164.nm.refs_1_, bf16[1024,640]{1,0:T(8,128)(2,1)S(1)} %get-tuple-element.178.refs_2_, ...), custom_call_target="tpu_custom_call" | custom-call | flops 6710886400 | bytes 16000000 | tf_op jit(solution)/shard_map/fb/pallas_call | solution.py:564
  112.2 14.3 %fb.3 = (bf16[2,2,8,160,128]{4,3,2,1,0:T(8,128)(2,1)S(1)}, bf16[2,2,8,160,128]{4,3,2,1,0:T(8,128)(2,1)S(1)}, f32[1024,640]{1,0:T(8,128)S(1)}) custom-call(s32[9]{0:T(128)S(1)} %stack.43.info.me_ref.refs_0_.s.i, bf16[1024,640]{1,0:T(8,128)(2,1)S(1)} %get-tuple-element.164.nm.refs_1_, bf16[1024,640]{1,0:T(8,128)(2,1)S(1)} %get-tuple-element.178.refs_2_, ...), custom_call_target="tpu_custom_call" | custom-call | flops 6710886400 | bytes 16000000 | tf_op jit(solution)/shard_map/fb/pallas_call | solution.py:564
  131.3 7.3 %fe.1 = (bf16[2,5,256,128]{3,2,1,0:T(8,128)(2,1)S(1)}, bf16[2,5,256,128]{3,2,1,0:T(8,128)(2,1)S(1)}, bf16[4,1024,256]{2,1,0:T(8,128)(2,1)S(1)}, bf16[1024,640]{1,0:T(8,128)(2,1)S(1)}, f32[16,640]{1,0:T(8,128)S(1)}) custom-call(s32[9]{0:T(128)S(1)} %stack.43.info.me_ref.refs_0_.s.i, bf16[4,512,256]{2,1,0:T(8,128)(2,1)S(1)} %get-tuple-element.162.o_lo, ...), custom_call_target="tpu_custom_call" | custom-call | flops 2684354560 | bytes 14000000 | tf_op jit(solution)/shard_map/fe/pallas_call | solution.py:622
  138.7 2.3 collective-permute-done.28
  141.7 1.6 collective-permute-start.30
  145.0 5.6 %att_back.2 = (bf16[512,1024]{1,0:T(8,128)(2,1)S(1)}, bf16[512,512]{1,0:T(8,128)(2,1)S(1)}, f32[512,512]{1,0:T(8,128)S(1)}, f32[8,256]{1,0:T(8,128)S(1)}) custom-call(bf16[4,1024,256]{2,1,0:T(8,128)(2,1)S(1)} %copy-done.38, bf16[4,1024,256]{2,1,0:T(8,128)(2,1)S(1)} %copy-done.36, bf16[512,512]{1,0:T(8,128)(2,1)S(1)} %copy-done.25, ...), custom_call_target="tpu_custom_call" | custom-call | flops 6000000000 | bytes 9000000 | tf_op jit(solution)/shard_map/att_back/pallas_call | solution.py:352
  151.3 2.7 %collective-permute-start.34 = (bf16[640,128]{1,0:T(8,128)(2,1)S(1)}, bf16[640,128]{1,0:T(8,128)(2,1)S(1)}, u32[]{:S(2)}, u32[]{:S(2)}) collective-permute-start(bf16[640,128]{1,0:T(8,128)(2,1)S(1)} %mix_sum.8.k), channel_id=1, source_target_pairs={{0,16},{1,17},{2,18},{3,19},{4,20},{5,21},{6,22},{7,23},{8,24},{9,... | collective-permute-start | bytes 491528 | tf_op jit(solution)/shard_map/ppermute | solution.py:869
  153.9 1.5 collective-permute-start.36
  157.5 1.6 mix_first.6
  159.1 2.1 collective-permute-start.39
  161.2 5.7 %att_back.3 = (bf16[512,1024]{1,0:T(8,128)(2,1)S(1)}, bf16[512,512]{1,0:T(8,128)(2,1)S(1)}, f32[512,512]{1,0:T(8,128)S(1)}, f32[8,256]{1,0:T(8,128)S(1)}) custom-call(bf16[4,1024,256]{2,1,0:T(8,128)(2,1)S(1)} %copy-done.38, bf16[4,1024,256]{2,1,0:T(8,128)(2,1)S(1)} %copy-done.36, bf16[512,512]{1,0:T(8,128)(2,1)S(1)} %copy-done.20, ...), custom_call_target="tpu_custom_call" | custom-call | flops 6000000000 | bytes 9000000 | tf_op jit(solution)/shard_map/att_back/pallas_call | solution.py:352
  168.1 10.4 %post.1 = (bf16[1024,640]{1,0:T(8,128)(2,1)}, bf16[2,2048,128]{2,1,0:T(8,128)(2,1)S(1)}, bf16[2,2048,128]{2,1,0:T(8,128)(2,1)S(1)}) custom-call(s32[9]{0:T(128)S(1)} %stack.43.info.me_ref.refs_0_.s.i, bf16[1024,640]{1,0:T(8,128)(2,1)S(1)} %copy-done, bf16[1024,640]{1,0:T(8,128)(2,1)S(1)} %get-tuple-element.198.dmid, bf16[1024,640]{1,0:T(8,128)(2,1)S(1)} %copy-done.16, ...), custom_call_target="tpu_custom_call" | custom-call | flops 4000000000 | bytes 15000000 | tf_op jit(solution)/shard_map/post/pallas_call | solution.py:732
  179.6 7.9 %collective-permute-done.37.b = bf16[640,128]{1,0:T(8,128)(2,1)S(1)} collective-permute-done((bf16[640,128]{1,0:T(8,128)(2,1)S(1)}, bf16[640,128]{1,0:T(8,128)(2,1)S(1)}, u32[]{:S(2)}, u32[]{:S(2)}) %collective-permute-start.37) | collective-permute-done | bytes 163872 | tf_op jit(solution)/shard_map/ppermute | solution.py:869
  188.1 1.8 collective-permute-done.38.g
  194.5 5.3 %collective-permute-done.41.b = bf16[640,128]{1,0:T(8,128)(2,1)S(1)} collective-permute-done((bf16[640,128]{1,0:T(8,128)(2,1)S(1)}, bf16[640,128]{1,0:T(8,128)(2,1)S(1)}, u32[]{:S(2)}, u32[]{:S(2)}) %collective-permute-start.41) | collective-permute-done | bytes 163872 | tf_op jit(solution)/shard_map/ppermute | solution.py:869
  200.4 4.9 %collective-permute-done.42 = bf16[1920,128]{1,0:T(8,128)(2,1)S(1)} collective-permute-done((bf16[1920,128]{1,0:T(8,128)(2,1)S(1)}, bf16[1920,128]{1,0:T(8,128)(2,1)S(1)}, u32[]{:S(2)}, u32[]{:S(2)}) %collective-permute-start.42) | collective-permute-done | bytes 491552 | tf_op jit(solution)/shard_map/ppermute | solution.py:869
  207.9 5.7 %collective-permute-done.44.g = bf16[960,128]{1,0:T(8,128)(2,1)S(1)} collective-permute-done((bf16[960,128]{1,0:T(8,128)(2,1)S(1)}, bf16[960,128]{1,0:T(8,128)(2,1)S(1)}, u32[]{:S(2)}, u32[]{:S(2)}) %collective-permute-start.44) | collective-permute-done | bytes 245792 | tf_op jit(solution)/shard_map/ppermute | solution.py:869
  214.3 1.6 collective-permute-start.46
  217.8 9.1 %collective-permute-done.46.g = bf16[960,128]{1,0:T(8,128)(2,1)S(1)} collective-permute-done((bf16[960,128]{1,0:T(8,128)(2,1)S(1)}, bf16[960,128]{1,0:T(8,128)(2,1)S(1)}, u32[]{:S(2)}, u32[]{:S(2)}) %collective-permute-start.46) | collective-permute-done | bytes 245792 | tf_op jit(solution)/shard_map/ppermute | solution.py:869
  228.1 2.8 %collective-permute-start.49 = (bf16[512,128]{1,0:T(8,128)(2,1)S(1)}, bf16[512,128]{1,0:T(8,128)(2,1)S(1)}, u32[]{:S(2)}, u32[]{:S(2)}) collective-permute-start(bf16[512,128]{1,0:T(8,128)(2,1)S(1)} %mix_sum.14.k), channel_id=1, source_target_pairs={{0,16},{1,17},{2,18},{3,19},{4,20},{5,21},{6,22},{7,23},{8,24},{9,... | collective-permute-start | bytes 393224 | tf_op jit(solution)/shard_map/ppermute | solution.py:869
  230.9 4.6 %collective-permute-done.48.b = bf16[960,128]{1,0:T(8,128)(2,1)S(1)} collective-permute-done((bf16[960,128]{1,0:T(8,128)(2,1)S(1)}, bf16[960,128]{1,0:T(8,128)(2,1)S(1)}, u32[]{:S(2)}, u32[]{:S(2)}) %collective-permute-start.48) | collective-permute-done | bytes 245792 | tf_op jit(solution)/shard_map/ppermute | solution.py:869
  238.0 3.7 %collective-permute-done.50.b = bf16[512,128]{1,0:T(8,128)(2,1)S(1)} collective-permute-done((bf16[512,128]{1,0:T(8,128)(2,1)S(1)}, bf16[512,128]{1,0:T(8,128)(2,1)S(1)}, u32[]{:S(2)}, u32[]{:S(2)}) %collective-permute-start.50) | collective-permute-done | bytes 131104 | tf_op jit(solution)/shard_map/ppermute | solution.py:869
  244.4 3.1 %collective-permute-done.54.b = bf16[1280,128]{1,0:T(8,128)(2,1)S(1)} collective-permute-done((bf16[1280,128]{1,0:T(8,128)(2,1)S(1)}, bf16[1280,128]{1,0:T(8,128)(2,1)S(1)}, u32[]{:S(2)}, u32[]{:S(2)}) %collective-permute-start.54) | collective-permute-done | bytes 327712 | tf_op jit(solution)/shard_map/ppermute | solution.py:869
  247.5 1.7 finish_one.1
  250.4 2.7 %collective-permute-done.51.b = bf16[1024,128]{1,0:T(8,128)(2,1)S(1)} collective-permute-done((bf16[1024,128]{1,0:T(8,128)(2,1)S(1)}, bf16[1024,128]{1,0:T(8,128)(2,1)S(1)}, u32[]{:S(2)}, u32[]{:S(2)}) %collective-permute-start.51) | collective-permute-done | bytes 262176 | tf_op jit(solution)/shard_map/ppermute | solution.py:869
  253.1 1.5 finish_three.1
  255.8 6.2 %collective-permute-done.52.oa = bf16[1280,128]{1,0:T(8,128)(2,1)S(1)} collective-permute-done((bf16[1280,128]{1,0:T(8,128)(2,1)S(1)}, bf16[1280,128]{1,0:T(8,128)(2,1)S(1)}, u32[]{:S(2)}, u32[]{:S(2)}) %collective-permute-start.52) | collective-permute-done | bytes 327712 | tf_op jit(solution)/shard_map/ppermute | solution.py:869
  261.9 2.5 finish_two.1
  (200 shorter events, 52.9 us)
Async XLA Ops:
  7.1 8.4 %collective-permute-start.1 = (bf16[176,512]{1,0:T(8,128)(2,1)S(1)}, bf16[176,512]{1,0:T(8,128)(2,1)S(1)}, u32[]{:S(2)}, u32[]{:S(2)}) collective-permute-start(bf16[176,512]{1,0:T(8,128)(2,1)S(1)} %pack.1.g0.w0.k0), channel_id=1, source_target_pairs={{0,2},{1,3},{2,0},{3,1},{4,6},{5,7},{6,4},{7,5},{8,10},{9,11},{10,... | collective-permute-start | bytes 540680 | tf_op jit(solution)/shard_map/ppermute | solution.py:758
  10.2 7.3 %collective-permute-start = (bf16[176,512]{1,0:T(8,128)(2,1)S(1)}, bf16[176,512]{1,0:T(8,128)(2,1)S(1)}, u32[]{:S(2)}, u32[]{:S(2)}) collective-permute-start(bf16[176,512]{1,0:T(8,128)(2,1)S(1)} %pack.1.g0.w0.k0), channel_id=1, source_target_pairs={{0,1},{1,0},{2,3},{3,2},{4,5},{5,4},{6,7},{7,6},{8,9},{9,8},{10,11... | collective-permute-start | bytes 540680 | tf_op jit(solution)/shard_map/ppermute | solution.py:758
  10.2 13.9 %collective-permute-start.4 = (bf16[160,1024]{1,0:T(8,128)(2,1)}, bf16[160,1024]{1,0:T(8,128)(2,1)}, u32[]{:S(2)}, u32[]{:S(2)}) collective-permute-start(bf16[160,1024]{1,0:T(8,128)(2,1)} %q0.1), channel_id=1, source_target_pairs={{0,2},{1,3},{2,0},{3,1},{4,6},{5,7},{6,4},{7,5},{8,10},{9,11},{10,... | collective-permute-start | bytes 983048 | tf_op jit(solution)/shard_map/ppermute | solution.py:758
  10.3 20.3 %collective-permute-start.3 = (bf16[160,1024]{1,0:T(8,128)(2,1)}, bf16[160,1024]{1,0:T(8,128)(2,1)}, u32[]{:S(2)}, u32[]{:S(2)}) collective-permute-start(bf16[160,1024]{1,0:T(8,128)(2,1)} %q0.1), channel_id=1, source_target_pairs={{0,1},{1,0},{2,3},{3,2},{4,5},{5,4},{6,7},{7,6},{8,9},{9,8},{10,11... | collective-permute-start | bytes 983048 | tf_op jit(solution)/shard_map/ppermute | solution.py:758
  24.1 6.6 %collective-permute-start.5 = (bf16[160,1024]{1,0:T(8,128)(2,1)}, bf16[160,1024]{1,0:T(8,128)(2,1)}, u32[]{:S(2)}, u32[]{:S(2)}) collective-permute-start(bf16[160,1024]{1,0:T(8,128)(2,1)} %collective-permute-done.4.w2.q2), channel_id=1, source_target_pairs={{0,1},{1,0},{2,3},{3,2},{4,5},{5,4},{6,7},{7,6},{8,9},{9,8},{10,11... | collective-permute-start | bytes 983048 | tf_op jit(solution)/shard_map/ppermute | solution.py:758
  24.9 21.5 %collective-permute-start.8 = (bf16[256,640]{1,0:T(8,128)(2,1)S(1)}, bf16[256,640]{1,0:T(8,128)(2,1)}, u32[]{:S(2)}, u32[]{:S(2)}) collective-permute-start(bf16[256,640]{1,0:T(8,128)(2,1)S(1)} %copy-done.3), channel_id=1, source_target_pairs={{0,2},{1,3},{2,0},{3,1},{4,6},{5,7},{6,4},{7,5},{8,10},{9,11},{10,... | collective-permute-start | bytes 983048 | tf_op jit(solution)/shard_map/ppermute | solution.py:758
  26.9 23.1 %collective-permute-start.7 = (bf16[256,640]{1,0:T(8,128)(2,1)S(1)}, bf16[256,640]{1,0:T(8,128)(2,1)}, u32[]{:S(2)}, u32[]{:S(2)}) collective-permute-start(bf16[256,640]{1,0:T(8,128)(2,1)S(1)} %copy-done.3), channel_id=1, source_target_pairs={{0,1},{1,0},{2,3},{3,2},{4,5},{5,4},{6,7},{7,6},{8,9},{9,8},{10,11... | collective-permute-start | bytes 983048 | tf_op jit(solution)/shard_map/ppermute | solution.py:758
  27.2 14.9 %collective-permute-start.6 = (bf16[512,512]{1,0:T(8,128)(2,1)}, bf16[512,512]{1,0:T(8,128)(2,1)S(1)}, u32[]{:S(2)}, u32[]{:S(2)}) collective-permute-start(bf16[512,512]{1,0:T(8,128)(2,1)} %copy-done.21), channel_id=1, source_target_pairs={{0,1},{1,2},{2,3},{3,4},{4,5},{5,6},{6,7},{8,9},{9,10},{10,11},{11... | collective-permute-start | bytes 1572872 | tf_op jit(solution)/shard_map/ppermute | solution.py:1107
  30.6 18.3 %collective-permute-start.11 = (bf16[80,2048]{1,0:T(8,128)(2,1)S(1)}, bf16[80,2048]{1,0:T(8,128)(2,1)S(1)}, u32[]{:S(2)}, u32[]{:S(2)}) collective-permute-start(bf16[80,2048]{1,0:T(8,128)(2,1)S(1)} %dynamic-slice_bitcast_fusion.2), channel_id=1, source_target_pairs={{0,2},{1,3},{2,0},{3,1},{4,6},{5,7},{6,4},{7,5},{8,10},{9,11},{10,... | collective-permute-start | bytes 983048 | tf_op jit(solution)/shard_map/ppermute | solution.py:758
  48.8 12.7 %collective-permute-start.10 = (bf16[160,2048]{1,0:T(8,128)(2,1)S(1)}, bf16[160,2048]{1,0:T(8,128)(2,1)S(1)}, u32[]{:S(2)}, u32[]{:S(2)}) collective-permute-start(bf16[160,2048]{1,0:T(8,128)(2,1)S(1)} %copy-done.5), channel_id=1, source_target_pairs={{0,1},{1,0},{2,3},{3,2},{4,5},{5,4},{6,7},{7,6},{8,9},{9,8},{10,11... | collective-permute-start | bytes 1966088 | tf_op jit(solution)/shard_map/ppermute | solution.py:758
  48.9 10.1 %collective-permute-start.12 = (bf16[80,2048]{1,0:T(8,128)(2,1)S(1)}, bf16[80,2048]{1,0:T(8,128)(2,1)S(1)}, u32[]{:S(2)}, u32[]{:S(2)}) collective-permute-start(bf16[80,2048]{1,0:T(8,128)(2,1)S(1)} %collective-permute-done.11.rest_2_.refs_8_), channel_id=1, source_target_pairs={{0,4},{4,0},{8,12},{12,8},{16,20},{20,16},{24,28},{28,24},{1,5},{5... | collective-permute-start | bytes 983048 | tf_op jit(solution)/shard_map/ppermute | solution.py:758
  49.8 11.8 %collective-permute-start.13 = (bf16[80,2048]{1,0:T(8,128)(2,1)S(1)}, bf16[80,2048]{1,0:T(8,128)(2,1)S(1)}, u32[]{:S(2)}, u32[]{:S(2)}) collective-permute-start(bf16[80,2048]{1,0:T(8,128)(2,1)S(1)} %collective-permute-done.11.rest_2_.refs_8_), channel_id=1, source_target_pairs={{0,1},{1,0},{2,3},{3,2},{4,5},{5,4},{6,7},{7,6},{8,9},{9,8},{10,11... | collective-permute-start | bytes 983048 | tf_op jit(solution)/shard_map/ppermute | solution.py:758
  50.1 10.9 %collective-permute-start.16 = (bf16[80,2048]{1,0:T(8,128)(2,1)S(1)}, bf16[80,2048]{1,0:T(8,128)(2,1)S(1)}, u32[]{:S(2)}, u32[]{:S(2)}) collective-permute-start(bf16[80,2048]{1,0:T(8,128)(2,1)S(1)} %dynamic-slice_bitcast_fusion.1), channel_id=1, source_target_pairs={{0,2},{1,3},{2,0},{3,1},{4,6},{5,7},{6,4},{7,5},{8,10},{9,11},{10,... | collective-permute-start | bytes 983048 | tf_op jit(solution)/shard_map/ppermute | solution.py:758
  59.0 16.0 %collective-permute-start.15 = (bf16[160,2048]{1,0:T(8,128)(2,1)S(1)}, bf16[160,2048]{1,0:T(8,128)(2,1)S(1)}, u32[]{:S(2)}, u32[]{:S(2)}) collective-permute-start(bf16[160,2048]{1,0:T(8,128)(2,1)S(1)} %copy-done.1), channel_id=1, source_target_pairs={{0,1},{1,0},{2,3},{3,2},{4,5},{5,4},{6,7},{7,6},{8,9},{9,8},{10,11... | collective-permute-start | bytes 1966088 | tf_op jit(solution)/shard_map/ppermute | solution.py:758
  61.0 12.2 %collective-permute-start.17 = (bf16[80,2048]{1,0:T(8,128)(2,1)S(1)}, bf16[80,2048]{1,0:T(8,128)(2,1)S(1)}, u32[]{:S(2)}, u32[]{:S(2)}) collective-permute-start(bf16[80,2048]{1,0:T(8,128)(2,1)S(1)} %collective-permute-done.16.rest_2_.refs_14_), channel_id=1, source_target_pairs={{0,4},{4,0},{8,12},{12,8},{16,20},{20,16},{24,28},{28,24},{1,5},{5... | collective-permute-start | bytes 983048 | tf_op jit(solution)/shard_map/ppermute | solution.py:758
  61.6 13.8 %collective-permute-start.18 = (bf16[80,2048]{1,0:T(8,128)(2,1)S(1)}, bf16[80,2048]{1,0:T(8,128)(2,1)S(1)}, u32[]{:S(2)}, u32[]{:S(2)}) collective-permute-start(bf16[80,2048]{1,0:T(8,128)(2,1)S(1)} %collective-permute-done.16.rest_2_.refs_14_), channel_id=1, source_target_pairs={{0,1},{1,0},{2,3},{3,2},{4,5},{5,4},{6,7},{7,6},{8,9},{9,8},{10,11... | collective-permute-start | bytes 983048 | tf_op jit(solution)/shard_map/ppermute | solution.py:758
  61.7 11.7 %collective-permute-start.21 = (bf16[256,640]{1,0:T(8,128)(2,1)S(1)}, bf16[256,640]{1,0:T(8,128)(2,1)S(1)}, u32[]{:S(2)}, u32[]{:S(2)}) collective-permute-start(bf16[256,640]{1,0:T(8,128)(2,1)S(1)} %dynamic-slice_bitcast_fusion), channel_id=1, source_target_pairs={{0,2},{1,3},{2,0},{3,1},{4,6},{5,7},{6,4},{7,5},{8,10},{9,11},{10,... | collective-permute-start | bytes 983048 | tf_op jit(solution)/shard_map/ppermute | solution.py:758
  73.4 10.7 %collective-permute-start.22 = (bf16[256,640]{1,0:T(8,128)(2,1)S(1)}, bf16[256,640]{1,0:T(8,128)(2,1)S(1)}, u32[]{:S(2)}, u32[]{:S(2)}) collective-permute-start(bf16[256,640]{1,0:T(8,128)(2,1)S(1)} %collective-permute-done.21.rest_2_), channel_id=1, source_target_pairs={{0,4},{4,0},{8,12},{12,8},{16,20},{20,16},{24,28},{28,24},{1,5},{5... | collective-permute-start | bytes 983048 | tf_op jit(solution)/shard_map/ppermute | solution.py:758
  74.9 9.3 %collective-permute-start.20 = (bf16[512,640]{1,0:T(8,128)(2,1)S(1)}, bf16[512,640]{1,0:T(8,128)(2,1)S(1)}, u32[]{:S(2)}, u32[]{:S(2)}) collective-permute-start(bf16[512,640]{1,0:T(8,128)(2,1)S(1)} %copy-done.4), channel_id=1, source_target_pairs={{0,1},{1,0},{2,3},{3,2},{4,5},{5,4},{6,7},{7,6},{8,9},{9,8},{10,11... | collective-permute-start | bytes 1966088 | tf_op jit(solution)/shard_map/ppermute | solution.py:758
  75.0 9.2 %collective-permute-start.23 = (bf16[256,640]{1,0:T(8,128)(2,1)S(1)}, bf16[256,640]{1,0:T(8,128)(2,1)S(1)}, u32[]{:S(2)}, u32[]{:S(2)}) collective-permute-start(bf16[256,640]{1,0:T(8,128)(2,1)S(1)} %collective-permute-done.21.rest_2_), channel_id=1, source_target_pairs={{0,1},{1,0},{2,3},{3,2},{4,5},{5,4},{6,7},{7,6},{8,9},{9,8},{10,11... | collective-permute-start | bytes 983048 | tf_op jit(solution)/shard_map/ppermute | solution.py:758
  95.5 15.0 %collective-permute-start.25 = (bf16[2,2560,128]{2,1,0:T(8,128)(2,1)S(1)}, bf16[2,2560,128]{2,1,0:T(8,128)(2,1)S(1)}, u32[]{:S(2)}, u32[]{:S(2)}) collective-permute-start(bf16[2,2560,128]{2,1,0:T(8,128)(2,1)S(1)} %bitcast.71), channel_id=1, source_target_pairs={{0,1},{1,0},{2,3},{3,2},{4,5},{5,4},{6,7},{7,6},{8,9},{9,8},{10,11... | collective-permute-start | bytes 3932168 | tf_op jit(solution)/shard_map/ppermute | solution.py:869
  110.0 17.0 %collective-permute-start.27 = (bf16[2,2560,128]{2,1,0:T(8,128)(2,1)S(1)}, bf16[2,2560,128]{2,1,0:T(8,128)(2,1)S(1)}, u32[]{:S(2)}, u32[]{:S(2)}) collective-permute-start(bf16[2,2560,128]{2,1,0:T(8,128)(2,1)S(1)} %bitcast.70), channel_id=1, source_target_pairs={{0,1},{1,0},{2,3},{3,2},{4,5},{5,4},{6,7},{7,6},{8,9},{9,8},{10,11... | collective-permute-start | bytes 3932168 | tf_op jit(solution)/shard_map/ppermute | solution.py:869
  111.8 15.2 %collective-permute-start.26 = (bf16[2,1280,128]{2,1,0:T(8,128)(2,1)S(1)}, bf16[2,1280,128]{2,1,0:T(8,128)(2,1)S(1)}, u32[]{:S(2)}, u32[]{:S(2)}) collective-permute-start(bf16[2,1280,128]{2,1,0:T(8,128)(2,1)S(1)} %get-tuple-element.185), channel_id=1, source_target_pairs={{0,2},{1,5},{2,0},{3,7},{4,6},{5,1},{6,4},{7,3},{8,10},{9,13},{10,... | collective-permute-start | bytes 1966088 | tf_op jit(solution)/shard_map/ppermute | solution.py:869
  126.5 24.8 %collective-permute-start.32 = (bf16[2,2560,128]{2,1,0:T(8,128)(2,1)S(1)}, bf16[2,2560,128]{2,1,0:T(8,128)(2,1)S(1)}, u32[]{:S(2)}, u32[]{:S(2)}) collective-permute-start(bf16[2,2560,128]{2,1,0:T(8,128)(2,1)S(1)} %bitcast.69), channel_id=1, source_target_pairs={{0,1},{1,0},{2,3},{3,2},{4,5},{5,4},{6,7},{7,6},{8,9},{9,8},{10,11... | collective-permute-start | bytes 3932168 | tf_op jit(solution)/shard_map/ppermute | solution.py:869
  129.0 14.3 %collective-permute-start.29 = (bf16[2,1280,128]{2,1,0:T(8,128)(2,1)S(1)}, bf16[2,1280,128]{2,1,0:T(8,128)(2,1)S(1)}, u32[]{:S(2)}, u32[]{:S(2)}) collective-permute-start(bf16[2,1280,128]{2,1,0:T(8,128)(2,1)S(1)} %get-tuple-element.196), channel_id=1, source_target_pairs={{0,2},{1,5},{2,0},{3,7},{4,6},{5,1},{6,4},{7,3},{8,10},{9,13},{10,... | collective-permute-start | bytes 1966088 | tf_op jit(solution)/shard_map/ppermute | solution.py:869
  130.4 10.7 %collective-permute-start.28 = (bf16[1280,128]{1,0:T(8,128)(2,1)S(1)}, bf16[1280,128]{1,0:T(8,128)(2,1)S(1)}, u32[]{:S(2)}, u32[]{:S(2)}) collective-permute-start(bf16[1280,128]{1,0:T(8,128)(2,1)S(1)} %get-tuple-element.192), channel_id=1, source_target_pairs={{0,4},{1,3},{2,6},{3,1},{4,0},{5,7},{6,2},{7,5},{8,12},{9,11},{10,... | collective-permute-start | bytes 983048 | tf_op jit(solution)/shard_map/ppermute | solution.py:869
  138.6 12.6 %collective-permute-start.33 = (bf16[2,1280,128]{2,1,0:T(8,128)(2,1)S(1)}, bf16[2,1280,128]{2,1,0:T(8,128)(2,1)S(1)}, u32[]{:S(2)}, u32[]{:S(2)}) collective-permute-start(bf16[2,1280,128]{2,1,0:T(8,128)(2,1)S(1)} %bitcast.72), channel_id=1, source_target_pairs={{0,1},{1,0},{2,3},{3,2},{4,5},{5,4},{6,7},{7,6},{8,9},{9,8},{10,11... | collective-permute-start | bytes 1966088 | tf_op jit(solution)/shard_map/ppermute | solution.py:869
  141.7 9.0 %collective-permute-start.30 = (bf16[640,128]{1,0:T(8,128)(2,1)S(1)}, bf16[640,128]{1,0:T(8,128)(2,1)S(1)}, u32[]{:S(2)}, u32[]{:S(2)}) collective-permute-start(bf16[640,128]{1,0:T(8,128)(2,1)S(1)} %get-tuple-element.207), channel_id=1, source_target_pairs={{0,8},{1,9},{2,10},{3,11},{4,12},{5,13},{6,14},{7,15},{8,0},{9,1},... | collective-permute-start | bytes 491528 | tf_op jit(solution)/shard_map/ppermute | solution.py:869
  144.0 11.4 %collective-permute-start.31 = (bf16[1280,128]{1,0:T(8,128)(2,1)S(1)}, bf16[1280,128]{1,0:T(8,128)(2,1)S(1)}, u32[]{:S(2)}, u32[]{:S(2)}) collective-permute-start(bf16[1280,128]{1,0:T(8,128)(2,1)S(1)} %get-tuple-element.210), channel_id=1, source_target_pairs={{0,4},{1,3},{2,6},{3,1},{4,0},{5,7},{6,2},{7,5},{8,12},{9,11},{10,... | collective-permute-start | bytes 983048 | tf_op jit(solution)/shard_map/ppermute | solution.py:869
  151.3 15.6 %collective-permute-start.34 = (bf16[640,128]{1,0:T(8,128)(2,1)S(1)}, bf16[640,128]{1,0:T(8,128)(2,1)S(1)}, u32[]{:S(2)}, u32[]{:S(2)}) collective-permute-start(bf16[640,128]{1,0:T(8,128)(2,1)S(1)} %mix_sum.8.k), channel_id=1, source_target_pairs={{0,16},{1,17},{2,18},{3,19},{4,20},{5,21},{6,22},{7,23},{8,24},{9,... | collective-permute-start | bytes 491528 | tf_op jit(solution)/shard_map/ppermute | solution.py:869
  153.9 14.2 %collective-permute-start.36 = (bf16[512,512]{1,0:T(8,128)(2,1)S(1)}, bf16[512,512]{1,0:T(8,128)(2,1)S(1)}, u32[]{:S(2)}, u32[]{:S(2)}) collective-permute-start(bf16[512,512]{1,0:T(8,128)(2,1)S(1)} %get-tuple-element.241), channel_id=1, source_target_pairs={{1,0},{2,1},{3,2},{4,3},{5,4},{6,5},{7,6},{9,8},{10,9},{11,10},{12... | collective-permute-start | bytes 1572872 | tf_op jit(solution)/shard_map/ppermute | solution.py:1162
  156.1 11.4 %collective-permute-start.35 = (bf16[640,128]{1,0:T(8,128)(2,1)S(1)}, bf16[640,128]{1,0:T(8,128)(2,1)S(1)}, u32[]{:S(2)}, u32[]{:S(2)}) collective-permute-start(bf16[640,128]{1,0:T(8,128)(2,1)S(1)} %get-tuple-element.222), channel_id=1, source_target_pairs={{0,8},{1,9},{2,10},{3,11},{4,12},{5,13},{6,14},{7,15},{8,0},{9,1},... | collective-permute-start | bytes 491528 | tf_op jit(solution)/shard_map/ppermute | solution.py:869
  159.1 31.3 %collective-permute-start.39 = (bf16[2,1920,128]{2,1,0:T(8,128)(2,1)S(1)}, bf16[2,1920,128]{2,1,0:T(8,128)(2,1)S(1)}, u32[]{:S(2)}, u32[]{:S(2)}) collective-permute-start(bf16[2,1920,128]{2,1,0:T(8,128)(2,1)S(1)} %get-tuple-element.229), channel_id=1, source_target_pairs={{0,2},{1,5},{2,0},{3,7},{4,6},{5,1},{6,4},{7,3},{8,10},{9,13},{10,... | collective-permute-start | bytes 2949128 | tf_op jit(solution)/shard_map/ppermute | solution.py:869
  178.6 13.9 %collective-permute-start.40 = (bf16[2,2048,128]{2,1,0:T(8,128)(2,1)S(1)}, bf16[2,2048,128]{2,1,0:T(8,128)(2,1)S(1)}, u32[]{:S(2)}, u32[]{:S(2)}) collective-permute-start(bf16[2,2048,128]{2,1,0:T(8,128)(2,1)S(1)} %get-tuple-element.258), channel_id=1, source_target_pairs={{0,1},{1,0},{2,3},{3,2},{4,5},{5,4},{6,7},{7,6},{8,9},{9,8},{10,11... | collective-permute-start | bytes 3145736 | tf_op jit(solution)/shard_map/ppermute | solution.py:869
  178.6 8.9 %collective-permute-start.37 = (bf16[640,128]{1,0:T(8,128)(2,1)S(1)}, bf16[640,128]{1,0:T(8,128)(2,1)S(1)}, u32[]{:S(2)}, u32[]{:S(2)}) collective-permute-start(bf16[640,128]{1,0:T(8,128)(2,1)S(1)} %mix_sum.9.a), channel_id=1, source_target_pairs={{0,8},{1,9},{2,10},{3,11},{4,12},{5,13},{6,14},{7,15},{8,0},{9,1},... | collective-permute-start | bytes 491528 | tf_op jit(solution)/shard_map/ppermute | solution.py:869
  179.2 10.7 %collective-permute-start.38 = (bf16[640,128]{1,0:T(8,128)(2,1)S(1)}, bf16[640,128]{1,0:T(8,128)(2,1)S(1)}, u32[]{:S(2)}, u32[]{:S(2)}) collective-permute-start(bf16[640,128]{1,0:T(8,128)(2,1)S(1)} %mix_sum.10.k), channel_id=1, source_target_pairs={{0,16},{1,17},{2,18},{3,19},{4,20},{5,21},{6,22},{7,23},{8,24},{9,... | collective-permute-start | bytes 491528 | tf_op jit(solution)/shard_map/ppermute | solution.py:869
  191.3 14.1 %collective-permute-start.42 = (bf16[1920,128]{1,0:T(8,128)(2,1)S(1)}, bf16[1920,128]{1,0:T(8,128)(2,1)S(1)}, u32[]{:S(2)}, u32[]{:S(2)}) collective-permute-start(bf16[1920,128]{1,0:T(8,128)(2,1)S(1)} %get-tuple-element.256), channel_id=1, source_target_pairs={{0,4},{1,3},{2,6},{3,1},{4,0},{5,7},{6,2},{7,5},{8,12},{9,11},{10,... | collective-permute-start | bytes 1474568 | tf_op jit(solution)/shard_map/ppermute | solution.py:869
  193.6 12.5 %collective-permute-start.43 = (bf16[2,1024,128]{2,1,0:T(8,128)(2,1)S(1)}, bf16[2,1024,128]{2,1,0:T(8,128)(2,1)S(1)}, u32[]{:S(2)}, u32[]{:S(2)}) collective-permute-start(bf16[2,1024,128]{2,1,0:T(8,128)(2,1)S(1)} %get-tuple-element.262), channel_id=1, source_target_pairs={{0,2},{1,5},{2,0},{3,7},{4,6},{5,1},{6,4},{7,3},{8,10},{9,13},{10,... | collective-permute-start | bytes 1572872 | tf_op jit(solution)/shard_map/ppermute | solution.py:869
  206.0 7.6 %collective-permute-start.44 = (bf16[960,128]{1,0:T(8,128)(2,1)S(1)}, bf16[960,128]{1,0:T(8,128)(2,1)S(1)}, u32[]{:S(2)}, u32[]{:S(2)}) collective-permute-start(bf16[960,128]{1,0:T(8,128)(2,1)S(1)} %get-tuple-element.267), channel_id=1, source_target_pairs={{0,8},{1,9},{2,10},{3,11},{4,12},{5,13},{6,14},{7,15},{8,0},{9,1},... | collective-permute-start | bytes 737288 | tf_op jit(solution)/shard_map/ppermute | solution.py:869
  206.8 9.1 %collective-permute-start.45 = (bf16[1024,128]{1,0:T(8,128)(2,1)S(1)}, bf16[1024,128]{1,0:T(8,128)(2,1)S(1)}, u32[]{:S(2)}, u32[]{:S(2)}) collective-permute-start(bf16[1024,128]{1,0:T(8,128)(2,1)S(1)} %get-tuple-element.272), channel_id=1, source_target_pairs={{0,4},{1,3},{2,6},{3,1},{4,0},{5,7},{6,2},{7,5},{8,12},{9,11},{10,... | collective-permute-start | bytes 786440 | tf_op jit(solution)/shard_map/ppermute | solution.py:869
  214.3 12.6 %collective-permute-start.46 = (bf16[960,128]{1,0:T(8,128)(2,1)S(1)}, bf16[960,128]{1,0:T(8,128)(2,1)S(1)}, u32[]{:S(2)}, u32[]{:S(2)}) collective-permute-start(bf16[960,128]{1,0:T(8,128)(2,1)S(1)} %mix_sum.12.k), channel_id=1, source_target_pairs={{0,16},{1,17},{2,18},{3,19},{4,20},{5,21},{6,22},{7,23},{8,24},{9,... | collective-permute-start | bytes 737288 | tf_op jit(solution)/shard_map/ppermute | solution.py:869
  216.5 11.1 %collective-permute-start.47 = (bf16[512,128]{1,0:T(8,128)(2,1)S(1)}, bf16[512,128]{1,0:T(8,128)(2,1)S(1)}, u32[]{:S(2)}, u32[]{:S(2)}) collective-permute-start(bf16[512,128]{1,0:T(8,128)(2,1)S(1)} %get-tuple-element.278), channel_id=1, source_target_pairs={{0,8},{1,9},{2,10},{3,11},{4,12},{5,13},{6,14},{7,15},{8,0},{9,1},... | collective-permute-start | bytes 393224 | tf_op jit(solution)/shard_map/ppermute | solution.py:869
  227.5 8.1 %collective-permute-start.48 = (bf16[960,128]{1,0:T(8,128)(2,1)S(1)}, bf16[960,128]{1,0:T(8,128)(2,1)S(1)}, u32[]{:S(2)}, u32[]{:S(2)}) collective-permute-start(bf16[960,128]{1,0:T(8,128)(2,1)S(1)} %mix_sum.13.a), channel_id=1, source_target_pairs={{0,8},{1,9},{2,10},{3,11},{4,12},{5,13},{6,14},{7,15},{8,0},{9,1},... | collective-permute-start | bytes 737288 | tf_op jit(solution)/shard_map/ppermute | solution.py:869
  228.1 8.0 %collective-permute-start.49 = (bf16[512,128]{1,0:T(8,128)(2,1)S(1)}, bf16[512,128]{1,0:T(8,128)(2,1)S(1)}, u32[]{:S(2)}, u32[]{:S(2)}) collective-permute-start(bf16[512,128]{1,0:T(8,128)(2,1)S(1)} %mix_sum.14.k), channel_id=1, source_target_pairs={{0,16},{1,17},{2,18},{3,19},{4,20},{5,21},{6,22},{7,23},{8,24},{9,... | collective-permute-start | bytes 393224 | tf_op jit(solution)/shard_map/ppermute | solution.py:869
  236.8 10.7 %collective-permute-start.54 = (bf16[1280,128]{1,0:T(8,128)(2,1)S(1)}, bf16[1280,128]{1,0:T(8,128)(2,1)S(1)}, u32[]{:S(2)}, u32[]{:S(2)}) collective-permute-start(bf16[1280,128]{1,0:T(8,128)(2,1)S(1)} %bitcast.52), channel_id=1, source_target_pairs={{0,4},{1,5},{2,6},{3,7},{4,0},{5,1},{6,2},{7,3},{8,12},{9,13},{10,... | collective-permute-start | bytes 983048 | tf_op jit(solution)/shard_map/ppermute | solution.py:869
  242.3 10.8 %collective-permute-start.51 = (bf16[1024,128]{1,0:T(8,128)(2,1)S(1)}, bf16[1024,128]{1,0:T(8,128)(2,1)S(1)}, u32[]{:S(2)}, u32[]{:S(2)}) collective-permute-start(bf16[1024,128]{1,0:T(8,128)(2,1)S(1)} %bitcast.56), channel_id=1, source_target_pairs={{0,4},{1,5},{2,6},{3,7},{4,0},{5,1},{6,2},{7,3},{8,12},{9,13},{10,... | collective-permute-start | bytes 786440 | tf_op jit(solution)/shard_map/ppermute | solution.py:869
  243.5 18.4 %collective-permute-start.53 = (bf16[1920,128]{1,0:T(8,128)(2,1)S(1)}, bf16[1920,128]{1,0:T(8,128)(2,1)S(1)}, u32[]{:S(2)}, u32[]{:S(2)}) collective-permute-start(bf16[1920,128]{1,0:T(8,128)(2,1)S(1)} %bitcast.46), channel_id=1, source_target_pairs={{0,4},{1,5},{2,6},{3,7},{4,0},{5,1},{6,2},{7,3},{8,12},{9,13},{10,... | collective-permute-start | bytes 1474568 | tf_op jit(solution)/shard_map/ppermute | solution.py:869
  249.2 12.7 %collective-permute-start.52 = (bf16[1280,128]{1,0:T(8,128)(2,1)S(1)}, bf16[1280,128]{1,0:T(8,128)(2,1)S(1)}, u32[]{:S(2)}, u32[]{:S(2)}) collective-permute-start(bf16[1280,128]{1,0:T(8,128)(2,1)S(1)} %bitcast.54), channel_id=1, source_target_pairs={{0,4},{1,5},{2,6},{3,7},{4,0},{5,1},{6,2},{7,3},{8,12},{9,13},{10,... | collective-permute-start | bytes 983048 | tf_op jit(solution)/shard_map/ppermute | solution.py:869
  (50 other events, 350.3 us)

commit v3 on v2

--- a/solution.py
+++ b/solution.py
@@ -26,7 +26,7 @@
 BF16 = jnp.bfloat16
 VM = pl.BlockSpec(memory_space=pltpu.VMEM)
 SM = pl.BlockSpec(memory_space=pltpu.SMEM)
-HB = pl.BlockSpec(memory_space=pl.ANY)
+HM = pl.BlockSpec(memory_space=pltpu.HBM)
 NN = (((1,), (0,)), ((), ()))
 NT = (((1,), (1,)), ((), ()))
 TN = (((0,), (0,)), ((), ()))
@@ -36,8 +36,8 @@
     return lax.dot_general(a, b, dims, preferred_element_type=F32)
 
 
-def params():
-    return pltpu.CompilerParams(vmem_limit_bytes=16 * 2**20)
+def params(mib=14):
+    return pltpu.CompilerParams(vmem_limit_bytes=mib * 2**20)
 
 
 def sds(shape, dtype=BF16):
@@ -73,6 +73,14 @@
 
 
 ME, XBIT, FLAG, EVEN, YBIT, SECOND, HERE = range(7)
+
+
+def pin(x):
+    return pltpu.with_memory_space_constraint(x, pltpu.HBM)
+
+
+def pinned(*arrays):
+    return tuple(pin(x) for x in arrays)
 
 
 def whole(piece):
@@ -99,25 +107,63 @@
     return copies
 
 
-def pack_kernel(info, k, v, g0, g1, g2, g3, g4, g5, out):
+def pack_kernel(info, k, v, g0, g1, g2, g3, g4, g5, out, r0, r1, r2, r3, r4, r5, sems):
     rows = D // 4
-    out[:rows, :HEAD_DIM] = k[...]
-    out[:rows, HEAD_DIM:] = v[...]
+    gains = (g0, g1, g2, g3, g4, g5)
+    places = (r0, r1, r2, r3, r4, r5)
+    copies = [
+        pltpu.make_async_copy(k, out.at[pl.ds(0, rows), pl.ds(0, HEAD_DIM)], sems.at[0]),
+        pltpu.make_async_copy(v, out.at[pl.ds(0, rows), pl.ds(HEAD_DIM, HEAD_DIM)], sems.at[1]),
+    ]
+    for i in range(6):
+        copies.append(pltpu.make_async_copy(gains[i], places[i], sems.at[2 + i]))
+    for c in copies:
+        c.start()
     out[rows:, :] = jnp.zeros((16, 2 * HEAD_DIM), BF16)
-    for i, g in enumerate((g0, g1, g2, g3, g4, g5)):
-        out[rows + i : rows + i + 1, : g.shape[0]] = g[...].reshape(1, -1)
+    for c in copies:
+        c.wait()
+    for i, r in enumerate(places):
+        out[rows + i : rows + i + 1, : r.shape[0]] = r[...].reshape(1, -1)
 
 
 def pack(info, k, v, *gains):
     return pl.pallas_call(
         pack_kernel,
         out_shape=sds((D // 4 + 16, 2 * HEAD_DIM)),
-        in_specs=[SM] + [VM] * 8,
+        in_specs=[SM] + [HM] * 8,
         out_specs=VM,
+        scratch_shapes=[pltpu.VMEM(g.shape, BF16) for g in gains] + [pltpu.SemaphoreType.DMA((8,))],
         compiler_params=params(),
         cost_estimate=cost(1e6, 4e5),
         name="pack",
-    )(info, k, v, *gains)
+    )(info, *(pin(w) for w in (k, v) + gains))
+
+
+def halves_kernel(info, *refs):
+    n = len(refs) // 2
+    ins, outs, sems = refs[:n], refs[n : 2 * n], refs[2 * n]
+    copies = []
+    for i, (w, o) in enumerate(zip(ins, outs)):
+        rows = w.shape[0] // 2
+        at = pl.multiple_of(info[XBIT] * rows, 16)
+        copies.append(pltpu.make_async_copy(w.at[pl.ds(at, rows)], o, sems.at[i]))
+    for c in copies:
+        c.start()
+    for c in copies:
+        c.wait()
+
+
+def halves(info, *weights):
+    return pl.pallas_call(
+        halves_kernel,
+        out_shape=tuple(sds((w.shape[0] // 2, w.shape[1])) for w in weights),
+        in_specs=[SM] + [HM] * len(weights),
+        out_specs=(VM,) * len(weights),
+        scratch_shapes=[pltpu.SemaphoreType.DMA((len(weights),))],
+        compiler_params=params(),
+        cost_estimate=cost(1e6, 2e6),
+        name="halves",
+    )(info, *(pin(w) for w in weights))
 
 
 def gains_kernel(me_ref, g0, g1, g2, g3, out):
@@ -196,7 +242,7 @@
             sds((HALF, 2 * HEAD_DIM)),
             sds((HALF, 2 * HEAD_DIM)),
         ),
-        in_specs=[SM, VM, VM, VM, VM, HB, HB, HB, HB],
+        in_specs=[SM, VM, VM, VM, VM, HM, HM, HM, HM],
         out_specs=(VM,) * 4,
         scratch_shapes=[pltpu.VMEM((D, 2 * HEAD_DIM), BF16), pltpu.SemaphoreType.DMA((4,))],
         compiler_params=params(),
@@ -234,7 +280,7 @@
         pre_q_kernel,
         grid=(HEADS,),
         out_shape=(hbm((HEADS, t, HEAD_DIM)), sds((HEADS, t, HEAD_DIM))),
-        in_specs=[SM, VM, VM, VM, VM, HB, HB, HB, HB],
+        in_specs=[SM, VM, VM, VM, VM, HM, HM, HM, HM],
         out_specs=(head, head),
         scratch_shapes=[pltpu.VMEM((D, HEADS * HEAD_DIM), BF16), pltpu.SemaphoreType.DMA((4,))],
         compiler_params=params(),
@@ -275,7 +321,8 @@
         out = dot(p1, v1) + dot(jnp.where(upper, pm, zero), v0) + dot(jnp.where(upper, zero, pm), v2)
         pm_o[:, sl, :] = pm.reshape(HEADS, QB, QB)
         p1_o[:, sl, :] = p1.reshape(HEADS, QB, QB)
-        o_o[:, sl, :] = out.astype(BF16).reshape(HEADS, QB, HEAD_DIM)
+        for h in range(HEADS):
+            o_o[sl, HEAD_DIM * h : HEAD_DIM * (h + 1)] = out[QB * h : QB * (h + 1), :].astype(BF16)
 
 
 def half_spec(half):
@@ -291,7 +338,7 @@
     return pl.pallas_call(
         body,
         grid=(1,),
-        out_shape=(shp, shp, shp),
+        out_shape=(sds((HALF, HEADS * HEAD_DIM)), shp, shp),
         in_specs=[SM, half_spec(half), VM, VM],
         out_specs=(VM,) * 3,
         compiler_params=params(),
@@ -376,9 +423,7 @@
         c.wait()
     for half, o in enumerate((o_lo, o_hi)):
         sl = slice(HALF * half, HALF * (half + 1))
-        proj = dot(o[0], wo[0:HEAD_DIM, :])
-        for h in range(1, HEADS):
-            proj = proj + dot(o[h], wo[HEAD_DIM * h : HEAD_DIM * (h + 1), :])
+        proj = dot(o[...], wo[...])
         ap_o[sl, :] = proj.astype(BF16)
         mid = tok[sl, :].astype(F32) + proj * rms_factor(proj) * gains[1:2, :]
         nm_o[sl, :] = (mid * rms_factor(mid) * gains[2:3, :]).astype(BF16)
@@ -389,7 +434,7 @@
     return pl.pallas_call(
         mid_kernel,
         out_shape=(sds((t, D)), sds((t, D))),
-        in_specs=[SM] + [VM] * 4 + [HB] * 4,
+        in_specs=[SM] + [VM] * 4 + [HM] * 4,
         out_specs=(VM, VM),
         scratch_shapes=[
             pltpu.VMEM((HEADS * HEAD_DIM, D), BF16),
@@ -402,48 +447,57 @@
 
 
 FH = FF // 2
-STEP = 256
+STEP = 512
+WIDE = 512
+RB = 512
+
+
+def by_columns(me_ref, pieces, buf, sems):
+    step = pl.program_id(0)
+
+    def copies(i):
+        at = pl.ds(pl.multiple_of(i * STEP, STEP), STEP)
+        return place_copies(
+            me_ref, pieces, lambda w: w.at[:, at], buf.at[:, at], D // 4, sems, 6 * i
+        )
+
+    @pl.when(step == 0)
+    def _():
+        for i in range(FF // STEP):
+            for c in copies(i):
+                c.start()
+
+    for c in copies(step):
+        c.wait()
+    return pl.ds(pl.multiple_of(step * STEP, STEP), STEP)
 
 
 def gate_kernel(me_ref, nm, *rest):
     pieces, (a_o, s_o, wg, sems) = rest[:6], rest[6:]
 
-    @pl.when(pl.program_id(0) == 0)
-    def _():
-        copies = place_copies(me_ref, pieces, whole, wg, D // 4, sems, 0)
-        for c in copies:
-            c.start()
-        for c in copies:
-            c.wait()
-
-    cs = pl.ds(pl.multiple_of(pl.program_id(0) * STEP, STEP), STEP)
-    g = dot(nm[...], wg[:, cs])
+    cs = by_columns(me_ref, pieces, wg, sems)
     c0 = 0.7978845608028654
     c1 = 0.044715 * c0
-    g2 = g * g
-    t = jnp.tanh(g * (c0 + c1 * g2))
-    h = 0.5 + 0.5 * t
-    a = g * h
-    slope = h + a * (1.0 - h) * (2.0 * c0 + (6.0 * c1) * g2)
-    a_o[...] = a.astype(BF16)
-    s_o[...] = slope.astype(BF16)
+    for r in range(0, nm.shape[0], RB):
+        g = dot(nm[r : r + RB, :], wg[:, cs])
+        g2 = g * g
+        t = jnp.tanh(g * (c0 + c1 * g2))
+        h = 0.5 + 0.5 * t
+        a = g * h
+        slope = h + a * (1.0 - h) * (2.0 * c0 + (6.0 * c1) * g2)
+        a_o[r : r + RB, :] = a.astype(BF16)
+        s_o[r : r + RB, :] = slope.astype(BF16)
 
 
 def up_kernel(me_ref, nm, a_i, s_i, *rest):
     pieces, (hid_o, b_o, wu, sems) = rest[:6], rest[6:]
 
-    @pl.when(pl.program_id(0) == 0)
-    def _():
-        copies = place_copies(me_ref, pieces, whole, wu, D // 4, sems, 0)
-        for c in copies:
-            c.start()
-        for c in copies:
-            c.wait()
-
-    cs = pl.ds(pl.multiple_of(pl.program_id(0) * STEP, STEP), STEP)
-    u = dot(nm[...], wu[:, cs])
-    hid_o[...] = (a_i[...].astype(F32) * u).astype(BF16)
-    b_o[...] = (u * s_i[...].astype(F32)).astype(BF16)
+    cs = by_columns(me_ref, pieces, wu, sems)
+    for r in range(0, nm.shape[0], RB):
+        rs = slice(r, r + RB)
+        u = dot(nm[rs, :], wu[:, cs])
+        hid_o[rs, :] = (a_i[rs, :].astype(F32) * u).astype(BF16)
+        b_o[rs, :] = (u * s_i[rs, :].astype(F32)).astype(BF16)
 
 
 def ff(me, nm, pieces, before=()):
@@ -453,9 +507,9 @@
         up_kernel if before else gate_kernel,
         grid=(FF // STEP,),
         out_shape=(sds((t, FF)),) * 2,
-        in_specs=[SM, VM] + [col] * len(before) + [HB] * 6,
+        in_specs=[SM, VM] + [col] * len(before) + [HM] * 6,
         out_specs=(col,) * 2,
-        scratch_shapes=[pltpu.VMEM((D, FF), BF16), pltpu.SemaphoreType.DMA((6,))],
+        scratch_shapes=[pltpu.VMEM((D, FF), BF16), pltpu.SemaphoreType.DMA((6 * FF // STEP,))],
         compiler_params=params(),
         cost_estimate=cost(2 * t * D * FF, 12e6),
         name="up" if before else "gate",
@@ -503,7 +557,7 @@
             sds((2, D // 128, FF // 4, 128)),
             sds((8, D), F32),
         ),
-        in_specs=[SM] + [VM] * 5 + [HB] * 6,
+        in_specs=[SM] + [VM] * 5 + [HM] * 6,
         out_specs=(VM,) * 6,
         scratch_shapes=[pltpu.SemaphoreType.DMA((6,))],
         compiler_params=params(),
@@ -521,15 +575,32 @@
         dnm_i, keep_o, send_o, dnm_o, wg, wu, gs, sems = rest
     core = me_ref[ME] % 2
 
+    copies = []
+    for k, (pieces, buf) in enumerate(((gates, wg), (ups, wu))):
+        copies += place_copies(
+            me_ref, pieces, lambda w: w.at[:, pl.ds(FH * half, FH)], buf, D // 4, sems, 6 * k
+        )
+
     @pl.when(pl.program_id(0) == 0)
     def _():
-        copies = []
-        for k, (pieces, buf) in enumerate(((gates, wg), (ups, wu))):
-            copies += place_copies(
-                me_ref, pieces, lambda w: w.at[:, pl.ds(FH * half, FH)], buf, D // 4, sems, 6 * k
-            )
         for c in copies:
             c.start()
+
+    cs = pl.ds(pl.multiple_of(pl.program_id(0) * WIDE, WIDE), WIDE)
+    dh = dot(dd[...], wd[...], NT)
+    dg = (dh * b_i[...].astype(F32)).astype(BF16)
+    du = (dh * a_i[...].astype(F32)).astype(BF16)
+    gr = D // 4
+    for k, d in enumerate((dg, du)):
+        gs[k] = dot(nm[...], d, TN).astype(BF16)
+        for y in range(2):
+            for part, o in ((core, keep_o), (1 - core, send_o)):
+                at = pl.ds(pl.multiple_of((2 * y + part) * gr, gr), gr)
+                for j in range(WIDE // 128):
+                    o[y, k, j] = gs[k, at, 128 * j : 128 * (j + 1)]
+
+    @pl.when(pl.program_id(0) == 0)
+    def _():
         for c in copies:
             c.wait()
         if first:
@@ -537,25 +608,13 @@
         else:
             dnm_o[...] = dnm_i[...]
 
-    cs = pl.ds(pl.multiple_of(pl.program_id(0) * STEP, STEP), STEP)
-    dh = dot(dd[...], wd[...], NT)
-    dg = (dh * b_i[...].astype(F32)).astype(BF16)
-    du = (dh * a_i[...].astype(F32)).astype(BF16)
     dnm_o[...] += dot(dg, wg[:, cs], NT) + dot(du, wu[:, cs], NT)
-    gr = D // 4
-    for k, d in enumerate((dg, du)):
-        gs[k] = dot(nm[...], d, TN).astype(BF16)
-        for y in range(2):
-            for part, o in ((core, keep_o), (1 - core, send_o)):
-                at = pl.ds(pl.multiple_of((2 * y + part) * gr, gr), gr)
-                for j in range(STEP // 128):
-                    o[y, k, j] = gs[k, at, 128 * j : 128 * (j + 1)]
 
 
 def fb(me, nm, dd, a, b, wd, gates, ups, part, dnm):
     t = nm.shape[0]
-    steps = FH // STEP
-    col = pl.BlockSpec((t, STEP), lambda i: (0, i + steps * part))
+    steps = FH // WIDE
+    col = pl.BlockSpec((t, WIDE), lambda i: (0, i + steps * part))
     extra = () if dnm is None else (dnm,)
 
     def body(*refs):
@@ -565,18 +624,18 @@
         body,
         grid=(steps,),
         out_shape=(sds((2, 2, FH // 128, D // 4, 128)),) * 2 + (sds((t, D), F32),),
-        in_specs=[SM, VM, VM, col, col, pl.BlockSpec((STEP, D), lambda i: (i + steps * part, 0))]
-        + [HB] * 12
+        in_specs=[SM, VM, VM, col, col, pl.BlockSpec((WIDE, D), lambda i: (i + steps * part, 0))]
+        + [HM] * 12
         + [VM] * len(extra),
-        out_specs=(pl.BlockSpec((2, 2, STEP // 128, D // 4, 128), lambda i: (0, 0, i, 0, 0)),) * 2
+        out_specs=(pl.BlockSpec((2, 2, WIDE // 128, D // 4, 128), lambda i: (0, 0, i, 0, 0)),) * 2
         + (VM,),
         scratch_shapes=[
             pltpu.VMEM((D, FH), BF16),
             pltpu.VMEM((D, FH), BF16),
-            pltpu.VMEM((2, D, STEP), BF16),
+            pltpu.VMEM((2, D, WIDE), BF16),
             pltpu.SemaphoreType.DMA((12,)),
         ],
-        compiler_params=params(),
+        compiler_params=params(20),
         cost_estimate=cost(10 * t * D * FH, 16e6),
         name="fb",
     )(me, nm, dd, a, b, wd, *gates, *ups, *extra)
@@ -611,8 +670,9 @@
     core = me_ref[ME] % 2
     for y in range(2):
         for part, o in ((core, keep_o), (1 - core, send_o)):
-            h = 2 * y + part
-            g = (dot(o_lo[h], datt[:HALF, :], TN) + dot(o_hi[h], datt[HALF:, :], TN)).astype(BF16)
+            cs = pl.ds(pl.multiple_of((2 * y + part) * HEAD_DIM, HEAD_DIM), HEAD_DIM)
+            g = dot(o_lo[:, cs], datt[:HALF, :], TN) + dot(o_hi[:, cs], datt[HALF:, :], TN)
+            g = g.astype(BF16)
             for j in range(D // 128):
                 o[y, j] = g[:, 128 * j : 128 * (j + 1)]
 
@@ -628,7 +688,7 @@
             sds((t, D)),
             sds((16, D), F32),
         ),
-        in_specs=[SM] + [VM] * 7 + [HB] * 4,
+        in_specs=[SM] + [VM] * 7 + [HM] * 4,
         out_specs=(VM,) * 5,
         scratch_shapes=[
             pltpu.VMEM((HEADS * HEAD_DIM, D), BF16),
@@ -645,19 +705,12 @@
 
 
 def post_kernel(
-    me_ref, tok, dmid, nin, dq_lo, dq_hi, kv_a, kv_b, kv_c, kv_d, kraw,
+    me_ref, nin, dq_lo, dq_hi, kv_a, kv_b, kv_c, kv_d, kraw,
     gains, cos_ref, sin_ref, gq_lo, gq_hi, gmid, gdown,
-    q0, q1, q2, q3, k0, k1, k2, k3,
-    gt_o, keep_o, send_o,
-    wq, wkv, dkv, gs, sums, small, sems,
+    dkv, keep_o, send_o,
+    gs, sums, small,
 ):
     rows = D // 4
-    copies = place_copies(me_ref, (q0, q1, q2, q3), lambda w: w, wq, rows, sems, 0)
-    copies += place_copies(
-        me_ref, (k0, k1, k2, k3), lambda w: w.at[pl.ds(0, rows)], wkv, rows, sems, 4
-    )
-    for c in copies:
-        c.start()
     hd = HEAD_DIM // 2
     gk = jnp.zeros((1, HEAD_DIM), F32)
     for half, (first, second) in enumerate(((kv_a, kv_b), (kv_c, kv_d))):
@@ -690,19 +743,8 @@
         put(h, dot(nin[:HALF, :], dq_lo[:, cs], TN) + dot(nin[HALF:, :], dq_hi[:, cs], TN))
     put(HEADS, dot(nin[...], dkv[:, :HEAD_DIM], TN))
     put(HEADS + 1, dot(nin[...], dkv[:, HEAD_DIM:], TN))
-    for c in copies:
-        c.wait()
-    gi = jnp.zeros((1, D), F32)
-    for half, dq in enumerate((dq_lo, dq_hi)):
-        sl = slice(HALF * half, HALF * (half + 1))
-        dnin = dot(dq[...], wq[...], NT) + dot(dkv[sl, :], wkv[...], NT)
-        x = tok[sl, :].astype(F32)
-        back, terms = norm_back(x, rms_factor(x), gains[0:1, :], dnin)
-        gi = gi + terms
-        gt_o[sl, :] = (dmid[sl, :].astype(F32) + back).astype(BF16)
     sums[...] = jnp.zeros_like(sums)
     small[...] = jnp.zeros_like(small)
-    sums[0:1, :] = gi
     sums[1:2, :] = gmid[8:9, :]
     sums[2:3, :] = gmid[0:1, :]
     sums[3:4, :] = gdown[0:1, :]
@@ -727,30 +769,63 @@
             o[y, base + 32 :, :] = jnp.zeros((LAST - base - 32, 128), BF16)
 
 
-def post(me, tok, dmid, nin, dqs, kvs, kraw, gains, cos, sin, sums, qs, kvgs):
-    t = tok.shape[0]
+def post(me, nin, dqs, kvs, kraw, gains, cos, sin, sums):
+    t = nin.shape[0]
     return pl.pallas_call(
         post_kernel,
         out_shape=(
-            sds((t, D)),
+            sds((t, 2 * HEAD_DIM)),
             sds((2, LAST, 128)),
             sds((2, LAST, 128)),
         ),
-        in_specs=[SM] + [VM] * 17 + [HB] * 8,
+        in_specs=[SM] + [VM] * 15,
         out_specs=(VM,) * 3,
+        scratch_shapes=[
+            pltpu.VMEM((HEADS + 2, D, HEAD_DIM), BF16),
+            pltpu.VMEM((16, D), F32),
+            pltpu.VMEM((16, HEAD_DIM), F32),
+        ],
+        compiler_params=params(),
+        cost_estimate=cost(2e9, 10e6),
+        name="post",
+    )(me, nin, *dqs, *kvs, kraw, gains, cos, sin, *sums)
+
+
+def last_kernel(me_ref, tok, dmid, dq_lo, dq_hi, dkv, gains, q0, q1, q2, q3, k0, k1, k2, k3, gt_o, wq, wkv, sems):
+    rows = D // 4
+    copies = place_copies(me_ref, (q0, q1, q2, q3), whole, wq, rows, sems, 0)
+    copies += place_copies(
+        me_ref, (k0, k1, k2, k3), lambda w: w.at[pl.ds(0, rows)], wkv, rows, sems, 4
+    )
+    for c in copies:
+        c.start()
+    for c in copies:
+        c.wait()
+    for half, dq in enumerate((dq_lo, dq_hi)):
+        for r in range(0, HALF, RB):
+            rs = slice(HALF * half + r, HALF * half + r + RB)
+            dnin = dot(dq[r : r + RB, :], wq[...], NT) + dot(dkv[rs, :], wkv[...], NT)
+            x = tok[rs, :].astype(F32)
+            back, _ = norm_back(x, rms_factor(x), gains[0:1, :], dnin)
+            gt_o[rs, :] = (dmid[rs, :].astype(F32) + back).astype(BF16)
+
+
+def last(me, tok, dmid, dqs, dkv, gains, qs, kvgs):
+    t = tok.shape[0]
+    return pl.pallas_call(
+        last_kernel,
+        out_shape=hbm((t, D)),
+        in_specs=[SM] + [VM] * 6 + [HM] * 8,
+        out_specs=VM,
         scratch_shapes=[
             pltpu.VMEM((D, HEADS * HEAD_DIM), BF16),
             pltpu.VMEM((D, 2 * HEAD_DIM), BF16),
-            pltpu.VMEM((t, 2 * HEAD_DIM), BF16),
-            pltpu.VMEM((HEADS + 2, D, HEAD_DIM), BF16),
-            pltpu.VMEM((16, D), F32),
-            pltpu.VMEM((16, HEAD_DIM), F32),
             pltpu.SemaphoreType.DMA((8,)),
         ],
         compiler_params=params(),
-        cost_estimate=cost(4e9, 15e6),
-        name="post",
-    )(me, tok, dmid, nin, *dqs, *kvs, kraw, gains, cos, sin, *sums, *qs, *kvgs)
+        cost_estimate=cost(2e9, 8e6),
+        name="last",
+    )(me, tok, dmid, *dqs, dkv, gains, *qs, *kvgs)
 
 
 def flip(x, axis, bit):
@@ -861,7 +936,7 @@
         here = [(seq >> i) & 1 for i in range(len(bits))]
         flag = (first_pos > 0).astype(jnp.int32)
         second = jnp.where(core == 0, x, y)
-        self.token = None
+        self.token = ()
         self.info = jnp.stack([shard, x, flag, 1 - core, y, second] + here).astype(jnp.int32)
 
     def send(self, x, even, odd):
@@ -869,7 +944,7 @@
         return lax.ppermute(x, ("seq", "shard"), pairs)
 
 
-ORDER = ("d", "da", "da", "dab", "da", "dabcabcbcbcbc")
+ORDER = ("d", "da", "da", "dab", "da", "b", "acbcbcbccb")
 
 
 class Chain:
@@ -882,7 +957,8 @@
         self.steps = [self.start, self.second]
         self.steps += [lambda i=i: self.halve(i) for i in range(1, n - 1)]
         self.steps += [self.exchange]
-        self.steps += [lambda i=i: self.double(i) for i in range(n - 2, -1, -1)]
+        self.steps += [lambda i=i: self.double(i) for i in range(n - 2, 1, -1)]
+        self.steps += [self.spread]
         self.count = len(self.steps)
 
     def add(self, keep, send):
@@ -906,10 +982,13 @@
 
     def go(self, out, even, odd):
         self.got = self.place.send(out, even, odd)
-        self.place.token = out
+        self.place.token = (out,)
 
     def turn(self, x):
-        return x if self.place.token is None else after(x, self.place.token)
+        return after(x, *self.place.token) if self.place.token else x
+
+    def collect(self):
+        self.place.token = tuple(self.parts)
 
     def start(self):
         out, self.keep = mix_first(self.place.info, self.keeps, self.gots)
@@ -932,18 +1011,28 @@
         self.go(self.keep, self.place.far[-1], self.place.far[-1])
         return self.keep
 
-    def double(self, i):
+    def settle(self, i):
         if i == len(self.place.far) - 2:
             self.keep = mix_sum(self.place.info, self.keep, self.got)
         else:
             self.keep = mix_both(self.place.info, HERE + i + 1, self.keep, self.got)
+
+    def spread(self):
+        self.settle(1)
+        x, z = self.place.far[:2]
+        self.place.token = (self.keep,)
+        self.parts = [self.keep] + [self.place.send(self.keep, f, f) for f in (x, z, x + z)]
+
+    def double(self, i):
+        self.settle(i)
         self.go(self.keep, self.place.far[i], self.place.far[i])
         return self.keep
 
 
-def gather_halves(info, own, other, total):
-    total[info[HERE]] = own[...]
-    total[1 - info[HERE]] = other[...]
+def gather_parts(info, parts, total):
+    x, z = info[HERE], info[HERE + 1]
+    for part, (i, j) in zip(parts, ((x, z), (1 - x, z), (x, 1 - z), (1 - x, 1 - z))):
+        total[2 * i + j] = part[...]
 
 
 def spread(o, total, at, rows, blocks):
@@ -957,30 +1046,32 @@
             done += n
 
 
-def finish_one(info, own, other):
-    def body(i, a, b, down, total):
-        gather_halves(i, a, b, total)
+def finish_one(info, parts):
+    def body(i, *refs):
+        down, total = refs[4:]
+        gather_parts(i, refs[:4], total)
         spread(down, total, 0, FF // 4, D // 128)
 
     return pl.pallas_call(
         body,
         out_shape=hbm((FF // 4, D), F32),
-        in_specs=[SM, VM, VM],
+        in_specs=[SM] + [VM] * 4,
         out_specs=VM,
-        scratch_shapes=[pltpu.VMEM((2,) + own.shape, BF16)],
+        scratch_shapes=[pltpu.VMEM((4,) + parts[0].shape, BF16)],
         compiler_params=params(),
         cost_estimate=cost(1e7, 1e7),
         name="finish_one",
-    )(info, own, other)
-
-
-def finish_two(info, own_a, other_a, own_b, other_b):
+    )(info, *parts)
+
+
+def finish_two(info, parts_a, parts_b):
     gr = D // 4
     blocks = FH // 128
 
-    def body(i, a, oa, b, ob, gate, up, out, total_a, total_b):
-        gather_halves(i, a, oa, total_a)
-        gather_halves(i, b, ob, total_b)
+    def body(i, *refs):
+        gate, up, out, total_a, total_b = refs[8:]
+        gather_parts(i, refs[:4], total_a)
+        gather_parts(i, refs[4:8], total_b)
         for k, total in enumerate((total_a, total_b)):
             spread(gate.at[:, pl.ds(FH * k, FH)], total, 0, gr, blocks)
             spread(up.at[:, pl.ds(FH * k, FH)], total, gr * blocks, gr, blocks)
@@ -989,27 +1080,37 @@
     return pl.pallas_call(
         body,
         out_shape=(hbm((gr, FF), F32), hbm((gr, FF), F32), hbm((HEAD_DIM, D), F32)),
-        in_specs=[SM] + [VM] * 4,
+        in_specs=[SM] + [VM] * 8,
         out_specs=(VM,) * 3,
         scratch_shapes=[
-            pltpu.VMEM((2,) + own_a.shape, BF16),
-            pltpu.VMEM((2,) + own_b.shape, BF16),
+            pltpu.VMEM((4,) + parts_a[0].shape, BF16),
+            pltpu.VMEM((4,) + parts_b[0].shape, BF16),
         ],
         compiler_params=params(),
         cost_estimate=cost(1e7, 1e7),
         name="finish_two",
-    )(info, own_a, other_a, own_b, other_b)
-
-
-def finish_three(info, own, other):
+    )(info, *parts_a, *parts_b)
+
+
+def finish_three(info, parts, query_w, key_w, value_w, gain):
     gr = D // 4
 
-    def body(i, a, b, query, key, value, gains, total):
-        gather_halves(i, a, b, total)
+    def body(i, *refs):
+        wq, wk, wv, g, query, key, value, gains, first, total, prod = refs[4:]
+        gather_parts(i, refs[:4], total)
         spread(query, total, 0, gr, 8)
         spread(key, total, 8 * gr, gr, 2)
         spread(value, total, 10 * gr, gr, 2)
         spread(gains, total, 12 * gr, 16, 2)
+        base = HEADS * HEAD_DIM
+        prod[:, :base] = query[...] * wq[...].astype(F32)
+        prod[:, base : base + HEAD_DIM] = key[...] * wk[...].astype(F32)
+        prod[:, base + HEAD_DIM :] = value[...] * wv[...].astype(F32)
+        p = prod[...]
+        high = p.astype(BF16)
+        low = (p - high.astype(F32)).astype(BF16)
+        ones = jnp.ones((16, 6 * HEAD_DIM), BF16)
+        first[...] = (dot(ones, high, NT) + dot(ones, low, NT)) / g[...].astype(F32).reshape(1, -1)
 
     return pl.pallas_call(
         body,
@@ -1018,14 +1119,18 @@
             hbm((gr, HEAD_DIM), F32),
             hbm((gr, HEAD_DIM), F32),
             sds((16, HEAD_DIM), F32),
+            sds((16, gr), F32),
         ),
-        in_specs=[SM, VM, VM],
-        out_specs=(VM,) * 4,
-        scratch_shapes=[pltpu.VMEM((2,) + own.shape, BF16)],
+        in_specs=[SM] + [VM] * 8,
+        out_specs=(VM,) * 5,
+        scratch_shapes=[
+            pltpu.VMEM((4,) + parts[0].shape, BF16),
+            pltpu.VMEM((gr, 6 * HEAD_DIM), F32),
+        ],
         compiler_params=params(),
         cost_estimate=cost(1e7, 1e7),
         name="finish_three",
-    )(info, own, other)
+    )(info, *parts, query_w, key_w, value_w, gain)
 
 
 def shards(
@@ -1048,7 +1153,6 @@
     n_seq = lax.axis_size("seq")
     n_shard = lax.axis_size("shard")
     shard = lax.axis_index("shard")
-    x_bit = lax.axis_index("seq") & 1
     count = tokens.shape[0]
     total = count * n_seq * n_shard
     length = min(SEQ_CAP, total)
@@ -1084,13 +1188,10 @@
         near(out_weight), near(gate_weight), near(up_weight), near(down_weight)
     )
 
-    def half(w):
-        return pick(w.reshape(2, w.shape[0] // 2, w.shape[1]), x_bit)
-
     def relay(x):
         return flip(x, "seq", 1)
 
-    gate_half, up_half, down_half = half(gate_weight), half(up_weight), half(down_weight)
+    gate_half, up_half, down_half = halves(me, gate_weight, up_weight, down_weight)
 
     positions = first_pos + jnp.arange(count, dtype=jnp.int32)
     hd = HEAD_DIM // 2
@@ -1100,37 +1201,37 @@
     sin = jnp.sin(angles)
 
     gains = gains_of(me, kvgs)
+    kvgs = pinned(*kvgs)
     nin, kraw, kv_lo, kv_hi = pre_kv(me, tokens, gains, cos, sin, kvgs)
     ranks = n_seq * n_shard
     per_seq = length // count
     pairs = [(i, i + 1) for i in range(ranks - 1) if (i + 1) % per_seq]
     halo = lax.ppermute(kv_hi, ("seq", "shard"), pairs)
     out_far = far(out_weight)
+    gate_a = far(gate_half)
     q_far = after(q_far, nin)
-    qs_w = (query_weight, q_near, q_far, near(q_far))
-    gate_a = far(gate_half)
+    qs_w = pinned(query_weight, q_near, q_far, near(q_far))
+    up_a = far(after(up_half, gate_a))
+    gate_b = relay(gate_a)
     qraw, qs = pre_q(me, nin, gains, cos, sin, qs_w)
+    qs = after(qs, out_far, gate_a)
     o_hi, pm_hi, p1_hi = att(flag, qs, kv_lo, kv_hi, False, 1)
     o_lo, pm_lo, p1_lo = att(flag, after(qs, o_hi), halo, kv_lo, True, 0)
-    out_far = after(out_far, o_lo)
-    gate_a = after(gate_a, o_lo)
-    up_a = far(after(up_half, gate_a))
-    gate_b = relay(gate_a)
-    outs = (out_weight, out_near, out_far, near(out_far))
-    ap, nm = mid_part(me, o_lo, o_hi, tokens, gains, outs)
-    gate_b = after(gate_b, nm)
-    up_a = after(up_a, nm)
+    gate_b = after(gate_b, o_lo)
+    up_a = after(up_a, o_lo)
     down_a = far(after(down_half, up_a))
     up_b = relay(up_a)
-    gates = (gate_weight, gate_near, gate_a, gate_b, near(gate_a), near(gate_b))
+    outs = pinned(out_weight, out_near, out_far, near(out_far))
+    ap, nm = mid_part(me, o_lo, o_hi, tokens, gains, outs)
+    gates = pinned(gate_weight, gate_near, gate_a, gate_b, near(gate_a), near(gate_b))
     act, slope = ff(me, nm, gates)
     up_b = after(up_b, act)
     down_a = after(down_a, act)
     down_b = relay(down_a)
-    ups = (up_weight, up_near, up_a, up_b, near(up_a), near(up_b))
+    ups = pinned(up_weight, up_near, up_a, up_b, near(up_a), near(up_b))
     hid, bact = ff(me, nm, ups, (act, slope))
     down_b = after(down_b, hid)
-    downs = (down_weight, down_near, down_a, down_b, near(down_a), near(down_b))
+    downs = pinned(down_weight, down_near, down_a, down_b, near(down_a), near(down_b))
     block_out, dd, wd, keep, send, gain_down = down_part(
         me, hid, tokens, cotangent, ap, gains, downs
     )
@@ -1138,8 +1239,11 @@
 
     def advance(order, *first):
         for name in order:
-            chain = chains[name]
-            if chain.steps:
+            chain = chains[name.lower()]
+            if name.isupper():
+                chain.parts = [after(x, *first) for x in chain.parts]
+                chain.collect()
+            elif chain.steps:
                 chain.wait(*first)
                 chain.step()
 
@@ -1147,48 +1251,53 @@
     keep, send, dnm = fb(me, nm, dd, act, bact, wd, gates, ups, 0, None)
     chains["a"].add(keep, send)
     advance(ORDER[0], dnm)
-    dnm = after(dnm, place.token)
+    dnm = after(dnm, *place.token)
     keep, send, dnm = fb(me, nm, dd, act, bact, wd, gates, ups, 1, dnm)
     chains["b"].add(keep, send)
     advance(ORDER[1], dnm)
     keep, send, d_o, d_mid, gain_mid = fe(
-        me, o_lo, o_hi, tokens, cotangent, gains, ap, after(dnm, place.token), outs
+        me, o_lo, o_hi, tokens, cotangent, gains, ap, after(dnm, *place.token), outs
     )
     chains["b"].add(keep, send)
     advance(ORDER[2], d_o)
     dq_lo, kv_back, kv_a, gq_lo = att_back(
-        qs, qraw, halo, kv_lo, pm_lo, p1_lo, after(d_o, place.token), gains, cos, sin, 0
+        qs, qraw, halo, kv_lo, pm_lo, p1_lo, after(d_o, *place.token), gains, cos, sin, 0
     )
     returned = lax.ppermute(kv_back, ("seq", "shard"), [(j, i) for i, j in pairs])
     advance(ORDER[3], dq_lo)
     dq_hi, kv_b, kv_c, gq_hi = att_back(
-        qs, qraw, kv_lo, kv_hi, pm_hi, p1_hi, after(d_o, dq_lo, place.token), gains, cos, sin, 1
+        qs, qraw, kv_lo, kv_hi, pm_hi, p1_hi, after(d_o, dq_lo, *place.token), gains, cos, sin, 1
     )
     advance(ORDER[4], dq_hi)
-    grad_tokens, keep, send = post(
+    dkv, keep, send = post(
         me,
-        tokens,
-        d_mid,
         nin,
-        (dq_lo, after(dq_hi, place.token)),
+        (dq_lo, after(dq_hi, *place.token)),
         (kv_a, kv_b, kv_c, returned),
         kraw,
         gains,
         cos,
         sin,
         (gq_lo, gq_hi, gain_mid, gain_down),
-        qs_w,
-        kvgs,
     )
     chains["c"].add(keep, send)
     advance(ORDER[5], keep)
+    grad_tokens = last(
+        me, tokens, d_mid, (dq_lo, dq_hi), after(dkv, *place.token), gains, qs_w, kvgs
+    )
+    advance(ORDER[6], grad_tokens)
     for name in "dacb":
         advance(name * len(chains[name].steps))
-    r_down = finish_one(me, chains["d"].keep, chains["d"].got)
-    r_query, r_key, r_value, tail = finish_three(me, chains["c"].keep, chains["c"].got)
-    r_gate, r_up, r_out = finish_two(
-        me, chains["a"].keep, chains["a"].got, chains["b"].keep, chains["b"].got
+    r_down = finish_one(me, chains["d"].parts)
+    r_query, r_key, r_value, tail, first = finish_three(
+        me,
+        chains["c"].parts,
+        query_weight,
+        key_weight,
+        value_weight,
+        input_gain,
     )
+    r_gate, r_up, r_out = finish_two(me, chains["a"].parts, chains["b"].parts)
     return (
         block_out,
         grad_tokens,
@@ -1199,7 +1308,7 @@
         r_gate,
         r_up,
         r_down,
-        tail[0, :gd],
+        first[0],
         tail[4, :gh],
         tail[5, :gh],
         tail[1, :gd],

time: 269 us -> 237 us (0.88)
  waiting for transfers between devices: 67.3 us -> 38.3 us
  local copies, waits for them, and re-layouts: 14.4 us -> 5.94 us
  starting transfers between devices: 49.2 us -> 56.3 us
    ppermute x29 -> x33, waiting for transfers between devices: 57.5 us -> 32 us  [send(): return lax.ppermute(x, ('seq', 'shard'), pairs)]
    unnamed x86 -> x88, local copies, waits for them, and re-layouts: 12.1 us -> 4.2 us
    ppermute x29 -> x33, starting transfers between devices: 27.3 us -> 32.7 us  [send(): return lax.ppermute(x, ('seq', 'shard'), pairs)]
    pallas_call x2, Pallas kernels: 28.6 us -> 24 us  [fb(): pl.pallas_call(body, grid=(steps,), out_shape=(sds((2, 2, FH // 128, D //...]
    ppermute x24, waiting for transfers between devices: 9.75 us -> 6.35 us  [flip(): return lax.ppermute(x, axis, [(i, i ^ bit) for i in range(n)])]
    pallas_call x4 -> x6, Pallas kernels: 18.7 us -> 21.3 us  [the longest x1 6.86 us: last(): pl.pallas_call(last_kernel, out_shape=hbm((t, D)), in_specs=[SM] + [VM] *...]
    pallas_call x24 -> x20, Pallas kernels: 17.6 us -> 15.4 us  [small_call(): pl.pallas_call(body, out_shape=tuple((sds(r + (128,)) for r in out_rows))...]
  transfers between devices with their start and end apart: 55 -> 59, of which waited for: 16 -> 16; matrix products, arithmetic and copies ran while one was open for 2% -> 1% of each run, Pallas kernels for 44% -> 49%
where the time goes in v3:
time: 237 us; the launch traced here: 233 us
  Pallas kernels  128 us (54%)
  starting transfers between devices  56.3 us (24%)
  waiting for transfers between devices  38.3 us (16%)
  local copies, waits for them, and re-layouts  5.94 us (3%)
    ppermute x33, starting transfers between devices, send(): return lax.ppermute(x, ('seq', 'shard'), pairs)  32.7 us
    ppermute x33, waiting for transfers between devices, send(): return lax.ppermute(x, ('seq', 'shard'), pairs)  32 us
    pallas_call x2, Pallas kernels, fb(): pl.pallas_call(body, grid=(steps,), out_shape=(sds((2, 2, FH // 128, D //...  24 us
    ppermute x24, starting transfers between devices, flip(): return lax.ppermute(x, axis, [(i, i ^ bit) for i in range(n)])  20.1 us
    pallas_call x2, Pallas kernels, ff(): pl.pallas_call(up_kernel if before else gate_kernel, grid=(FF // STEP,),...  17.9 us
    pallas_call x20, Pallas kernels, small_call(): pl.pallas_call(body, out_shape=tuple((sds(r + (128,)) for r in out_rows))...  15.4 us
    pallas_call x2, Pallas kernels, att_back(): pl.pallas_call(att_back_kernel, grid=(1,), out_shape=(sds((HALF, HEADS *...  11.7 us
    pallas_call x1, Pallas kernels, down_part(): pl.pallas_call(down_kernel, out_shape=(sds((t, D)), sds((t, D)), sds((FF,...  10.3 us
  transfers between devices with their start and end apart: 59, of which 16 were waited for; matrix products, arithmetic and copies ran while one was open for 1% of the time, Pallas kernels for 49%

profile of v3, /device:TPU:0, one launch (start us, length us, event | category | flops | bytes accessed | tf_op | source)
XLA Modules:
  0.0 232.6 jit_solution(6022990239453110221)
XLA Ops:
  0.8 1.6 pack.1.g0.w0.k0
  2.3 3.0 %collective-permute-start.1 = (bf16[176,512]{1,0:T(8,128)(2,1)S(1)}, bf16[176,512]{1,0:T(8,128)(2,1)S(1)}, u32[]{:S(2)}, u32[]{:S(2)}) collective-permute-start(bf16[176,512]{1,0:T(8,128)(2,1)S(1)} %pack.1.g0.w0.k0), channel_id=1, source_target_pairs={{0,2},{1,3},{2,0},{3,1},{4,6},{5,7},{6,4},{7,5},{8,10},{9,11},{10,... | collective-permute-start | bytes 540680 | tf_op jit(solution)/shard_map/ppermute | solution.py:833
  5.9 1.7 halves.1
  7.6 1.8 collective-permute-start.7
  10.8 1.9 multiply_sine_fusion
  13.6 3.2 %pre_kv.1 = (bf16[1024,640]{1,0:T(8,128)(2,1)S(1)}, bf16[1024,256]{1,0:T(8,128)(2,1)S(1)}, bf16[512,512]{1,0:T(8,128)(2,1)S(1)}, bf16[512,512]{1,0:T(8,128)(2,1)S(1)}) custom-call(s32[9]{0:T(128)S(1)} %stack.43.info.me_ref.refs_0_.s.i, bf16[1024,640]{1,0:T(8,128)(2,1)S(1)} %copy-done, f32[8,640]{1,0:T(8,128)S(1)} %gains.1, ...), custom_call_target="tpu_custom_call" | custom-call | flops 671088640 | bytes 5000000 | tf_op jit(solution)/shard_map/pre_kv/pallas_call | solution.py:237
  17.8 2.1 collective-permute-start.6
  19.9 2.3 collective-permute-start.8
  22.2 2.6 %collective-permute-done.7.rest_2_.refs_8_ = bf16[80,2048]{1,0:T(8,128)(2,1)S(1)} collective-permute-done((bf16[80,2048]{1,0:T(8,128)(2,1)S(1)}, bf16[80,2048]{1,0:T(8,128)(2,1)S(1)}, u32[]{:S(2)}, u32[]{:S(2)}) %collective-permute-start.7) | collective-permute-done | bytes 327712 | tf_op jit(solution)/shard_map/ppermute | solution.py:833
  25.4 2.1 collective-permute-start.16
  27.4 5.9 %pre_q.1 = (bf16[4,1024,256]{2,1,0:T(8,128)(2,1)}, bf16[4,1024,256]{2,1,0:T(8,128)(2,1)S(1)}) custom-call(s32[9]{0:T(128)S(1)} %stack.43.info.me_ref.refs_0_.s.i, bf16[1024,640]{1,0:T(8,128)(2,1)S(1)} %get-tuple-element.152.nin_i.nin, f32[8,640]{1,0:T(8,128)S(1)} %gains.1, f32[1024,128]{1,0:T(8,128)S(1)} %get-tuple-element.295.cos_ref, ...), custom_call_target="tpu_custom_call" | custom-call | flops 1342177280 | bytes 5000000 | tf_op jit(solution)/shard_map/pre_q/pallas_call | solution.py:279
  33.4 6.1 %collective-permute-start.12 = (bf16[80,2048]{1,0:T(8,128)(2,1)S(1)}, bf16[80,2048]{1,0:T(8,128)(2,1)S(1)}, u32[]{:S(2)}, u32[]{:S(2)}) collective-permute-start(bf16[80,2048]{1,0:T(8,128)(2,1)S(1)} %collective-permute-done.7.rest_2_.refs_8_), channel_id=1, source_target_pairs={{0,4},{4,0},{8,12},{12,8},{16,20},{20,16},{24,28},{28,24},{1,5},{5... | collective-permute-start | bytes 983048 | tf_op jit(solution)/shard_map/ppermute | solution.py:833
  39.5 3.2 %att.2 = (bf16[512,1024]{1,0:T(8,128)(2,1)S(1)}, bf16[4,512,256]{2,1,0:T(8,128)(2,1)S(1)}, bf16[4,512,256]{2,1,0:T(8,128)(2,1)S(1)}) custom-call(s32[9]{0:T(128)S(1)} %stack.43.info.me_ref.refs_0_.s.i, bf16[4,1024,256]{2,1,0:T(8,128)(2,1)S(1)} %get-tuple-element.160.refs_1_.qs, bf16[512,512]{1,0:T(8,128)(2,1)S(1)} %get-tuple-element.157.refs_2_.refs_3_.kvs.kvp, ...), custom_call_target="tpu_custom_call" | custom-call | flops 3000000000 | bytes 5000000 | tf_op jit(solution)/shard_map/att/pallas_call | solution.py:338
  43.8 3.3 %att.3 = (bf16[512,1024]{1,0:T(8,128)(2,1)S(1)}, bf16[4,512,256]{2,1,0:T(8,128)(2,1)S(1)}, bf16[4,512,256]{2,1,0:T(8,128)(2,1)S(1)}) custom-call(s32[9]{0:T(128)S(1)} %stack.43.info.me_ref.refs_0_.s.i, bf16[4,1024,256]{2,1,0:T(8,128)(2,1)S(1)} %get-tuple-element.160.refs_1_.qs, bf16[512,512]{1,0:T(8,128)(2,1)S(1)} %collective-permute-done.8.refs_2_.kvp, ...), custom_call_target="tpu_custom_call" | custom-call | flops 3000000000 | bytes 5000000 | tf_op jit(solution)/shard_map/att/pallas_call | solution.py:338
  49.0 4.3 %mid.1 = (bf16[1024,640]{1,0:T(8,128)(2,1)S(1)}, bf16[1024,640]{1,0:T(8,128)(2,1)S(1)}) custom-call(s32[9]{0:T(128)S(1)} %stack.43.info.me_ref.refs_0_.s.i, bf16[512,1024]{1,0:T(8,128)(2,1)S(1)} %get-tuple-element.161.o_lo, bf16[512,1024]{1,0:T(8,128)(2,1)S(1)} %get-tuple-element.159.o_hi, bf16[1024,640]{1,0:T(8,128)(2,1)S(1)} %copy-done, ...), custom_call_target="tpu_custom_call" | custom-call | flops 1342177280 | bytes 8000000 | tf_op jit(solution)/shard_map/mid/pallas_call | solution.py:434
  54.5 9.8 %gate.1 = (bf16[1024,2048]{1,0:T(8,128)(2,1)S(1)}, bf16[1024,2048]{1,0:T(8,128)(2,1)S(1)}) custom-call(s32[9]{0:T(128)S(1)} %stack.43.info.me_ref.refs_0_.s.i, bf16[1024,640]{1,0:T(8,128)(2,1)S(1)} %get-tuple-element.162.nm.refs_1_, bf16[160,2048]{1,0:T(8,128)(2,1)} %refs_6_.4, bf16[160,2048]{1,0:T(8,128)(2,1)} %copy-done.34, bf16[80,2048]{1,0:T(8,128)(2,1)} %copy-done.36, ...), custom_call_target="tpu_custom_call" | custom-call | flops 2684354560 | bytes 12000000 | tf_op jit(solution)/shard_map/gate/pallas_call | solution.py:506
  67.3 8.1 %up.1 = (bf16[1024,2048]{1,0:T(8,128)(2,1)S(1)}, bf16[1024,2048]{1,0:T(8,128)(2,1)S(1)}) custom-call(s32[9]{0:T(128)S(1)} %stack.43.info.me_ref.refs_0_.s.i, bf16[1024,640]{1,0:T(8,128)(2,1)S(1)} %get-tuple-element.162.nm.refs_1_, bf16[1024,2048]{1,0:T(8,128)(2,1)S(1)} %get-tuple-element.164.a_i.refs_3_, bf16[1024,2048]{1,0:T(8,128)(2,1)S(1)} %get-tuple-element.165.s_i, ...), custom_call_target="tpu_custom_call" | custom-call | flops 2684354560 | bytes 12000000 | tf_op jit(solution)/shard_map/up/pallas_call | solution.py:506
  77.8 10.3 %down.1 = (bf16[1024,640]{1,0:T(8,128)(2,1)}, bf16[1024,640]{1,0:T(8,128)(2,1)S(1)}, bf16[2048,640]{1,0:T(8,128)(2,1)S(1)}, bf16[2,5,512,128]{3,2,1,0:T(8,128)(2...) custom-call(s32[9]{0:T(128)S(1)} %stack.43.info.me_ref.refs_0_.s.i, ...), custom_call_target="tpu_custom_call" | custom-call | flops 5368709120 | bytes 20000000 | tf_op jit(solution)/shard_map/down/pallas_call | solution.py:550
  88.4 11.9 %fb.2 = (bf16[2,2,8,160,128]{4,3,2,1,0:T(8,128)(2,1)S(1)}, bf16[2,2,8,160,128]{4,3,2,1,0:T(8,128)(2,1)S(1)}, f32[1024,640]{1,0:T(8,128)S(1)}) custom-call(s32[9]{0:T(128)S(1)} %stack.43.info.me_ref.refs_0_.s.i, bf16[1024,640]{1,0:T(8,128)(2,1)S(1)} %get-tuple-element.162.nm.refs_1_, bf16[1024,640]{1,0:T(8,128)(2,1)S(1)} %get-tuple-element.177.refs_2_, ...), custom_call_target="tpu_custom_call" | custom-call | flops 6710886400 | bytes 16000000 | tf_op jit(solution)/shard_map/fb/pallas_call | solution.py:623
  102.0 1.7 collective-permute-start.26
  103.7 12.1 %fb.3 = (bf16[2,2,8,160,128]{4,3,2,1,0:T(8,128)(2,1)S(1)}, bf16[2,2,8,160,128]{4,3,2,1,0:T(8,128)(2,1)S(1)}, f32[1024,640]{1,0:T(8,128)S(1)}) custom-call(s32[9]{0:T(128)S(1)} %stack.43.info.me_ref.refs_0_.s.i, bf16[1024,640]{1,0:T(8,128)(2,1)S(1)} %get-tuple-element.162.nm.refs_1_, bf16[1024,640]{1,0:T(8,128)(2,1)S(1)} %get-tuple-element.177.refs_2_, ...), custom_call_target="tpu_custom_call" | custom-call | flops 6710886400 | bytes 16000000 | tf_op jit(solution)/shard_map/fb/pallas_call | solution.py:623
  119.9 8.0 %fe.1 = (bf16[2,5,256,128]{3,2,1,0:T(8,128)(2,1)S(1)}, bf16[2,5,256,128]{3,2,1,0:T(8,128)(2,1)S(1)}, bf16[4,1024,256]{2,1,0:T(8,128)(2,1)S(1)}, bf16[1024,640]{1,0:T(8,128)(2,1)S(1)}, f32[16,640]{1,0:T(8,128)S(1)}) custom-call(s32[9]{0:T(128)S(1)} %stack.43.info.me_ref.refs_0_.s.i, bf16[512,1024]{1,0:T(8,128)(2,1)S(1)} %get-tuple-element.161.o_lo, ...), custom_call_target="tpu_custom_call" | custom-call | flops 2684354560 | bytes 14000000 | tf_op jit(solution)/shard_map/fe/pallas_call | solution.py:682
  130.0 1.6 collective-permute-start.30
  133.8 5.9 %att_back.2 = (bf16[512,1024]{1,0:T(8,128)(2,1)S(1)}, bf16[512,512]{1,0:T(8,128)(2,1)S(1)}, f32[512,512]{1,0:T(8,128)S(1)}, f32[8,256]{1,0:T(8,128)S(1)}) custom-call(bf16[4,1024,256]{2,1,0:T(8,128)(2,1)S(1)} %copy-done.12, bf16[4,1024,256]{2,1,0:T(8,128)(2,1)S(1)} %copy-done.10, bf16[512,512]{1,0:T(8,128)(2,1)S(1)} %collective-permute-done.8.refs_2_.kvp, ...), custom_call_target="tpu_custom_call" | custom-call | flops 6000000000 | bytes 9000000 | tf_op jit(solution)/shard_map/att_back/pallas_call | solution.py:399
  140.3 2.6 %collective-permute-start.34 = (bf16[640,128]{1,0:T(8,128)(2,1)S(1)}, bf16[640,128]{1,0:T(8,128)(2,1)S(1)}, u32[]{:S(2)}, u32[]{:S(2)}) collective-permute-start(bf16[640,128]{1,0:T(8,128)(2,1)S(1)} %mix_sum.8.k), channel_id=1, source_target_pairs={{0,16},{1,17},{2,18},{3,19},{4,20},{5,21},{6,22},{7,23},{8,24},{9,... | collective-permute-start | bytes 491528 | tf_op jit(solution)/shard_map/ppermute | solution.py:944
  144.9 1.6 collective-permute-start.35
  146.6 1.6 mix_first.6
  148.2 1.4 collective-permute-start.37
  149.6 5.7 %att_back.3 = (bf16[512,1024]{1,0:T(8,128)(2,1)S(1)}, bf16[512,512]{1,0:T(8,128)(2,1)S(1)}, f32[512,512]{1,0:T(8,128)S(1)}, f32[8,256]{1,0:T(8,128)S(1)}) custom-call(bf16[4,1024,256]{2,1,0:T(8,128)(2,1)S(1)} %copy-done.12, bf16[4,1024,256]{2,1,0:T(8,128)(2,1)S(1)} %copy-done.10, bf16[512,512]{1,0:T(8,128)(2,1)S(1)} %get-tuple-element.157.refs_2_.refs_3_.kvs.kvp, ...), custom_call_target="tpu_custom_call" | custom-call | flops 6000000000 | bytes 9000000 | tf_op jit(solution)/shard_map/att_back/pallas_call | solution.py:399
  156.6 4.4 %post.1 = (bf16[1024,512]{1,0:T(8,128)(2,1)S(1)}, bf16[2,2048,128]{2,1,0:T(8,128)(2,1)S(1)}, bf16[2,2048,128]{2,1,0:T(8,128)(2,1)S(1)}) custom-call(s32[9]{0:T(128)S(1)} %stack.43.info.me_ref.refs_0_.s.i, bf16[1024,640]{1,0:T(8,128)(2,1)S(1)} %get-tuple-element.152.nin_i.nin, bf16[512,1024]{1,0:T(8,128)(2,1)S(1)} %get-tuple-element.211.dq_lo, ...), custom_call_target="tpu_custom_call" | custom-call | flops 2000000000 | bytes 10000000 | tf_op jit(solution)/shard_map/post/pallas_call | solution.py:774
  161.7 1.7 collective-permute-done.37.g
  165.4 6.9 %last.1 = bf16[1024,640]{1,0:T(8,128)(2,1)} custom-call(s32[9]{0:T(128)S(1)} %stack.43.info.me_ref.refs_0_.s.i, bf16[1024,640]{1,0:T(8,128)(2,1)S(1)} %copy-done, bf16[1024,640]{1,0:T(8,128)(2,1)S(1)} %get-tuple-element.197.dmid, bf16[512,1024]{1,0:T(8,128)(2,1)S(1)} %get-tuple-element.211.dq_lo, bf16[512,1024]{1,0:T(8,128)(2,1)S(1)} %get-tuple-element.236.dq_hi, ...), custom_call_target="tpu_custom_call" | custom-call | flops 2000000000 | bytes 8000000 | tf_op jit(solution)/shard_map/last/pallas_call | solution.py:815
  175.5 1.7 collective-permute-start.42
  177.2 6.1 %collective-permute-done.41.g = bf16[2,1024,128]{2,1,0:T(8,128)(2,1)S(1)} collective-permute-done((bf16[2,1024,128]{2,1,0:T(8,128)(2,1)S(1)}, bf16[2,1024,128]{2,1,0:T(8,128)(2,1)S(1)}, u32[]{:S(2)}, u32[]{:S(2)}) %collective-permute-start.41) | collective-permute-done | bytes 524320 | tf_op jit(solution)/shard_map/ppermute | solution.py:944
  186.4 1.5 collective-permute-start.58
  187.9 5.3 %collective-permute-done.43 = bf16[1024,128]{1,0:T(8,128)(2,1)S(1)} collective-permute-done((bf16[1024,128]{1,0:T(8,128)(2,1)S(1)}, bf16[1024,128]{1,0:T(8,128)(2,1)S(1)}, u32[]{:S(2)}, u32[]{:S(2)}) %collective-permute-start.43) | collective-permute-done | bytes 262176 | tf_op jit(solution)/shard_map/ppermute | solution.py:944
  193.9 2.0 collective-permute-start.57
  197.1 1.4 collective-permute-done.44.g
  199.1 2.1 collective-permute-done.45.g
  201.8 1.9 collective-permute-start.46
  203.8 1.5 collective-permute-start.55
  207.5 4.4 %collective-permute-done.52.refs_3_ = bf16[640,128]{1,0:T(8,128)(2,1)S(1)} collective-permute-done((bf16[640,128]{1,0:T(8,128)(2,1)S(1)}, bf16[640,128]{1,0:T(8,128)(2,1)S(1)}, u32[]{:S(2)}, u32[]{:S(2)}) %collective-permute-start.52) | collective-permute-done | bytes 163872 | tf_op jit(solution)/shard_map/ppermute | solution.py:944
  212.7 6.7 %collective-permute-done.51.refs_2_ = bf16[640,128]{1,0:T(8,128)(2,1)S(1)} collective-permute-done((bf16[640,128]{1,0:T(8,128)(2,1)S(1)}, bf16[640,128]{1,0:T(8,128)(2,1)S(1)}, u32[]{:S(2)}, u32[]{:S(2)}) %collective-permute-start.51) | collective-permute-done | bytes 163872 | tf_op jit(solution)/shard_map/ppermute | solution.py:944
  220.3 2.5 %collective-permute-start.48 = (bf16[512,128]{1,0:T(8,128)(2,1)S(1)}, bf16[512,128]{1,0:T(8,128)(2,1)S(1)}, u32[]{:S(2)}, u32[]{:S(2)}) collective-permute-start(bf16[512,128]{1,0:T(8,128)(2,1)S(1)} %mix_sum.15.refs_0_), channel_id=1, source_target_pairs={{0,8},{1,9},{2,10},{3,11},{4,12},{5,13},{6,14},{7,15},{8,0},{9,1},... | collective-permute-start | bytes 393224 | tf_op jit(solution)/shard_map/ppermute | solution.py:944
  222.9 1.7 finish_one.1
  224.6 2.5 %finish_two.1 = (f32[160,2048]{1,0:T(8,128)}, f32[160,2048]{1,0:T(8,128)}, f32[256,640]{1,0:T(8,128)}) custom-call(s32[9]{0:T(128)S(1)} %stack.43.info.me_ref.refs_0_.s.i, bf16[640,128]{1,0:T(8,128)(2,1)S(1)} %mix_sum.11.refs_0_, bf16[640,128]{1,0:T(8,128)(2,1)S(1)} %collective-permute-done.50.refs_1_, bf16[640,128]{1,0:T(8,128)(2,1)S(1)} %collective-permute-done.51.refs_2_, ...), custom_call_target="tpu_custom_call" | custom-call | flops 10000000 | bytes 10000000 | tf_op jit(solution)/shard_map/finish_two/pallas_call | solution.py:1080
  227.1 1.7 collective-permute-done.49.refs_3_
  229.1 1.6 finish_three.1
  (206 shorter events, 45.4 us)
Async XLA Ops:
  5.4 12.4 %collective-permute-start.4 = (bf16[160,1024]{1,0:T(8,128)(2,1)}, bf16[160,1024]{1,0:T(8,128)(2,1)S(1)}, u32[]{:S(2)}, u32[]{:S(2)}) collective-permute-start(bf16[160,1024]{1,0:T(8,128)(2,1)} %refs_4_.1), channel_id=1, source_target_pairs={{0,2},{1,3},{2,0},{3,1},{4,6},{5,7},{6,4},{7,5},{8,10},{9,11},{10,... | collective-permute-start | bytes 983048 | tf_op jit(solution)/shard_map/ppermute | solution.py:833
  5.5 19.3 %collective-permute-start.3 = (bf16[160,1024]{1,0:T(8,128)(2,1)}, bf16[160,1024]{1,0:T(8,128)(2,1)S(1)}, u32[]{:S(2)}, u32[]{:S(2)}) collective-permute-start(bf16[160,1024]{1,0:T(8,128)(2,1)} %refs_4_.1), channel_id=1, source_target_pairs={{0,1},{1,0},{2,3},{3,2},{4,5},{5,4},{6,7},{7,6},{8,9},{9,8},{10,11... | collective-permute-start | bytes 983048 | tf_op jit(solution)/shard_map/ppermute | solution.py:833
  7.6 17.1 %collective-permute-start.7 = (bf16[80,2048]{1,0:T(8,128)(2,1)S(1)}, bf16[80,2048]{1,0:T(8,128)(2,1)S(1)}, u32[]{:S(2)}, u32[]{:S(2)}) collective-permute-start(bf16[80,2048]{1,0:T(8,128)(2,1)S(1)} %get-tuple-element.155), channel_id=1, source_target_pairs={{0,2},{1,3},{2,0},{3,1},{4,6},{5,7},{6,4},{7,5},{8,10},{9,11},{10,... | collective-permute-start | bytes 983048 | tf_op jit(solution)/shard_map/ppermute | solution.py:833
  17.8 15.6 %collective-permute-start.6 = (bf16[256,640]{1,0:T(8,128)(2,1)S(1)}, bf16[256,640]{1,0:T(8,128)(2,1)S(1)}, u32[]{:S(2)}, u32[]{:S(2)}) collective-permute-start(bf16[256,640]{1,0:T(8,128)(2,1)S(1)} %copy-done.23), channel_id=1, source_target_pairs={{0,2},{1,3},{2,0},{3,1},{4,6},{5,7},{6,4},{7,5},{8,10},{9,11},{10,... | collective-permute-start | bytes 983048 | tf_op jit(solution)/shard_map/ppermute | solution.py:833
  19.9 23.8 %collective-permute-start.8 = (bf16[512,512]{1,0:T(8,128)(2,1)S(1)}, bf16[512,512]{1,0:T(8,128)(2,1)S(1)}, u32[]{:S(2)}, u32[]{:S(2)}) collective-permute-start(bf16[512,512]{1,0:T(8,128)(2,1)S(1)} %get-tuple-element.158.refs_3_.kvs), channel_id=1, source_target_pairs={{0,1},{1,2},{2,3},{3,4},{4,5},{5,6},{6,7},{8,9},{9,10},{10,11},{11... | collective-permute-start | bytes 1572872 | tf_op jit(solution)/shard_map/ppermute | solution.py:1209
  24.8 23.0 %collective-permute-start.9 = (bf16[256,640]{1,0:T(8,128)(2,1)S(1)}, bf16[256,640]{1,0:T(8,128)(2,1)S(1)}, u32[]{:S(2)}, u32[]{:S(2)}) collective-permute-start(bf16[256,640]{1,0:T(8,128)(2,1)S(1)} %copy-done.23), channel_id=1, source_target_pairs={{0,1},{1,0},{2,3},{3,2},{4,5},{5,4},{6,7},{7,6},{8,9},{9,8},{10,11... | collective-permute-start | bytes 983048 | tf_op jit(solution)/shard_map/ppermute | solution.py:833
  24.8 28.5 %collective-permute-start.11 = (bf16[160,2048]{1,0:T(8,128)(2,1)S(1)}, bf16[160,2048]{1,0:T(8,128)(2,1)S(1)}, u32[]{:S(2)}, u32[]{:S(2)}) collective-permute-start(bf16[160,2048]{1,0:T(8,128)(2,1)S(1)} %copy-done.22), channel_id=1, source_target_pairs={{0,1},{1,0},{2,3},{3,2},{4,5},{5,4},{6,7},{7,6},{8,9},{9,8},{10,11... | collective-permute-start | bytes 1966088 | tf_op jit(solution)/shard_map/ppermute | solution.py:833
  25.4 22.3 %collective-permute-start.16 = (bf16[80,2048]{1,0:T(8,128)(2,1)S(1)}, bf16[80,2048]{1,0:T(8,128)(2,1)S(1)}, u32[]{:S(2)}, u32[]{:S(2)}) collective-permute-start(bf16[80,2048]{1,0:T(8,128)(2,1)S(1)} %get-tuple-element.167), channel_id=1, source_target_pairs={{0,2},{1,3},{2,0},{3,1},{4,6},{5,7},{6,4},{7,5},{8,10},{9,11},{10,... | collective-permute-start | bytes 983048 | tf_op jit(solution)/shard_map/ppermute | solution.py:833
  33.4 13.7 %collective-permute-start.12 = (bf16[80,2048]{1,0:T(8,128)(2,1)S(1)}, bf16[80,2048]{1,0:T(8,128)(2,1)S(1)}, u32[]{:S(2)}, u32[]{:S(2)}) collective-permute-start(bf16[80,2048]{1,0:T(8,128)(2,1)S(1)} %collective-permute-done.7.rest_2_.refs_8_), channel_id=1, source_target_pairs={{0,4},{4,0},{8,12},{12,8},{16,20},{20,16},{24,28},{28,24},{1,5},{5... | collective-permute-start | bytes 983048 | tf_op jit(solution)/shard_map/ppermute | solution.py:833
  47.8 18.1 %collective-permute-start.15 = (bf16[160,2048]{1,0:T(8,128)(2,1)S(1)}, bf16[160,2048]{1,0:T(8,128)(2,1)S(1)}, u32[]{:S(2)}, u32[]{:S(2)}) collective-permute-start(bf16[160,2048]{1,0:T(8,128)(2,1)S(1)} %copy-done.19), channel_id=1, source_target_pairs={{0,1},{1,0},{2,3},{3,2},{4,5},{5,4},{6,7},{7,6},{8,9},{9,8},{10,11... | collective-permute-start | bytes 1966088 | tf_op jit(solution)/shard_map/ppermute | solution.py:833
  48.2 16.1 %collective-permute-start.17 = (bf16[80,2048]{1,0:T(8,128)(2,1)S(1)}, bf16[80,2048]{1,0:T(8,128)(2,1)S(1)}, u32[]{:S(2)}, u32[]{:S(2)}) collective-permute-start(bf16[80,2048]{1,0:T(8,128)(2,1)S(1)} %collective-permute-done.16.rest_2_.refs_14_), channel_id=1, source_target_pairs={{0,4},{4,0},{8,12},{12,8},{16,20},{20,16},{24,28},{28,24},{1,5},{5... | collective-permute-start | bytes 983048 | tf_op jit(solution)/shard_map/ppermute | solution.py:833
  53.3 13.1 %collective-permute-start.18 = (bf16[80,2048]{1,0:T(8,128)(2,1)S(1)}, bf16[80,2048]{1,0:T(8,128)(2,1)S(1)}, u32[]{:S(2)}, u32[]{:S(2)}) collective-permute-start(bf16[80,2048]{1,0:T(8,128)(2,1)S(1)} %collective-permute-done.16.rest_2_.refs_14_), channel_id=1, source_target_pairs={{0,1},{1,0},{2,3},{3,2},{4,5},{5,4},{6,7},{7,6},{8,9},{9,8},{10,11... | collective-permute-start | bytes 983048 | tf_op jit(solution)/shard_map/ppermute | solution.py:833
  53.7 10.9 %collective-permute-start.21 = (bf16[256,640]{1,0:T(8,128)(2,1)S(1)}, bf16[256,640]{1,0:T(8,128)(2,1)S(1)}, u32[]{:S(2)}, u32[]{:S(2)}) collective-permute-start(bf16[256,640]{1,0:T(8,128)(2,1)S(1)} %get-tuple-element.173), channel_id=1, source_target_pairs={{0,2},{1,3},{2,0},{3,1},{4,6},{5,7},{6,4},{7,5},{8,10},{9,11},{10,... | collective-permute-start | bytes 983048 | tf_op jit(solution)/shard_map/ppermute | solution.py:833
  64.6 10.8 %collective-permute-start.22 = (bf16[256,640]{1,0:T(8,128)(2,1)S(1)}, bf16[256,640]{1,0:T(8,128)(2,1)S(1)}, u32[]{:S(2)}, u32[]{:S(2)}) collective-permute-start(bf16[256,640]{1,0:T(8,128)(2,1)S(1)} %collective-permute-done.21.rest_2_), channel_id=1, source_target_pairs={{0,4},{4,0},{8,12},{12,8},{16,20},{20,16},{24,28},{28,24},{1,5},{5... | collective-permute-start | bytes 983048 | tf_op jit(solution)/shard_map/ppermute | solution.py:833
  65.9 9.8 %collective-permute-start.20 = (bf16[512,640]{1,0:T(8,128)(2,1)S(1)}, bf16[512,640]{1,0:T(8,128)(2,1)S(1)}, u32[]{:S(2)}, u32[]{:S(2)}) collective-permute-start(bf16[512,640]{1,0:T(8,128)(2,1)S(1)} %copy-done.21), channel_id=1, source_target_pairs={{0,1},{1,0},{2,3},{3,2},{4,5},{5,4},{6,7},{7,6},{8,9},{9,8},{10,11... | collective-permute-start | bytes 1966088 | tf_op jit(solution)/shard_map/ppermute | solution.py:833
  65.9 9.8 %collective-permute-start.23 = (bf16[256,640]{1,0:T(8,128)(2,1)S(1)}, bf16[256,640]{1,0:T(8,128)(2,1)S(1)}, u32[]{:S(2)}, u32[]{:S(2)}) collective-permute-start(bf16[256,640]{1,0:T(8,128)(2,1)S(1)} %collective-permute-done.21.rest_2_), channel_id=1, source_target_pairs={{0,1},{1,0},{2,3},{3,2},{4,5},{5,4},{6,7},{7,6},{8,9},{9,8},{10,11... | collective-permute-start | bytes 983048 | tf_op jit(solution)/shard_map/ppermute | solution.py:833
  88.1 12.6 %collective-permute-start.25 = (bf16[2,2560,128]{2,1,0:T(8,128)(2,1)S(1)}, bf16[2,2560,128]{2,1,0:T(8,128)(2,1)S(1)}, u32[]{:S(2)}, u32[]{:S(2)}) collective-permute-start(bf16[2,2560,128]{2,1,0:T(8,128)(2,1)S(1)} %bitcast.47), channel_id=1, source_target_pairs={{0,1},{1,0},{2,3},{3,2},{4,5},{5,4},{6,7},{7,6},{8,9},{9,8},{10,11... | collective-permute-start | bytes 3932168 | tf_op jit(solution)/shard_map/ppermute | solution.py:944
  100.3 15.6 %collective-permute-start.27 = (bf16[2,2560,128]{2,1,0:T(8,128)(2,1)S(1)}, bf16[2,2560,128]{2,1,0:T(8,128)(2,1)S(1)}, u32[]{:S(2)}, u32[]{:S(2)}) collective-permute-start(bf16[2,2560,128]{2,1,0:T(8,128)(2,1)S(1)} %bitcast.46), channel_id=1, source_target_pairs={{0,1},{1,0},{2,3},{3,2},{4,5},{5,4},{6,7},{7,6},{8,9},{9,8},{10,11... | collective-permute-start | bytes 3932168 | tf_op jit(solution)/shard_map/ppermute | solution.py:944
  102.0 13.9 %collective-permute-start.26 = (bf16[2,1280,128]{2,1,0:T(8,128)(2,1)S(1)}, bf16[2,1280,128]{2,1,0:T(8,128)(2,1)S(1)}, u32[]{:S(2)}, u32[]{:S(2)}) collective-permute-start(bf16[2,1280,128]{2,1,0:T(8,128)(2,1)S(1)} %get-tuple-element.184), channel_id=1, source_target_pairs={{0,2},{1,5},{2,0},{3,7},{4,6},{5,1},{6,4},{7,3},{8,10},{9,13},{10,... | collective-permute-start | bytes 1966088 | tf_op jit(solution)/shard_map/ppermute | solution.py:944
  115.8 28.4 %collective-permute-start.32 = (bf16[2,2560,128]{2,1,0:T(8,128)(2,1)S(1)}, bf16[2,2560,128]{2,1,0:T(8,128)(2,1)S(1)}, u32[]{:S(2)}, u32[]{:S(2)}) collective-permute-start(bf16[2,2560,128]{2,1,0:T(8,128)(2,1)S(1)} %bitcast.45), channel_id=1, source_target_pairs={{0,1},{1,0},{2,3},{3,2},{4,5},{5,4},{6,7},{7,6},{8,9},{9,8},{10,11... | collective-permute-start | bytes 3932168 | tf_op jit(solution)/shard_map/ppermute | solution.py:944
  117.9 14.2 %collective-permute-start.29 = (bf16[2,1280,128]{2,1,0:T(8,128)(2,1)S(1)}, bf16[2,1280,128]{2,1,0:T(8,128)(2,1)S(1)}, u32[]{:S(2)}, u32[]{:S(2)}) collective-permute-start(bf16[2,1280,128]{2,1,0:T(8,128)(2,1)S(1)} %get-tuple-element.195), channel_id=1, source_target_pairs={{0,2},{1,5},{2,0},{3,7},{4,6},{5,1},{6,4},{7,3},{8,10},{9,13},{10,... | collective-permute-start | bytes 1966088 | tf_op jit(solution)/shard_map/ppermute | solution.py:944
  118.8 10.6 %collective-permute-start.28 = (bf16[1280,128]{1,0:T(8,128)(2,1)S(1)}, bf16[1280,128]{1,0:T(8,128)(2,1)S(1)}, u32[]{:S(2)}, u32[]{:S(2)}) collective-permute-start(bf16[1280,128]{1,0:T(8,128)(2,1)S(1)} %get-tuple-element.191), channel_id=1, source_target_pairs={{0,4},{1,3},{2,6},{3,1},{4,0},{5,7},{6,2},{7,5},{8,12},{9,11},{10,... | collective-permute-start | bytes 983048 | tf_op jit(solution)/shard_map/ppermute | solution.py:944
  127.9 12.4 %collective-permute-start.33 = (bf16[2,1280,128]{2,1,0:T(8,128)(2,1)S(1)}, bf16[2,1280,128]{2,1,0:T(8,128)(2,1)S(1)}, u32[]{:S(2)}, u32[]{:S(2)}) collective-permute-start(bf16[2,1280,128]{2,1,0:T(8,128)(2,1)S(1)} %bitcast.48), channel_id=1, source_target_pairs={{0,1},{1,0},{2,3},{3,2},{4,5},{5,4},{6,7},{7,6},{8,9},{9,8},{10,11... | collective-permute-start | bytes 1966088 | tf_op jit(solution)/shard_map/ppermute | solution.py:944
  130.0 9.7 %collective-permute-start.30 = (bf16[640,128]{1,0:T(8,128)(2,1)S(1)}, bf16[640,128]{1,0:T(8,128)(2,1)S(1)}, u32[]{:S(2)}, u32[]{:S(2)}) collective-permute-start(bf16[640,128]{1,0:T(8,128)(2,1)S(1)} %get-tuple-element.206), channel_id=1, source_target_pairs={{0,8},{1,9},{2,10},{3,11},{4,12},{5,13},{6,14},{7,15},{8,0},{9,1},... | collective-permute-start | bytes 491528 | tf_op jit(solution)/shard_map/ppermute | solution.py:944
  132.8 11.5 %collective-permute-start.31 = (bf16[1280,128]{1,0:T(8,128)(2,1)S(1)}, bf16[1280,128]{1,0:T(8,128)(2,1)S(1)}, u32[]{:S(2)}, u32[]{:S(2)}) collective-permute-start(bf16[1280,128]{1,0:T(8,128)(2,1)S(1)} %get-tuple-element.209), channel_id=1, source_target_pairs={{0,4},{1,3},{2,6},{3,1},{4,0},{5,7},{6,2},{7,5},{8,12},{9,11},{10,... | collective-permute-start | bytes 983048 | tf_op jit(solution)/shard_map/ppermute | solution.py:944
  140.3 15.0 %collective-permute-start.34 = (bf16[640,128]{1,0:T(8,128)(2,1)S(1)}, bf16[640,128]{1,0:T(8,128)(2,1)S(1)}, u32[]{:S(2)}, u32[]{:S(2)}) collective-permute-start(bf16[640,128]{1,0:T(8,128)(2,1)S(1)} %mix_sum.8.k), channel_id=1, source_target_pairs={{0,16},{1,17},{2,18},{3,19},{4,20},{5,21},{6,22},{7,23},{8,24},{9,... | collective-permute-start | bytes 491528 | tf_op jit(solution)/shard_map/ppermute | solution.py:944
  143.0 13.6 %collective-permute-start.36 = (bf16[512,512]{1,0:T(8,128)(2,1)S(1)}, bf16[512,512]{1,0:T(8,128)(2,1)S(1)}, u32[]{:S(2)}, u32[]{:S(2)}) collective-permute-start(bf16[512,512]{1,0:T(8,128)(2,1)S(1)} %get-tuple-element.240), channel_id=1, source_target_pairs={{1,0},{2,1},{3,2},{4,3},{5,4},{6,5},{7,6},{9,8},{10,9},{11,10},{12... | collective-permute-start | bytes 1572872 | tf_op jit(solution)/shard_map/ppermute | solution.py:1266
  144.9 11.0 %collective-permute-start.35 = (bf16[640,128]{1,0:T(8,128)(2,1)S(1)}, bf16[640,128]{1,0:T(8,128)(2,1)S(1)}, u32[]{:S(2)}, u32[]{:S(2)}) collective-permute-start(bf16[640,128]{1,0:T(8,128)(2,1)S(1)} %get-tuple-element.221), channel_id=1, source_target_pairs={{0,8},{1,9},{2,10},{3,11},{4,12},{5,13},{6,14},{7,15},{8,0},{9,1},... | collective-permute-start | bytes 491528 | tf_op jit(solution)/shard_map/ppermute | solution.py:944
  148.2 15.2 %collective-permute-start.37 = (bf16[2,1920,128]{2,1,0:T(8,128)(2,1)S(1)}, bf16[2,1920,128]{2,1,0:T(8,128)(2,1)S(1)}, u32[]{:S(2)}, u32[]{:S(2)}) collective-permute-start(bf16[2,1920,128]{2,1,0:T(8,128)(2,1)S(1)} %get-tuple-element.228), channel_id=1, source_target_pairs={{0,2},{1,5},{2,0},{3,7},{4,6},{5,1},{6,4},{7,3},{8,10},{9,13},{10,... | collective-permute-start | bytes 2949128 | tf_op jit(solution)/shard_map/ppermute | solution.py:944
  161.0 11.9 %collective-permute-start.39 = (bf16[2,2048,128]{2,1,0:T(8,128)(2,1)S(1)}, bf16[2,2048,128]{2,1,0:T(8,128)(2,1)S(1)}, u32[]{:S(2)}, u32[]{:S(2)}) collective-permute-start(bf16[2,2048,128]{2,1,0:T(8,128)(2,1)S(1)} %get-tuple-element.256), channel_id=1, source_target_pairs={{0,1},{1,0},{2,3},{3,2},{4,5},{5,4},{6,7},{7,6},{8,9},{9,8},{10,11... | collective-permute-start | bytes 3145736 | tf_op jit(solution)/shard_map/ppermute | solution.py:944
  161.3 10.9 %collective-permute-start.38 = (bf16[640,128]{1,0:T(8,128)(2,1)S(1)}, bf16[640,128]{1,0:T(8,128)(2,1)S(1)}, u32[]{:S(2)}, u32[]{:S(2)}) collective-permute-start(bf16[640,128]{1,0:T(8,128)(2,1)S(1)} %mix_sum.10.k), channel_id=1, source_target_pairs={{0,16},{1,17},{2,18},{3,19},{4,20},{5,21},{6,22},{7,23},{8,24},{9,... | collective-permute-start | bytes 491528 | tf_op jit(solution)/shard_map/ppermute | solution.py:944
  164.2 10.6 %collective-permute-start.40 = (bf16[1920,128]{1,0:T(8,128)(2,1)S(1)}, bf16[1920,128]{1,0:T(8,128)(2,1)S(1)}, u32[]{:S(2)}, u32[]{:S(2)}) collective-permute-start(bf16[1920,128]{1,0:T(8,128)(2,1)S(1)} %get-tuple-element.251), channel_id=1, source_target_pairs={{0,4},{1,3},{2,6},{3,1},{4,0},{5,7},{6,2},{7,5},{8,12},{9,11},{10,... | collective-permute-start | bytes 1474568 | tf_op jit(solution)/shard_map/ppermute | solution.py:944
  174.0 9.2 %collective-permute-start.41 = (bf16[2,1024,128]{2,1,0:T(8,128)(2,1)S(1)}, bf16[2,1024,128]{2,1,0:T(8,128)(2,1)S(1)}, u32[]{:S(2)}, u32[]{:S(2)}) collective-permute-start(bf16[2,1024,128]{2,1,0:T(8,128)(2,1)S(1)} %get-tuple-element.260), channel_id=1, source_target_pairs={{0,2},{1,5},{2,0},{3,7},{4,6},{5,1},{6,4},{7,3},{8,10},{9,13},{10,... | collective-permute-start | bytes 1572872 | tf_op jit(solution)/shard_map/ppermute | solution.py:944
  175.5 9.4 %collective-permute-start.42 = (bf16[960,128]{1,0:T(8,128)(2,1)S(1)}, bf16[960,128]{1,0:T(8,128)(2,1)S(1)}, u32[]{:S(2)}, u32[]{:S(2)}) collective-permute-start(bf16[960,128]{1,0:T(8,128)(2,1)S(1)} %get-tuple-element.263), channel_id=1, source_target_pairs={{0,8},{1,9},{2,10},{3,11},{4,12},{5,13},{6,14},{7,15},{8,0},{9,1},... | collective-permute-start | bytes 737288 | tf_op jit(solution)/shard_map/ppermute | solution.py:944
  183.9 9.3 %collective-permute-start.43 = (bf16[1024,128]{1,0:T(8,128)(2,1)S(1)}, bf16[1024,128]{1,0:T(8,128)(2,1)S(1)}, u32[]{:S(2)}, u32[]{:S(2)}) collective-permute-start(bf16[1024,128]{1,0:T(8,128)(2,1)S(1)} %get-tuple-element.268), channel_id=1, source_target_pairs={{0,4},{1,3},{2,6},{3,1},{4,0},{5,7},{6,2},{7,5},{8,12},{9,11},{10,... | collective-permute-start | bytes 786440 | tf_op jit(solution)/shard_map/ppermute | solution.py:944
  185.5 13.0 %collective-permute-start.44 = (bf16[960,128]{1,0:T(8,128)(2,1)S(1)}, bf16[960,128]{1,0:T(8,128)(2,1)S(1)}, u32[]{:S(2)}, u32[]{:S(2)}) collective-permute-start(bf16[960,128]{1,0:T(8,128)(2,1)S(1)} %mix_sum.12.k), channel_id=1, source_target_pairs={{0,16},{1,17},{2,18},{3,19},{4,20},{5,21},{6,22},{7,23},{8,24},{9,... | collective-permute-start | bytes 737288 | tf_op jit(solution)/shard_map/ppermute | solution.py:944
  186.4 17.4 %collective-permute-start.58 = (bf16[640,128]{1,0:T(8,128)(2,1)S(1)}, bf16[640,128]{1,0:T(8,128)(2,1)S(1)}, u32[]{:S(2)}, u32[]{:S(2)}) collective-permute-start(bf16[640,128]{1,0:T(8,128)(2,1)S(1)} %mix_sum.9.refs_0_), channel_id=1, source_target_pairs={{0,12},{1,13},{2,14},{3,15},{4,8},{5,9},{6,10},{7,11},{8,4},{9,5},... | collective-permute-start | bytes 491528 | tf_op jit(solution)/shard_map/ppermute | solution.py:944
  193.9 11.7 %collective-permute-start.57 = (bf16[640,128]{1,0:T(8,128)(2,1)S(1)}, bf16[640,128]{1,0:T(8,128)(2,1)S(1)}, u32[]{:S(2)}, u32[]{:S(2)}) collective-permute-start(bf16[640,128]{1,0:T(8,128)(2,1)S(1)} %mix_sum.9.refs_0_), channel_id=1, source_target_pairs={{0,8},{1,9},{2,10},{3,11},{4,12},{5,13},{6,14},{7,15},{8,0},{9,1},... | collective-permute-start | bytes 491528 | tf_op jit(solution)/shard_map/ppermute | solution.py:944
  195.9 10.4 %collective-permute-start.56 = (bf16[640,128]{1,0:T(8,128)(2,1)S(1)}, bf16[640,128]{1,0:T(8,128)(2,1)S(1)}, u32[]{:S(2)}, u32[]{:S(2)}) collective-permute-start(bf16[640,128]{1,0:T(8,128)(2,1)S(1)} %mix_sum.9.refs_0_), channel_id=1, source_target_pairs={{0,4},{1,5},{2,6},{3,7},{4,0},{5,1},{6,2},{7,3},{8,12},{9,13},{10,... | collective-permute-start | bytes 491528 | tf_op jit(solution)/shard_map/ppermute | solution.py:944
  198.5 13.5 %collective-permute-start.52 = (bf16[640,128]{1,0:T(8,128)(2,1)S(1)}, bf16[640,128]{1,0:T(8,128)(2,1)S(1)}, u32[]{:S(2)}, u32[]{:S(2)}) collective-permute-start(bf16[640,128]{1,0:T(8,128)(2,1)S(1)} %mix_sum.11.refs_0_), channel_id=1, source_target_pairs={{0,12},{1,13},{2,14},{3,15},{4,8},{5,9},{6,10},{7,11},{8,4},{9,5},... | collective-permute-start | bytes 491528 | tf_op jit(solution)/shard_map/ppermute | solution.py:944
  201.8 10.1 %collective-permute-start.46 = (bf16[512,128]{1,0:T(8,128)(2,1)S(1)}, bf16[512,128]{1,0:T(8,128)(2,1)S(1)}, u32[]{:S(2)}, u32[]{:S(2)}) collective-permute-start(bf16[512,128]{1,0:T(8,128)(2,1)S(1)} %mix_sum.14.k), channel_id=1, source_target_pairs={{0,16},{1,17},{2,18},{3,19},{4,20},{5,21},{6,22},{7,23},{8,24},{9,... | collective-permute-start | bytes 393224 | tf_op jit(solution)/shard_map/ppermute | solution.py:944
  203.8 18.9 %collective-permute-start.55 = (bf16[960,128]{1,0:T(8,128)(2,1)S(1)}, bf16[960,128]{1,0:T(8,128)(2,1)S(1)}, u32[]{:S(2)}, u32[]{:S(2)}) collective-permute-start(bf16[960,128]{1,0:T(8,128)(2,1)S(1)} %mix_sum.13.refs_4_), channel_id=1, source_target_pairs={{0,12},{1,13},{2,14},{3,15},{4,8},{5,9},{6,10},{7,11},{8,4},{9,5},... | collective-permute-start | bytes 737288 | tf_op jit(solution)/shard_map/ppermute | solution.py:944
  205.6 13.7 %collective-permute-start.51 = (bf16[640,128]{1,0:T(8,128)(2,1)S(1)}, bf16[640,128]{1,0:T(8,128)(2,1)S(1)}, u32[]{:S(2)}, u32[]{:S(2)}) collective-permute-start(bf16[640,128]{1,0:T(8,128)(2,1)S(1)} %mix_sum.11.refs_0_), channel_id=1, source_target_pairs={{0,8},{1,9},{2,10},{3,11},{4,12},{5,13},{6,14},{7,15},{8,0},{9,1},... | collective-permute-start | bytes 491528 | tf_op jit(solution)/shard_map/ppermute | solution.py:944
  206.4 13.9 %collective-permute-start.50 = (bf16[640,128]{1,0:T(8,128)(2,1)S(1)}, bf16[640,128]{1,0:T(8,128)(2,1)S(1)}, u32[]{:S(2)}, u32[]{:S(2)}) collective-permute-start(bf16[640,128]{1,0:T(8,128)(2,1)S(1)} %mix_sum.11.refs_0_), channel_id=1, source_target_pairs={{0,4},{1,5},{2,6},{3,7},{4,0},{5,1},{6,2},{7,3},{8,12},{9,13},{10,... | collective-permute-start | bytes 491528 | tf_op jit(solution)/shard_map/ppermute | solution.py:944
  212.0 12.7 %collective-permute-start.54 = (bf16[960,128]{1,0:T(8,128)(2,1)S(1)}, bf16[960,128]{1,0:T(8,128)(2,1)S(1)}, u32[]{:S(2)}, u32[]{:S(2)}) collective-permute-start(bf16[960,128]{1,0:T(8,128)(2,1)S(1)} %mix_sum.13.refs_4_), channel_id=1, source_target_pairs={{0,8},{1,9},{2,10},{3,11},{4,12},{5,13},{6,14},{7,15},{8,0},{9,1},... | collective-permute-start | bytes 737288 | tf_op jit(solution)/shard_map/ppermute | solution.py:944
  212.0 12.7 %collective-permute-start.53 = (bf16[960,128]{1,0:T(8,128)(2,1)S(1)}, bf16[960,128]{1,0:T(8,128)(2,1)S(1)}, u32[]{:S(2)}, u32[]{:S(2)}) collective-permute-start(bf16[960,128]{1,0:T(8,128)(2,1)S(1)} %mix_sum.13.refs_4_), channel_id=1, source_target_pairs={{0,4},{1,5},{2,6},{3,7},{4,0},{5,1},{6,2},{7,3},{8,12},{9,13},{10,... | collective-permute-start | bytes 737288 | tf_op jit(solution)/shard_map/ppermute | solution.py:944
  219.4 9.5 %collective-permute-start.49 = (bf16[512,128]{1,0:T(8,128)(2,1)S(1)}, bf16[512,128]{1,0:T(8,128)(2,1)S(1)}, u32[]{:S(2)}, u32[]{:S(2)}) collective-permute-start(bf16[512,128]{1,0:T(8,128)(2,1)S(1)} %mix_sum.15.refs_0_), channel_id=1, source_target_pairs={{0,12},{1,13},{2,14},{3,15},{4,8},{5,9},{6,10},{7,11},{8,4},{9,5},... | collective-permute-start | bytes 393224 | tf_op jit(solution)/shard_map/ppermute | solution.py:944
  220.3 8.8 %collective-permute-start.48 = (bf16[512,128]{1,0:T(8,128)(2,1)S(1)}, bf16[512,128]{1,0:T(8,128)(2,1)S(1)}, u32[]{:S(2)}, u32[]{:S(2)}) collective-permute-start(bf16[512,128]{1,0:T(8,128)(2,1)S(1)} %mix_sum.15.refs_0_), channel_id=1, source_target_pairs={{0,8},{1,9},{2,10},{3,11},{4,12},{5,13},{6,14},{7,15},{8,0},{9,1},... | collective-permute-start | bytes 393224 | tf_op jit(solution)/shard_map/ppermute | solution.py:944
  (55 other events, 309.2 us)

commit v4 on v3

--- a/solution.py
+++ b/solution.py
@@ -452,63 +452,65 @@
 RB = 512
 
 
-def by_columns(me_ref, pieces, buf, sems):
-    step = pl.program_id(0)
-
+def by_columns(me_ref, pieces, buf, sems, body):
     def copies(i):
         at = pl.ds(pl.multiple_of(i * STEP, STEP), STEP)
         return place_copies(
             me_ref, pieces, lambda w: w.at[:, at], buf.at[:, at], D // 4, sems, 6 * i
         )
 
-    @pl.when(step == 0)
-    def _():
-        for i in range(FF // STEP):
-            for c in copies(i):
-                c.start()
-
-    for c in copies(step):
-        c.wait()
-    return pl.ds(pl.multiple_of(step * STEP, STEP), STEP)
+    for i in range(FF // STEP):
+        for c in copies(i):
+            c.start()
+
+    def step(i, carry):
+        for c in copies(i):
+            c.wait()
+        body(pl.ds(pl.multiple_of(i * STEP, STEP), STEP))
+        return carry
+
+    lax.fori_loop(0, FF // STEP, step, 0)
 
 
 def gate_kernel(me_ref, nm, *rest):
     pieces, (a_o, s_o, wg, sems) = rest[:6], rest[6:]
-
-    cs = by_columns(me_ref, pieces, wg, sems)
     c0 = 0.7978845608028654
     c1 = 0.044715 * c0
-    for r in range(0, nm.shape[0], RB):
-        g = dot(nm[r : r + RB, :], wg[:, cs])
-        g2 = g * g
-        t = jnp.tanh(g * (c0 + c1 * g2))
-        h = 0.5 + 0.5 * t
-        a = g * h
-        slope = h + a * (1.0 - h) * (2.0 * c0 + (6.0 * c1) * g2)
-        a_o[r : r + RB, :] = a.astype(BF16)
-        s_o[r : r + RB, :] = slope.astype(BF16)
+
+    def body(cs):
+        for r in range(0, nm.shape[0], RB):
+            rs = slice(r, r + RB)
+            g = dot(nm[rs, :], wg[:, cs]).astype(BF16)
+            g2 = g * g
+            t = jnp.tanh(g * (c0 + c1 * g2))
+            h = 0.5 + 0.5 * t
+            a = g * h
+            a_o[rs, cs] = a
+            s_o[rs, cs] = h + a * (1.0 - h) * (2.0 * c0 + (6.0 * c1) * g2)
+
+    by_columns(me_ref, pieces, wg, sems, body)
 
 
 def up_kernel(me_ref, nm, a_i, s_i, *rest):
     pieces, (hid_o, b_o, wu, sems) = rest[:6], rest[6:]
 
-    cs = by_columns(me_ref, pieces, wu, sems)
-    for r in range(0, nm.shape[0], RB):
-        rs = slice(r, r + RB)
-        u = dot(nm[rs, :], wu[:, cs])
-        hid_o[rs, :] = (a_i[rs, :].astype(F32) * u).astype(BF16)
-        b_o[rs, :] = (u * s_i[rs, :].astype(F32)).astype(BF16)
+    def body(cs):
+        for r in range(0, nm.shape[0], RB):
+            rs = slice(r, r + RB)
+            u = dot(nm[rs, :], wu[:, cs]).astype(BF16)
+            hid_o[rs, cs] = a_i[rs, cs] * u
+            b_o[rs, cs] = u * s_i[rs, cs]
+
+    by_columns(me_ref, pieces, wu, sems, body)
 
 
 def ff(me, nm, pieces, before=()):
     t = nm.shape[0]
-    col = pl.BlockSpec((t, STEP), lambda i: (0, i))
     return pl.pallas_call(
         up_kernel if before else gate_kernel,
-        grid=(FF // STEP,),
         out_shape=(sds((t, FF)),) * 2,
-        in_specs=[SM, VM] + [col] * len(before) + [HM] * 6,
-        out_specs=(col,) * 2,
+        in_specs=[SM, VM] + [VM] * len(before) + [HM] * 6,
+        out_specs=(VM,) * 2,
         scratch_shapes=[pltpu.VMEM((D, FF), BF16), pltpu.SemaphoreType.DMA((6 * FF // STEP,))],
         compiler_params=params(),
         cost_estimate=cost(2 * t * D * FF, 12e6),
@@ -580,41 +582,37 @@
         copies += place_copies(
             me_ref, pieces, lambda w: w.at[:, pl.ds(FH * half, FH)], buf, D // 4, sems, 6 * k
         )
-
-    @pl.when(pl.program_id(0) == 0)
-    def _():
-        for c in copies:
-            c.start()
-
-    cs = pl.ds(pl.multiple_of(pl.program_id(0) * WIDE, WIDE), WIDE)
-    dh = dot(dd[...], wd[...], NT)
-    dg = (dh * b_i[...].astype(F32)).astype(BF16)
-    du = (dh * a_i[...].astype(F32)).astype(BF16)
+    for c in copies:
+        c.start()
     gr = D // 4
-    for k, d in enumerate((dg, du)):
-        gs[k] = dot(nm[...], d, TN).astype(BF16)
-        for y in range(2):
-            for part, o in ((core, keep_o), (1 - core, send_o)):
-                at = pl.ds(pl.multiple_of((2 * y + part) * gr, gr), gr)
-                for j in range(WIDE // 128):
-                    o[y, k, j] = gs[k, at, 128 * j : 128 * (j + 1)]
-
-    @pl.when(pl.program_id(0) == 0)
-    def _():
-        for c in copies:
-            c.wait()
-        if first:
-            dnm_o[...] = jnp.zeros_like(dnm_o)
+    for i in range(FH // WIDE):
+        cs = slice(WIDE * i, WIDE * (i + 1))
+        at = slice(FH * half + WIDE * i, FH * half + WIDE * (i + 1))
+        dh = dot(dd[...], wd[at, :], NT).astype(BF16)
+        dg = dh * b_i[:, at]
+        du = dh * a_i[:, at]
+        for k, d in enumerate((dg, du)):
+            gs[k] = dot(nm[...], d, TN).astype(BF16)
+            for y in range(2):
+                for part, o in ((core, keep_o), (1 - core, send_o)):
+                    rows = pl.ds(pl.multiple_of((2 * y + part) * gr, gr), gr)
+                    for j in range(WIDE // 128):
+                        to = WIDE // 128 * i + j
+                        o[y, k, to] = gs[k, rows, 128 * j : 128 * (j + 1)]
+        if i == 0:
+            for c in copies:
+                c.wait()
+        back = dot(dg, wg[:, cs], NT) + dot(du, wu[:, cs], NT)
+        if i > 0:
+            dnm_o[...] += back
+        elif first:
+            dnm_o[...] = back
         else:
-            dnm_o[...] = dnm_i[...]
-
-    dnm_o[...] += dot(dg, wg[:, cs], NT) + dot(du, wu[:, cs], NT)
+            dnm_o[...] = dnm_i[...] + back
 
 
 def fb(me, nm, dd, a, b, wd, gates, ups, part, dnm):
     t = nm.shape[0]
-    steps = FH // WIDE
-    col = pl.BlockSpec((t, WIDE), lambda i: (0, i + steps * part))
     extra = () if dnm is None else (dnm,)
 
     def body(*refs):
@@ -622,20 +620,16 @@
 
     return pl.pallas_call(
         body,
-        grid=(steps,),
         out_shape=(sds((2, 2, FH // 128, D // 4, 128)),) * 2 + (sds((t, D), F32),),
-        in_specs=[SM, VM, VM, col, col, pl.BlockSpec((WIDE, D), lambda i: (i + steps * part, 0))]
-        + [HM] * 12
-        + [VM] * len(extra),
-        out_specs=(pl.BlockSpec((2, 2, WIDE // 128, D // 4, 128), lambda i: (0, 0, i, 0, 0)),) * 2
-        + (VM,),
+        in_specs=[SM] + [VM] * 5 + [HM] * 12 + [VM] * len(extra),
+        out_specs=(VM,) * 3,
         scratch_shapes=[
             pltpu.VMEM((D, FH), BF16),
             pltpu.VMEM((D, FH), BF16),
             pltpu.VMEM((2, D, WIDE), BF16),
             pltpu.SemaphoreType.DMA((12,)),
         ],
-        compiler_params=params(20),
+        compiler_params=params(16),
         cost_estimate=cost(10 * t * D * FH, 16e6),
         name="fb",
     )(me, nm, dd, a, b, wd, *gates, *ups, *extra)

time: 237 us -> 233 us (0.983)
  Pallas kernels: 128 us -> 122 us
    pallas_call x4, Pallas kernels: 41.9 us -> 36.3 us  [the longest x2 22.4 us: fb(): pl.pallas_call(body, out_shape=(sds((2, 2, FH // 128, D // 4, 128)),) * 2...]
    unnamed x88 -> x80, local copies, waits for them, and re-layouts: 4.2 us -> 5.19 us
  transfers between devices with their start and end apart: 59 -> 59, of which waited for: 16 -> 18; matrix products, arithmetic and copies ran while one was open for 1% -> 1% of each run, Pallas kernels for 49% -> 48%
where the time goes in v4:
time: 233 us; the launch traced here: 228 us
  Pallas kernels  122 us (52%)
  starting transfers between devices  56.9 us (24%)
  waiting for transfers between devices  38.7 us (17%)
  local copies, waits for them, and re-layouts  6.93 us (3%)
    ppermute x33, starting transfers between devices, send(): return lax.ppermute(x, ('seq', 'shard'), pairs)  32.8 us
    ppermute x33, waiting for transfers between devices, send(): return lax.ppermute(x, ('seq', 'shard'), pairs)  31.1 us
    pallas_call x2, Pallas kernels, fb(): pl.pallas_call(body, out_shape=(sds((2, 2, FH // 128, D // 4, 128)),) * 2...  22.4 us
    ppermute x24, starting transfers between devices, flip(): return lax.ppermute(x, axis, [(i, i ^ bit) for i in range(n)])  20 us
    pallas_call x20, Pallas kernels, small_call(): pl.pallas_call(body, out_shape=tuple((sds(r + (128,)) for r in out_rows))...  15.4 us
    pallas_call x2, Pallas kernels, ff(): pl.pallas_call(up_kernel if before else gate_kernel, out_shape=(sds((t, F...  13.9 us
    pallas_call x2, Pallas kernels, att_back(): pl.pallas_call(att_back_kernel, grid=(1,), out_shape=(sds((HALF, HEADS *...  11.3 us
    pallas_call x1, Pallas kernels, down_part(): pl.pallas_call(down_kernel, out_shape=(sds((t, D)), sds((t, D)), sds((FF,...  10.2 us
  transfers between devices with their start and end apart: 59, of which 18 were waited for; matrix products, arithmetic and copies ran while one was open for 1% of the time, Pallas kernels for 48%

profile of v4, /device:TPU:0, one launch (start us, length us, event | category | flops | bytes accessed | tf_op | source)
XLA Modules:
  0.0 228.4 jit_solution(1261340250847646059)
XLA Ops:
  0.8 1.6 pack.1.g0.w0.k0
  2.3 3.0 %collective-permute-start.1 = (bf16[176,512]{1,0:T(8,128)(2,1)S(1)}, bf16[176,512]{1,0:T(8,128)(2,1)S(1)}, u32[]{:S(2)}, u32[]{:S(2)}) collective-permute-start(bf16[176,512]{1,0:T(8,128)(2,1)S(1)} %pack.1.g0.w0.k0), channel_id=1, source_target_pairs={{0,2},{1,3},{2,0},{3,1},{4,6},{5,7},{6,4},{7,5},{8,10},{9,11},{10,... | collective-permute-start | bytes 540680 | tf_op jit(solution)/shard_map/ppermute | solution.py:827
  5.9 1.7 halves.1
  7.6 1.8 collective-permute-start.7
  10.8 1.9 multiply_sine_fusion
  13.6 3.2 %pre_kv.1 = (bf16[1024,640]{1,0:T(8,128)(2,1)S(1)}, bf16[1024,256]{1,0:T(8,128)(2,1)S(1)}, bf16[512,512]{1,0:T(8,128)(2,1)S(1)}, bf16[512,512]{1,0:T(8,128)(2,1)S(1)}) custom-call(s32[9]{0:T(128)S(1)} %stack.43.info.me_ref.refs_0_.s.i, bf16[1024,640]{1,0:T(8,128)(2,1)S(1)} %copy-done, f32[8,640]{1,0:T(8,128)S(1)} %gains.1, ...), custom_call_target="tpu_custom_call" | custom-call | flops 671088640 | bytes 5000000 | tf_op jit(solution)/shard_map/pre_kv/pallas_call | solution.py:237
  17.8 2.1 collective-permute-start.6
  19.9 2.4 %collective-permute-start.8 = (bf16[512,512]{1,0:T(8,128)(2,1)S(1)}, bf16[512,512]{1,0:T(8,128)(2,1)S(1)}, u32[]{:S(2)}, u32[]{:S(2)}) collective-permute-start(bf16[512,512]{1,0:T(8,128)(2,1)S(1)} %get-tuple-element.158.refs_3_.kvs), channel_id=1, source_target_pairs={{0,1},{1,2},{2,3},{3,4},{4,5},{5,6},{6,7},{8,9},{9,10},{10,11},{11... | collective-permute-start | bytes 1572872 | tf_op jit(solution)/shard_map/ppermute | solution.py:1203
  22.3 2.5 %collective-permute-done.7.rest_2_.refs_8_ = bf16[80,2048]{1,0:T(8,128)(2,1)S(1)} collective-permute-done((bf16[80,2048]{1,0:T(8,128)(2,1)S(1)}, bf16[80,2048]{1,0:T(8,128)(2,1)S(1)}, u32[]{:S(2)}, u32[]{:S(2)}) %collective-permute-start.7) | collective-permute-done | bytes 327712 | tf_op jit(solution)/shard_map/ppermute | solution.py:827
  25.4 2.1 collective-permute-start.16
  27.4 5.9 %pre_q.1 = (bf16[4,1024,256]{2,1,0:T(8,128)(2,1)}, bf16[4,1024,256]{2,1,0:T(8,128)(2,1)S(1)}) custom-call(s32[9]{0:T(128)S(1)} %stack.43.info.me_ref.refs_0_.s.i, bf16[1024,640]{1,0:T(8,128)(2,1)S(1)} %get-tuple-element.152.nin_i.nin, f32[8,640]{1,0:T(8,128)S(1)} %gains.1, f32[1024,128]{1,0:T(8,128)S(1)} %get-tuple-element.295.cos_ref, ...), custom_call_target="tpu_custom_call" | custom-call | flops 1342177280 | bytes 5000000 | tf_op jit(solution)/shard_map/pre_q/pallas_call | solution.py:279
  33.4 6.1 %collective-permute-start.12 = (bf16[80,2048]{1,0:T(8,128)(2,1)S(1)}, bf16[80,2048]{1,0:T(8,128)(2,1)S(1)}, u32[]{:S(2)}, u32[]{:S(2)}) collective-permute-start(bf16[80,2048]{1,0:T(8,128)(2,1)S(1)} %collective-permute-done.7.rest_2_.refs_8_), channel_id=1, source_target_pairs={{0,4},{4,0},{8,12},{12,8},{16,20},{20,16},{24,28},{28,24},{1,5},{5... | collective-permute-start | bytes 983048 | tf_op jit(solution)/shard_map/ppermute | solution.py:827
  39.5 3.2 %att.2 = (bf16[512,1024]{1,0:T(8,128)(2,1)S(1)}, bf16[4,512,256]{2,1,0:T(8,128)(2,1)S(1)}, bf16[4,512,256]{2,1,0:T(8,128)(2,1)S(1)}) custom-call(s32[9]{0:T(128)S(1)} %stack.43.info.me_ref.refs_0_.s.i, bf16[4,1024,256]{2,1,0:T(8,128)(2,1)S(1)} %get-tuple-element.160.refs_1_.qs, bf16[512,512]{1,0:T(8,128)(2,1)S(1)} %get-tuple-element.157.refs_2_.refs_3_.kvs.kvp, ...), custom_call_target="tpu_custom_call" | custom-call | flops 3000000000 | bytes 5000000 | tf_op jit(solution)/shard_map/att/pallas_call | solution.py:338
  43.7 3.3 %att.3 = (bf16[512,1024]{1,0:T(8,128)(2,1)S(1)}, bf16[4,512,256]{2,1,0:T(8,128)(2,1)S(1)}, bf16[4,512,256]{2,1,0:T(8,128)(2,1)S(1)}) custom-call(s32[9]{0:T(128)S(1)} %stack.43.info.me_ref.refs_0_.s.i, bf16[4,1024,256]{2,1,0:T(8,128)(2,1)S(1)} %get-tuple-element.160.refs_1_.qs, bf16[512,512]{1,0:T(8,128)(2,1)S(1)} %collective-permute-done.8.refs_2_.kvp, ...), custom_call_target="tpu_custom_call" | custom-call | flops 3000000000 | bytes 5000000 | tf_op jit(solution)/shard_map/att/pallas_call | solution.py:338
  49.9 4.3 %mid.1 = (bf16[1024,640]{1,0:T(8,128)(2,1)S(1)}, bf16[1024,640]{1,0:T(8,128)(2,1)S(1)}) custom-call(s32[9]{0:T(128)S(1)} %stack.43.info.me_ref.refs_0_.s.i, bf16[512,1024]{1,0:T(8,128)(2,1)S(1)} %get-tuple-element.161.o_lo, bf16[512,1024]{1,0:T(8,128)(2,1)S(1)} %get-tuple-element.159.o_hi, bf16[1024,640]{1,0:T(8,128)(2,1)S(1)} %copy-done, ...), custom_call_target="tpu_custom_call" | custom-call | flops 1342177280 | bytes 8000000 | tf_op jit(solution)/shard_map/mid/pallas_call | solution.py:434
  55.3 7.3 %gate.1 = (bf16[1024,2048]{1,0:T(8,128)(2,1)S(1)}, bf16[1024,2048]{1,0:T(8,128)(2,1)S(1)}) custom-call(s32[9]{0:T(128)S(1)} %stack.43.info.me_ref.refs_0_.s.i, bf16[1024,640]{1,0:T(8,128)(2,1)S(1)} %get-tuple-element.162.nm.refs_1_, bf16[160,2048]{1,0:T(8,128)(2,1)} %refs_6_.4, bf16[160,2048]{1,0:T(8,128)(2,1)} %copy-done.30, bf16[80,2048]{1,0:T(8,128)(2,1)} %copy-done.32, ...), custom_call_target="tpu_custom_call" | custom-call | flops 2684354560 | bytes 12000000 | tf_op jit(solution)/shard_map/gate/pallas_call | solution.py:509
  67.1 6.6 %up.1 = (bf16[1024,2048]{1,0:T(8,128)(2,1)S(1)}, bf16[1024,2048]{1,0:T(8,128)(2,1)S(1)}) custom-call(s32[9]{0:T(128)S(1)} %stack.43.info.me_ref.refs_0_.s.i, bf16[1024,640]{1,0:T(8,128)(2,1)S(1)} %get-tuple-element.162.nm.refs_1_, bf16[1024,2048]{1,0:T(8,128)(2,1)S(1)} %get-tuple-element.164.a_i.refs_3_, bf16[1024,2048]{1,0:T(8,128)(2,1)S(1)} %get-tuple-element.165.s_i, ...), custom_call_target="tpu_custom_call" | custom-call | flops 2684354560 | bytes 12000000 | tf_op jit(solution)/shard_map/up/pallas_call | solution.py:509
  74.0 1.4 collective-permute-done.24.rest_5_
  76.1 10.2 %down.1 = (bf16[1024,640]{1,0:T(8,128)(2,1)}, bf16[1024,640]{1,0:T(8,128)(2,1)S(1)}, bf16[2048,640]{1,0:T(8,128)(2,1)S(1)}, bf16[2,5,512,128]{3,2,1,0:T(8,128)(2...) custom-call(s32[9]{0:T(128)S(1)} %stack.43.info.me_ref.refs_0_.s.i, ...), custom_call_target="tpu_custom_call" | custom-call | flops 5368709120 | bytes 20000000 | tf_op jit(solution)/shard_map/down/pallas_call | solution.py:552
  86.6 11.2 %fb.2 = (bf16[2,2,8,160,128]{4,3,2,1,0:T(8,128)(2,1)S(1)}, bf16[2,2,8,160,128]{4,3,2,1,0:T(8,128)(2,1)S(1)}, f32[1024,640]{1,0:T(8,128)S(1)}) custom-call(s32[9]{0:T(128)S(1)} %stack.43.info.me_ref.refs_0_.s.i, bf16[1024,640]{1,0:T(8,128)(2,1)S(1)} %get-tuple-element.162.nm.refs_1_, bf16[1024,640]{1,0:T(8,128)(2,1)S(1)} %get-tuple-element.177.refs_2_, ...), custom_call_target="tpu_custom_call" | custom-call | flops 6710886400 | bytes 16000000 | tf_op jit(solution)/shard_map/fb/pallas_call | solution.py:621
  100.5 11.2 %fb.3 = (bf16[2,2,8,160,128]{4,3,2,1,0:T(8,128)(2,1)S(1)}, bf16[2,2,8,160,128]{4,3,2,1,0:T(8,128)(2,1)S(1)}, f32[1024,640]{1,0:T(8,128)S(1)}) custom-call(s32[9]{0:T(128)S(1)} %stack.43.info.me_ref.refs_0_.s.i, bf16[1024,640]{1,0:T(8,128)(2,1)S(1)} %get-tuple-element.162.nm.refs_1_, bf16[1024,640]{1,0:T(8,128)(2,1)S(1)} %get-tuple-element.177.refs_2_, ...), custom_call_target="tpu_custom_call" | custom-call | flops 6710886400 | bytes 16000000 | tf_op jit(solution)/shard_map/fb/pallas_call | solution.py:621
  116.2 8.2 %fe.1 = (bf16[2,5,256,128]{3,2,1,0:T(8,128)(2,1)S(1)}, bf16[2,5,256,128]{3,2,1,0:T(8,128)(2,1)S(1)}, bf16[4,1024,256]{2,1,0:T(8,128)(2,1)S(1)}, bf16[1024,640]{1,0:T(8,128)(2,1)S(1)}, f32[16,640]{1,0:T(8,128)S(1)}) custom-call(s32[9]{0:T(128)S(1)} %stack.43.info.me_ref.refs_0_.s.i, bf16[512,1024]{1,0:T(8,128)(2,1)S(1)} %get-tuple-element.161.o_lo, ...), custom_call_target="tpu_custom_call" | custom-call | flops 2684354560 | bytes 14000000 | tf_op jit(solution)/shard_map/fe/pallas_call | solution.py:676
  126.3 1.6 collective-permute-start.30
  130.0 5.6 %att_back.2 = (bf16[512,1024]{1,0:T(8,128)(2,1)S(1)}, bf16[512,512]{1,0:T(8,128)(2,1)S(1)}, f32[512,512]{1,0:T(8,128)S(1)}, f32[8,256]{1,0:T(8,128)S(1)}) custom-call(bf16[4,1024,256]{2,1,0:T(8,128)(2,1)S(1)} %get-tuple-element.160.refs_1_.qs, bf16[4,1024,256]{2,1,0:T(8,128)(2,1)S(1)} %copy-done.10, bf16[512,512]{1,0:T(8,128)(2,1)S(1)} %collective-permute-done.8.refs_2_.kvp, ...), custom_call_target="tpu_custom_call" | custom-call | flops 6000000000 | bytes 9000000 | tf_op jit(solution)/shard_map/att_back/pallas_call | solution.py:399
  136.3 2.7 %collective-permute-start.34 = (bf16[640,128]{1,0:T(8,128)(2,1)S(1)}, bf16[640,128]{1,0:T(8,128)(2,1)S(1)}, u32[]{:S(2)}, u32[]{:S(2)}) collective-permute-start(bf16[640,128]{1,0:T(8,128)(2,1)S(1)} %mix_sum.8.k), channel_id=1, source_target_pairs={{0,16},{1,17},{2,18},{3,19},{4,20},{5,21},{6,22},{7,23},{8,24},{9,... | collective-permute-start | bytes 491528 | tf_op jit(solution)/shard_map/ppermute | solution.py:938
  138.9 1.7 collective-permute-start.36
  141.3 1.6 collective-permute-start.35
  142.9 1.6 mix_first.6
  144.5 1.8 collective-permute-start.37
  146.3 5.6 %att_back.3 = (bf16[512,1024]{1,0:T(8,128)(2,1)S(1)}, bf16[512,512]{1,0:T(8,128)(2,1)S(1)}, f32[512,512]{1,0:T(8,128)S(1)}, f32[8,256]{1,0:T(8,128)S(1)}) custom-call(bf16[4,1024,256]{2,1,0:T(8,128)(2,1)S(1)} %get-tuple-element.160.refs_1_.qs, bf16[4,1024,256]{2,1,0:T(8,128)(2,1)S(1)} %copy-done.10, ...), custom_call_target="tpu_custom_call" | custom-call | flops 6000000000 | bytes 9000000 | tf_op jit(solution)/shard_map/att_back/pallas_call | solution.py:399
  153.2 4.4 %post.1 = (bf16[1024,512]{1,0:T(8,128)(2,1)S(1)}, bf16[2,2048,128]{2,1,0:T(8,128)(2,1)S(1)}, bf16[2,2048,128]{2,1,0:T(8,128)(2,1)S(1)}) custom-call(s32[9]{0:T(128)S(1)} %stack.43.info.me_ref.refs_0_.s.i, bf16[1024,640]{1,0:T(8,128)(2,1)S(1)} %get-tuple-element.152.nin_i.nin, bf16[512,1024]{1,0:T(8,128)(2,1)S(1)} %get-tuple-element.211.dq_lo, ...), custom_call_target="tpu_custom_call" | custom-call | flops 2000000000 | bytes 10000000 | tf_op jit(solution)/shard_map/post/pallas_call | solution.py:768
  158.0 1.6 collective-permute-done.37.g
  161.2 6.8 %last.1 = bf16[1024,640]{1,0:T(8,128)(2,1)} custom-call(s32[9]{0:T(128)S(1)} %stack.43.info.me_ref.refs_0_.s.i, bf16[1024,640]{1,0:T(8,128)(2,1)S(1)} %copy-done, bf16[1024,640]{1,0:T(8,128)(2,1)S(1)} %get-tuple-element.197.dmid, bf16[512,1024]{1,0:T(8,128)(2,1)S(1)} %get-tuple-element.211.dq_lo, bf16[512,1024]{1,0:T(8,128)(2,1)S(1)} %get-tuple-element.236.dq_hi, ...), custom_call_target="tpu_custom_call" | custom-call | flops 2000000000 | bytes 8000000 | tf_op jit(solution)/shard_map/last/pallas_call | solution.py:809
  171.3 1.4 collective-permute-start.42
  172.8 6.7 %collective-permute-done.41.g = bf16[2,1024,128]{2,1,0:T(8,128)(2,1)S(1)} collective-permute-done((bf16[2,1024,128]{2,1,0:T(8,128)(2,1)S(1)}, bf16[2,1024,128]{2,1,0:T(8,128)(2,1)S(1)}, u32[]{:S(2)}, u32[]{:S(2)}) %collective-permute-start.41) | collective-permute-done | bytes 524320 | tf_op jit(solution)/shard_map/ppermute | solution.py:938
  183.8 5.3 %collective-permute-done.43 = bf16[1024,128]{1,0:T(8,128)(2,1)S(1)} collective-permute-done((bf16[1024,128]{1,0:T(8,128)(2,1)S(1)}, bf16[1024,128]{1,0:T(8,128)(2,1)S(1)}, u32[]{:S(2)}, u32[]{:S(2)}) %collective-permute-start.43) | collective-permute-done | bytes 262176 | tf_op jit(solution)/shard_map/ppermute | solution.py:938
  189.8 2.0 collective-permute-start.57
  191.8 2.1 collective-permute-start.56
  194.9 2.1 collective-permute-done.45.g
  197.6 2.3 %collective-permute-start.46 = (bf16[512,128]{1,0:T(8,128)(2,1)S(1)}, bf16[512,128]{1,0:T(8,128)(2,1)S(1)}, u32[]{:S(2)}, u32[]{:S(2)}) collective-permute-start(bf16[512,128]{1,0:T(8,128)(2,1)S(1)} %mix_sum.14.k), channel_id=1, source_target_pairs={{0,16},{1,17},{2,18},{3,19},{4,20},{5,21},{6,22},{7,23},{8,24},{9,... | collective-permute-start | bytes 393224 | tf_op jit(solution)/shard_map/ppermute | solution.py:938
  200.0 1.6 collective-permute-start.55
  203.4 4.4 %collective-permute-done.52.refs_3_ = bf16[640,128]{1,0:T(8,128)(2,1)S(1)} collective-permute-done((bf16[640,128]{1,0:T(8,128)(2,1)S(1)}, bf16[640,128]{1,0:T(8,128)(2,1)S(1)}, u32[]{:S(2)}, u32[]{:S(2)}) %collective-permute-start.52) | collective-permute-done | bytes 163872 | tf_op jit(solution)/shard_map/ppermute | solution.py:938
  208.5 6.6 %collective-permute-done.51.refs_2_ = bf16[640,128]{1,0:T(8,128)(2,1)S(1)} collective-permute-done((bf16[640,128]{1,0:T(8,128)(2,1)S(1)}, bf16[640,128]{1,0:T(8,128)(2,1)S(1)}, u32[]{:S(2)}, u32[]{:S(2)}) %collective-permute-start.51) | collective-permute-done | bytes 163872 | tf_op jit(solution)/shard_map/ppermute | solution.py:938
  216.2 2.5 %collective-permute-start.48 = (bf16[512,128]{1,0:T(8,128)(2,1)S(1)}, bf16[512,128]{1,0:T(8,128)(2,1)S(1)}, u32[]{:S(2)}, u32[]{:S(2)}) collective-permute-start(bf16[512,128]{1,0:T(8,128)(2,1)S(1)} %mix_sum.15.refs_0_), channel_id=1, source_target_pairs={{0,8},{1,9},{2,10},{3,11},{4,12},{5,13},{6,14},{7,15},{8,0},{9,1},... | collective-permute-start | bytes 393224 | tf_op jit(solution)/shard_map/ppermute | solution.py:938
  218.6 1.7 finish_one.1
  220.4 2.5 %finish_two.1 = (f32[160,2048]{1,0:T(8,128)}, f32[160,2048]{1,0:T(8,128)}, f32[256,640]{1,0:T(8,128)}) custom-call(s32[9]{0:T(128)S(1)} %stack.43.info.me_ref.refs_0_.s.i, bf16[640,128]{1,0:T(8,128)(2,1)S(1)} %mix_sum.11.refs_0_, bf16[640,128]{1,0:T(8,128)(2,1)S(1)} %collective-permute-done.50.refs_1_, bf16[640,128]{1,0:T(8,128)(2,1)S(1)} %collective-permute-done.51.refs_2_, ...), custom_call_target="tpu_custom_call" | custom-call | flops 10000000 | bytes 10000000 | tf_op jit(solution)/shard_map/finish_two/pallas_call | solution.py:1074
  222.9 1.8 collective-permute-done.49.refs_3_
  225.0 1.6 finish_three.1
  (198 shorter events, 45.8 us)
Async XLA Ops:
  2.3 8.4 %collective-permute-start.1 = (bf16[176,512]{1,0:T(8,128)(2,1)S(1)}, bf16[176,512]{1,0:T(8,128)(2,1)S(1)}, u32[]{:S(2)}, u32[]{:S(2)}) collective-permute-start(bf16[176,512]{1,0:T(8,128)(2,1)S(1)} %pack.1.g0.w0.k0), channel_id=1, source_target_pairs={{0,2},{1,3},{2,0},{3,1},{4,6},{5,7},{6,4},{7,5},{8,10},{9,11},{10,... | collective-permute-start | bytes 540680 | tf_op jit(solution)/shard_map/ppermute | solution.py:827
  5.4 12.4 %collective-permute-start.4 = (bf16[160,1024]{1,0:T(8,128)(2,1)}, bf16[160,1024]{1,0:T(8,128)(2,1)S(1)}, u32[]{:S(2)}, u32[]{:S(2)}) collective-permute-start(bf16[160,1024]{1,0:T(8,128)(2,1)} %refs_4_.1), channel_id=1, source_target_pairs={{0,2},{1,3},{2,0},{3,1},{4,6},{5,7},{6,4},{7,5},{8,10},{9,11},{10,... | collective-permute-start | bytes 983048 | tf_op jit(solution)/shard_map/ppermute | solution.py:827
  5.5 19.3 %collective-permute-start.3 = (bf16[160,1024]{1,0:T(8,128)(2,1)}, bf16[160,1024]{1,0:T(8,128)(2,1)S(1)}, u32[]{:S(2)}, u32[]{:S(2)}) collective-permute-start(bf16[160,1024]{1,0:T(8,128)(2,1)} %refs_4_.1), channel_id=1, source_target_pairs={{0,1},{1,0},{2,3},{3,2},{4,5},{5,4},{6,7},{7,6},{8,9},{9,8},{10,11... | collective-permute-start | bytes 983048 | tf_op jit(solution)/shard_map/ppermute | solution.py:827
  7.6 17.1 %collective-permute-start.7 = (bf16[80,2048]{1,0:T(8,128)(2,1)S(1)}, bf16[80,2048]{1,0:T(8,128)(2,1)S(1)}, u32[]{:S(2)}, u32[]{:S(2)}) collective-permute-start(bf16[80,2048]{1,0:T(8,128)(2,1)S(1)} %get-tuple-element.155), channel_id=1, source_target_pairs={{0,2},{1,3},{2,0},{3,1},{4,6},{5,7},{6,4},{7,5},{8,10},{9,11},{10,... | collective-permute-start | bytes 983048 | tf_op jit(solution)/shard_map/ppermute | solution.py:827
  17.8 15.6 %collective-permute-start.6 = (bf16[256,640]{1,0:T(8,128)(2,1)S(1)}, bf16[256,640]{1,0:T(8,128)(2,1)S(1)}, u32[]{:S(2)}, u32[]{:S(2)}) collective-permute-start(bf16[256,640]{1,0:T(8,128)(2,1)S(1)} %copy-done.19), channel_id=1, source_target_pairs={{0,2},{1,3},{2,0},{3,1},{4,6},{5,7},{6,4},{7,5},{8,10},{9,11},{10,... | collective-permute-start | bytes 983048 | tf_op jit(solution)/shard_map/ppermute | solution.py:827
  19.9 23.8 %collective-permute-start.8 = (bf16[512,512]{1,0:T(8,128)(2,1)S(1)}, bf16[512,512]{1,0:T(8,128)(2,1)S(1)}, u32[]{:S(2)}, u32[]{:S(2)}) collective-permute-start(bf16[512,512]{1,0:T(8,128)(2,1)S(1)} %get-tuple-element.158.refs_3_.kvs), channel_id=1, source_target_pairs={{0,1},{1,2},{2,3},{3,4},{4,5},{5,6},{6,7},{8,9},{9,10},{10,11},{11... | collective-permute-start | bytes 1572872 | tf_op jit(solution)/shard_map/ppermute | solution.py:1203
  24.8 23.9 %collective-permute-start.9 = (bf16[256,640]{1,0:T(8,128)(2,1)S(1)}, bf16[256,640]{1,0:T(8,128)(2,1)S(1)}, u32[]{:S(2)}, u32[]{:S(2)}) collective-permute-start(bf16[256,640]{1,0:T(8,128)(2,1)S(1)} %copy-done.19), channel_id=1, source_target_pairs={{0,1},{1,0},{2,3},{3,2},{4,5},{5,4},{6,7},{7,6},{8,9},{9,8},{10,11... | collective-permute-start | bytes 983048 | tf_op jit(solution)/shard_map/ppermute | solution.py:827
  24.8 29.4 %collective-permute-start.11 = (bf16[160,2048]{1,0:T(8,128)(2,1)S(1)}, bf16[160,2048]{1,0:T(8,128)(2,1)S(1)}, u32[]{:S(2)}, u32[]{:S(2)}) collective-permute-start(bf16[160,2048]{1,0:T(8,128)(2,1)S(1)} %copy-done.18), channel_id=1, source_target_pairs={{0,1},{1,0},{2,3},{3,2},{4,5},{5,4},{6,7},{7,6},{8,9},{9,8},{10,11... | collective-permute-start | bytes 1966088 | tf_op jit(solution)/shard_map/ppermute | solution.py:827
  25.4 23.2 %collective-permute-start.16 = (bf16[80,2048]{1,0:T(8,128)(2,1)S(1)}, bf16[80,2048]{1,0:T(8,128)(2,1)S(1)}, u32[]{:S(2)}, u32[]{:S(2)}) collective-permute-start(bf16[80,2048]{1,0:T(8,128)(2,1)S(1)} %get-tuple-element.167), channel_id=1, source_target_pairs={{0,2},{1,3},{2,0},{3,1},{4,6},{5,7},{6,4},{7,5},{8,10},{9,11},{10,... | collective-permute-start | bytes 983048 | tf_op jit(solution)/shard_map/ppermute | solution.py:827
  33.4 14.6 %collective-permute-start.12 = (bf16[80,2048]{1,0:T(8,128)(2,1)S(1)}, bf16[80,2048]{1,0:T(8,128)(2,1)S(1)}, u32[]{:S(2)}, u32[]{:S(2)}) collective-permute-start(bf16[80,2048]{1,0:T(8,128)(2,1)S(1)} %collective-permute-done.7.rest_2_.refs_8_), channel_id=1, source_target_pairs={{0,4},{4,0},{8,12},{12,8},{16,20},{20,16},{24,28},{28,24},{1,5},{5... | collective-permute-start | bytes 983048 | tf_op jit(solution)/shard_map/ppermute | solution.py:827
  48.7 17.0 %collective-permute-start.15 = (bf16[160,2048]{1,0:T(8,128)(2,1)S(1)}, bf16[160,2048]{1,0:T(8,128)(2,1)S(1)}, u32[]{:S(2)}, u32[]{:S(2)}) collective-permute-start(bf16[160,2048]{1,0:T(8,128)(2,1)S(1)} %copy-done.15), channel_id=1, source_target_pairs={{0,1},{1,0},{2,3},{3,2},{4,5},{5,4},{6,7},{7,6},{8,9},{9,8},{10,11... | collective-permute-start | bytes 1966088 | tf_op jit(solution)/shard_map/ppermute | solution.py:827
  49.2 13.4 %collective-permute-start.17 = (bf16[80,2048]{1,0:T(8,128)(2,1)S(1)}, bf16[80,2048]{1,0:T(8,128)(2,1)S(1)}, u32[]{:S(2)}, u32[]{:S(2)}) collective-permute-start(bf16[80,2048]{1,0:T(8,128)(2,1)S(1)} %collective-permute-done.16.rest_2_.refs_14_), channel_id=1, source_target_pairs={{0,4},{4,0},{8,12},{12,8},{16,20},{20,16},{24,28},{28,24},{1,5},{5... | collective-permute-start | bytes 983048 | tf_op jit(solution)/shard_map/ppermute | solution.py:827
  54.2 12.0 %collective-permute-start.18 = (bf16[80,2048]{1,0:T(8,128)(2,1)S(1)}, bf16[80,2048]{1,0:T(8,128)(2,1)S(1)}, u32[]{:S(2)}, u32[]{:S(2)}) collective-permute-start(bf16[80,2048]{1,0:T(8,128)(2,1)S(1)} %collective-permute-done.16.rest_2_.refs_14_), channel_id=1, source_target_pairs={{0,1},{1,0},{2,3},{3,2},{4,5},{5,4},{6,7},{7,6},{8,9},{9,8},{10,11... | collective-permute-start | bytes 983048 | tf_op jit(solution)/shard_map/ppermute | solution.py:827
  54.4 10.0 %collective-permute-start.21 = (bf16[256,640]{1,0:T(8,128)(2,1)S(1)}, bf16[256,640]{1,0:T(8,128)(2,1)S(1)}, u32[]{:S(2)}, u32[]{:S(2)}) collective-permute-start(bf16[256,640]{1,0:T(8,128)(2,1)S(1)} %get-tuple-element.173), channel_id=1, source_target_pairs={{0,2},{1,3},{2,0},{3,1},{4,6},{5,7},{6,4},{7,5},{8,10},{9,11},{10,... | collective-permute-start | bytes 983048 | tf_op jit(solution)/shard_map/ppermute | solution.py:827
  64.4 9.3 %collective-permute-start.22 = (bf16[256,640]{1,0:T(8,128)(2,1)S(1)}, bf16[256,640]{1,0:T(8,128)(2,1)S(1)}, u32[]{:S(2)}, u32[]{:S(2)}) collective-permute-start(bf16[256,640]{1,0:T(8,128)(2,1)S(1)} %collective-permute-done.21.rest_2_), channel_id=1, source_target_pairs={{0,4},{4,0},{8,12},{12,8},{16,20},{20,16},{24,28},{28,24},{1,5},{5... | collective-permute-start | bytes 983048 | tf_op jit(solution)/shard_map/ppermute | solution.py:827
  65.7 8.3 %collective-permute-start.20 = (bf16[512,640]{1,0:T(8,128)(2,1)S(1)}, bf16[512,640]{1,0:T(8,128)(2,1)S(1)}, u32[]{:S(2)}, u32[]{:S(2)}) collective-permute-start(bf16[512,640]{1,0:T(8,128)(2,1)S(1)} %copy-done.17), channel_id=1, source_target_pairs={{0,1},{1,0},{2,3},{3,2},{4,5},{5,4},{6,7},{7,6},{8,9},{9,8},{10,11... | collective-permute-start | bytes 1966088 | tf_op jit(solution)/shard_map/ppermute | solution.py:827
  86.4 11.9 %collective-permute-start.25 = (bf16[2,2560,128]{2,1,0:T(8,128)(2,1)S(1)}, bf16[2,2560,128]{2,1,0:T(8,128)(2,1)S(1)}, u32[]{:S(2)}, u32[]{:S(2)}) collective-permute-start(bf16[2,2560,128]{2,1,0:T(8,128)(2,1)S(1)} %bitcast.47), channel_id=1, source_target_pairs={{0,1},{1,0},{2,3},{3,2},{4,5},{5,4},{6,7},{7,6},{8,9},{9,8},{10,11... | collective-permute-start | bytes 3932168 | tf_op jit(solution)/shard_map/ppermute | solution.py:938
  97.9 14.1 %collective-permute-start.27 = (bf16[2,2560,128]{2,1,0:T(8,128)(2,1)S(1)}, bf16[2,2560,128]{2,1,0:T(8,128)(2,1)S(1)}, u32[]{:S(2)}, u32[]{:S(2)}) collective-permute-start(bf16[2,2560,128]{2,1,0:T(8,128)(2,1)S(1)} %bitcast.46), channel_id=1, source_target_pairs={{0,1},{1,0},{2,3},{3,2},{4,5},{5,4},{6,7},{7,6},{8,9},{9,8},{10,11... | collective-permute-start | bytes 3932168 | tf_op jit(solution)/shard_map/ppermute | solution.py:938
  99.5 12.4 %collective-permute-start.26 = (bf16[2,1280,128]{2,1,0:T(8,128)(2,1)S(1)}, bf16[2,1280,128]{2,1,0:T(8,128)(2,1)S(1)}, u32[]{:S(2)}, u32[]{:S(2)}) collective-permute-start(bf16[2,1280,128]{2,1,0:T(8,128)(2,1)S(1)} %get-tuple-element.184), channel_id=1, source_target_pairs={{0,2},{1,5},{2,0},{3,7},{4,6},{5,1},{6,4},{7,3},{8,10},{9,13},{10,... | collective-permute-start | bytes 1966088 | tf_op jit(solution)/shard_map/ppermute | solution.py:938
  111.7 28.9 %collective-permute-start.32 = (bf16[2,2560,128]{2,1,0:T(8,128)(2,1)S(1)}, bf16[2,2560,128]{2,1,0:T(8,128)(2,1)S(1)}, u32[]{:S(2)}, u32[]{:S(2)}) collective-permute-start(bf16[2,2560,128]{2,1,0:T(8,128)(2,1)S(1)} %bitcast.45), channel_id=1, source_target_pairs={{0,1},{1,0},{2,3},{3,2},{4,5},{5,4},{6,7},{7,6},{8,9},{9,8},{10,11... | collective-permute-start | bytes 3932168 | tf_op jit(solution)/shard_map/ppermute | solution.py:938
  113.9 14.2 %collective-permute-start.29 = (bf16[2,1280,128]{2,1,0:T(8,128)(2,1)S(1)}, bf16[2,1280,128]{2,1,0:T(8,128)(2,1)S(1)}, u32[]{:S(2)}, u32[]{:S(2)}) collective-permute-start(bf16[2,1280,128]{2,1,0:T(8,128)(2,1)S(1)} %get-tuple-element.195), channel_id=1, source_target_pairs={{0,2},{1,5},{2,0},{3,7},{4,6},{5,1},{6,4},{7,3},{8,10},{9,13},{10,... | collective-permute-start | bytes 1966088 | tf_op jit(solution)/shard_map/ppermute | solution.py:938
  115.0 10.6 %collective-permute-start.28 = (bf16[1280,128]{1,0:T(8,128)(2,1)S(1)}, bf16[1280,128]{1,0:T(8,128)(2,1)S(1)}, u32[]{:S(2)}, u32[]{:S(2)}) collective-permute-start(bf16[1280,128]{1,0:T(8,128)(2,1)S(1)} %get-tuple-element.191), channel_id=1, source_target_pairs={{0,4},{1,3},{2,6},{3,1},{4,0},{5,7},{6,2},{7,5},{8,12},{9,11},{10,... | collective-permute-start | bytes 983048 | tf_op jit(solution)/shard_map/ppermute | solution.py:938
  124.4 11.8 %collective-permute-start.33 = (bf16[2,1280,128]{2,1,0:T(8,128)(2,1)S(1)}, bf16[2,1280,128]{2,1,0:T(8,128)(2,1)S(1)}, u32[]{:S(2)}, u32[]{:S(2)}) collective-permute-start(bf16[2,1280,128]{2,1,0:T(8,128)(2,1)S(1)} %bitcast.48), channel_id=1, source_target_pairs={{0,1},{1,0},{2,3},{3,2},{4,5},{5,4},{6,7},{7,6},{8,9},{9,8},{10,11... | collective-permute-start | bytes 1966088 | tf_op jit(solution)/shard_map/ppermute | solution.py:938
  126.3 9.4 %collective-permute-start.30 = (bf16[640,128]{1,0:T(8,128)(2,1)S(1)}, bf16[640,128]{1,0:T(8,128)(2,1)S(1)}, u32[]{:S(2)}, u32[]{:S(2)}) collective-permute-start(bf16[640,128]{1,0:T(8,128)(2,1)S(1)} %get-tuple-element.206), channel_id=1, source_target_pairs={{0,8},{1,9},{2,10},{3,11},{4,12},{5,13},{6,14},{7,15},{8,0},{9,1},... | collective-permute-start | bytes 491528 | tf_op jit(solution)/shard_map/ppermute | solution.py:938
  128.8 11.8 %collective-permute-start.31 = (bf16[1280,128]{1,0:T(8,128)(2,1)S(1)}, bf16[1280,128]{1,0:T(8,128)(2,1)S(1)}, u32[]{:S(2)}, u32[]{:S(2)}) collective-permute-start(bf16[1280,128]{1,0:T(8,128)(2,1)S(1)} %get-tuple-element.209), channel_id=1, source_target_pairs={{0,4},{1,3},{2,6},{3,1},{4,0},{5,7},{6,2},{7,5},{8,12},{9,11},{10,... | collective-permute-start | bytes 983048 | tf_op jit(solution)/shard_map/ppermute | solution.py:938
  136.3 15.7 %collective-permute-start.34 = (bf16[640,128]{1,0:T(8,128)(2,1)S(1)}, bf16[640,128]{1,0:T(8,128)(2,1)S(1)}, u32[]{:S(2)}, u32[]{:S(2)}) collective-permute-start(bf16[640,128]{1,0:T(8,128)(2,1)S(1)} %mix_sum.8.k), channel_id=1, source_target_pairs={{0,16},{1,17},{2,18},{3,19},{4,20},{5,21},{6,22},{7,23},{8,24},{9,... | collective-permute-start | bytes 491528 | tf_op jit(solution)/shard_map/ppermute | solution.py:938
  138.9 14.2 %collective-permute-start.36 = (bf16[512,512]{1,0:T(8,128)(2,1)S(1)}, bf16[512,512]{1,0:T(8,128)(2,1)S(1)}, u32[]{:S(2)}, u32[]{:S(2)}) collective-permute-start(bf16[512,512]{1,0:T(8,128)(2,1)S(1)} %get-tuple-element.240), channel_id=1, source_target_pairs={{1,0},{2,1},{3,2},{4,3},{5,4},{6,5},{7,6},{9,8},{10,9},{11,10},{12... | collective-permute-start | bytes 1572872 | tf_op jit(solution)/shard_map/ppermute | solution.py:1260
  141.3 11.3 %collective-permute-start.35 = (bf16[640,128]{1,0:T(8,128)(2,1)S(1)}, bf16[640,128]{1,0:T(8,128)(2,1)S(1)}, u32[]{:S(2)}, u32[]{:S(2)}) collective-permute-start(bf16[640,128]{1,0:T(8,128)(2,1)S(1)} %get-tuple-element.221), channel_id=1, source_target_pairs={{0,8},{1,9},{2,10},{3,11},{4,12},{5,13},{6,14},{7,15},{8,0},{9,1},... | collective-permute-start | bytes 491528 | tf_op jit(solution)/shard_map/ppermute | solution.py:938
  144.5 15.0 %collective-permute-start.37 = (bf16[2,1920,128]{2,1,0:T(8,128)(2,1)S(1)}, bf16[2,1920,128]{2,1,0:T(8,128)(2,1)S(1)}, u32[]{:S(2)}, u32[]{:S(2)}) collective-permute-start(bf16[2,1920,128]{2,1,0:T(8,128)(2,1)S(1)} %get-tuple-element.228), channel_id=1, source_target_pairs={{0,2},{1,5},{2,0},{3,7},{4,6},{5,1},{6,4},{7,3},{8,10},{9,13},{10,... | collective-permute-start | bytes 2949128 | tf_op jit(solution)/shard_map/ppermute | solution.py:938
  157.6 11.5 %collective-permute-start.39 = (bf16[2,2048,128]{2,1,0:T(8,128)(2,1)S(1)}, bf16[2,2048,128]{2,1,0:T(8,128)(2,1)S(1)}, u32[]{:S(2)}, u32[]{:S(2)}) collective-permute-start(bf16[2,2048,128]{2,1,0:T(8,128)(2,1)S(1)} %get-tuple-element.256), channel_id=1, source_target_pairs={{0,1},{1,0},{2,3},{3,2},{4,5},{5,4},{6,7},{7,6},{8,9},{9,8},{10,11... | collective-permute-start | bytes 3145736 | tf_op jit(solution)/shard_map/ppermute | solution.py:938
  157.6 10.9 %collective-permute-start.38 = (bf16[640,128]{1,0:T(8,128)(2,1)S(1)}, bf16[640,128]{1,0:T(8,128)(2,1)S(1)}, u32[]{:S(2)}, u32[]{:S(2)}) collective-permute-start(bf16[640,128]{1,0:T(8,128)(2,1)S(1)} %mix_sum.10.k), channel_id=1, source_target_pairs={{0,16},{1,17},{2,18},{3,19},{4,20},{5,21},{6,22},{7,23},{8,24},{9,... | collective-permute-start | bytes 491528 | tf_op jit(solution)/shard_map/ppermute | solution.py:938
  160.3 10.3 %collective-permute-start.40 = (bf16[1920,128]{1,0:T(8,128)(2,1)S(1)}, bf16[1920,128]{1,0:T(8,128)(2,1)S(1)}, u32[]{:S(2)}, u32[]{:S(2)}) collective-permute-start(bf16[1920,128]{1,0:T(8,128)(2,1)S(1)} %get-tuple-element.251), channel_id=1, source_target_pairs={{0,4},{1,3},{2,6},{3,1},{4,0},{5,7},{6,2},{7,5},{8,12},{9,11},{10,... | collective-permute-start | bytes 1474568 | tf_op jit(solution)/shard_map/ppermute | solution.py:938
  170.2 9.2 %collective-permute-start.41 = (bf16[2,1024,128]{2,1,0:T(8,128)(2,1)S(1)}, bf16[2,1024,128]{2,1,0:T(8,128)(2,1)S(1)}, u32[]{:S(2)}, u32[]{:S(2)}) collective-permute-start(bf16[2,1024,128]{2,1,0:T(8,128)(2,1)S(1)} %get-tuple-element.260), channel_id=1, source_target_pairs={{0,2},{1,5},{2,0},{3,7},{4,6},{5,1},{6,4},{7,3},{8,10},{9,13},{10,... | collective-permute-start | bytes 1572872 | tf_op jit(solution)/shard_map/ppermute | solution.py:938
  171.3 9.7 %collective-permute-start.42 = (bf16[960,128]{1,0:T(8,128)(2,1)S(1)}, bf16[960,128]{1,0:T(8,128)(2,1)S(1)}, u32[]{:S(2)}, u32[]{:S(2)}) collective-permute-start(bf16[960,128]{1,0:T(8,128)(2,1)S(1)} %get-tuple-element.263), channel_id=1, source_target_pairs={{0,8},{1,9},{2,10},{3,11},{4,12},{5,13},{6,14},{7,15},{8,0},{9,1},... | collective-permute-start | bytes 737288 | tf_op jit(solution)/shard_map/ppermute | solution.py:938
  180.2 8.9 %collective-permute-start.43 = (bf16[1024,128]{1,0:T(8,128)(2,1)S(1)}, bf16[1024,128]{1,0:T(8,128)(2,1)S(1)}, u32[]{:S(2)}, u32[]{:S(2)}) collective-permute-start(bf16[1024,128]{1,0:T(8,128)(2,1)S(1)} %get-tuple-element.268), channel_id=1, source_target_pairs={{0,4},{1,3},{2,6},{3,1},{4,0},{5,7},{6,2},{7,5},{8,12},{9,11},{10,... | collective-permute-start | bytes 786440 | tf_op jit(solution)/shard_map/ppermute | solution.py:938
  181.7 12.6 %collective-permute-start.44 = (bf16[960,128]{1,0:T(8,128)(2,1)S(1)}, bf16[960,128]{1,0:T(8,128)(2,1)S(1)}, u32[]{:S(2)}, u32[]{:S(2)}) collective-permute-start(bf16[960,128]{1,0:T(8,128)(2,1)S(1)} %mix_sum.12.k), channel_id=1, source_target_pairs={{0,16},{1,17},{2,18},{3,19},{4,20},{5,21},{6,22},{7,23},{8,24},{9,... | collective-permute-start | bytes 737288 | tf_op jit(solution)/shard_map/ppermute | solution.py:938
  182.6 17.3 %collective-permute-start.58 = (bf16[640,128]{1,0:T(8,128)(2,1)S(1)}, bf16[640,128]{1,0:T(8,128)(2,1)S(1)}, u32[]{:S(2)}, u32[]{:S(2)}) collective-permute-start(bf16[640,128]{1,0:T(8,128)(2,1)S(1)} %mix_sum.9.refs_0_), channel_id=1, source_target_pairs={{0,12},{1,13},{2,14},{3,15},{4,8},{5,9},{6,10},{7,11},{8,4},{9,5},... | collective-permute-start | bytes 491528 | tf_op jit(solution)/shard_map/ppermute | solution.py:938
  189.8 11.8 %collective-permute-start.57 = (bf16[640,128]{1,0:T(8,128)(2,1)S(1)}, bf16[640,128]{1,0:T(8,128)(2,1)S(1)}, u32[]{:S(2)}, u32[]{:S(2)}) collective-permute-start(bf16[640,128]{1,0:T(8,128)(2,1)S(1)} %mix_sum.9.refs_0_), channel_id=1, source_target_pairs={{0,8},{1,9},{2,10},{3,11},{4,12},{5,13},{6,14},{7,15},{8,0},{9,1},... | collective-permute-start | bytes 491528 | tf_op jit(solution)/shard_map/ppermute | solution.py:938
  191.8 10.5 %collective-permute-start.56 = (bf16[640,128]{1,0:T(8,128)(2,1)S(1)}, bf16[640,128]{1,0:T(8,128)(2,1)S(1)}, u32[]{:S(2)}, u32[]{:S(2)}) collective-permute-start(bf16[640,128]{1,0:T(8,128)(2,1)S(1)} %mix_sum.9.refs_0_), channel_id=1, source_target_pairs={{0,4},{1,5},{2,6},{3,7},{4,0},{5,1},{6,2},{7,3},{8,12},{9,13},{10,... | collective-permute-start | bytes 491528 | tf_op jit(solution)/shard_map/ppermute | solution.py:938
  194.3 13.6 %collective-permute-start.52 = (bf16[640,128]{1,0:T(8,128)(2,1)S(1)}, bf16[640,128]{1,0:T(8,128)(2,1)S(1)}, u32[]{:S(2)}, u32[]{:S(2)}) collective-permute-start(bf16[640,128]{1,0:T(8,128)(2,1)S(1)} %mix_sum.11.refs_0_), channel_id=1, source_target_pairs={{0,12},{1,13},{2,14},{3,15},{4,8},{5,9},{6,10},{7,11},{8,4},{9,5},... | collective-permute-start | bytes 491528 | tf_op jit(solution)/shard_map/ppermute | solution.py:938
  197.6 10.3 %collective-permute-start.46 = (bf16[512,128]{1,0:T(8,128)(2,1)S(1)}, bf16[512,128]{1,0:T(8,128)(2,1)S(1)}, u32[]{:S(2)}, u32[]{:S(2)}) collective-permute-start(bf16[512,128]{1,0:T(8,128)(2,1)S(1)} %mix_sum.14.k), channel_id=1, source_target_pairs={{0,16},{1,17},{2,18},{3,19},{4,20},{5,21},{6,22},{7,23},{8,24},{9,... | collective-permute-start | bytes 393224 | tf_op jit(solution)/shard_map/ppermute | solution.py:938
  200.0 18.7 %collective-permute-start.55 = (bf16[960,128]{1,0:T(8,128)(2,1)S(1)}, bf16[960,128]{1,0:T(8,128)(2,1)S(1)}, u32[]{:S(2)}, u32[]{:S(2)}) collective-permute-start(bf16[960,128]{1,0:T(8,128)(2,1)S(1)} %mix_sum.13.refs_4_), channel_id=1, source_target_pairs={{0,12},{1,13},{2,14},{3,15},{4,8},{5,9},{6,10},{7,11},{8,4},{9,5},... | collective-permute-start | bytes 737288 | tf_op jit(solution)/shard_map/ppermute | solution.py:938
  201.5 13.6 %collective-permute-start.51 = (bf16[640,128]{1,0:T(8,128)(2,1)S(1)}, bf16[640,128]{1,0:T(8,128)(2,1)S(1)}, u32[]{:S(2)}, u32[]{:S(2)}) collective-permute-start(bf16[640,128]{1,0:T(8,128)(2,1)S(1)} %mix_sum.11.refs_0_), channel_id=1, source_target_pairs={{0,8},{1,9},{2,10},{3,11},{4,12},{5,13},{6,14},{7,15},{8,0},{9,1},... | collective-permute-start | bytes 491528 | tf_op jit(solution)/shard_map/ppermute | solution.py:938
  202.2 13.9 %collective-permute-start.50 = (bf16[640,128]{1,0:T(8,128)(2,1)S(1)}, bf16[640,128]{1,0:T(8,128)(2,1)S(1)}, u32[]{:S(2)}, u32[]{:S(2)}) collective-permute-start(bf16[640,128]{1,0:T(8,128)(2,1)S(1)} %mix_sum.11.refs_0_), channel_id=1, source_target_pairs={{0,4},{1,5},{2,6},{3,7},{4,0},{5,1},{6,2},{7,3},{8,12},{9,13},{10,... | collective-permute-start | bytes 491528 | tf_op jit(solution)/shard_map/ppermute | solution.py:938
  207.9 12.5 %collective-permute-start.54 = (bf16[960,128]{1,0:T(8,128)(2,1)S(1)}, bf16[960,128]{1,0:T(8,128)(2,1)S(1)}, u32[]{:S(2)}, u32[]{:S(2)}) collective-permute-start(bf16[960,128]{1,0:T(8,128)(2,1)S(1)} %mix_sum.13.refs_4_), channel_id=1, source_target_pairs={{0,8},{1,9},{2,10},{3,11},{4,12},{5,13},{6,14},{7,15},{8,0},{9,1},... | collective-permute-start | bytes 737288 | tf_op jit(solution)/shard_map/ppermute | solution.py:938
  207.9 12.5 %collective-permute-start.53 = (bf16[960,128]{1,0:T(8,128)(2,1)S(1)}, bf16[960,128]{1,0:T(8,128)(2,1)S(1)}, u32[]{:S(2)}, u32[]{:S(2)}) collective-permute-start(bf16[960,128]{1,0:T(8,128)(2,1)S(1)} %mix_sum.13.refs_4_), channel_id=1, source_target_pairs={{0,4},{1,5},{2,6},{3,7},{4,0},{5,1},{6,2},{7,3},{8,12},{9,13},{10,... | collective-permute-start | bytes 737288 | tf_op jit(solution)/shard_map/ppermute | solution.py:938
  215.1 9.6 %collective-permute-start.49 = (bf16[512,128]{1,0:T(8,128)(2,1)S(1)}, bf16[512,128]{1,0:T(8,128)(2,1)S(1)}, u32[]{:S(2)}, u32[]{:S(2)}) collective-permute-start(bf16[512,128]{1,0:T(8,128)(2,1)S(1)} %mix_sum.15.refs_0_), channel_id=1, source_target_pairs={{0,12},{1,13},{2,14},{3,15},{4,8},{5,9},{6,10},{7,11},{8,4},{9,5},... | collective-permute-start | bytes 393224 | tf_op jit(solution)/shard_map/ppermute | solution.py:938
  216.2 8.7 %collective-permute-start.48 = (bf16[512,128]{1,0:T(8,128)(2,1)S(1)}, bf16[512,128]{1,0:T(8,128)(2,1)S(1)}, u32[]{:S(2)}, u32[]{:S(2)}) collective-permute-start(bf16[512,128]{1,0:T(8,128)(2,1)S(1)} %mix_sum.15.refs_0_), channel_id=1, source_target_pairs={{0,8},{1,9},{2,10},{3,11},{4,12},{5,13},{6,14},{7,15},{8,0},{9,1},... | collective-permute-start | bytes 393224 | tf_op jit(solution)/shard_map/ppermute | solution.py:938
  (51 other events, 258.2 us)

commit v5 on v4

--- a/solution.py
+++ b/solution.py
@@ -1090,7 +1090,8 @@
     gr = D // 4
 
     def body(i, *refs):
-        wq, wk, wv, g, query, key, value, gains, first, total, prod = refs[4:]
+        wq, wk, wv, g, query, key, value = refs[4:11]
+        first, g_query, g_key, g_att, g_mid, g_out, total, prod, gains = refs[11:]
         gather_parts(i, refs[:4], total)
         spread(query, total, 0, gr, 8)
         spread(key, total, 8 * gr, gr, 2)
@@ -1104,7 +1105,10 @@
         high = p.astype(BF16)
         low = (p - high.astype(F32)).astype(BF16)
         ones = jnp.ones((16, 6 * HEAD_DIM), BF16)
-        first[...] = (dot(ones, high, NT) + dot(ones, low, NT)) / g[...].astype(F32).reshape(1, -1)
+        summed = dot(ones, high, NT) + dot(ones, low, NT)
+        first[...] = summed[0:1, :].reshape(-1) / g[...].astype(F32)
+        for row, o in ((1, g_att), (2, g_mid), (3, g_out), (4, g_query), (5, g_key)):
+            o[...] = gains[row : row + 1, : o.shape[0]].reshape(-1)
 
     return pl.pallas_call(
         body,
@@ -1112,14 +1116,19 @@
             hbm((gr, HEADS * HEAD_DIM), F32),
             hbm((gr, HEAD_DIM), F32),
             hbm((gr, HEAD_DIM), F32),
-            sds((16, HEAD_DIM), F32),
-            sds((16, gr), F32),
+            sds((gr,), F32),
+            sds((HEAD_DIM // 4,), F32),
+            sds((HEAD_DIM // 4,), F32),
+            sds((gr,), F32),
+            sds((gr,), F32),
+            sds((gr,), F32),
         ),
         in_specs=[SM] + [VM] * 8,
-        out_specs=(VM,) * 5,
+        out_specs=(VM,) * 9,
         scratch_shapes=[
             pltpu.VMEM((4,) + parts[0].shape, BF16),
             pltpu.VMEM((gr, 6 * HEAD_DIM), F32),
+            pltpu.VMEM((16, HEAD_DIM), F32),
         ],
         compiler_params=params(),
         cost_estimate=cost(1e7, 1e7),
@@ -1283,7 +1292,7 @@
     for name in "dacb":
         advance(name * len(chains[name].steps))
     r_down = finish_one(me, chains["d"].parts)
-    r_query, r_key, r_value, tail, first = finish_three(
+    r_query, r_key, r_value, *r_gains = finish_three(
         me,
         chains["c"].parts,
         query_weight,
@@ -1302,12 +1311,7 @@
         r_gate,
         r_up,
         r_down,
-        first[0],
-        tail[4, :gh],
-        tail[5, :gh],
-        tail[1, :gd],
-        tail[2, :gd],
-        tail[3, :gd],
+        *r_gains,
     )
 
 

time: 233 us -> 231 us (level)
  no operation moved by 1% of the time
where the time goes in v5:
time: 231 us; the launch traced here: 227 us
  Pallas kernels  122 us (53%)
  starting transfers between devices  56.9 us (25%)
  waiting for transfers between devices  38.7 us (17%)
  local copies, waits for them, and re-layouts  5.3 us (2%)
    ppermute x33, starting transfers between devices, send(): return lax.ppermute(x, ('seq', 'shard'), pairs)  32.8 us
    ppermute x33, waiting for transfers between devices, send(): return lax.ppermute(x, ('seq', 'shard'), pairs)  31.1 us
    pallas_call x2, Pallas kernels, fb(): pl.pallas_call(body, out_shape=(sds((2, 2, FH // 128, D // 4, 128)),) * 2...  22.4 us
    ppermute x24, starting transfers between devices, flip(): return lax.ppermute(x, axis, [(i, i ^ bit) for i in range(n)])  20 us
    pallas_call x20, Pallas kernels, small_call(): pl.pallas_call(body, out_shape=tuple((sds(r + (128,)) for r in out_rows))...  15.4 us
    pallas_call x2, Pallas kernels, ff(): pl.pallas_call(up_kernel if before else gate_kernel, out_shape=(sds((t, F...  13.9 us
    pallas_call x2, Pallas kernels, att_back(): pl.pallas_call(att_back_kernel, grid=(1,), out_shape=(sds((HALF, HEADS *...  11.3 us
    pallas_call x1, Pallas kernels, down_part(): pl.pallas_call(down_kernel, out_shape=(sds((t, D)), sds((t, D)), sds((FF,...  10.2 us
  transfers between devices with their start and end apart: 59, of which 18 were waited for; matrix products, arithmetic and copies ran while one was open for 1% of the time, Pallas kernels for 48%

profile of v5, /device:TPU:0, one launch (start us, length us, event | category | flops | bytes accessed | tf_op | source)
XLA Modules:
  0.0 226.8 jit_solution(3463198368961291315)
XLA Ops:
  0.8 1.6 pack.1.g0.w0.k0
  2.3 3.0 %collective-permute-start.1 = (bf16[176,512]{1,0:T(8,128)(2,1)S(1)}, bf16[176,512]{1,0:T(8,128)(2,1)S(1)}, u32[]{:S(2)}, u32[]{:S(2)}) collective-permute-start(bf16[176,512]{1,0:T(8,128)(2,1)S(1)} %pack.1.g0.w0.k0), channel_id=1, source_target_pairs={{0,2},{1,3},{2,0},{3,1},{4,6},{5,7},{6,4},{7,5},{8,10},{9,11},{10,... | collective-permute-start | bytes 540680 | tf_op jit(solution)/shard_map/ppermute | solution.py:827
  5.9 1.7 halves.1
  7.6 1.8 collective-permute-start.7
  10.8 1.9 multiply_sine_fusion
  13.6 3.2 %pre_kv.1 = (bf16[1024,640]{1,0:T(8,128)(2,1)S(1)}, bf16[1024,256]{1,0:T(8,128)(2,1)S(1)}, bf16[512,512]{1,0:T(8,128)(2,1)S(1)}, bf16[512,512]{1,0:T(8,128)(2,1)S(1)}) custom-call(s32[9]{0:T(128)S(1)} %stack.43.info.me_ref.refs_0_.s.i, bf16[1024,640]{1,0:T(8,128)(2,1)S(1)} %copy-done, f32[8,640]{1,0:T(8,128)S(1)} %gains.1, ...), custom_call_target="tpu_custom_call" | custom-call | flops 671088640 | bytes 5000000 | tf_op jit(solution)/shard_map/pre_kv/pallas_call | solution.py:237
  17.8 2.1 collective-permute-start.6
  19.9 2.4 %collective-permute-start.8 = (bf16[512,512]{1,0:T(8,128)(2,1)S(1)}, bf16[512,512]{1,0:T(8,128)(2,1)S(1)}, u32[]{:S(2)}, u32[]{:S(2)}) collective-permute-start(bf16[512,512]{1,0:T(8,128)(2,1)S(1)} %get-tuple-element.162.refs_3_.kvs), channel_id=1, source_target_pairs={{0,1},{1,2},{2,3},{3,4},{4,5},{5,6},{6,7},{8,9},{9,10},{10,11},{11... | collective-permute-start | bytes 1572872 | tf_op jit(solution)/shard_map/ppermute | solution.py:1212
  22.3 2.5 %collective-permute-done.7.rest_2_.refs_8_ = bf16[80,2048]{1,0:T(8,128)(2,1)S(1)} collective-permute-done((bf16[80,2048]{1,0:T(8,128)(2,1)S(1)}, bf16[80,2048]{1,0:T(8,128)(2,1)S(1)}, u32[]{:S(2)}, u32[]{:S(2)}) %collective-permute-start.7) | collective-permute-done | bytes 327712 | tf_op jit(solution)/shard_map/ppermute | solution.py:827
  25.4 2.1 collective-permute-start.16
  27.4 5.9 %pre_q.1 = (bf16[4,1024,256]{2,1,0:T(8,128)(2,1)}, bf16[4,1024,256]{2,1,0:T(8,128)(2,1)S(1)}) custom-call(s32[9]{0:T(128)S(1)} %stack.43.info.me_ref.refs_0_.s.i, bf16[1024,640]{1,0:T(8,128)(2,1)S(1)} %get-tuple-element.156.nin_i.nin, f32[8,640]{1,0:T(8,128)S(1)} %gains.1, f32[1024,128]{1,0:T(8,128)S(1)} %get-tuple-element.298.cos_ref, ...), custom_call_target="tpu_custom_call" | custom-call | flops 1342177280 | bytes 5000000 | tf_op jit(solution)/shard_map/pre_q/pallas_call | solution.py:279
  33.4 6.1 %collective-permute-start.12 = (bf16[80,2048]{1,0:T(8,128)(2,1)S(1)}, bf16[80,2048]{1,0:T(8,128)(2,1)S(1)}, u32[]{:S(2)}, u32[]{:S(2)}) collective-permute-start(bf16[80,2048]{1,0:T(8,128)(2,1)S(1)} %collective-permute-done.7.rest_2_.refs_8_), channel_id=1, source_target_pairs={{0,4},{4,0},{8,12},{12,8},{16,20},{20,16},{24,28},{28,24},{1,5},{5... | collective-permute-start | bytes 983048 | tf_op jit(solution)/shard_map/ppermute | solution.py:827
  39.5 3.2 %att.2 = (bf16[512,1024]{1,0:T(8,128)(2,1)S(1)}, bf16[4,512,256]{2,1,0:T(8,128)(2,1)S(1)}, bf16[4,512,256]{2,1,0:T(8,128)(2,1)S(1)}) custom-call(s32[9]{0:T(128)S(1)} %stack.43.info.me_ref.refs_0_.s.i, bf16[4,1024,256]{2,1,0:T(8,128)(2,1)S(1)} %get-tuple-element.164.refs_1_.qs, bf16[512,512]{1,0:T(8,128)(2,1)S(1)} %get-tuple-element.161.refs_2_.refs_3_.kvs.kvp, ...), custom_call_target="tpu_custom_call" | custom-call | flops 3000000000 | bytes 5000000 | tf_op jit(solution)/shard_map/att/pallas_call | solution.py:338
  43.7 3.3 %att.3 = (bf16[512,1024]{1,0:T(8,128)(2,1)S(1)}, bf16[4,512,256]{2,1,0:T(8,128)(2,1)S(1)}, bf16[4,512,256]{2,1,0:T(8,128)(2,1)S(1)}) custom-call(s32[9]{0:T(128)S(1)} %stack.43.info.me_ref.refs_0_.s.i, bf16[4,1024,256]{2,1,0:T(8,128)(2,1)S(1)} %get-tuple-element.164.refs_1_.qs, bf16[512,512]{1,0:T(8,128)(2,1)S(1)} %collective-permute-done.8.refs_2_.kvp, ...), custom_call_target="tpu_custom_call" | custom-call | flops 3000000000 | bytes 5000000 | tf_op jit(solution)/shard_map/att/pallas_call | solution.py:338
  49.9 4.3 %mid.1 = (bf16[1024,640]{1,0:T(8,128)(2,1)S(1)}, bf16[1024,640]{1,0:T(8,128)(2,1)S(1)}) custom-call(s32[9]{0:T(128)S(1)} %stack.43.info.me_ref.refs_0_.s.i, bf16[512,1024]{1,0:T(8,128)(2,1)S(1)} %get-tuple-element.165.o_lo, bf16[512,1024]{1,0:T(8,128)(2,1)S(1)} %get-tuple-element.163.o_hi, bf16[1024,640]{1,0:T(8,128)(2,1)S(1)} %copy-done, ...), custom_call_target="tpu_custom_call" | custom-call | flops 1342177280 | bytes 8000000 | tf_op jit(solution)/shard_map/mid/pallas_call | solution.py:434
  55.3 7.3 %gate.1 = (bf16[1024,2048]{1,0:T(8,128)(2,1)S(1)}, bf16[1024,2048]{1,0:T(8,128)(2,1)S(1)}) custom-call(s32[9]{0:T(128)S(1)} %stack.43.info.me_ref.refs_0_.s.i, bf16[1024,640]{1,0:T(8,128)(2,1)S(1)} %get-tuple-element.166.nm.refs_1_, bf16[160,2048]{1,0:T(8,128)(2,1)} %refs_6_.4, bf16[160,2048]{1,0:T(8,128)(2,1)} %copy-done.30, bf16[80,2048]{1,0:T(8,128)(2,1)} %copy-done.32, ...), custom_call_target="tpu_custom_call" | custom-call | flops 2684354560 | bytes 12000000 | tf_op jit(solution)/shard_map/gate/pallas_call | solution.py:509
  67.1 6.6 %up.1 = (bf16[1024,2048]{1,0:T(8,128)(2,1)S(1)}, bf16[1024,2048]{1,0:T(8,128)(2,1)S(1)}) custom-call(s32[9]{0:T(128)S(1)} %stack.43.info.me_ref.refs_0_.s.i, bf16[1024,640]{1,0:T(8,128)(2,1)S(1)} %get-tuple-element.166.nm.refs_1_, bf16[1024,2048]{1,0:T(8,128)(2,1)S(1)} %get-tuple-element.168.a_i.refs_3_, bf16[1024,2048]{1,0:T(8,128)(2,1)S(1)} %get-tuple-element.169.s_i, ...), custom_call_target="tpu_custom_call" | custom-call | flops 2684354560 | bytes 12000000 | tf_op jit(solution)/shard_map/up/pallas_call | solution.py:509
  74.0 1.4 collective-permute-done.24.rest_5_
  76.1 10.2 %down.1 = (bf16[1024,640]{1,0:T(8,128)(2,1)}, bf16[1024,640]{1,0:T(8,128)(2,1)S(1)}, bf16[2048,640]{1,0:T(8,128)(2,1)S(1)}, bf16[2,5,512,128]{3,2,1,0:T(8,128)(2...) custom-call(s32[9]{0:T(128)S(1)} %stack.43.info.me_ref.refs_0_.s.i, ...), custom_call_target="tpu_custom_call" | custom-call | flops 5368709120 | bytes 20000000 | tf_op jit(solution)/shard_map/down/pallas_call | solution.py:552
  86.6 11.2 %fb.2 = (bf16[2,2,8,160,128]{4,3,2,1,0:T(8,128)(2,1)S(1)}, bf16[2,2,8,160,128]{4,3,2,1,0:T(8,128)(2,1)S(1)}, f32[1024,640]{1,0:T(8,128)S(1)}) custom-call(s32[9]{0:T(128)S(1)} %stack.43.info.me_ref.refs_0_.s.i, bf16[1024,640]{1,0:T(8,128)(2,1)S(1)} %get-tuple-element.166.nm.refs_1_, bf16[1024,640]{1,0:T(8,128)(2,1)S(1)} %get-tuple-element.181.refs_2_, ...), custom_call_target="tpu_custom_call" | custom-call | flops 6710886400 | bytes 16000000 | tf_op jit(solution)/shard_map/fb/pallas_call | solution.py:621
  100.5 11.2 %fb.3 = (bf16[2,2,8,160,128]{4,3,2,1,0:T(8,128)(2,1)S(1)}, bf16[2,2,8,160,128]{4,3,2,1,0:T(8,128)(2,1)S(1)}, f32[1024,640]{1,0:T(8,128)S(1)}) custom-call(s32[9]{0:T(128)S(1)} %stack.43.info.me_ref.refs_0_.s.i, bf16[1024,640]{1,0:T(8,128)(2,1)S(1)} %get-tuple-element.166.nm.refs_1_, bf16[1024,640]{1,0:T(8,128)(2,1)S(1)} %get-tuple-element.181.refs_2_, ...), custom_call_target="tpu_custom_call" | custom-call | flops 6710886400 | bytes 16000000 | tf_op jit(solution)/shard_map/fb/pallas_call | solution.py:621
  116.2 8.2 %fe.1 = (bf16[2,5,256,128]{3,2,1,0:T(8,128)(2,1)S(1)}, bf16[2,5,256,128]{3,2,1,0:T(8,128)(2,1)S(1)}, bf16[4,1024,256]{2,1,0:T(8,128)(2,1)S(1)}, bf16[1024,640]{1,0:T(8,128)(2,1)S(1)}, f32[16,640]{1,0:T(8,128)S(1)}) custom-call(s32[9]{0:T(128)S(1)} %stack.43.info.me_ref.refs_0_.s.i, bf16[512,1024]{1,0:T(8,128)(2,1)S(1)} %get-tuple-element.165.o_lo, ...), custom_call_target="tpu_custom_call" | custom-call | flops 2684354560 | bytes 14000000 | tf_op jit(solution)/shard_map/fe/pallas_call | solution.py:676
  126.3 1.6 collective-permute-start.30
  130.0 5.6 %att_back.2 = (bf16[512,1024]{1,0:T(8,128)(2,1)S(1)}, bf16[512,512]{1,0:T(8,128)(2,1)S(1)}, f32[512,512]{1,0:T(8,128)S(1)}, f32[8,256]{1,0:T(8,128)S(1)}) custom-call(bf16[4,1024,256]{2,1,0:T(8,128)(2,1)S(1)} %get-tuple-element.164.refs_1_.qs, bf16[4,1024,256]{2,1,0:T(8,128)(2,1)S(1)} %copy-done.10, bf16[512,512]{1,0:T(8,128)(2,1)S(1)} %collective-permute-done.8.refs_2_.kvp, ...), custom_call_target="tpu_custom_call" | custom-call | flops 6000000000 | bytes 9000000 | tf_op jit(solution)/shard_map/att_back/pallas_call | solution.py:399
  136.3 2.7 %collective-permute-start.34 = (bf16[640,128]{1,0:T(8,128)(2,1)S(1)}, bf16[640,128]{1,0:T(8,128)(2,1)S(1)}, u32[]{:S(2)}, u32[]{:S(2)}) collective-permute-start(bf16[640,128]{1,0:T(8,128)(2,1)S(1)} %mix_sum.8.k), channel_id=1, source_target_pairs={{0,16},{1,17},{2,18},{3,19},{4,20},{5,21},{6,22},{7,23},{8,24},{9,... | collective-permute-start | bytes 491528 | tf_op jit(solution)/shard_map/ppermute | solution.py:938
  138.9 1.7 collective-permute-start.36
  141.3 1.6 collective-permute-start.35
  142.9 1.6 mix_first.6
  144.6 1.7 collective-permute-start.37
  146.3 5.6 %att_back.3 = (bf16[512,1024]{1,0:T(8,128)(2,1)S(1)}, bf16[512,512]{1,0:T(8,128)(2,1)S(1)}, f32[512,512]{1,0:T(8,128)S(1)}, f32[8,256]{1,0:T(8,128)S(1)}) custom-call(bf16[4,1024,256]{2,1,0:T(8,128)(2,1)S(1)} %get-tuple-element.164.refs_1_.qs, bf16[4,1024,256]{2,1,0:T(8,128)(2,1)S(1)} %copy-done.10, ...), custom_call_target="tpu_custom_call" | custom-call | flops 6000000000 | bytes 9000000 | tf_op jit(solution)/shard_map/att_back/pallas_call | solution.py:399
  153.2 4.4 %post.1 = (bf16[1024,512]{1,0:T(8,128)(2,1)S(1)}, bf16[2,2048,128]{2,1,0:T(8,128)(2,1)S(1)}, bf16[2,2048,128]{2,1,0:T(8,128)(2,1)S(1)}) custom-call(s32[9]{0:T(128)S(1)} %stack.43.info.me_ref.refs_0_.s.i, bf16[1024,640]{1,0:T(8,128)(2,1)S(1)} %get-tuple-element.156.nin_i.nin, bf16[512,1024]{1,0:T(8,128)(2,1)S(1)} %get-tuple-element.215.dq_lo, ...), custom_call_target="tpu_custom_call" | custom-call | flops 2000000000 | bytes 10000000 | tf_op jit(solution)/shard_map/post/pallas_call | solution.py:768
  158.0 1.6 collective-permute-done.37.g
  161.3 6.8 %last.1 = bf16[1024,640]{1,0:T(8,128)(2,1)} custom-call(s32[9]{0:T(128)S(1)} %stack.43.info.me_ref.refs_0_.s.i, bf16[1024,640]{1,0:T(8,128)(2,1)S(1)} %copy-done, bf16[1024,640]{1,0:T(8,128)(2,1)S(1)} %get-tuple-element.201.dmid, bf16[512,1024]{1,0:T(8,128)(2,1)S(1)} %get-tuple-element.215.dq_lo, bf16[512,1024]{1,0:T(8,128)(2,1)S(1)} %get-tuple-element.240.dq_hi, ...), custom_call_target="tpu_custom_call" | custom-call | flops 2000000000 | bytes 8000000 | tf_op jit(solution)/shard_map/last/pallas_call | solution.py:809
  171.3 1.5 collective-permute-start.42
  172.8 6.7 %collective-permute-done.41.g = bf16[2,1024,128]{2,1,0:T(8,128)(2,1)S(1)} collective-permute-done((bf16[2,1024,128]{2,1,0:T(8,128)(2,1)S(1)}, bf16[2,1024,128]{2,1,0:T(8,128)(2,1)S(1)}, u32[]{:S(2)}, u32[]{:S(2)}) %collective-permute-start.41) | collective-permute-done | bytes 524320 | tf_op jit(solution)/shard_map/ppermute | solution.py:938
  183.8 5.3 %collective-permute-done.43 = bf16[1024,128]{1,0:T(8,128)(2,1)S(1)} collective-permute-done((bf16[1024,128]{1,0:T(8,128)(2,1)S(1)}, bf16[1024,128]{1,0:T(8,128)(2,1)S(1)}, u32[]{:S(2)}, u32[]{:S(2)}) %collective-permute-start.43) | collective-permute-done | bytes 262176 | tf_op jit(solution)/shard_map/ppermute | solution.py:938
  189.8 2.0 collective-permute-start.57
  191.8 2.1 collective-permute-start.56
  194.9 2.1 collective-permute-done.45.g
  197.6 2.3 %collective-permute-start.46 = (bf16[512,128]{1,0:T(8,128)(2,1)S(1)}, bf16[512,128]{1,0:T(8,128)(2,1)S(1)}, u32[]{:S(2)}, u32[]{:S(2)}) collective-permute-start(bf16[512,128]{1,0:T(8,128)(2,1)S(1)} %mix_sum.14.k), channel_id=1, source_target_pairs={{0,16},{1,17},{2,18},{3,19},{4,20},{5,21},{6,22},{7,23},{8,24},{9,... | collective-permute-start | bytes 393224 | tf_op jit(solution)/shard_map/ppermute | solution.py:938
  200.0 1.6 collective-permute-start.55
  203.5 4.4 %collective-permute-done.52.refs_3_ = bf16[640,128]{1,0:T(8,128)(2,1)S(1)} collective-permute-done((bf16[640,128]{1,0:T(8,128)(2,1)S(1)}, bf16[640,128]{1,0:T(8,128)(2,1)S(1)}, u32[]{:S(2)}, u32[]{:S(2)}) %collective-permute-start.52) | collective-permute-done | bytes 163872 | tf_op jit(solution)/shard_map/ppermute | solution.py:938
  208.5 6.6 %collective-permute-done.51.refs_2_ = bf16[640,128]{1,0:T(8,128)(2,1)S(1)} collective-permute-done((bf16[640,128]{1,0:T(8,128)(2,1)S(1)}, bf16[640,128]{1,0:T(8,128)(2,1)S(1)}, u32[]{:S(2)}, u32[]{:S(2)}) %collective-permute-start.51) | collective-permute-done | bytes 163872 | tf_op jit(solution)/shard_map/ppermute | solution.py:938
  216.1 2.5 %collective-permute-start.48 = (bf16[512,128]{1,0:T(8,128)(2,1)S(1)}, bf16[512,128]{1,0:T(8,128)(2,1)S(1)}, u32[]{:S(2)}, u32[]{:S(2)}) collective-permute-start(bf16[512,128]{1,0:T(8,128)(2,1)S(1)} %mix_sum.15.refs_0_), channel_id=1, source_target_pairs={{0,8},{1,9},{2,10},{3,11},{4,12},{5,13},{6,14},{7,15},{8,0},{9,1},... | collective-permute-start | bytes 393224 | tf_op jit(solution)/shard_map/ppermute | solution.py:938
  218.6 1.7 finish_one.1
  220.4 2.5 %finish_two.1 = (f32[160,2048]{1,0:T(8,128)}, f32[160,2048]{1,0:T(8,128)}, f32[256,640]{1,0:T(8,128)}) custom-call(s32[9]{0:T(128)S(1)} %stack.43.info.me_ref.refs_0_.s.i, bf16[640,128]{1,0:T(8,128)(2,1)S(1)} %mix_sum.11.refs_0_, bf16[640,128]{1,0:T(8,128)(2,1)S(1)} %collective-permute-done.50.refs_1_, bf16[640,128]{1,0:T(8,128)(2,1)S(1)} %collective-permute-done.51.refs_2_, ...), custom_call_target="tpu_custom_call" | custom-call | flops 10000000 | bytes 10000000 | tf_op jit(solution)/shard_map/finish_two/pallas_call | solution.py:1074
  222.9 1.8 collective-permute-done.49.refs_3_
  225.0 1.7 finish_three.1
  (195 shorter events, 44.3 us)
Async XLA Ops:
  2.3 8.4 %collective-permute-start.1 = (bf16[176,512]{1,0:T(8,128)(2,1)S(1)}, bf16[176,512]{1,0:T(8,128)(2,1)S(1)}, u32[]{:S(2)}, u32[]{:S(2)}) collective-permute-start(bf16[176,512]{1,0:T(8,128)(2,1)S(1)} %pack.1.g0.w0.k0), channel_id=1, source_target_pairs={{0,2},{1,3},{2,0},{3,1},{4,6},{5,7},{6,4},{7,5},{8,10},{9,11},{10,... | collective-permute-start | bytes 540680 | tf_op jit(solution)/shard_map/ppermute | solution.py:827
  5.4 12.4 %collective-permute-start.4 = (bf16[160,1024]{1,0:T(8,128)(2,1)}, bf16[160,1024]{1,0:T(8,128)(2,1)S(1)}, u32[]{:S(2)}, u32[]{:S(2)}) collective-permute-start(bf16[160,1024]{1,0:T(8,128)(2,1)} %refs_4_.1), channel_id=1, source_target_pairs={{0,2},{1,3},{2,0},{3,1},{4,6},{5,7},{6,4},{7,5},{8,10},{9,11},{10,... | collective-permute-start | bytes 983048 | tf_op jit(solution)/shard_map/ppermute | solution.py:827
  5.5 19.3 %collective-permute-start.3 = (bf16[160,1024]{1,0:T(8,128)(2,1)}, bf16[160,1024]{1,0:T(8,128)(2,1)S(1)}, u32[]{:S(2)}, u32[]{:S(2)}) collective-permute-start(bf16[160,1024]{1,0:T(8,128)(2,1)} %refs_4_.1), channel_id=1, source_target_pairs={{0,1},{1,0},{2,3},{3,2},{4,5},{5,4},{6,7},{7,6},{8,9},{9,8},{10,11... | collective-permute-start | bytes 983048 | tf_op jit(solution)/shard_map/ppermute | solution.py:827
  7.6 17.1 %collective-permute-start.7 = (bf16[80,2048]{1,0:T(8,128)(2,1)S(1)}, bf16[80,2048]{1,0:T(8,128)(2,1)S(1)}, u32[]{:S(2)}, u32[]{:S(2)}) collective-permute-start(bf16[80,2048]{1,0:T(8,128)(2,1)S(1)} %get-tuple-element.159), channel_id=1, source_target_pairs={{0,2},{1,3},{2,0},{3,1},{4,6},{5,7},{6,4},{7,5},{8,10},{9,11},{10,... | collective-permute-start | bytes 983048 | tf_op jit(solution)/shard_map/ppermute | solution.py:827
  17.8 15.6 %collective-permute-start.6 = (bf16[256,640]{1,0:T(8,128)(2,1)S(1)}, bf16[256,640]{1,0:T(8,128)(2,1)S(1)}, u32[]{:S(2)}, u32[]{:S(2)}) collective-permute-start(bf16[256,640]{1,0:T(8,128)(2,1)S(1)} %copy-done.19), channel_id=1, source_target_pairs={{0,2},{1,3},{2,0},{3,1},{4,6},{5,7},{6,4},{7,5},{8,10},{9,11},{10,... | collective-permute-start | bytes 983048 | tf_op jit(solution)/shard_map/ppermute | solution.py:827
  19.9 23.8 %collective-permute-start.8 = (bf16[512,512]{1,0:T(8,128)(2,1)S(1)}, bf16[512,512]{1,0:T(8,128)(2,1)S(1)}, u32[]{:S(2)}, u32[]{:S(2)}) collective-permute-start(bf16[512,512]{1,0:T(8,128)(2,1)S(1)} %get-tuple-element.162.refs_3_.kvs), channel_id=1, source_target_pairs={{0,1},{1,2},{2,3},{3,4},{4,5},{5,6},{6,7},{8,9},{9,10},{10,11},{11... | collective-permute-start | bytes 1572872 | tf_op jit(solution)/shard_map/ppermute | solution.py:1212
  24.8 23.9 %collective-permute-start.9 = (bf16[256,640]{1,0:T(8,128)(2,1)S(1)}, bf16[256,640]{1,0:T(8,128)(2,1)S(1)}, u32[]{:S(2)}, u32[]{:S(2)}) collective-permute-start(bf16[256,640]{1,0:T(8,128)(2,1)S(1)} %copy-done.19), channel_id=1, source_target_pairs={{0,1},{1,0},{2,3},{3,2},{4,5},{5,4},{6,7},{7,6},{8,9},{9,8},{10,11... | collective-permute-start | bytes 983048 | tf_op jit(solution)/shard_map/ppermute | solution.py:827
  24.8 29.4 %collective-permute-start.11 = (bf16[160,2048]{1,0:T(8,128)(2,1)S(1)}, bf16[160,2048]{1,0:T(8,128)(2,1)S(1)}, u32[]{:S(2)}, u32[]{:S(2)}) collective-permute-start(bf16[160,2048]{1,0:T(8,128)(2,1)S(1)} %copy-done.18), channel_id=1, source_target_pairs={{0,1},{1,0},{2,3},{3,2},{4,5},{5,4},{6,7},{7,6},{8,9},{9,8},{10,11... | collective-permute-start | bytes 1966088 | tf_op jit(solution)/shard_map/ppermute | solution.py:827
  25.4 23.2 %collective-permute-start.16 = (bf16[80,2048]{1,0:T(8,128)(2,1)S(1)}, bf16[80,2048]{1,0:T(8,128)(2,1)S(1)}, u32[]{:S(2)}, u32[]{:S(2)}) collective-permute-start(bf16[80,2048]{1,0:T(8,128)(2,1)S(1)} %get-tuple-element.171), channel_id=1, source_target_pairs={{0,2},{1,3},{2,0},{3,1},{4,6},{5,7},{6,4},{7,5},{8,10},{9,11},{10,... | collective-permute-start | bytes 983048 | tf_op jit(solution)/shard_map/ppermute | solution.py:827
  33.4 14.6 %collective-permute-start.12 = (bf16[80,2048]{1,0:T(8,128)(2,1)S(1)}, bf16[80,2048]{1,0:T(8,128)(2,1)S(1)}, u32[]{:S(2)}, u32[]{:S(2)}) collective-permute-start(bf16[80,2048]{1,0:T(8,128)(2,1)S(1)} %collective-permute-done.7.rest_2_.refs_8_), channel_id=1, source_target_pairs={{0,4},{4,0},{8,12},{12,8},{16,20},{20,16},{24,28},{28,24},{1,5},{5... | collective-permute-start | bytes 983048 | tf_op jit(solution)/shard_map/ppermute | solution.py:827
  48.7 17.0 %collective-permute-start.15 = (bf16[160,2048]{1,0:T(8,128)(2,1)S(1)}, bf16[160,2048]{1,0:T(8,128)(2,1)S(1)}, u32[]{:S(2)}, u32[]{:S(2)}) collective-permute-start(bf16[160,2048]{1,0:T(8,128)(2,1)S(1)} %copy-done.15), channel_id=1, source_target_pairs={{0,1},{1,0},{2,3},{3,2},{4,5},{5,4},{6,7},{7,6},{8,9},{9,8},{10,11... | collective-permute-start | bytes 1966088 | tf_op jit(solution)/shard_map/ppermute | solution.py:827
  49.2 13.4 %collective-permute-start.17 = (bf16[80,2048]{1,0:T(8,128)(2,1)S(1)}, bf16[80,2048]{1,0:T(8,128)(2,1)S(1)}, u32[]{:S(2)}, u32[]{:S(2)}) collective-permute-start(bf16[80,2048]{1,0:T(8,128)(2,1)S(1)} %collective-permute-done.16.rest_2_.refs_14_), channel_id=1, source_target_pairs={{0,4},{4,0},{8,12},{12,8},{16,20},{20,16},{24,28},{28,24},{1,5},{5... | collective-permute-start | bytes 983048 | tf_op jit(solution)/shard_map/ppermute | solution.py:827
  54.2 12.0 %collective-permute-start.18 = (bf16[80,2048]{1,0:T(8,128)(2,1)S(1)}, bf16[80,2048]{1,0:T(8,128)(2,1)S(1)}, u32[]{:S(2)}, u32[]{:S(2)}) collective-permute-start(bf16[80,2048]{1,0:T(8,128)(2,1)S(1)} %collective-permute-done.16.rest_2_.refs_14_), channel_id=1, source_target_pairs={{0,1},{1,0},{2,3},{3,2},{4,5},{5,4},{6,7},{7,6},{8,9},{9,8},{10,11... | collective-permute-start | bytes 983048 | tf_op jit(solution)/shard_map/ppermute | solution.py:827
  54.4 10.0 %collective-permute-start.21 = (bf16[256,640]{1,0:T(8,128)(2,1)S(1)}, bf16[256,640]{1,0:T(8,128)(2,1)S(1)}, u32[]{:S(2)}, u32[]{:S(2)}) collective-permute-start(bf16[256,640]{1,0:T(8,128)(2,1)S(1)} %get-tuple-element.177), channel_id=1, source_target_pairs={{0,2},{1,3},{2,0},{3,1},{4,6},{5,7},{6,4},{7,5},{8,10},{9,11},{10,... | collective-permute-start | bytes 983048 | tf_op jit(solution)/shard_map/ppermute | solution.py:827
  64.4 9.3 %collective-permute-start.22 = (bf16[256,640]{1,0:T(8,128)(2,1)S(1)}, bf16[256,640]{1,0:T(8,128)(2,1)S(1)}, u32[]{:S(2)}, u32[]{:S(2)}) collective-permute-start(bf16[256,640]{1,0:T(8,128)(2,1)S(1)} %collective-permute-done.21.rest_2_), channel_id=1, source_target_pairs={{0,4},{4,0},{8,12},{12,8},{16,20},{20,16},{24,28},{28,24},{1,5},{5... | collective-permute-start | bytes 983048 | tf_op jit(solution)/shard_map/ppermute | solution.py:827
  65.7 8.3 %collective-permute-start.20 = (bf16[512,640]{1,0:T(8,128)(2,1)S(1)}, bf16[512,640]{1,0:T(8,128)(2,1)S(1)}, u32[]{:S(2)}, u32[]{:S(2)}) collective-permute-start(bf16[512,640]{1,0:T(8,128)(2,1)S(1)} %copy-done.17), channel_id=1, source_target_pairs={{0,1},{1,0},{2,3},{3,2},{4,5},{5,4},{6,7},{7,6},{8,9},{9,8},{10,11... | collective-permute-start | bytes 1966088 | tf_op jit(solution)/shard_map/ppermute | solution.py:827
  86.4 11.9 %collective-permute-start.25 = (bf16[2,2560,128]{2,1,0:T(8,128)(2,1)S(1)}, bf16[2,2560,128]{2,1,0:T(8,128)(2,1)S(1)}, u32[]{:S(2)}, u32[]{:S(2)}) collective-permute-start(bf16[2,2560,128]{2,1,0:T(8,128)(2,1)S(1)} %bitcast.39), channel_id=1, source_target_pairs={{0,1},{1,0},{2,3},{3,2},{4,5},{5,4},{6,7},{7,6},{8,9},{9,8},{10,11... | collective-permute-start | bytes 3932168 | tf_op jit(solution)/shard_map/ppermute | solution.py:938
  97.9 14.0 %collective-permute-start.27 = (bf16[2,2560,128]{2,1,0:T(8,128)(2,1)S(1)}, bf16[2,2560,128]{2,1,0:T(8,128)(2,1)S(1)}, u32[]{:S(2)}, u32[]{:S(2)}) collective-permute-start(bf16[2,2560,128]{2,1,0:T(8,128)(2,1)S(1)} %bitcast.38), channel_id=1, source_target_pairs={{0,1},{1,0},{2,3},{3,2},{4,5},{5,4},{6,7},{7,6},{8,9},{9,8},{10,11... | collective-permute-start | bytes 3932168 | tf_op jit(solution)/shard_map/ppermute | solution.py:938
  99.5 12.4 %collective-permute-start.26 = (bf16[2,1280,128]{2,1,0:T(8,128)(2,1)S(1)}, bf16[2,1280,128]{2,1,0:T(8,128)(2,1)S(1)}, u32[]{:S(2)}, u32[]{:S(2)}) collective-permute-start(bf16[2,1280,128]{2,1,0:T(8,128)(2,1)S(1)} %get-tuple-element.188), channel_id=1, source_target_pairs={{0,2},{1,5},{2,0},{3,7},{4,6},{5,1},{6,4},{7,3},{8,10},{9,13},{10,... | collective-permute-start | bytes 1966088 | tf_op jit(solution)/shard_map/ppermute | solution.py:938
  111.7 28.9 %collective-permute-start.32 = (bf16[2,2560,128]{2,1,0:T(8,128)(2,1)S(1)}, bf16[2,2560,128]{2,1,0:T(8,128)(2,1)S(1)}, u32[]{:S(2)}, u32[]{:S(2)}) collective-permute-start(bf16[2,2560,128]{2,1,0:T(8,128)(2,1)S(1)} %bitcast.37), channel_id=1, source_target_pairs={{0,1},{1,0},{2,3},{3,2},{4,5},{5,4},{6,7},{7,6},{8,9},{9,8},{10,11... | collective-permute-start | bytes 3932168 | tf_op jit(solution)/shard_map/ppermute | solution.py:938
  113.9 14.2 %collective-permute-start.29 = (bf16[2,1280,128]{2,1,0:T(8,128)(2,1)S(1)}, bf16[2,1280,128]{2,1,0:T(8,128)(2,1)S(1)}, u32[]{:S(2)}, u32[]{:S(2)}) collective-permute-start(bf16[2,1280,128]{2,1,0:T(8,128)(2,1)S(1)} %get-tuple-element.199), channel_id=1, source_target_pairs={{0,2},{1,5},{2,0},{3,7},{4,6},{5,1},{6,4},{7,3},{8,10},{9,13},{10,... | collective-permute-start | bytes 1966088 | tf_op jit(solution)/shard_map/ppermute | solution.py:938
  115.0 10.6 %collective-permute-start.28 = (bf16[1280,128]{1,0:T(8,128)(2,1)S(1)}, bf16[1280,128]{1,0:T(8,128)(2,1)S(1)}, u32[]{:S(2)}, u32[]{:S(2)}) collective-permute-start(bf16[1280,128]{1,0:T(8,128)(2,1)S(1)} %get-tuple-element.195), channel_id=1, source_target_pairs={{0,4},{1,3},{2,6},{3,1},{4,0},{5,7},{6,2},{7,5},{8,12},{9,11},{10,... | collective-permute-start | bytes 983048 | tf_op jit(solution)/shard_map/ppermute | solution.py:938
  124.5 11.8 %collective-permute-start.33 = (bf16[2,1280,128]{2,1,0:T(8,128)(2,1)S(1)}, bf16[2,1280,128]{2,1,0:T(8,128)(2,1)S(1)}, u32[]{:S(2)}, u32[]{:S(2)}) collective-permute-start(bf16[2,1280,128]{2,1,0:T(8,128)(2,1)S(1)} %bitcast.40), channel_id=1, source_target_pairs={{0,1},{1,0},{2,3},{3,2},{4,5},{5,4},{6,7},{7,6},{8,9},{9,8},{10,11... | collective-permute-start | bytes 1966088 | tf_op jit(solution)/shard_map/ppermute | solution.py:938
  126.3 9.4 %collective-permute-start.30 = (bf16[640,128]{1,0:T(8,128)(2,1)S(1)}, bf16[640,128]{1,0:T(8,128)(2,1)S(1)}, u32[]{:S(2)}, u32[]{:S(2)}) collective-permute-start(bf16[640,128]{1,0:T(8,128)(2,1)S(1)} %get-tuple-element.210), channel_id=1, source_target_pairs={{0,8},{1,9},{2,10},{3,11},{4,12},{5,13},{6,14},{7,15},{8,0},{9,1},... | collective-permute-start | bytes 491528 | tf_op jit(solution)/shard_map/ppermute | solution.py:938
  128.8 11.9 %collective-permute-start.31 = (bf16[1280,128]{1,0:T(8,128)(2,1)S(1)}, bf16[1280,128]{1,0:T(8,128)(2,1)S(1)}, u32[]{:S(2)}, u32[]{:S(2)}) collective-permute-start(bf16[1280,128]{1,0:T(8,128)(2,1)S(1)} %get-tuple-element.213), channel_id=1, source_target_pairs={{0,4},{1,3},{2,6},{3,1},{4,0},{5,7},{6,2},{7,5},{8,12},{9,11},{10,... | collective-permute-start | bytes 983048 | tf_op jit(solution)/shard_map/ppermute | solution.py:938
  136.3 15.7 %collective-permute-start.34 = (bf16[640,128]{1,0:T(8,128)(2,1)S(1)}, bf16[640,128]{1,0:T(8,128)(2,1)S(1)}, u32[]{:S(2)}, u32[]{:S(2)}) collective-permute-start(bf16[640,128]{1,0:T(8,128)(2,1)S(1)} %mix_sum.8.k), channel_id=1, source_target_pairs={{0,16},{1,17},{2,18},{3,19},{4,20},{5,21},{6,22},{7,23},{8,24},{9,... | collective-permute-start | bytes 491528 | tf_op jit(solution)/shard_map/ppermute | solution.py:938
  138.9 14.2 %collective-permute-start.36 = (bf16[512,512]{1,0:T(8,128)(2,1)S(1)}, bf16[512,512]{1,0:T(8,128)(2,1)S(1)}, u32[]{:S(2)}, u32[]{:S(2)}) collective-permute-start(bf16[512,512]{1,0:T(8,128)(2,1)S(1)} %get-tuple-element.244), channel_id=1, source_target_pairs={{1,0},{2,1},{3,2},{4,3},{5,4},{6,5},{7,6},{9,8},{10,9},{11,10},{12... | collective-permute-start | bytes 1572872 | tf_op jit(solution)/shard_map/ppermute | solution.py:1269
  141.3 11.3 %collective-permute-start.35 = (bf16[640,128]{1,0:T(8,128)(2,1)S(1)}, bf16[640,128]{1,0:T(8,128)(2,1)S(1)}, u32[]{:S(2)}, u32[]{:S(2)}) collective-permute-start(bf16[640,128]{1,0:T(8,128)(2,1)S(1)} %get-tuple-element.225), channel_id=1, source_target_pairs={{0,8},{1,9},{2,10},{3,11},{4,12},{5,13},{6,14},{7,15},{8,0},{9,1},... | collective-permute-start | bytes 491528 | tf_op jit(solution)/shard_map/ppermute | solution.py:938
  144.6 15.0 %collective-permute-start.37 = (bf16[2,1920,128]{2,1,0:T(8,128)(2,1)S(1)}, bf16[2,1920,128]{2,1,0:T(8,128)(2,1)S(1)}, u32[]{:S(2)}, u32[]{:S(2)}) collective-permute-start(bf16[2,1920,128]{2,1,0:T(8,128)(2,1)S(1)} %get-tuple-element.232), channel_id=1, source_target_pairs={{0,2},{1,5},{2,0},{3,7},{4,6},{5,1},{6,4},{7,3},{8,10},{9,13},{10,... | collective-permute-start | bytes 2949128 | tf_op jit(solution)/shard_map/ppermute | solution.py:938
  157.6 11.5 %collective-permute-start.39 = (bf16[2,2048,128]{2,1,0:T(8,128)(2,1)S(1)}, bf16[2,2048,128]{2,1,0:T(8,128)(2,1)S(1)}, u32[]{:S(2)}, u32[]{:S(2)}) collective-permute-start(bf16[2,2048,128]{2,1,0:T(8,128)(2,1)S(1)} %get-tuple-element.260), channel_id=1, source_target_pairs={{0,1},{1,0},{2,3},{3,2},{4,5},{5,4},{6,7},{7,6},{8,9},{9,8},{10,11... | collective-permute-start | bytes 3145736 | tf_op jit(solution)/shard_map/ppermute | solution.py:938
  157.6 10.9 %collective-permute-start.38 = (bf16[640,128]{1,0:T(8,128)(2,1)S(1)}, bf16[640,128]{1,0:T(8,128)(2,1)S(1)}, u32[]{:S(2)}, u32[]{:S(2)}) collective-permute-start(bf16[640,128]{1,0:T(8,128)(2,1)S(1)} %mix_sum.10.k), channel_id=1, source_target_pairs={{0,16},{1,17},{2,18},{3,19},{4,20},{5,21},{6,22},{7,23},{8,24},{9,... | collective-permute-start | bytes 491528 | tf_op jit(solution)/shard_map/ppermute | solution.py:938
  160.4 10.3 %collective-permute-start.40 = (bf16[1920,128]{1,0:T(8,128)(2,1)S(1)}, bf16[1920,128]{1,0:T(8,128)(2,1)S(1)}, u32[]{:S(2)}, u32[]{:S(2)}) collective-permute-start(bf16[1920,128]{1,0:T(8,128)(2,1)S(1)} %get-tuple-element.255), channel_id=1, source_target_pairs={{0,4},{1,3},{2,6},{3,1},{4,0},{5,7},{6,2},{7,5},{8,12},{9,11},{10,... | collective-permute-start | bytes 1474568 | tf_op jit(solution)/shard_map/ppermute | solution.py:938
  170.2 9.2 %collective-permute-start.41 = (bf16[2,1024,128]{2,1,0:T(8,128)(2,1)S(1)}, bf16[2,1024,128]{2,1,0:T(8,128)(2,1)S(1)}, u32[]{:S(2)}, u32[]{:S(2)}) collective-permute-start(bf16[2,1024,128]{2,1,0:T(8,128)(2,1)S(1)} %get-tuple-element.264), channel_id=1, source_target_pairs={{0,2},{1,5},{2,0},{3,7},{4,6},{5,1},{6,4},{7,3},{8,10},{9,13},{10,... | collective-permute-start | bytes 1572872 | tf_op jit(solution)/shard_map/ppermute | solution.py:938
  171.3 9.7 %collective-permute-start.42 = (bf16[960,128]{1,0:T(8,128)(2,1)S(1)}, bf16[960,128]{1,0:T(8,128)(2,1)S(1)}, u32[]{:S(2)}, u32[]{:S(2)}) collective-permute-start(bf16[960,128]{1,0:T(8,128)(2,1)S(1)} %get-tuple-element.267), channel_id=1, source_target_pairs={{0,8},{1,9},{2,10},{3,11},{4,12},{5,13},{6,14},{7,15},{8,0},{9,1},... | collective-permute-start | bytes 737288 | tf_op jit(solution)/shard_map/ppermute | solution.py:938
  180.2 8.9 %collective-permute-start.43 = (bf16[1024,128]{1,0:T(8,128)(2,1)S(1)}, bf16[1024,128]{1,0:T(8,128)(2,1)S(1)}, u32[]{:S(2)}, u32[]{:S(2)}) collective-permute-start(bf16[1024,128]{1,0:T(8,128)(2,1)S(1)} %get-tuple-element.272), channel_id=1, source_target_pairs={{0,4},{1,3},{2,6},{3,1},{4,0},{5,7},{6,2},{7,5},{8,12},{9,11},{10,... | collective-permute-start | bytes 786440 | tf_op jit(solution)/shard_map/ppermute | solution.py:938
  181.7 12.6 %collective-permute-start.44 = (bf16[960,128]{1,0:T(8,128)(2,1)S(1)}, bf16[960,128]{1,0:T(8,128)(2,1)S(1)}, u32[]{:S(2)}, u32[]{:S(2)}) collective-permute-start(bf16[960,128]{1,0:T(8,128)(2,1)S(1)} %mix_sum.12.k), channel_id=1, source_target_pairs={{0,16},{1,17},{2,18},{3,19},{4,20},{5,21},{6,22},{7,23},{8,24},{9,... | collective-permute-start | bytes 737288 | tf_op jit(solution)/shard_map/ppermute | solution.py:938
  182.6 17.3 %collective-permute-start.58 = (bf16[640,128]{1,0:T(8,128)(2,1)S(1)}, bf16[640,128]{1,0:T(8,128)(2,1)S(1)}, u32[]{:S(2)}, u32[]{:S(2)}) collective-permute-start(bf16[640,128]{1,0:T(8,128)(2,1)S(1)} %mix_sum.9.refs_0_), channel_id=1, source_target_pairs={{0,12},{1,13},{2,14},{3,15},{4,8},{5,9},{6,10},{7,11},{8,4},{9,5},... | collective-permute-start | bytes 491528 | tf_op jit(solution)/shard_map/ppermute | solution.py:938
  189.8 11.7 %collective-permute-start.57 = (bf16[640,128]{1,0:T(8,128)(2,1)S(1)}, bf16[640,128]{1,0:T(8,128)(2,1)S(1)}, u32[]{:S(2)}, u32[]{:S(2)}) collective-permute-start(bf16[640,128]{1,0:T(8,128)(2,1)S(1)} %mix_sum.9.refs_0_), channel_id=1, source_target_pairs={{0,8},{1,9},{2,10},{3,11},{4,12},{5,13},{6,14},{7,15},{8,0},{9,1},... | collective-permute-start | bytes 491528 | tf_op jit(solution)/shard_map/ppermute | solution.py:938
  191.8 10.5 %collective-permute-start.56 = (bf16[640,128]{1,0:T(8,128)(2,1)S(1)}, bf16[640,128]{1,0:T(8,128)(2,1)S(1)}, u32[]{:S(2)}, u32[]{:S(2)}) collective-permute-start(bf16[640,128]{1,0:T(8,128)(2,1)S(1)} %mix_sum.9.refs_0_), channel_id=1, source_target_pairs={{0,4},{1,5},{2,6},{3,7},{4,0},{5,1},{6,2},{7,3},{8,12},{9,13},{10,... | collective-permute-start | bytes 491528 | tf_op jit(solution)/shard_map/ppermute | solution.py:938
  194.3 13.6 %collective-permute-start.52 = (bf16[640,128]{1,0:T(8,128)(2,1)S(1)}, bf16[640,128]{1,0:T(8,128)(2,1)S(1)}, u32[]{:S(2)}, u32[]{:S(2)}) collective-permute-start(bf16[640,128]{1,0:T(8,128)(2,1)S(1)} %mix_sum.11.refs_0_), channel_id=1, source_target_pairs={{0,12},{1,13},{2,14},{3,15},{4,8},{5,9},{6,10},{7,11},{8,4},{9,5},... | collective-permute-start | bytes 491528 | tf_op jit(solution)/shard_map/ppermute | solution.py:938
  197.6 10.3 %collective-permute-start.46 = (bf16[512,128]{1,0:T(8,128)(2,1)S(1)}, bf16[512,128]{1,0:T(8,128)(2,1)S(1)}, u32[]{:S(2)}, u32[]{:S(2)}) collective-permute-start(bf16[512,128]{1,0:T(8,128)(2,1)S(1)} %mix_sum.14.k), channel_id=1, source_target_pairs={{0,16},{1,17},{2,18},{3,19},{4,20},{5,21},{6,22},{7,23},{8,24},{9,... | collective-permute-start | bytes 393224 | tf_op jit(solution)/shard_map/ppermute | solution.py:938
  200.0 18.7 %collective-permute-start.55 = (bf16[960,128]{1,0:T(8,128)(2,1)S(1)}, bf16[960,128]{1,0:T(8,128)(2,1)S(1)}, u32[]{:S(2)}, u32[]{:S(2)}) collective-permute-start(bf16[960,128]{1,0:T(8,128)(2,1)S(1)} %mix_sum.13.refs_4_), channel_id=1, source_target_pairs={{0,12},{1,13},{2,14},{3,15},{4,8},{5,9},{6,10},{7,11},{8,4},{9,5},... | collective-permute-start | bytes 737288 | tf_op jit(solution)/shard_map/ppermute | solution.py:938
  201.5 13.6 %collective-permute-start.51 = (bf16[640,128]{1,0:T(8,128)(2,1)S(1)}, bf16[640,128]{1,0:T(8,128)(2,1)S(1)}, u32[]{:S(2)}, u32[]{:S(2)}) collective-permute-start(bf16[640,128]{1,0:T(8,128)(2,1)S(1)} %mix_sum.11.refs_0_), channel_id=1, source_target_pairs={{0,8},{1,9},{2,10},{3,11},{4,12},{5,13},{6,14},{7,15},{8,0},{9,1},... | collective-permute-start | bytes 491528 | tf_op jit(solution)/shard_map/ppermute | solution.py:938
  202.3 13.9 %collective-permute-start.50 = (bf16[640,128]{1,0:T(8,128)(2,1)S(1)}, bf16[640,128]{1,0:T(8,128)(2,1)S(1)}, u32[]{:S(2)}, u32[]{:S(2)}) collective-permute-start(bf16[640,128]{1,0:T(8,128)(2,1)S(1)} %mix_sum.11.refs_0_), channel_id=1, source_target_pairs={{0,4},{1,5},{2,6},{3,7},{4,0},{5,1},{6,2},{7,3},{8,12},{9,13},{10,... | collective-permute-start | bytes 491528 | tf_op jit(solution)/shard_map/ppermute | solution.py:938
  207.9 12.5 %collective-permute-start.54 = (bf16[960,128]{1,0:T(8,128)(2,1)S(1)}, bf16[960,128]{1,0:T(8,128)(2,1)S(1)}, u32[]{:S(2)}, u32[]{:S(2)}) collective-permute-start(bf16[960,128]{1,0:T(8,128)(2,1)S(1)} %mix_sum.13.refs_4_), channel_id=1, source_target_pairs={{0,8},{1,9},{2,10},{3,11},{4,12},{5,13},{6,14},{7,15},{8,0},{9,1},... | collective-permute-start | bytes 737288 | tf_op jit(solution)/shard_map/ppermute | solution.py:938
  207.9 12.5 %collective-permute-start.53 = (bf16[960,128]{1,0:T(8,128)(2,1)S(1)}, bf16[960,128]{1,0:T(8,128)(2,1)S(1)}, u32[]{:S(2)}, u32[]{:S(2)}) collective-permute-start(bf16[960,128]{1,0:T(8,128)(2,1)S(1)} %mix_sum.13.refs_4_), channel_id=1, source_target_pairs={{0,4},{1,5},{2,6},{3,7},{4,0},{5,1},{6,2},{7,3},{8,12},{9,13},{10,... | collective-permute-start | bytes 737288 | tf_op jit(solution)/shard_map/ppermute | solution.py:938
  215.1 9.5 %collective-permute-start.49 = (bf16[512,128]{1,0:T(8,128)(2,1)S(1)}, bf16[512,128]{1,0:T(8,128)(2,1)S(1)}, u32[]{:S(2)}, u32[]{:S(2)}) collective-permute-start(bf16[512,128]{1,0:T(8,128)(2,1)S(1)} %mix_sum.15.refs_0_), channel_id=1, source_target_pairs={{0,12},{1,13},{2,14},{3,15},{4,8},{5,9},{6,10},{7,11},{8,4},{9,5},... | collective-permute-start | bytes 393224 | tf_op jit(solution)/shard_map/ppermute | solution.py:938
  216.1 8.7 %collective-permute-start.48 = (bf16[512,128]{1,0:T(8,128)(2,1)S(1)}, bf16[512,128]{1,0:T(8,128)(2,1)S(1)}, u32[]{:S(2)}, u32[]{:S(2)}) collective-permute-start(bf16[512,128]{1,0:T(8,128)(2,1)S(1)} %mix_sum.15.refs_0_), channel_id=1, source_target_pairs={{0,8},{1,9},{2,10},{3,11},{4,12},{5,13},{6,14},{7,15},{8,0},{9,1},... | collective-permute-start | bytes 393224 | tf_op jit(solution)/shard_map/ppermute | solution.py:938
  (51 other events, 258.3 us)

commit v6 on v5

--- a/solution.py
+++ b/solution.py
@@ -45,7 +45,7 @@
 
 
 def cost(flops, nbytes):
-    return pl.CostEstimate(flops=int(flops), bytes_accessed=int(nbytes), transcendentals=0)
+    return pl.CostEstimate(flops=int(1.5 * flops), bytes_accessed=int(1.5 * nbytes), transcendentals=0)
 
 
 def rms_factor(v):

time: 231 us -> 241 us (1.043)
  waiting for transfers between devices: 38.7 us -> 53.5 us
  starting transfers between devices: 56.9 us -> 53.2 us
    ppermute x24, waiting for transfers between devices: 7.6 us -> 20.7 us  [flip(): return lax.ppermute(x, axis, [(i, i ^ bit) for i in range(n)])]
    ppermute x24, starting transfers between devices: 20 us -> 17.4 us  [flip(): return lax.ppermute(x, axis, [(i, i ^ bit) for i in range(n)])]
    unnamed x80 -> x84, local copies, waits for them, and re-layouts: 5.21 us -> 3.75 us
  transfers between devices with their start and end apart: 59 -> 59, of which waited for: 18 -> 19; matrix products, arithmetic and copies ran while one was open for 1% -> 1% of each run, Pallas kernels for 48% -> 45%
where the time goes in v6:
time: 241 us; the launch traced here: 237 us
  Pallas kernels  123 us (51%)
  waiting for transfers between devices  53.5 us (22%)
  starting transfers between devices  53.2 us (22%)
  local copies, waits for them, and re-layouts  3.84 us (2%)
    ppermute x33, waiting for transfers between devices, send(): return lax.ppermute(x, ('seq', 'shard'), pairs)  32.8 us
    ppermute x33, starting transfers between devices, send(): return lax.ppermute(x, ('seq', 'shard'), pairs)  31.6 us
    pallas_call x2, Pallas kernels, fb(): pl.pallas_call(body, out_shape=(sds((2, 2, FH // 128, D // 4, 128)),) * 2...  22.5 us
    ppermute x24, waiting for transfers between devices, flip(): return lax.ppermute(x, axis, [(i, i ^ bit) for i in range(n)])  20.7 us
    ppermute x24, starting transfers between devices, flip(): return lax.ppermute(x, axis, [(i, i ^ bit) for i in range(n)])  17.4 us
    pallas_call x20, Pallas kernels, small_call(): pl.pallas_call(body, out_shape=tuple((sds(r + (128,)) for r in out_rows))...  15.3 us
    pallas_call x2, Pallas kernels, ff(): pl.pallas_call(up_kernel if before else gate_kernel, out_shape=(sds((t, F...  13.9 us
    pallas_call x2, Pallas kernels, att_back(): pl.pallas_call(att_back_kernel, grid=(1,), out_shape=(sds((HALF, HEADS *...  11.4 us
  transfers between devices with their start and end apart: 59, of which 19 were waited for; matrix products, arithmetic and copies ran while one was open for 1% of the time, Pallas kernels for 45%

profile of v6, /device:TPU:0, one launch (start us, length us, event | category | flops | bytes accessed | tf_op | source)
XLA Modules:
  0.0 236.8 jit_solution(1545836447831650878)
XLA Ops:
  0.8 1.6 pack.1.g0.w0.k0
  2.3 3.0 %collective-permute-start.1 = (bf16[176,512]{1,0:T(8,128)(2,1)S(1)}, bf16[176,512]{1,0:T(8,128)(2,1)S(1)}, u32[]{:S(2)}, u32[]{:S(2)}) collective-permute-start(bf16[176,512]{1,0:T(8,128)(2,1)S(1)} %pack.1.g0.w0.k0), channel_id=1, source_target_pairs={{0,2},{1,3},{2,0},{3,1},{4,6},{5,7},{6,4},{7,5},{8,10},{9,11},{10,... | collective-permute-start | bytes 540680 | tf_op jit(solution)/shard_map/ppermute | solution.py:827
  5.9 1.7 collective-permute-start.6
  7.6 1.7 halves.1
  10.8 1.9 multiply_sine_fusion
  12.7 2.1 collective-permute-start.7
  15.7 3.2 %pre_kv.1 = (bf16[1024,640]{1,0:T(8,128)(2,1)S(1)}, bf16[1024,256]{1,0:T(8,128)(2,1)S(1)}, bf16[512,512]{1,0:T(8,128)(2,1)S(1)}, bf16[512,512]{1,0:T(8,128)(2,1)S(1)}) custom-call(s32[9]{0:T(128)S(1)} %stack.43.info.me_ref.refs_0_.s.i, bf16[1024,640]{1,0:T(8,128)(2,1)S(1)} %copy-done.9, f32[8,640]{1,0:T(8,128)S(1)} %gains.1, ...), custom_call_target="tpu_custom_call" | custom-call | flops 1006632960 | bytes 7500000 | tf_op jit(solution)/shard_map/pre_kv/pallas_call | solution.py:237
  19.5 11.5 %collective-permute-done.7.rest_2_.refs_8_ = bf16[80,2048]{1,0:T(8,128)(2,1)S(1)} collective-permute-done((bf16[80,2048]{1,0:T(8,128)(2,1)S(1)}, bf16[80,2048]{1,0:T(8,128)(2,1)S(1)}, u32[]{:S(2)}, u32[]{:S(2)}) %collective-permute-start.7) | collective-permute-done | bytes 327712 | tf_op jit(solution)/shard_map/ppermute | solution.py:827
  31.0 1.8 collective-permute-start.16
  33.0 2.6 %collective-permute-start.8 = (bf16[512,512]{1,0:T(8,128)(2,1)S(1)}, bf16[512,512]{1,0:T(8,128)(2,1)S(1)}, u32[]{:S(2)}, u32[]{:S(2)}) collective-permute-start(bf16[512,512]{1,0:T(8,128)(2,1)S(1)} %get-tuple-element.162.refs_3_.kvs), channel_id=1, source_target_pairs={{0,1},{1,2},{2,3},{3,4},{4,5},{5,6},{6,7},{8,9},{9,10},{10,11},{11... | collective-permute-start | bytes 1572872 | tf_op jit(solution)/shard_map/ppermute | solution.py:1212
  35.6 5.9 %pre_q.1 = (bf16[4,1024,256]{2,1,0:T(8,128)(2,1)}, bf16[4,1024,256]{2,1,0:T(8,128)(2,1)S(1)}) custom-call(s32[9]{0:T(128)S(1)} %stack.43.info.me_ref.refs_0_.s.i, bf16[1024,640]{1,0:T(8,128)(2,1)S(1)} %get-tuple-element.156.nin_i.nin, f32[8,640]{1,0:T(8,128)S(1)} %gains.1, f32[1024,128]{1,0:T(8,128)S(1)} %get-tuple-element.298.cos_ref, ...), custom_call_target="tpu_custom_call" | custom-call | flops 2013265920 | bytes 7500000 | tf_op jit(solution)/shard_map/pre_q/pallas_call | solution.py:279
  41.5 3.2 %att.2 = (bf16[512,1024]{1,0:T(8,128)(2,1)S(1)}, bf16[4,512,256]{2,1,0:T(8,128)(2,1)S(1)}, bf16[4,512,256]{2,1,0:T(8,128)(2,1)S(1)}) custom-call(s32[9]{0:T(128)S(1)} %stack.43.info.me_ref.refs_0_.s.i, bf16[4,1024,256]{2,1,0:T(8,128)(2,1)S(1)} %get-tuple-element.164.refs_1_.qs, bf16[512,512]{1,0:T(8,128)(2,1)S(1)} %get-tuple-element.161.refs_2_.refs_3_.kvs.kvp, ...), custom_call_target="tpu_custom_call" | custom-call | flops 4499999744 | bytes 7500000 | tf_op jit(solution)/shard_map/att/pallas_call | solution.py:338
  47.2 3.3 %att.3 = (bf16[512,1024]{1,0:T(8,128)(2,1)S(1)}, bf16[4,512,256]{2,1,0:T(8,128)(2,1)S(1)}, bf16[4,512,256]{2,1,0:T(8,128)(2,1)S(1)}) custom-call(s32[9]{0:T(128)S(1)} %stack.43.info.me_ref.refs_0_.s.i, bf16[4,1024,256]{2,1,0:T(8,128)(2,1)S(1)} %get-tuple-element.164.refs_1_.qs, bf16[512,512]{1,0:T(8,128)(2,1)S(1)} %collective-permute-done.8.refs_2_.kvp, ...), custom_call_target="tpu_custom_call" | custom-call | flops 4499999744 | bytes 7500000 | tf_op jit(solution)/shard_map/att/pallas_call | solution.py:338
  50.4 5.3 %collective-permute-done.12.rest_3_.refs_9_ = bf16[80,2048]{1,0:T(8,128)(2,1)S(1)} collective-permute-done((bf16[80,2048]{1,0:T(8,128)(2,1)S(1)}, bf16[80,2048]{1,0:T(8,128)(2,1)S(1)}, u32[]{:S(2)}, u32[]{:S(2)}) %collective-permute-start.12) | collective-permute-done | bytes 327712 | tf_op jit(solution)/shard_map/ppermute | solution.py:827
  57.2 4.3 %mid.1 = (bf16[1024,640]{1,0:T(8,128)(2,1)S(1)}, bf16[1024,640]{1,0:T(8,128)(2,1)S(1)}) custom-call(s32[9]{0:T(128)S(1)} %stack.43.info.me_ref.refs_0_.s.i, bf16[512,1024]{1,0:T(8,128)(2,1)S(1)} %get-tuple-element.165.o_lo, bf16[512,1024]{1,0:T(8,128)(2,1)S(1)} %get-tuple-element.163.o_hi, bf16[1024,640]{1,0:T(8,128)(2,1)S(1)} %copy-done.9, ...), custom_call_target="tpu_custom_call" | custom-call | flops 2013265920 | bytes 12000000 | tf_op jit(solution)/shard_map/mid/pallas_call | solution.py:434
  61.5 1.6 collective-permute-start.17
  64.8 7.3 %gate.1 = (bf16[1024,2048]{1,0:T(8,128)(2,1)S(1)}, bf16[1024,2048]{1,0:T(8,128)(2,1)S(1)}) custom-call(s32[9]{0:T(128)S(1)} %stack.43.info.me_ref.refs_0_.s.i, bf16[1024,640]{1,0:T(8,128)(2,1)S(1)} %get-tuple-element.166.nm.refs_1_, bf16[160,2048]{1,0:T(8,128)(2,1)} %refs_6_.4, bf16[160,2048]{1,0:T(8,128)(2,1)} %copy-done.20, bf16[80,2048]{1,0:T(8,128)(2,1)} %copy-done.30, ...), custom_call_target="tpu_custom_call" | custom-call | flops 4026531840 | bytes 18000000 | tf_op jit(solution)/shard_map/gate/pallas_call | solution.py:509
  72.8 1.7 collective-permute-start.22
  75.5 6.6 %up.1 = (bf16[1024,2048]{1,0:T(8,128)(2,1)S(1)}, bf16[1024,2048]{1,0:T(8,128)(2,1)S(1)}) custom-call(s32[9]{0:T(128)S(1)} %stack.43.info.me_ref.refs_0_.s.i, bf16[1024,640]{1,0:T(8,128)(2,1)S(1)} %get-tuple-element.166.nm.refs_1_, bf16[1024,2048]{1,0:T(8,128)(2,1)S(1)} %get-tuple-element.168.a_i.refs_3_, bf16[1024,2048]{1,0:T(8,128)(2,1)S(1)} %get-tuple-element.169.s_i, ...), custom_call_target="tpu_custom_call" | custom-call | flops 4026531840 | bytes 18000000 | tf_op jit(solution)/shard_map/up/pallas_call | solution.py:509
  83.0 1.6 collective-permute-done.24.rest_5_
  85.3 10.2 %down.1 = (bf16[1024,640]{1,0:T(8,128)(2,1)}, bf16[1024,640]{1,0:T(8,128)(2,1)S(1)}, bf16[2048,640]{1,0:T(8,128)(2,1)S(1)}, bf16[2,5,512,128]{3,2,1,0:T(8,128)(2...) custom-call(s32[9]{0:T(128)S(1)} %stack.43.info.me_ref.refs_0_.s.i, ...), custom_call_target="tpu_custom_call" | custom-call | flops 8053063680 | bytes 30000000 | tf_op jit(solution)/shard_map/down/pallas_call | solution.py:552
  95.8 11.3 %fb.2 = (bf16[2,2,8,160,128]{4,3,2,1,0:T(8,128)(2,1)S(1)}, bf16[2,2,8,160,128]{4,3,2,1,0:T(8,128)(2,1)S(1)}, f32[1024,640]{1,0:T(8,128)S(1)}) custom-call(s32[9]{0:T(128)S(1)} %stack.43.info.me_ref.refs_0_.s.i, bf16[1024,640]{1,0:T(8,128)(2,1)S(1)} %get-tuple-element.166.nm.refs_1_, bf16[1024,640]{1,0:T(8,128)(2,1)S(1)} %get-tuple-element.181.refs_2_, ...), custom_call_target="tpu_custom_call" | custom-call | flops 10066329600 | bytes 24000000 | tf_op jit(solution)/shard_map/fb/pallas_call | solution.py:621
  108.8 1.6 collective-permute-start.26
  110.4 11.2 %fb.3 = (bf16[2,2,8,160,128]{4,3,2,1,0:T(8,128)(2,1)S(1)}, bf16[2,2,8,160,128]{4,3,2,1,0:T(8,128)(2,1)S(1)}, f32[1024,640]{1,0:T(8,128)S(1)}) custom-call(s32[9]{0:T(128)S(1)} %stack.43.info.me_ref.refs_0_.s.i, bf16[1024,640]{1,0:T(8,128)(2,1)S(1)} %get-tuple-element.166.nm.refs_1_, bf16[1024,640]{1,0:T(8,128)(2,1)S(1)} %get-tuple-element.181.refs_2_, ...), custom_call_target="tpu_custom_call" | custom-call | flops 10066329600 | bytes 24000000 | tf_op jit(solution)/shard_map/fb/pallas_call | solution.py:621
  124.2 1.6 collective-permute-start.28
  125.9 8.3 %fe.1 = (bf16[2,5,256,128]{3,2,1,0:T(8,128)(2,1)S(1)}, bf16[2,5,256,128]{3,2,1,0:T(8,128)(2,1)S(1)}, bf16[4,1024,256]{2,1,0:T(8,128)(2,1)S(1)}, bf16[1024,640]{1,0:T(8,128)(2,1)S(1)}, f32[16,640]{1,0:T(8,128)S(1)}) custom-call(s32[9]{0:T(128)S(1)} %stack.43.info.me_ref.refs_0_.s.i, bf16[512,1024]{1,0:T(8,128)(2,1)S(1)} %copy-done.12, ...), custom_call_target="tpu_custom_call" | custom-call | flops 4026531840 | bytes 21000000 | tf_op jit(solution)/shard_map/fe/pallas_call | solution.py:676
  135.5 1.6 collective-permute-start.30
  139.8 5.7 %att_back.2 = (bf16[512,1024]{1,0:T(8,128)(2,1)S(1)}, bf16[512,512]{1,0:T(8,128)(2,1)S(1)}, f32[512,512]{1,0:T(8,128)S(1)}, f32[8,256]{1,0:T(8,128)S(1)}) custom-call(bf16[4,1024,256]{2,1,0:T(8,128)(2,1)S(1)} %get-tuple-element.164.refs_1_.qs, bf16[4,1024,256]{2,1,0:T(8,128)(2,1)S(1)} %copy-done.10, bf16[512,512]{1,0:T(8,128)(2,1)S(1)} %collective-permute-done.8.refs_2_.kvp, ...), custom_call_target="tpu_custom_call" | custom-call | flops 8999999488 | bytes 13500000 | tf_op jit(solution)/shard_map/att_back/pallas_call | solution.py:399
  146.1 2.7 %collective-permute-start.34 = (bf16[640,128]{1,0:T(8,128)(2,1)S(1)}, bf16[640,128]{1,0:T(8,128)(2,1)S(1)}, u32[]{:S(2)}, u32[]{:S(2)}) collective-permute-start(bf16[640,128]{1,0:T(8,128)(2,1)S(1)} %mix_sum.8.k), channel_id=1, source_target_pairs={{0,16},{1,17},{2,18},{3,19},{4,20},{5,21},{6,22},{7,23},{8,24},{9,... | collective-permute-start | bytes 491528 | tf_op jit(solution)/shard_map/ppermute | solution.py:938
  148.8 1.7 collective-permute-start.36
  151.1 1.6 collective-permute-start.35
  152.8 1.6 mix_first.6
  154.4 1.6 collective-permute-start.37
  156.0 5.7 %att_back.3 = (bf16[512,1024]{1,0:T(8,128)(2,1)S(1)}, bf16[512,512]{1,0:T(8,128)(2,1)S(1)}, f32[512,512]{1,0:T(8,128)S(1)}, f32[8,256]{1,0:T(8,128)S(1)}) custom-call(bf16[4,1024,256]{2,1,0:T(8,128)(2,1)S(1)} %get-tuple-element.164.refs_1_.qs, bf16[4,1024,256]{2,1,0:T(8,128)(2,1)S(1)} %copy-done.10, ...), custom_call_target="tpu_custom_call" | custom-call | flops 8999999488 | bytes 13500000 | tf_op jit(solution)/shard_map/att_back/pallas_call | solution.py:399
  162.9 4.5 %post.1 = (bf16[1024,512]{1,0:T(8,128)(2,1)S(1)}, bf16[2,2048,128]{2,1,0:T(8,128)(2,1)S(1)}, bf16[2,2048,128]{2,1,0:T(8,128)(2,1)S(1)}) custom-call(s32[9]{0:T(128)S(1)} %stack.43.info.me_ref.refs_0_.s.i, bf16[1024,640]{1,0:T(8,128)(2,1)S(1)} %get-tuple-element.156.nin_i.nin, bf16[512,1024]{1,0:T(8,128)(2,1)S(1)} %get-tuple-element.215.dq_lo, ...), custom_call_target="tpu_custom_call" | custom-call | flops 3000000000 | bytes 15000000 | tf_op jit(solution)/shard_map/post/pallas_call | solution.py:768
  167.8 1.5 collective-permute-done.37.g
  170.9 6.8 %last.1 = bf16[1024,640]{1,0:T(8,128)(2,1)} custom-call(s32[9]{0:T(128)S(1)} %stack.43.info.me_ref.refs_0_.s.i, bf16[1024,640]{1,0:T(8,128)(2,1)S(1)} %copy-done.9, bf16[1024,640]{1,0:T(8,128)(2,1)S(1)} %get-tuple-element.201.dmid, bf16[512,1024]{1,0:T(8,128)(2,1)S(1)} %get-tuple-element.215.dq_lo, bf16[512,1024]{1,0:T(8,128)(2,1)S(1)} %get-tuple-element.240.dq_hi, ...), custom_call_target="tpu_custom_call" | custom-call | flops 3000000000 | bytes 12000000 | tf_op jit(solution)/shard_map/last/pallas_call | solution.py:809
  182.5 6.8 %collective-permute-done.41.g = bf16[2,1024,128]{2,1,0:T(8,128)(2,1)S(1)} collective-permute-done((bf16[2,1024,128]{2,1,0:T(8,128)(2,1)S(1)}, bf16[2,1024,128]{2,1,0:T(8,128)(2,1)S(1)}, u32[]{:S(2)}, u32[]{:S(2)}) %collective-permute-start.41) | collective-permute-done | bytes 524320 | tf_op jit(solution)/shard_map/ppermute | solution.py:938
  193.4 5.7 %collective-permute-done.43 = bf16[1024,128]{1,0:T(8,128)(2,1)S(1)} collective-permute-done((bf16[1024,128]{1,0:T(8,128)(2,1)S(1)}, bf16[1024,128]{1,0:T(8,128)(2,1)S(1)}, u32[]{:S(2)}, u32[]{:S(2)}) %collective-permute-start.43) | collective-permute-done | bytes 262176 | tf_op jit(solution)/shard_map/ppermute | solution.py:938
  199.8 2.0 collective-permute-start.57
  204.9 2.3 collective-permute-done.45.g
  207.7 2.0 collective-permute-start.46
  213.2 4.4 %collective-permute-done.52.refs_3_ = bf16[640,128]{1,0:T(8,128)(2,1)S(1)} collective-permute-done((bf16[640,128]{1,0:T(8,128)(2,1)S(1)}, bf16[640,128]{1,0:T(8,128)(2,1)S(1)}, u32[]{:S(2)}, u32[]{:S(2)}) %collective-permute-start.52) | collective-permute-done | bytes 163872 | tf_op jit(solution)/shard_map/ppermute | solution.py:938
  218.9 6.7 %collective-permute-done.51.refs_2_ = bf16[640,128]{1,0:T(8,128)(2,1)S(1)} collective-permute-done((bf16[640,128]{1,0:T(8,128)(2,1)S(1)}, bf16[640,128]{1,0:T(8,128)(2,1)S(1)}, u32[]{:S(2)}, u32[]{:S(2)}) %collective-permute-start.51) | collective-permute-done | bytes 163872 | tf_op jit(solution)/shard_map/ppermute | solution.py:938
  225.9 2.5 %collective-permute-start.48 = (bf16[512,128]{1,0:T(8,128)(2,1)S(1)}, bf16[512,128]{1,0:T(8,128)(2,1)S(1)}, u32[]{:S(2)}, u32[]{:S(2)}) collective-permute-start(bf16[512,128]{1,0:T(8,128)(2,1)S(1)} %mix_sum.15.refs_0_), channel_id=1, source_target_pairs={{0,8},{1,9},{2,10},{3,11},{4,12},{5,13},{6,14},{7,15},{8,0},{9,1},... | collective-permute-start | bytes 393224 | tf_op jit(solution)/shard_map/ppermute | solution.py:938
  229.0 1.7 finish_one.1
  230.8 2.5 %finish_two.1 = (f32[160,2048]{1,0:T(8,128)}, f32[160,2048]{1,0:T(8,128)}, f32[256,640]{1,0:T(8,128)}) custom-call(s32[9]{0:T(128)S(1)} %stack.43.info.me_ref.refs_0_.s.i, bf16[640,128]{1,0:T(8,128)(2,1)S(1)} %mix_sum.11.refs_0_, bf16[640,128]{1,0:T(8,128)(2,1)S(1)} %collective-permute-done.50.refs_1_, bf16[640,128]{1,0:T(8,128)(2,1)S(1)} %collective-permute-done.51.refs_2_, ...), custom_call_target="tpu_custom_call" | custom-call | flops 15000000 | bytes 15000000 | tf_op jit(solution)/shard_map/finish_two/pallas_call | solution.py:1074
  235.0 1.7 finish_three.1
  (199 shorter events, 45.8 us)
Async XLA Ops:
  5.4 13.5 %collective-permute-start.4 = (bf16[160,1024]{1,0:T(8,128)(2,1)}, bf16[160,1024]{1,0:T(8,128)(2,1)S(1)}, u32[]{:S(2)}, u32[]{:S(2)}) collective-permute-start(bf16[160,1024]{1,0:T(8,128)(2,1)} %refs_4_.1), channel_id=1, source_target_pairs={{0,2},{1,3},{2,0},{3,1},{4,6},{5,7},{6,4},{7,5},{8,10},{9,11},{10,... | collective-permute-start | bytes 983048 | tf_op jit(solution)/shard_map/ppermute | solution.py:827
  5.5 27.3 %collective-permute-start.3 = (bf16[160,1024]{1,0:T(8,128)(2,1)}, bf16[160,1024]{1,0:T(8,128)(2,1)S(1)}, u32[]{:S(2)}, u32[]{:S(2)}) collective-permute-start(bf16[160,1024]{1,0:T(8,128)(2,1)} %refs_4_.1), channel_id=1, source_target_pairs={{0,1},{1,0},{2,3},{3,2},{4,5},{5,4},{6,7},{7,6},{8,9},{9,8},{10,11... | collective-permute-start | bytes 983048 | tf_op jit(solution)/shard_map/ppermute | solution.py:827
  5.9 25.1 %collective-permute-start.6 = (bf16[256,640]{1,0:T(8,128)(2,1)}, bf16[256,640]{1,0:T(8,128)(2,1)S(1)}, u32[]{:S(2)}, u32[]{:S(2)}) collective-permute-start(bf16[256,640]{1,0:T(8,128)(2,1)} %w0.5), channel_id=1, source_target_pairs={{0,2},{1,3},{2,0},{3,1},{4,6},{5,7},{6,4},{7,5},{8,10},{9,11},{10,... | collective-permute-start | bytes 983048 | tf_op jit(solution)/shard_map/ppermute | solution.py:827
  12.7 18.3 %collective-permute-start.7 = (bf16[80,2048]{1,0:T(8,128)(2,1)S(1)}, bf16[80,2048]{1,0:T(8,128)(2,1)S(1)}, u32[]{:S(2)}, u32[]{:S(2)}) collective-permute-start(bf16[80,2048]{1,0:T(8,128)(2,1)S(1)} %get-tuple-element.159), channel_id=1, source_target_pairs={{0,2},{1,3},{2,0},{3,1},{4,6},{5,7},{6,4},{7,5},{8,10},{9,11},{10,... | collective-permute-start | bytes 983048 | tf_op jit(solution)/shard_map/ppermute | solution.py:827
  18.9 14.1 %collective-permute-start.5 = (bf16[160,1024]{1,0:T(8,128)(2,1)S(1)}, bf16[160,1024]{1,0:T(8,128)(2,1)S(1)}, u32[]{:S(2)}, u32[]{:S(2)}) collective-permute-start(bf16[160,1024]{1,0:T(8,128)(2,1)S(1)} %collective-permute-done.4.w2.q2), channel_id=1, source_target_pairs={{0,1},{1,0},{2,3},{3,2},{4,5},{5,4},{6,7},{7,6},{8,9},{9,8},{10,11... | collective-permute-start | bytes 983048 | tf_op jit(solution)/shard_map/ppermute | solution.py:827
  19.2 37.1 %collective-permute-start.9 = (bf16[256,640]{1,0:T(8,128)(2,1)S(1)}, bf16[256,640]{1,0:T(8,128)(2,1)S(1)}, u32[]{:S(2)}, u32[]{:S(2)}) collective-permute-start(bf16[256,640]{1,0:T(8,128)(2,1)S(1)} %copy-done.23), channel_id=1, source_target_pairs={{0,1},{1,0},{2,3},{3,2},{4,5},{5,4},{6,7},{7,6},{8,9},{9,8},{10,11... | collective-permute-start | bytes 983048 | tf_op jit(solution)/shard_map/ppermute | solution.py:827
  31.0 30.5 %collective-permute-start.11 = (bf16[160,2048]{1,0:T(8,128)(2,1)S(1)}, bf16[160,2048]{1,0:T(8,128)(2,1)S(1)}, u32[]{:S(2)}, u32[]{:S(2)}) collective-permute-start(bf16[160,2048]{1,0:T(8,128)(2,1)S(1)} %copy-done.18), channel_id=1, source_target_pairs={{0,1},{1,0},{2,3},{3,2},{4,5},{5,4},{6,7},{7,6},{8,9},{9,8},{10,11... | collective-permute-start | bytes 1966088 | tf_op jit(solution)/shard_map/ppermute | solution.py:827
  31.0 24.7 %collective-permute-start.16 = (bf16[80,2048]{1,0:T(8,128)(2,1)S(1)}, bf16[80,2048]{1,0:T(8,128)(2,1)S(1)}, u32[]{:S(2)}, u32[]{:S(2)}) collective-permute-start(bf16[80,2048]{1,0:T(8,128)(2,1)S(1)} %get-tuple-element.171), channel_id=1, source_target_pairs={{0,2},{1,3},{2,0},{3,1},{4,6},{5,7},{6,4},{7,5},{8,10},{9,11},{10,... | collective-permute-start | bytes 983048 | tf_op jit(solution)/shard_map/ppermute | solution.py:827
  32.8 23.6 %collective-permute-start.10 = (bf16[256,640]{1,0:T(8,128)(2,1)S(1)}, bf16[256,640]{1,0:T(8,128)(2,1)S(1)}, u32[]{:S(2)}, u32[]{:S(2)}) collective-permute-start(bf16[256,640]{1,0:T(8,128)(2,1)S(1)} %collective-permute-done.6.w2), channel_id=1, source_target_pairs={{0,1},{1,0},{2,3},{3,2},{4,5},{5,4},{6,7},{7,6},{8,9},{9,8},{10,11... | collective-permute-start | bytes 983048 | tf_op jit(solution)/shard_map/ppermute | solution.py:827
  33.0 12.7 %collective-permute-start.8 = (bf16[512,512]{1,0:T(8,128)(2,1)S(1)}, bf16[512,512]{1,0:T(8,128)(2,1)S(1)}, u32[]{:S(2)}, u32[]{:S(2)}) collective-permute-start(bf16[512,512]{1,0:T(8,128)(2,1)S(1)} %get-tuple-element.162.refs_3_.kvs), channel_id=1, source_target_pairs={{0,1},{1,2},{2,3},{3,4},{4,5},{5,6},{6,7},{8,9},{9,10},{10,11},{11... | collective-permute-start | bytes 1572872 | tf_op jit(solution)/shard_map/ppermute | solution.py:1212
  45.7 10.1 %collective-permute-start.12 = (bf16[80,2048]{1,0:T(8,128)(2,1)S(1)}, bf16[80,2048]{1,0:T(8,128)(2,1)S(1)}, u32[]{:S(2)}, u32[]{:S(2)}) collective-permute-start(bf16[80,2048]{1,0:T(8,128)(2,1)S(1)} %collective-permute-done.7.rest_2_.refs_8_), channel_id=1, source_target_pairs={{0,4},{4,0},{8,12},{12,8},{16,20},{20,16},{24,28},{28,24},{1,5},{5... | collective-permute-start | bytes 983048 | tf_op jit(solution)/shard_map/ppermute | solution.py:827
  56.3 16.5 %collective-permute-start.15 = (bf16[160,2048]{1,0:T(8,128)(2,1)S(1)}, bf16[160,2048]{1,0:T(8,128)(2,1)S(1)}, u32[]{:S(2)}, u32[]{:S(2)}) collective-permute-start(bf16[160,2048]{1,0:T(8,128)(2,1)S(1)} %copy-done.19), channel_id=1, source_target_pairs={{0,1},{1,0},{2,3},{3,2},{4,5},{5,4},{6,7},{7,6},{8,9},{9,8},{10,11... | collective-permute-start | bytes 1966088 | tf_op jit(solution)/shard_map/ppermute | solution.py:827
  56.4 18.1 %collective-permute-start.18 = (bf16[80,2048]{1,0:T(8,128)(2,1)S(1)}, bf16[80,2048]{1,0:T(8,128)(2,1)S(1)}, u32[]{:S(2)}, u32[]{:S(2)}) collective-permute-start(bf16[80,2048]{1,0:T(8,128)(2,1)S(1)} %collective-permute-done.16.rest_2_.refs_14_), channel_id=1, source_target_pairs={{0,1},{1,0},{2,3},{3,2},{4,5},{5,4},{6,7},{7,6},{8,9},{9,8},{10,11... | collective-permute-start | bytes 983048 | tf_op jit(solution)/shard_map/ppermute | solution.py:827
  61.5 10.7 %collective-permute-start.17 = (bf16[80,2048]{1,0:T(8,128)(2,1)S(1)}, bf16[80,2048]{1,0:T(8,128)(2,1)S(1)}, u32[]{:S(2)}, u32[]{:S(2)}) collective-permute-start(bf16[80,2048]{1,0:T(8,128)(2,1)S(1)} %collective-permute-done.16.rest_2_.refs_14_), channel_id=1, source_target_pairs={{0,4},{4,0},{8,12},{12,8},{16,20},{20,16},{24,28},{28,24},{1,5},{5... | collective-permute-start | bytes 983048 | tf_op jit(solution)/shard_map/ppermute | solution.py:827
  63.0 9.8 %collective-permute-start.21 = (bf16[256,640]{1,0:T(8,128)(2,1)S(1)}, bf16[256,640]{1,0:T(8,128)(2,1)S(1)}, u32[]{:S(2)}, u32[]{:S(2)}) collective-permute-start(bf16[256,640]{1,0:T(8,128)(2,1)S(1)} %get-tuple-element.177), channel_id=1, source_target_pairs={{0,2},{1,3},{2,0},{3,1},{4,6},{5,7},{6,4},{7,5},{8,10},{9,11},{10,... | collective-permute-start | bytes 983048 | tf_op jit(solution)/shard_map/ppermute | solution.py:827
  72.2 10.7 %collective-permute-start.20 = (bf16[512,640]{1,0:T(8,128)(2,1)S(1)}, bf16[512,640]{1,0:T(8,128)(2,1)S(1)}, u32[]{:S(2)}, u32[]{:S(2)}) collective-permute-start(bf16[512,640]{1,0:T(8,128)(2,1)S(1)} %copy-done.17), channel_id=1, source_target_pairs={{0,1},{1,0},{2,3},{3,2},{4,5},{5,4},{6,7},{7,6},{8,9},{9,8},{10,11... | collective-permute-start | bytes 1966088 | tf_op jit(solution)/shard_map/ppermute | solution.py:827
  72.8 10.2 %collective-permute-start.23 = (bf16[256,640]{1,0:T(8,128)(2,1)S(1)}, bf16[256,640]{1,0:T(8,128)(2,1)S(1)}, u32[]{:S(2)}, u32[]{:S(2)}) collective-permute-start(bf16[256,640]{1,0:T(8,128)(2,1)S(1)} %collective-permute-done.21.rest_2_), channel_id=1, source_target_pairs={{0,1},{1,0},{2,3},{3,2},{4,5},{5,4},{6,7},{7,6},{8,9},{9,8},{10,11... | collective-permute-start | bytes 983048 | tf_op jit(solution)/shard_map/ppermute | solution.py:827
  72.8 10.1 %collective-permute-start.22 = (bf16[256,640]{1,0:T(8,128)(2,1)S(1)}, bf16[256,640]{1,0:T(8,128)(2,1)S(1)}, u32[]{:S(2)}, u32[]{:S(2)}) collective-permute-start(bf16[256,640]{1,0:T(8,128)(2,1)S(1)} %collective-permute-done.21.rest_2_), channel_id=1, source_target_pairs={{0,4},{4,0},{8,12},{12,8},{16,20},{20,16},{24,28},{28,24},{1,5},{5... | collective-permute-start | bytes 983048 | tf_op jit(solution)/shard_map/ppermute | solution.py:827
  95.6 11.9 %collective-permute-start.25 = (bf16[2,2560,128]{2,1,0:T(8,128)(2,1)S(1)}, bf16[2,2560,128]{2,1,0:T(8,128)(2,1)S(1)}, u32[]{:S(2)}, u32[]{:S(2)}) collective-permute-start(bf16[2,2560,128]{2,1,0:T(8,128)(2,1)S(1)} %bitcast.39), channel_id=1, source_target_pairs={{0,1},{1,0},{2,3},{3,2},{4,5},{5,4},{6,7},{7,6},{8,9},{9,8},{10,11... | collective-permute-start | bytes 3932168 | tf_op jit(solution)/shard_map/ppermute | solution.py:938
  107.0 14.6 %collective-permute-start.27 = (bf16[2,2560,128]{2,1,0:T(8,128)(2,1)S(1)}, bf16[2,2560,128]{2,1,0:T(8,128)(2,1)S(1)}, u32[]{:S(2)}, u32[]{:S(2)}) collective-permute-start(bf16[2,2560,128]{2,1,0:T(8,128)(2,1)S(1)} %bitcast.38), channel_id=1, source_target_pairs={{0,1},{1,0},{2,3},{3,2},{4,5},{5,4},{6,7},{7,6},{8,9},{9,8},{10,11... | collective-permute-start | bytes 3932168 | tf_op jit(solution)/shard_map/ppermute | solution.py:938
  108.8 12.9 %collective-permute-start.26 = (bf16[2,1280,128]{2,1,0:T(8,128)(2,1)S(1)}, bf16[2,1280,128]{2,1,0:T(8,128)(2,1)S(1)}, u32[]{:S(2)}, u32[]{:S(2)}) collective-permute-start(bf16[2,1280,128]{2,1,0:T(8,128)(2,1)S(1)} %get-tuple-element.188), channel_id=1, source_target_pairs={{0,2},{1,5},{2,0},{3,7},{4,6},{5,1},{6,4},{7,3},{8,10},{9,13},{10,... | collective-permute-start | bytes 1966088 | tf_op jit(solution)/shard_map/ppermute | solution.py:938
  123.7 14.2 %collective-permute-start.29 = (bf16[2,1280,128]{2,1,0:T(8,128)(2,1)S(1)}, bf16[2,1280,128]{2,1,0:T(8,128)(2,1)S(1)}, u32[]{:S(2)}, u32[]{:S(2)}) collective-permute-start(bf16[2,1280,128]{2,1,0:T(8,128)(2,1)S(1)} %get-tuple-element.199), channel_id=1, source_target_pairs={{0,2},{1,5},{2,0},{3,7},{4,6},{5,1},{6,4},{7,3},{8,10},{9,13},{10,... | collective-permute-start | bytes 1966088 | tf_op jit(solution)/shard_map/ppermute | solution.py:938
  124.2 26.3 %collective-permute-start.32 = (bf16[2,2560,128]{2,1,0:T(8,128)(2,1)S(1)}, bf16[2,2560,128]{2,1,0:T(8,128)(2,1)S(1)}, u32[]{:S(2)}, u32[]{:S(2)}) collective-permute-start(bf16[2,2560,128]{2,1,0:T(8,128)(2,1)S(1)} %bitcast.37), channel_id=1, source_target_pairs={{0,1},{1,0},{2,3},{3,2},{4,5},{5,4},{6,7},{7,6},{8,9},{9,8},{10,11... | collective-permute-start | bytes 3932168 | tf_op jit(solution)/shard_map/ppermute | solution.py:938
  124.2 10.6 %collective-permute-start.28 = (bf16[1280,128]{1,0:T(8,128)(2,1)S(1)}, bf16[1280,128]{1,0:T(8,128)(2,1)S(1)}, u32[]{:S(2)}, u32[]{:S(2)}) collective-permute-start(bf16[1280,128]{1,0:T(8,128)(2,1)S(1)} %get-tuple-element.195), channel_id=1, source_target_pairs={{0,4},{1,3},{2,6},{3,1},{4,0},{5,7},{6,2},{7,5},{8,12},{9,11},{10,... | collective-permute-start | bytes 983048 | tf_op jit(solution)/shard_map/ppermute | solution.py:938
  134.1 12.0 %collective-permute-start.33 = (bf16[2,1280,128]{2,1,0:T(8,128)(2,1)S(1)}, bf16[2,1280,128]{2,1,0:T(8,128)(2,1)S(1)}, u32[]{:S(2)}, u32[]{:S(2)}) collective-permute-start(bf16[2,1280,128]{2,1,0:T(8,128)(2,1)S(1)} %bitcast.40), channel_id=1, source_target_pairs={{0,1},{1,0},{2,3},{3,2},{4,5},{5,4},{6,7},{7,6},{8,9},{9,8},{10,11... | collective-permute-start | bytes 1966088 | tf_op jit(solution)/shard_map/ppermute | solution.py:938
  135.5 10.0 %collective-permute-start.30 = (bf16[640,128]{1,0:T(8,128)(2,1)S(1)}, bf16[640,128]{1,0:T(8,128)(2,1)S(1)}, u32[]{:S(2)}, u32[]{:S(2)}) collective-permute-start(bf16[640,128]{1,0:T(8,128)(2,1)S(1)} %get-tuple-element.210), channel_id=1, source_target_pairs={{0,8},{1,9},{2,10},{3,11},{4,12},{5,13},{6,14},{7,15},{8,0},{9,1},... | collective-permute-start | bytes 491528 | tf_op jit(solution)/shard_map/ppermute | solution.py:938
  138.5 12.0 %collective-permute-start.31 = (bf16[1280,128]{1,0:T(8,128)(2,1)S(1)}, bf16[1280,128]{1,0:T(8,128)(2,1)S(1)}, u32[]{:S(2)}, u32[]{:S(2)}) collective-permute-start(bf16[1280,128]{1,0:T(8,128)(2,1)S(1)} %get-tuple-element.213), channel_id=1, source_target_pairs={{0,4},{1,3},{2,6},{3,1},{4,0},{5,7},{6,2},{7,5},{8,12},{9,11},{10,... | collective-permute-start | bytes 983048 | tf_op jit(solution)/shard_map/ppermute | solution.py:938
  146.1 15.6 %collective-permute-start.34 = (bf16[640,128]{1,0:T(8,128)(2,1)S(1)}, bf16[640,128]{1,0:T(8,128)(2,1)S(1)}, u32[]{:S(2)}, u32[]{:S(2)}) collective-permute-start(bf16[640,128]{1,0:T(8,128)(2,1)S(1)} %mix_sum.8.k), channel_id=1, source_target_pairs={{0,16},{1,17},{2,18},{3,19},{4,20},{5,21},{6,22},{7,23},{8,24},{9,... | collective-permute-start | bytes 491528 | tf_op jit(solution)/shard_map/ppermute | solution.py:938
  148.8 14.1 %collective-permute-start.36 = (bf16[512,512]{1,0:T(8,128)(2,1)S(1)}, bf16[512,512]{1,0:T(8,128)(2,1)S(1)}, u32[]{:S(2)}, u32[]{:S(2)}) collective-permute-start(bf16[512,512]{1,0:T(8,128)(2,1)S(1)} %get-tuple-element.244), channel_id=1, source_target_pairs={{1,0},{2,1},{3,2},{4,3},{5,4},{6,5},{7,6},{9,8},{10,9},{11,10},{12... | collective-permute-start | bytes 1572872 | tf_op jit(solution)/shard_map/ppermute | solution.py:1269
  151.1 11.2 %collective-permute-start.35 = (bf16[640,128]{1,0:T(8,128)(2,1)S(1)}, bf16[640,128]{1,0:T(8,128)(2,1)S(1)}, u32[]{:S(2)}, u32[]{:S(2)}) collective-permute-start(bf16[640,128]{1,0:T(8,128)(2,1)S(1)} %get-tuple-element.225), channel_id=1, source_target_pairs={{0,8},{1,9},{2,10},{3,11},{4,12},{5,13},{6,14},{7,15},{8,0},{9,1},... | collective-permute-start | bytes 491528 | tf_op jit(solution)/shard_map/ppermute | solution.py:938
  154.4 14.9 %collective-permute-start.37 = (bf16[2,1920,128]{2,1,0:T(8,128)(2,1)S(1)}, bf16[2,1920,128]{2,1,0:T(8,128)(2,1)S(1)}, u32[]{:S(2)}, u32[]{:S(2)}) collective-permute-start(bf16[2,1920,128]{2,1,0:T(8,128)(2,1)S(1)} %get-tuple-element.232), channel_id=1, source_target_pairs={{0,2},{1,5},{2,0},{3,7},{4,6},{5,1},{6,4},{7,3},{8,10},{9,13},{10,... | collective-permute-start | bytes 2949128 | tf_op jit(solution)/shard_map/ppermute | solution.py:938
  167.4 11.5 %collective-permute-start.39 = (bf16[2,2048,128]{2,1,0:T(8,128)(2,1)S(1)}, bf16[2,2048,128]{2,1,0:T(8,128)(2,1)S(1)}, u32[]{:S(2)}, u32[]{:S(2)}) collective-permute-start(bf16[2,2048,128]{2,1,0:T(8,128)(2,1)S(1)} %get-tuple-element.260), channel_id=1, source_target_pairs={{0,1},{1,0},{2,3},{3,2},{4,5},{5,4},{6,7},{7,6},{8,9},{9,8},{10,11... | collective-permute-start | bytes 3145736 | tf_op jit(solution)/shard_map/ppermute | solution.py:938
  167.4 10.9 %collective-permute-start.38 = (bf16[640,128]{1,0:T(8,128)(2,1)S(1)}, bf16[640,128]{1,0:T(8,128)(2,1)S(1)}, u32[]{:S(2)}, u32[]{:S(2)}) collective-permute-start(bf16[640,128]{1,0:T(8,128)(2,1)S(1)} %mix_sum.10.k), channel_id=1, source_target_pairs={{0,16},{1,17},{2,18},{3,19},{4,20},{5,21},{6,22},{7,23},{8,24},{9,... | collective-permute-start | bytes 491528 | tf_op jit(solution)/shard_map/ppermute | solution.py:938
  170.1 10.6 %collective-permute-start.40 = (bf16[1920,128]{1,0:T(8,128)(2,1)S(1)}, bf16[1920,128]{1,0:T(8,128)(2,1)S(1)}, u32[]{:S(2)}, u32[]{:S(2)}) collective-permute-start(bf16[1920,128]{1,0:T(8,128)(2,1)S(1)} %get-tuple-element.255), channel_id=1, source_target_pairs={{0,4},{1,3},{2,6},{3,1},{4,0},{5,7},{6,2},{7,5},{8,12},{9,11},{10,... | collective-permute-start | bytes 1474568 | tf_op jit(solution)/shard_map/ppermute | solution.py:938
  180.0 9.2 %collective-permute-start.41 = (bf16[2,1024,128]{2,1,0:T(8,128)(2,1)S(1)}, bf16[2,1024,128]{2,1,0:T(8,128)(2,1)S(1)}, u32[]{:S(2)}, u32[]{:S(2)}) collective-permute-start(bf16[2,1024,128]{2,1,0:T(8,128)(2,1)S(1)} %get-tuple-element.264), channel_id=1, source_target_pairs={{0,2},{1,5},{2,0},{3,7},{4,6},{5,1},{6,4},{7,3},{8,10},{9,13},{10,... | collective-permute-start | bytes 1572872 | tf_op jit(solution)/shard_map/ppermute | solution.py:938
  181.3 9.5 %collective-permute-start.42 = (bf16[960,128]{1,0:T(8,128)(2,1)S(1)}, bf16[960,128]{1,0:T(8,128)(2,1)S(1)}, u32[]{:S(2)}, u32[]{:S(2)}) collective-permute-start(bf16[960,128]{1,0:T(8,128)(2,1)S(1)} %get-tuple-element.267), channel_id=1, source_target_pairs={{0,8},{1,9},{2,10},{3,11},{4,12},{5,13},{6,14},{7,15},{8,0},{9,1},... | collective-permute-start | bytes 737288 | tf_op jit(solution)/shard_map/ppermute | solution.py:938
  190.0 9.2 %collective-permute-start.43 = (bf16[1024,128]{1,0:T(8,128)(2,1)S(1)}, bf16[1024,128]{1,0:T(8,128)(2,1)S(1)}, u32[]{:S(2)}, u32[]{:S(2)}) collective-permute-start(bf16[1024,128]{1,0:T(8,128)(2,1)S(1)} %get-tuple-element.272), channel_id=1, source_target_pairs={{0,4},{1,3},{2,6},{3,1},{4,0},{5,7},{6,2},{7,5},{8,12},{9,11},{10,... | collective-permute-start | bytes 786440 | tf_op jit(solution)/shard_map/ppermute | solution.py:938
  191.4 12.9 %collective-permute-start.44 = (bf16[960,128]{1,0:T(8,128)(2,1)S(1)}, bf16[960,128]{1,0:T(8,128)(2,1)S(1)}, u32[]{:S(2)}, u32[]{:S(2)}) collective-permute-start(bf16[960,128]{1,0:T(8,128)(2,1)S(1)} %mix_sum.12.k), channel_id=1, source_target_pairs={{0,16},{1,17},{2,18},{3,19},{4,20},{5,21},{6,22},{7,23},{8,24},{9,... | collective-permute-start | bytes 737288 | tf_op jit(solution)/shard_map/ppermute | solution.py:938
  192.5 17.2 %collective-permute-start.58 = (bf16[640,128]{1,0:T(8,128)(2,1)S(1)}, bf16[640,128]{1,0:T(8,128)(2,1)S(1)}, u32[]{:S(2)}, u32[]{:S(2)}) collective-permute-start(bf16[640,128]{1,0:T(8,128)(2,1)S(1)} %mix_sum.9.refs_0_), channel_id=1, source_target_pairs={{0,12},{1,13},{2,14},{3,15},{4,8},{5,9},{6,10},{7,11},{8,4},{9,5},... | collective-permute-start | bytes 491528 | tf_op jit(solution)/shard_map/ppermute | solution.py:938
  199.8 12.0 %collective-permute-start.57 = (bf16[640,128]{1,0:T(8,128)(2,1)S(1)}, bf16[640,128]{1,0:T(8,128)(2,1)S(1)}, u32[]{:S(2)}, u32[]{:S(2)}) collective-permute-start(bf16[640,128]{1,0:T(8,128)(2,1)S(1)} %mix_sum.9.refs_0_), channel_id=1, source_target_pairs={{0,8},{1,9},{2,10},{3,11},{4,12},{5,13},{6,14},{7,15},{8,0},{9,1},... | collective-permute-start | bytes 491528 | tf_op jit(solution)/shard_map/ppermute | solution.py:938
  201.8 10.0 %collective-permute-start.56 = (bf16[640,128]{1,0:T(8,128)(2,1)S(1)}, bf16[640,128]{1,0:T(8,128)(2,1)S(1)}, u32[]{:S(2)}, u32[]{:S(2)}) collective-permute-start(bf16[640,128]{1,0:T(8,128)(2,1)S(1)} %mix_sum.9.refs_0_), channel_id=1, source_target_pairs={{0,4},{1,5},{2,6},{3,7},{4,0},{5,1},{6,2},{7,3},{8,12},{9,13},{10,... | collective-permute-start | bytes 491528 | tf_op jit(solution)/shard_map/ppermute | solution.py:938
  204.3 13.3 %collective-permute-start.52 = (bf16[640,128]{1,0:T(8,128)(2,1)S(1)}, bf16[640,128]{1,0:T(8,128)(2,1)S(1)}, u32[]{:S(2)}, u32[]{:S(2)}) collective-permute-start(bf16[640,128]{1,0:T(8,128)(2,1)S(1)} %mix_sum.11.refs_0_), channel_id=1, source_target_pairs={{0,12},{1,13},{2,14},{3,15},{4,8},{5,9},{6,10},{7,11},{8,4},{9,5},... | collective-permute-start | bytes 491528 | tf_op jit(solution)/shard_map/ppermute | solution.py:938
  207.7 9.9 %collective-permute-start.46 = (bf16[512,128]{1,0:T(8,128)(2,1)S(1)}, bf16[512,128]{1,0:T(8,128)(2,1)S(1)}, u32[]{:S(2)}, u32[]{:S(2)}) collective-permute-start(bf16[512,128]{1,0:T(8,128)(2,1)S(1)} %mix_sum.14.k), channel_id=1, source_target_pairs={{0,16},{1,17},{2,18},{3,19},{4,20},{5,21},{6,22},{7,23},{8,24},{9,... | collective-permute-start | bytes 393224 | tf_op jit(solution)/shard_map/ppermute | solution.py:938
  209.7 18.7 %collective-permute-start.55 = (bf16[960,128]{1,0:T(8,128)(2,1)S(1)}, bf16[960,128]{1,0:T(8,128)(2,1)S(1)}, u32[]{:S(2)}, u32[]{:S(2)}) collective-permute-start(bf16[960,128]{1,0:T(8,128)(2,1)S(1)} %mix_sum.13.refs_4_), channel_id=1, source_target_pairs={{0,12},{1,13},{2,14},{3,15},{4,8},{5,9},{6,10},{7,11},{8,4},{9,5},... | collective-permute-start | bytes 737288 | tf_op jit(solution)/shard_map/ppermute | solution.py:938
  211.8 13.7 %collective-permute-start.51 = (bf16[640,128]{1,0:T(8,128)(2,1)S(1)}, bf16[640,128]{1,0:T(8,128)(2,1)S(1)}, u32[]{:S(2)}, u32[]{:S(2)}) collective-permute-start(bf16[640,128]{1,0:T(8,128)(2,1)S(1)} %mix_sum.11.refs_0_), channel_id=1, source_target_pairs={{0,8},{1,9},{2,10},{3,11},{4,12},{5,13},{6,14},{7,15},{8,0},{9,1},... | collective-permute-start | bytes 491528 | tf_op jit(solution)/shard_map/ppermute | solution.py:938
  211.8 14.1 %collective-permute-start.50 = (bf16[640,128]{1,0:T(8,128)(2,1)S(1)}, bf16[640,128]{1,0:T(8,128)(2,1)S(1)}, u32[]{:S(2)}, u32[]{:S(2)}) collective-permute-start(bf16[640,128]{1,0:T(8,128)(2,1)S(1)} %mix_sum.11.refs_0_), channel_id=1, source_target_pairs={{0,4},{1,5},{2,6},{3,7},{4,0},{5,1},{6,2},{7,3},{8,12},{9,13},{10,... | collective-permute-start | bytes 491528 | tf_op jit(solution)/shard_map/ppermute | solution.py:938
  217.6 13.2 %collective-permute-start.54 = (bf16[960,128]{1,0:T(8,128)(2,1)S(1)}, bf16[960,128]{1,0:T(8,128)(2,1)S(1)}, u32[]{:S(2)}, u32[]{:S(2)}) collective-permute-start(bf16[960,128]{1,0:T(8,128)(2,1)S(1)} %mix_sum.13.refs_4_), channel_id=1, source_target_pairs={{0,8},{1,9},{2,10},{3,11},{4,12},{5,13},{6,14},{7,15},{8,0},{9,1},... | collective-permute-start | bytes 737288 | tf_op jit(solution)/shard_map/ppermute | solution.py:938
  217.6 13.2 %collective-permute-start.53 = (bf16[960,128]{1,0:T(8,128)(2,1)S(1)}, bf16[960,128]{1,0:T(8,128)(2,1)S(1)}, u32[]{:S(2)}, u32[]{:S(2)}) collective-permute-start(bf16[960,128]{1,0:T(8,128)(2,1)S(1)} %mix_sum.13.refs_4_), channel_id=1, source_target_pairs={{0,4},{1,5},{2,6},{3,7},{4,0},{5,1},{6,2},{7,3},{8,12},{9,13},{10,... | collective-permute-start | bytes 737288 | tf_op jit(solution)/shard_map/ppermute | solution.py:938
  (53 other events, 314.7 us)
